TPU v7x, 32 devices: a whole 2x2x4 slice. The times are simulated.
32 devices in a mesh: group: 2 (over y), row: 8 (over z, x), probe: 2 (over core).
Axes of the slice: x: 2, y: 2, z: 4, core: 2. Of those that a mesh axis runs over, the one named last changes fastest.
Arguments:
- observations: float32 [4, 64, 8192], P('group', 'row'), parts along dimension 0, may hold values from -3 to 3
- coefficients: float32 [18, 64, 8192], P('group', 'row'), parts along dimension 0, may hold values from -0.25 to 3, as said below
- probes: float32 [4, 4, 64, 8192], P('probe', 'group', 'row'), parts along dimension 1, may hold values from -6 to 6
Outputs:
- gradient: float32 [18, 64, 8192], P('group', 'row', 'probe'), parts along dimension 0
There are 2 independent parts, one for each index of `group`. A program takes and returns all parts, laid end to end along the dimension named above; each array names one. Nothing has to cross between parts.
Inputs may be any that keep to these rules, and one draw needn't show every extreme that they name: `coefficients`: channels 0 and 1 lie in [1, 3], channels 2 and 3 in [0.25, 1], channels 4 and 5 in [0.9, 1], channels 6 and 7 in [-0.25, 0.25], channel 8 in [-0.2, 0.2].
All inputs are finite; a program needn't handle non-finite values.
Results may differ from a plain program's by a relative error of at most 0.00002.
Values sent between devices are 32-bit elements; how exact they have to be, the bound alone decides.
No kernel may reach another device: no remote copies, remote signals or barrier semaphores. Data moves between devices by JAX's collectives and lax.ppermute only.
A program may use at most 64 MiB of HBM per device.

v0:
```python
import math

import jax
import jax.numpy as jnp
from jax import lax
from jax.sharding import PartitionSpec as P

CHEB = 6


lower_edge = 0.25
upper_edge = 12.0


def extended(shard, sides, width):
    for axis, dim in sides:
        size, length = (lax.axis_size(axis), shard.shape[dim])
        up = [(i, (i + 1) % size) for i in range(size - 1)]
        down = [(j, i) for i, j in up]
        last = lax.slice_in_dim(shard, length - width, length, axis=dim)
        initial = lax.slice_in_dim(shard, 0, width, axis=dim)
        before = lax.ppermute(last, axis, up)
        after = lax.ppermute(initial, axis, down)
        shard = jnp.concatenate([before, shard, after], axis=dim)
    return shard


def cheb_weights(degree, low_end, high_end):
    count = degree + 1
    values = []
    for order in range(count):
        accum = 0.0
        for node in range(count):
            angle = math.pi * (node + 0.5) / count
            point = 0.5 * (high_end - low_end) * math.cos(angle) + 0.5 * (high_end + low_end)
            accum += math.cos(order * angle) / point
        accum = accum * 2.0 / count
        if order == 0:
            accum = accum * 0.5
        values.append(accum)
    return values


def stencil_terms(padded):
    spread = [(0, 0)] * (padded.ndim - 1) + [(1, 1)]
    wide = jnp.pad(padded, spread)
    center = wide[..., 1:-1, 1:-1]
    across = wide[..., 1:-1, 2:] - 2.0 * center + wide[..., 1:-1, :-2]
    along = wide[..., 2:, 1:-1] - 2.0 * center + wide[..., :-2, 1:-1]
    skewed = (
        wide[..., 2:, 2:] - wide[..., 2:, :-2] - wide[..., :-2, 2:] + wide[..., :-2, :-2]
    ) * 0.25
    return (center, across, along, skewed)


def apply_operator(coefficients, padded):
    center, across, along, skewed = stencil_terms(padded)
    return (
        coefficients[0:2] * center
        - coefficients[2:4] * across
        - coefficients[4:6] * along
        - 2.0 * coefficients[6:8] * skewed
        + coefficients[8] * jnp.flip(center, axis=-3)
    )


def scaled(coefficients, padded):
    center = padded[..., 1:-1, :]
    return (2.0 * apply_operator(coefficients, padded) - (lower_edge + upper_edge) * center) / (
        upper_edge - lower_edge
    )


def gradient_terms(left, right_padded):
    center, across, along, skewed = stencil_terms(right_padded)
    cross_term = (
        left[..., 0:1, :, :] * center[..., 1:2, :, :]
        + left[..., 1:2, :, :] * center[..., 0:1, :, :]
    )
    return jnp.concatenate(
        (left * center, -left * across, -left * along, -2.0 * left * skewed, cross_term), axis=-3
    )


def per_device(observations, coefficients, probes):
    weights = cheb_weights(CHEB, lower_edge, upper_edge)

    def product(field):
        return scaled(coefficients, extended(field, (("row", 2),), 1))

    previous = probes
    current = product(previous)
    series = weights[0] * previous + weights[1] * current
    for degree in range(2, CHEB + 1):
        following = 2.0 * product(current) - previous
        series = series + weights[degree] * following
        previous, current = (current, following)
    flat_series = series.reshape((-1,) + series.shape[2:])
    joined = extended(jnp.concatenate((flat_series, observations), axis=0), (("row", 1),), 1)
    count = flat_series.shape[0]
    series_wide = joined[:count].reshape(series.shape[:2] + joined.shape[1:])
    observed_wide = joined[count:]
    probe_sum = jnp.sum(gradient_terms(probes, series_wide), axis=0)
    data_part = gradient_terms(observations, observed_wide)
    share = probe_sum.shape[-1] // lax.axis_size("probe")
    offset = lax.axis_index("probe") * share
    summed = lax.psum_scatter(probe_sum, "probe", scatter_dimension=2, tiled=True)
    own_data = lax.dynamic_slice_in_dim(data_part, offset, share, 2)
    total_probes = probes.shape[0] * lax.axis_size("probe")
    return 0.5 / total_probes * summed - 0.5 * own_data


def solution(mesh):
    in_specs = (P("group", "row", None), P("group", "row", None), P("probe", "group", "row", None))
    out_specs = P("group", "row", "probe")
    return jax.shard_map(
        per_device, mesh=mesh, in_specs=in_specs, out_specs=out_specs, check_vma=False
    )
```

profile of v0, /device:TPU:0, one launch (start us, length us, event | category | flops | bytes accessed | tf_op | source)
XLA Modules:
  0.0 145.0 jit_solution(6990375353570962203)
XLA Ops:
  6.5 1.7 %fusion.109 = (f32[2,2,1,8192]{3,2,1,0:T(1,128)S(1)}, f32[2,2,1,8192]{3,2,1,0:T(1,128)S(1)}) fusion(f32[2,2,8,8192]{3,2,1,0:T(8,128)} %param.5), kind=kLoop, calls=%fused_computation.201 | loop fusion | bytes 524288 | tf_op jit(solution)/shard_map/slice | solution.py:20
  8.3 4.8 %collective-permute-start = (f32[2,2,1,8192]{3,2,1,0:T(1,128)S(1)}, f32[2,2,1,8192]{3,2,1,0:T(1,128)S(1)}, u32[]{:S(2)}, u32[]{:S(2)}) collective-permute-start(f32[2,2,1,8192]{3,2,1,0:T(1,128)S(1)} %get-tuple-element.24), channel_id=1, source_target_pairs={{0,2},{2,4},{4,6},{6,8},{8,10},{10,12},{12,14},{1,3},{3,5},{5,7},{... | collective-permute-start | bytes 393224 | tf_op jit(solution)/shard_map/ppermute | solution.py:22
  13.1 1.4 collective-permute-start.1
  14.6 1.7 %broadcast_multiply_fusion.1 = (f32[2,8,8192]{2,1,0:T(8,128)S(1)}, f32[2,8,8192]{2,1,0:T(8,128)S(1)}, f32[2,8,8192]{2,1,0:T(8,128)S(1)}, f32[2,8,8192]{2,1,0:T(8,128)S(1)}, f32[2,8,8192]{2,1,0:T(8,128)S(1)}) fusion(f32[9,8,8192]{2,1,0:T(8,128)} %param.4), kind=kLoop, calls=%fused_computation.191 | loop fusion | flops 262144 | bytes 4718592 | tf_op jit(solution)/shard_map/mul | solution.py:59
  17.3 2.8 %collective-permute-done.1 = f32[2,2,1,8192]{3,2,1,0:T(1,128)S(1)} collective-permute-done((f32[2,2,1,8192]{3,2,1,0:T(1,128)S(1)}, f32[2,2,1,8192]{3,2,1,0:T(1,128)S(1)}, u32[]{:S(2)}, u32[]{:S(2)}) %collective-permute-start.1) | collective-permute-done | bytes 131104 | tf_op jit(solution)/shard_map/ppermute | solution.py:23
  20.1 1.2 select_maximum_fusion.10
  21.3 1.6 %broadcast_multiply_fusion = (f32[2,2,8,8192]{3,2,1,0:T(8,128)S(1)}, f32[2,2,8,8192]{3,2,1,0:T(8,128)S(1)}) fusion(f32[2,2,8,8192]{3,2,1,0:T(8,128)S(1)} %copy-done, f32[8,8192]{1,0:T(8,128)S(1)} %slice_bitcast_fusion, f32[2,8,8192]{2,1,0:T(8,128)S(1)} %get-tuple-element.11, f32[2,2,10,8194]{3,2,1,0:T(8,128)S(1)} %select_maximum_fusion.10, ...), kind=kLoop, calls=%fused_computation.188 | loop fusion | flops 6029312 | bytes 12058624 | tf_op jit(solution)/shard_map/div | solution.py:69
  23.1 4.4 %collective-permute-start.2 = (f32[2,2,1,8192]{3,2,1,0:T(1,128)S(1)}, f32[2,2,1,8192]{3,2,1,0:T(1,128)S(1)}, u32[]{:S(2)}, u32[]{:S(2)}) collective-permute-start(f32[2,2,1,8192]{3,2,1,0:T(1,128)S(1)} %get-tuple-element.22), channel_id=1, source_target_pairs={{0,2},{2,4},{4,6},{6,8},{8,10},{10,12},{12,14},{1,3},{3,5},{5,7},{... | collective-permute-start | bytes 393224 | tf_op jit(solution)/shard_map/ppermute | solution.py:22
  27.5 1.3 collective-permute-start.3
  30.0 4.4 %collective-permute-done.3 = f32[2,2,1,8192]{3,2,1,0:T(1,128)S(1)} collective-permute-done((f32[2,2,1,8192]{3,2,1,0:T(1,128)S(1)}, f32[2,2,1,8192]{3,2,1,0:T(1,128)S(1)}, u32[]{:S(2)}, u32[]{:S(2)}) %collective-permute-start.3) | collective-permute-done | bytes 131104 | tf_op jit(solution)/shard_map/ppermute | solution.py:23
  34.3 1.2 select_maximum_fusion.8
  35.5 1.8 %fusion.74 = f32[2,2,8,8192]{3,2,1,0:T(8,128)S(1)} fusion(f32[2,2,8,8192]{3,2,1,0:T(8,128)S(1)} %copy-done, f32[2,2,10,8194]{3,2,1,0:T(8,128)S(1)} %select_maximum_fusion.8, f32[2,2,8,8192]{3,2,1,0:T(8,128)S(1)} %get-tuple-element.5, f32[2,2,1,8192]{3,2,1,0:T(1,128)S(1)} %collective-permute-done.2, f32[2,2,1,8192]{3,2,1,0:T(1,128)S(1)} %collective-permute-done.3, ...), kind=kLoop, calls=%fused_computation.132 | loop fusion | flops 6291456 | bytes 13107200 | tf_op jit(solution)/shard_map/sub | solution.py:95
  37.4 3.8 %collective-permute-start.4 = (f32[2,2,1,8192]{3,2,1,0:T(1,128)S(1)}, f32[2,2,1,8192]{3,2,1,0:T(1,128)S(1)}, u32[]{:S(2)}, u32[]{:S(2)}) collective-permute-start(f32[2,2,1,8192]{3,2,1,0:T(1,128)S(1)} %get-tuple-element.20), channel_id=1, source_target_pairs={{0,2},{2,4},{4,6},{6,8},{8,10},{10,12},{12,14},{1,3},{3,5},{5,7},{... | collective-permute-start | bytes 393224 | tf_op jit(solution)/shard_map/ppermute | solution.py:22
  41.3 1.3 collective-permute-start.5
  42.6 2.6 %collective-permute-done.4 = f32[2,2,1,8192]{3,2,1,0:T(1,128)S(1)} collective-permute-done((f32[2,2,1,8192]{3,2,1,0:T(1,128)S(1)}, f32[2,2,1,8192]{3,2,1,0:T(1,128)S(1)}, u32[]{:S(2)}, u32[]{:S(2)}) %collective-permute-start.4) | collective-permute-done | bytes 131104 | tf_op jit(solution)/shard_map/ppermute | solution.py:22
  45.2 3.0 %collective-permute-done.5 = f32[2,2,1,8192]{3,2,1,0:T(1,128)S(1)} collective-permute-done((f32[2,2,1,8192]{3,2,1,0:T(1,128)S(1)}, f32[2,2,1,8192]{3,2,1,0:T(1,128)S(1)}, u32[]{:S(2)}, u32[]{:S(2)}) %collective-permute-start.5) | collective-permute-done | bytes 131104 | tf_op jit(solution)/shard_map/ppermute | solution.py:23
  48.1 1.2 select_maximum_fusion.6
  49.3 1.8 %fusion.61 = f32[2,2,8,8192]{3,2,1,0:T(8,128)S(1)} fusion(f32[2,2,10,8194]{3,2,1,0:T(8,128)S(1)} %select_maximum_fusion.6, f32[2,2,8,8192]{3,2,1,0:T(8,128)S(1)} %fusion.74, f32[2,2,1,8192]{3,2,1,0:T(1,128)S(1)} %collective-permute-done.4, f32[2,2,1,8192]{3,2,1,0:T(1,128)S(1)} %collective-permute-done.5, f32[8,8192]{1,0:T(8,128)S(1)} %slice_bitcast_fusion, ...), kind=kLoop, calls=%fused_computation.112 | loop fusion | flops 6553600 | bytes 12058624 | tf_op jit(solution)/shard_map/sub | solution.py:95
  51.3 3.9 %collective-permute-start.6 = (f32[2,2,1,8192]{3,2,1,0:T(1,128)S(1)}, f32[2,2,1,8192]{3,2,1,0:T(1,128)S(1)}, u32[]{:S(2)}, u32[]{:S(2)}) collective-permute-start(f32[2,2,1,8192]{3,2,1,0:T(1,128)S(1)} %get-tuple-element.18), channel_id=1, source_target_pairs={{0,2},{2,4},{4,6},{6,8},{8,10},{10,12},{12,14},{1,3},{3,5},{5,7},{... | collective-permute-start | bytes 393224 | tf_op jit(solution)/shard_map/ppermute | solution.py:22
  55.2 1.3 collective-permute-start.7
  56.5 2.6 %collective-permute-done.6 = f32[2,2,1,8192]{3,2,1,0:T(1,128)S(1)} collective-permute-done((f32[2,2,1,8192]{3,2,1,0:T(1,128)S(1)}, f32[2,2,1,8192]{3,2,1,0:T(1,128)S(1)}, u32[]{:S(2)}, u32[]{:S(2)}) %collective-permute-start.6) | collective-permute-done | bytes 131104 | tf_op jit(solution)/shard_map/ppermute | solution.py:22
  59.1 3.0 %collective-permute-done.7 = f32[2,2,1,8192]{3,2,1,0:T(1,128)S(1)} collective-permute-done((f32[2,2,1,8192]{3,2,1,0:T(1,128)S(1)}, f32[2,2,1,8192]{3,2,1,0:T(1,128)S(1)}, u32[]{:S(2)}, u32[]{:S(2)}) %collective-permute-start.7) | collective-permute-done | bytes 131104 | tf_op jit(solution)/shard_map/ppermute | solution.py:23
  62.1 1.2 select_maximum_fusion.4
  63.3 1.8 %fusion.48 = f32[2,2,8,8192]{3,2,1,0:T(8,128)S(1)} fusion(f32[2,2,8,8192]{3,2,1,0:T(8,128)S(1)} %fusion.74, f32[2,2,10,8194]{3,2,1,0:T(8,128)S(1)} %select_maximum_fusion.4, f32[2,2,8,8192]{3,2,1,0:T(8,128)S(1)} %fusion.61, f32[2,2,1,8192]{3,2,1,0:T(1,128)S(1)} %collective-permute-done.6, f32[2,2,1,8192]{3,2,1,0:T(1,128)S(1)} %collective-permute-done.7, ...), kind=kLoop, calls=%fused_computation.92 | loop fusion | flops 6291456 | bytes 12058624 | tf_op jit(solution)/shard_map/sub | solution.py:95
  65.2 3.8 %collective-permute-start.8 = (f32[2,2,1,8192]{3,2,1,0:T(1,128)S(1)}, f32[2,2,1,8192]{3,2,1,0:T(1,128)S(1)}, u32[]{:S(2)}, u32[]{:S(2)}) collective-permute-start(f32[2,2,1,8192]{3,2,1,0:T(1,128)S(1)} %get-tuple-element.16), channel_id=1, source_target_pairs={{0,2},{2,4},{4,6},{6,8},{8,10},{10,12},{12,14},{1,3},{3,5},{5,7},{... | collective-permute-start | bytes 393224 | tf_op jit(solution)/shard_map/ppermute | solution.py:22
  69.1 1.5 %collective-permute-start.9 = (f32[2,2,1,8192]{3,2,1,0:T(1,128)S(1)}, f32[2,2,1,8192]{3,2,1,0:T(1,128)S(1)}, u32[]{:S(2)}, u32[]{:S(2)}) collective-permute-start(f32[2,2,1,8192]{3,2,1,0:T(1,128)S(1)} %get-tuple-element.17), channel_id=1, source_target_pairs={{2,0},{4,2},{6,4},{8,6},{10,8},{12,10},{14,12},{3,1},{5,3},{7,5},{... | collective-permute-start | bytes 393224 | tf_op jit(solution)/shard_map/ppermute | solution.py:23
  70.5 2.4 %collective-permute-done.8 = f32[2,2,1,8192]{3,2,1,0:T(1,128)S(1)} collective-permute-done((f32[2,2,1,8192]{3,2,1,0:T(1,128)S(1)}, f32[2,2,1,8192]{3,2,1,0:T(1,128)S(1)}, u32[]{:S(2)}, u32[]{:S(2)}) %collective-permute-start.8) | collective-permute-done | bytes 131104 | tf_op jit(solution)/shard_map/ppermute | solution.py:22
  72.9 3.0 %collective-permute-done.9 = f32[2,2,1,8192]{3,2,1,0:T(1,128)S(1)} collective-permute-done((f32[2,2,1,8192]{3,2,1,0:T(1,128)S(1)}, f32[2,2,1,8192]{3,2,1,0:T(1,128)S(1)}, u32[]{:S(2)}, u32[]{:S(2)}) %collective-permute-start.9) | collective-permute-done | bytes 131104 | tf_op jit(solution)/shard_map/ppermute | solution.py:23
  75.9 1.2 select_maximum_fusion.2
  77.1 1.8 %fusion.35 = f32[2,2,8,8192]{3,2,1,0:T(8,128)S(1)} fusion(f32[2,2,8,8192]{3,2,1,0:T(8,128)S(1)} %fusion.61, f32[2,2,10,8194]{3,2,1,0:T(8,128)S(1)} %select_maximum_fusion.2, f32[2,2,8,8192]{3,2,1,0:T(8,128)S(1)} %fusion.48, f32[2,2,1,8192]{3,2,1,0:T(1,128)S(1)} %collective-permute-done.8, f32[2,2,1,8192]{3,2,1,0:T(1,128)S(1)} %collective-permute-done.9, ...), kind=kLoop, calls=%fused_computation.72 | loop fusion | flops 6291456 | bytes 12058624 | tf_op jit(solution)/shard_map/sub | solution.py:95
  79.1 3.9 %collective-permute-start.10 = (f32[2,2,1,8192]{3,2,1,0:T(1,128)S(1)}, f32[2,2,1,8192]{3,2,1,0:T(1,128)S(1)}, u32[]{:S(2)}, u32[]{:S(2)}) collective-permute-start(f32[2,2,1,8192]{3,2,1,0:T(1,128)S(1)} %get-tuple-element.14), channel_id=1, source_target_pairs={{0,2},{2,4},{4,6},{6,8},{8,10},{10,12},{12,14},{1,3},{3,5},{5,7},{... | collective-permute-start | bytes 393224 | tf_op jit(solution)/shard_map/ppermute | solution.py:22
  83.0 1.3 collective-permute-start.11
  84.3 2.6 %collective-permute-done.10 = f32[2,2,1,8192]{3,2,1,0:T(1,128)S(1)} collective-permute-done((f32[2,2,1,8192]{3,2,1,0:T(1,128)S(1)}, f32[2,2,1,8192]{3,2,1,0:T(1,128)S(1)}, u32[]{:S(2)}, u32[]{:S(2)}) %collective-permute-start.10) | collective-permute-done | bytes 131104 | tf_op jit(solution)/shard_map/ppermute | solution.py:22
  86.9 3.0 %collective-permute-done.11 = f32[2,2,1,8192]{3,2,1,0:T(1,128)S(1)} collective-permute-done((f32[2,2,1,8192]{3,2,1,0:T(1,128)S(1)}, f32[2,2,1,8192]{3,2,1,0:T(1,128)S(1)}, u32[]{:S(2)}, u32[]{:S(2)}) %collective-permute-start.11) | collective-permute-done | bytes 131104 | tf_op jit(solution)/shard_map/ppermute | solution.py:23
  89.9 1.2 select_maximum_fusion
  91.0 2.1 %fusion.22 = f32[2,2,8,8192]{3,2,1,0:T(8,128)S(1)} fusion(f32[2,2,8,8192]{3,2,1,0:T(8,128)S(1)} %fusion.48, f32[2,2,10,8194]{3,2,1,0:T(8,128)S(1)} %select_maximum_fusion, f32[2,2,8,8192]{3,2,1,0:T(8,128)S(1)} %fusion.35, f32[2,2,1,8192]{3,2,1,0:T(1,128)S(1)} %collective-permute-done.10, f32[2,2,1,8192]{3,2,1,0:T(1,128)S(1)} %collective-permute-done.11, ...), kind=kLoop, calls=%fused_computation.52 | loop fusion | flops 9699328 | bytes 16252928 | tf_op jit(solution)/shard_map/add | solution.py:96
  93.6 3.8 %collective-permute-start.12 = (f32[6,1,8192]{2,0,1:T(8,128)S(1)}, f32[6,1,8192]{2,0,1:T(8,128)S(1)}, u32[]{:S(2)}, u32[]{:S(2)}) collective-permute-start(f32[6,1,8192]{2,0,1:T(8,128)S(1)} %copy.21), channel_id=1, source_target_pairs={{0,2},{2,4},{4,6},{6,8},{8,10},{10,12},{12,14},{1,3},{3,5},{5,7},{... | collective-permute-start | bytes 589832 | tf_op jit(solution)/shard_map/ppermute | solution.py:22
  97.5 1.3 collective-permute-start.13
  99.7 7.2 %collective-permute-done.12 = f32[6,1,8192]{2,0,1:T(8,128)S(1)} collective-permute-done((f32[6,1,8192]{2,0,1:T(8,128)S(1)}, f32[6,1,8192]{2,0,1:T(8,128)S(1)}, u32[]{:S(2)}, u32[]{:S(2)}) %collective-permute-start.12) | collective-permute-done | bytes 196640 | tf_op jit(solution)/shard_map/ppermute | solution.py:22
  108.8 1.6 %select_maximum_fusion.12 = f32[2,10,8194]{2,1,0:T(8,128)} fusion(f32[6,1,8192]{2,1,0:T(1,128)S(1)} %copy.24, f32[6,1,8192]{2,1,0:T(1,128)S(1)} %copy.23, f32[2,8,8192]{2,1,0:T(8,128)S(1)} %copy-done.1, f32[4,8,8192]{2,1,0:T(8,128)S(1)} %bitcast.13), kind=kLoop, calls=%fused_computation.25 | loop fusion | flops 1638800 | bytes 2621600 | tf_op jit(solution)/shard_map/slice | solution.py:102
  110.5 1.2 multiply_dynamic-update-slice_fusion
  111.7 1.6 %fusion.5 = f32[2,9,8,8192]{3,2,1,0:T(8,128)} fusion(f32[2,9,8,8192]{3,2,1,0:T(8,128)} %multiply_dynamic-update-slice_fusion, f32[2,2,10,8192]{3,2,1,0:T(8,128)S(1)} %bitcast.7, f32[2,2,8,8192]{3,2,1,0:T(8,128)S(1)} %copy-done), kind=kLoop, calls=%fused_computation.32 | loop fusion | flops 1310720 | bytes 5242880
  113.3 1.3 fusion.13
  114.6 2.1 %fusion.11 = f32[2,9,8,8192]{3,2,1,0:T(8,128)} fusion(f32[2,9,8,8192]{3,2,1,0:T(8,128)} %fusion.13, f32[2,2,10,8192]{3,2,1,0:T(8,128)S(1)} %bitcast.9, f32[2,2,8,8192]{3,2,1,0:T(8,128)S(1)} %copy-done), kind=kLoop, calls=%fused_computation.38 | loop fusion | flops 1572864 | bytes 3407872
  117.6 4.4 %reduce_sum.9 = f32[9,8,8192]{2,1,0:T(8,128)} reduce(f32[2,9,8,8192]{3,2,1,0:T(8,128)} %fusion.102, f32[]{:T(128)} %constant.46.clone.1), dimensions={0}, to_apply=%region_0.1 | reduce | flops 589824 | bytes 7077892 | tf_op jit(solution)/shard_map/reduce_sum | solution.py:103
  122.1 2.8 %fusion.100 = f32[9,8,8192]{2,1,0:T(8,128)} fusion(f32[9,8,8192]{2,1,0:T(8,128)} %multiply_dynamic-update-slice_fusion.1, f32[2,10,8194]{2,1,0:T(8,128)} %select_maximum_fusion.12, f32[2,8,8192]{2,1,0:T(8,128)S(1)} %copy-done.1), kind=kLoop, calls=%fused_computation.181 | loop fusion | flops 655360 | bytes 2097152
  127.8 7.6 %reduce-scatter.2.cloned.1.call-done = f32[9,8,4096]{2,1,0:T(8,128)} async-done(((f32[9,8,8192]{2,1,0:T(8,128)}), f32[9,8,4096]{2,1,0:T(8,128)}) %reduce-scatter.2.cloned.1.call-update) | async-done | bytes 1179664 | tf_op jit(solution)/shard_map/reduce_scatter | solution.py:107
  135.4 2.8 %multiply_subtract_fusion = f32[9,8,4096]{2,1,0:T(8,128)} fusion(f32[9,8,8192]{2,1,0:T(8,128)} %multiply_dynamic-update-slice_fusion.2, s32[]{:T(128)S(6)} %select_n.3, f32[9,8,4096]{2,1,0:T(8,128)} %reduce-scatter.2.cloned.1.call-done), kind=kLoop, calls=%fused_computation.24 | loop fusion | flops 884736 | bytes 3538948 | tf_op jit(solution)/shard_map/sub | solution.py:110
  (30 shorter events, 10.3 us)
Async XLA Ops:
  6.5 128.9 %reduce-scatter.2.cloned.1.call-start = ((), (), s32[]{:S(2)}) async-start(), calls=%async_computation.1 | async-start | bytes 3538944 | tf_op jit(solution)/shard_map/reduce_scatter | solution.py:107
  8.3 9.0 %collective-permute-start = (f32[2,2,1,8192]{3,2,1,0:T(1,128)S(1)}, f32[2,2,1,8192]{3,2,1,0:T(1,128)S(1)}, u32[]{:S(2)}, u32[]{:S(2)}) collective-permute-start(f32[2,2,1,8192]{3,2,1,0:T(1,128)S(1)} %get-tuple-element.24), channel_id=1, source_target_pairs={{0,2},{2,4},{4,6},{6,8},{8,10},{10,12},{12,14},{1,3},{3,5},{5,7},{... | collective-permute-start | bytes 393224 | tf_op jit(solution)/shard_map/ppermute | solution.py:22
  13.1 7.0 %copy-start = (f32[2,2,8,8192]{3,2,1,0:T(8,128)S(1)}, f32[2,2,8,8192]{3,2,1,0:T(8,128)}, u32[]{:S(2)}) copy-start(f32[2,2,8,8192]{3,2,1,0:T(8,128)} %param.5) | copy-start | bytes 3145732
  13.1 7.0 %collective-permute-start.1 = (f32[2,2,1,8192]{3,2,1,0:T(1,128)S(1)}, f32[2,2,1,8192]{3,2,1,0:T(1,128)S(1)}, u32[]{:S(2)}, u32[]{:S(2)}) collective-permute-start(f32[2,2,1,8192]{3,2,1,0:T(1,128)S(1)} %get-tuple-element.25), channel_id=1, source_target_pairs={{2,0},{4,2},{6,4},{8,6},{10,8},{12,10},{14,12},{3,1},{5,3},{7,5},{... | collective-permute-start | bytes 393224 | tf_op jit(solution)/shard_map/ppermute | solution.py:23
  23.1 6.9 %collective-permute-start.2 = (f32[2,2,1,8192]{3,2,1,0:T(1,128)S(1)}, f32[2,2,1,8192]{3,2,1,0:T(1,128)S(1)}, u32[]{:S(2)}, u32[]{:S(2)}) collective-permute-start(f32[2,2,1,8192]{3,2,1,0:T(1,128)S(1)} %get-tuple-element.22), channel_id=1, source_target_pairs={{0,2},{2,4},{4,6},{6,8},{8,10},{10,12},{12,14},{1,3},{3,5},{5,7},{... | collective-permute-start | bytes 393224 | tf_op jit(solution)/shard_map/ppermute | solution.py:22
  27.5 6.9 %collective-permute-start.3 = (f32[2,2,1,8192]{3,2,1,0:T(1,128)S(1)}, f32[2,2,1,8192]{3,2,1,0:T(1,128)S(1)}, u32[]{:S(2)}, u32[]{:S(2)}) collective-permute-start(f32[2,2,1,8192]{3,2,1,0:T(1,128)S(1)} %get-tuple-element.23), channel_id=1, source_target_pairs={{2,0},{4,2},{6,4},{8,6},{10,8},{12,10},{14,12},{3,1},{5,3},{7,5},{... | collective-permute-start | bytes 393224 | tf_op jit(solution)/shard_map/ppermute | solution.py:23
  37.4 7.7 %collective-permute-start.4 = (f32[2,2,1,8192]{3,2,1,0:T(1,128)S(1)}, f32[2,2,1,8192]{3,2,1,0:T(1,128)S(1)}, u32[]{:S(2)}, u32[]{:S(2)}) collective-permute-start(f32[2,2,1,8192]{3,2,1,0:T(1,128)S(1)} %get-tuple-element.20), channel_id=1, source_target_pairs={{0,2},{2,4},{4,6},{6,8},{8,10},{10,12},{12,14},{1,3},{3,5},{5,7},{... | collective-permute-start | bytes 393224 | tf_op jit(solution)/shard_map/ppermute | solution.py:22
  41.3 6.9 %collective-permute-start.5 = (f32[2,2,1,8192]{3,2,1,0:T(1,128)S(1)}, f32[2,2,1,8192]{3,2,1,0:T(1,128)S(1)}, u32[]{:S(2)}, u32[]{:S(2)}) collective-permute-start(f32[2,2,1,8192]{3,2,1,0:T(1,128)S(1)} %get-tuple-element.21), channel_id=1, source_target_pairs={{2,0},{4,2},{6,4},{8,6},{10,8},{12,10},{14,12},{3,1},{5,3},{7,5},{... | collective-permute-start | bytes 393224 | tf_op jit(solution)/shard_map/ppermute | solution.py:23
  51.3 7.8 %collective-permute-start.6 = (f32[2,2,1,8192]{3,2,1,0:T(1,128)S(1)}, f32[2,2,1,8192]{3,2,1,0:T(1,128)S(1)}, u32[]{:S(2)}, u32[]{:S(2)}) collective-permute-start(f32[2,2,1,8192]{3,2,1,0:T(1,128)S(1)} %get-tuple-element.18), channel_id=1, source_target_pairs={{0,2},{2,4},{4,6},{6,8},{8,10},{10,12},{12,14},{1,3},{3,5},{5,7},{... | collective-permute-start | bytes 393224 | tf_op jit(solution)/shard_map/ppermute | solution.py:22
  55.2 6.9 %collective-permute-start.7 = (f32[2,2,1,8192]{3,2,1,0:T(1,128)S(1)}, f32[2,2,1,8192]{3,2,1,0:T(1,128)S(1)}, u32[]{:S(2)}, u32[]{:S(2)}) collective-permute-start(f32[2,2,1,8192]{3,2,1,0:T(1,128)S(1)} %get-tuple-element.19), channel_id=1, source_target_pairs={{2,0},{4,2},{6,4},{8,6},{10,8},{12,10},{14,12},{3,1},{5,3},{7,5},{... | collective-permute-start | bytes 393224 | tf_op jit(solution)/shard_map/ppermute | solution.py:23
  65.2 7.7 %collective-permute-start.8 = (f32[2,2,1,8192]{3,2,1,0:T(1,128)S(1)}, f32[2,2,1,8192]{3,2,1,0:T(1,128)S(1)}, u32[]{:S(2)}, u32[]{:S(2)}) collective-permute-start(f32[2,2,1,8192]{3,2,1,0:T(1,128)S(1)} %get-tuple-element.16), channel_id=1, source_target_pairs={{0,2},{2,4},{4,6},{6,8},{8,10},{10,12},{12,14},{1,3},{3,5},{5,7},{... | collective-permute-start | bytes 393224 | tf_op jit(solution)/shard_map/ppermute | solution.py:22
  69.1 6.9 %collective-permute-start.9 = (f32[2,2,1,8192]{3,2,1,0:T(1,128)S(1)}, f32[2,2,1,8192]{3,2,1,0:T(1,128)S(1)}, u32[]{:S(2)}, u32[]{:S(2)}) collective-permute-start(f32[2,2,1,8192]{3,2,1,0:T(1,128)S(1)} %get-tuple-element.17), channel_id=1, source_target_pairs={{2,0},{4,2},{6,4},{8,6},{10,8},{12,10},{14,12},{3,1},{5,3},{7,5},{... | collective-permute-start | bytes 393224 | tf_op jit(solution)/shard_map/ppermute | solution.py:23
  79.1 7.8 %collective-permute-start.10 = (f32[2,2,1,8192]{3,2,1,0:T(1,128)S(1)}, f32[2,2,1,8192]{3,2,1,0:T(1,128)S(1)}, u32[]{:S(2)}, u32[]{:S(2)}) collective-permute-start(f32[2,2,1,8192]{3,2,1,0:T(1,128)S(1)} %get-tuple-element.14), channel_id=1, source_target_pairs={{0,2},{2,4},{4,6},{6,8},{8,10},{10,12},{12,14},{1,3},{3,5},{5,7},{... | collective-permute-start | bytes 393224 | tf_op jit(solution)/shard_map/ppermute | solution.py:22
  83.0 6.9 %collective-permute-start.11 = (f32[2,2,1,8192]{3,2,1,0:T(1,128)S(1)}, f32[2,2,1,8192]{3,2,1,0:T(1,128)S(1)}, u32[]{:S(2)}, u32[]{:S(2)}) collective-permute-start(f32[2,2,1,8192]{3,2,1,0:T(1,128)S(1)} %get-tuple-element.15), channel_id=1, source_target_pairs={{2,0},{4,2},{6,4},{8,6},{10,8},{12,10},{14,12},{3,1},{5,3},{7,5},{... | collective-permute-start | bytes 393224 | tf_op jit(solution)/shard_map/ppermute | solution.py:23
  91.0 2.2 %copy-start.1 = (f32[2,8,8192]{2,1,0:T(8,128)S(1)}, f32[2,8,8192]{2,1,0:T(8,128)}, u32[]{:S(2)}) copy-start(f32[2,8,8192]{2,1,0:T(8,128)} %param.3) | copy-start | bytes 1572868
  93.6 13.3 %collective-permute-start.12 = (f32[6,1,8192]{2,0,1:T(8,128)S(1)}, f32[6,1,8192]{2,0,1:T(8,128)S(1)}, u32[]{:S(2)}, u32[]{:S(2)}) collective-permute-start(f32[6,1,8192]{2,0,1:T(8,128)S(1)} %copy.21), channel_id=1, source_target_pairs={{0,2},{2,4},{4,6},{6,8},{8,10},{10,12},{12,14},{1,3},{3,5},{5,7},{... | collective-permute-start | bytes 589832 | tf_op jit(solution)/shard_map/ppermute | solution.py:22
  97.5 9.6 %collective-permute-start.13 = (f32[6,1,8192]{2,0,1:T(8,128)S(1)}, f32[6,1,8192]{2,0,1:T(8,128)}, u32[]{:S(2)}, u32[]{:S(2)}) collective-permute-start(f32[6,1,8192]{2,0,1:T(8,128)S(1)} %copy.22), channel_id=1, source_target_pairs={{2,0},{4,2},{6,4},{8,6},{10,8},{12,10},{14,12},{3,1},{5,3},{7,5},{... | collective-permute-start | bytes 589832 | tf_op jit(solution)/shard_map/ppermute | solution.py:23
  122.0 3.9 %copy-start.2 = (f32[2,10,8194]{2,1,0:T(8,128)S(1)}, f32[2,10,8194]{2,1,0:T(8,128)}, u32[]{:S(2)}) copy-start(f32[2,10,8194]{2,1,0:T(8,128)} %select_maximum_fusion.12) | copy-start | bytes 1966564
Sparse Core Ops, SparseCore 0:
  122.2 13.2 reduce-scatter.1
where the time goes:
time: 146 us; the launch traced here: 145 us
  waiting for transfers between devices  44.3 us (30%)
  other arithmetic  43.8 us (30%)
  starting transfers between devices  37.9 us (26%)
  between operations  13.7 us (9%)
  local copies, waits for them, and re-layouts  5.26 us (4%)
    ppermute x7, starting transfers between devices, extended(): before = lax.ppermute(last, axis, up)  28.5 us
    ppermute x7, waiting for transfers between devices, extended(): after = lax.ppermute(initial, axis, down)  19.1 us
    ppermute x7, waiting for transfers between devices, extended(): before = lax.ppermute(last, axis, up)  17.6 us
    unnamed x8, other arithmetic  12 us
    ppermute x7, starting transfers between devices, extended(): after = lax.ppermute(initial, axis, down)  9.36 us
    reduce_scatter x1, waiting for transfers between devices, per_device(): lax.psum_scatter(probe_sum, 'probe', scatter_dimension=2, tiled=True)  7.61 us
    concatenate x7, other arithmetic, extended(): shard = jnp.concatenate([before, shard, after], axis=dim)  7.52 us
    sub x4, other arithmetic, per_device(): following = 2.0 * product(current) - previous  7.14 us
  transfers between devices with their start and end apart: 15, of which 13 were waited for; matrix products, arithmetic and copies ran while one was open for 7% of the time, Pallas kernels for 0%

commit v1 on v0

v1 whole, which is shorter than its diff:
```python
import functools
import math

import jax
import jax.numpy as jnp
from jax import lax
from jax.experimental import pallas as pl
from jax.experimental.pallas import tpu as pltpu
from jax.sharding import PartitionSpec as P

CHEB = 6
LANES = 128
SUBS = 8
CHUNK = 3

lower_edge = 0.25
upper_edge = 12.0


def cheb_weights(degree, low_end, high_end):
    count = degree + 1
    values = []
    for order in range(count):
        accum = 0.0
        for node in range(count):
            angle = math.pi * (node + 0.5) / count
            point = 0.5 * (high_end - low_end) * math.cos(angle) + 0.5 * (high_end + low_end)
            accum += math.cos(order * angle) / point
        accum = accum * 2.0 / count
        if order == 0:
            accum = accum * 0.5
        values.append(accum)
    return values


def vmem_spec():
    return pl.BlockSpec(memory_space=pltpu.VMEM)


def any_spec():
    return pl.BlockSpec(memory_space=pl.ANY)


def params():
    return pltpu.CompilerParams(vmem_limit_bytes=40 * 1024 * 1024)


def cost(vregs):
    return pl.CostEstimate(flops=vregs * 1024 * 20, bytes_accessed=vregs * 4096 * 4, transcendentals=0)


def lane_index():
    return lax.broadcasted_iota(jnp.int32, (SUBS, LANES), 1)


def sideways(load, first, count, total):
    lane = lane_index()
    tiles = [load(first + k) for k in range(count)]
    before = load(jnp.maximum(first - 1, 0))
    after = load(jnp.minimum(first + count, total - 1))
    from_left = [jnp.where(first > 0, pltpu.roll(before, 1, 1), 0.0)]
    from_left += [pltpu.roll(tile, 1, 1) for tile in tiles]
    from_right = [pltpu.roll(tile, LANES - 1, 1) for tile in tiles]
    from_right += [jnp.where(first + count < total, pltpu.roll(after, LANES - 1, 1), 0.0)]
    result = []
    for k in range(count):
        left = jnp.where(lane == 0, from_left[k], from_left[k + 1])
        right = jnp.where(lane == LANES - 1, from_right[k + 1], from_right[k])
        result.append((tiles[k], left + right, right - left))
    return result


def sub(row):
    return pl.ds(row * SUBS, SUBS)


def prep_kernel(width, coefficients_ref, expanded_ref, window, sem):
    start = pl.multiple_of(lax.axis_index("probe") * (coefficients_ref.shape[2] - width), LANES)
    copy = pltpu.make_async_copy(coefficients_ref.at[:, :, pl.ds(start, width)], window, sem)
    copy.start()
    copy.wait()
    scale = 4.0 / (upper_edge - lower_edge)
    shift = 2.0 * (upper_edge + lower_edge) / (upper_edge - lower_edge)

    def body(tile, carry):
        cols = pl.ds(pl.multiple_of(tile * LANES, LANES), LANES)
        kappa, across, along, skew = [
            [window[2 * kind + c, :, cols] for c in range(2)] for kind in range(4)
        ]
        coupling = scale * window[8, :, cols]
        for c in range(2):
            values = (
                scale * (kappa[c] + 2.0 * (across[c] + along[c])) - shift,
                -scale * across[c],
                -scale * along[c],
                -0.5 * scale * skew[c],
                coupling,
            )
            for kind, value in enumerate(values):
                for probe in range(4):
                    expanded_ref[kind, tile, pl.ds(4 * c + probe, SUBS, stride=SUBS), :] = value
        return carry

    lax.fori_loop(0, width // LANES, body, 0)


def layout_kernel(width, probes_ref, other_ref, observed_ref, z_ref, top_ref, bottom_ref, seen_ref, own, sem):
    start = pl.multiple_of(lax.axis_index("probe") * (probes_ref.shape[3] - width), LANES)
    copies = [
        pltpu.make_async_copy(probes_ref.at[:, :, :, pl.ds(start, width)], own, sem.at[0]),
        pltpu.make_async_copy(observed_ref.at[:, :, pl.ds(start, width)], seen_ref, sem.at[1]),
    ]
    for copy in copies:
        copy.start()
    for copy in copies:
        copy.wait()
    tiles = width // LANES

    def body(tile, carry):
        cols = pl.ds(pl.multiple_of(tile * LANES, LANES), LANES)
        for c in range(2):
            for probe in range(2):
                z_ref[tile, pl.ds(4 * c + probe, SUBS, stride=SUBS), :] = own[probe, c, :, cols]
                z_ref[tile, pl.ds(4 * c + 2 + probe, SUBS, stride=SUBS), :] = other_ref[probe, c, :, cols]
        return carry

    lax.fori_loop(0, tiles, body, 0)

    def edges(tile, carry):
        top_ref[tile] = z_ref[tile, sub(0), :]
        bottom_ref[tile] = z_ref[tile, sub(SUBS - 1), :]
        return carry

    lax.fori_loop(0, tiles, edges, 0)
    for c in range(2):
        for tile in range(tiles):
            place = c * tiles + tile
            cols = pl.ds(tile * LANES, LANES)
            at = (tiles + place // SUBS, pl.ds(place % SUBS, 1))
            top_ref[at[0], at[1], :] = seen_ref[c, 0:1, cols]
            bottom_ref[at[0], at[1], :] = seen_ref[c, SUBS - 1 : SUBS, cols]


def step_kernel(upper, constants, offset, other_row, tiles, *refs):
    weight, scale, subtract = constants
    own_ref, other_ref, halo_ref, z_ref, coefficients_ref = refs[:5]
    rest = refs[5:]
    before_ref = None
    if subtract:
        before_ref, rest = rest[0], rest[1:]
    out_ref, edge_ref = rest
    first_row = 0 if upper else 4

    def load(row):
        if row == (-1 if upper else 4):
            return lambda tile: halo_ref[tile]
        if row == (4 if upper else -1):
            return lambda tile: other_ref[tile, sub(other_row), :]
        return lambda tile: own_ref[tile, sub(offset + row), :]

    def body(step, carry):
        first = step * CHUNK
        above = sideways(load(-1), first, CHUNK, tiles)
        here = sideways(load(0), first, CHUNK, tiles)
        for row in range(4):
            below = sideways(load(row + 1), first, CHUNK, tiles)
            for k in range(CHUNK):
                tile = first + k
                rows = sub(first_row + row)
                value, beside, _ = here[k]
                coefs = [coefficients_ref[kind, tile, rows, :] for kind in range(5)]
                total = (
                    coefs[0] * value
                    + coefs[1] * beside
                    + coefs[2] * (above[k][0] + below[k][0])
                    + coefs[3] * (below[k][2] - above[k][2])
                    + coefs[4] * pltpu.roll(value, 4, 0)
                )
                if scale != 1.0:
                    total = scale * total
                total = total + weight * z_ref[tile, rows, :]
                if subtract:
                    total = total - before_ref[tile, sub(row), :]
                out_ref[tile, sub(row), :] = total
                if row == (0 if upper else 3):
                    edge_ref[tile] = total
            above, here = here, below
        return carry

    lax.fori_loop(0, tiles // CHUNK, body, 0)


def data_kernel(tiles, seen_ref, up_ref, down_ref, out_ref):
    row = lax.broadcasted_iota(jnp.int32, (SUBS, LANES), 0)
    lane = lane_index()

    def halo(ref, c, tile):
        place = c * tiles + tile
        return ref[tiles + place // SUBS, pl.ds(place % SUBS, 1), :]

    def body(tile, carry):
        values = []
        for c in range(2):

            def load(at):
                return seen_ref[c, :, pl.ds(pl.multiple_of(at * LANES, LANES), LANES)]

            def edge(ref, at):
                return jnp.broadcast_to(halo(ref, c, at), (SUBS, LANES))

            def shifted(at):
                value = load(at)
                above = jnp.where(row == 0, edge(up_ref, at), pltpu.roll(value, 1, 0))
                below = jnp.where(row == SUBS - 1, edge(down_ref, at), pltpu.roll(value, SUBS - 1, 0))
                return value, above + below, below - above

            left = shifted(jnp.maximum(tile - 1, 0))
            center = shifted(tile)
            right = shifted(jnp.minimum(tile + 1, tiles - 1))

            def from_left(a, b):
                edge_value = jnp.where(tile > 0, pltpu.roll(a, 1, 1), 0.0)
                return jnp.where(lane == 0, edge_value, pltpu.roll(b, 1, 1))

            def from_right(a, b):
                edge_value = jnp.where(tile < tiles - 1, pltpu.roll(a, LANES - 1, 1), 0.0)
                return jnp.where(lane == LANES - 1, edge_value, pltpu.roll(b, LANES - 1, 1))

            value, along, _ = center
            across = from_left(left[0], value) + from_right(right[0], value)
            skew = from_right(right[2], center[2]) - from_left(left[2], center[2])
            half = -0.5 * value
            out_ref[tile, c] = half * value
            out_ref[tile, 2 + c] = -half * (across - 2.0 * value)
            out_ref[tile, 4 + c] = -half * (along - 2.0 * value)
            out_ref[tile, 6 + c] = -0.5 * half * skew
            values.append(value)
        out_ref[tile, 8] = -(values[0] * values[1])
        return carry

    lax.fori_loop(0, tiles, body, 0)


def gradient_kernel(tiles, factor, z_ref, top_ref, bottom_ref, up_ref, down_ref, data_ref, out_ref, products):
    kept = out_ref.shape[2] // LANES
    offset = lax.axis_index("probe") * (tiles - kept)

    def load(row):
        if row < 0:
            return lambda tile: up_ref[tile]
        if row >= SUBS:
            return lambda tile: down_ref[tile]
        if row < 4:
            return lambda tile: top_ref[tile, sub(row), :]
        return lambda tile: bottom_ref[tile, sub(row - 4), :]

    def body(index, carry):
        tile = index + offset
        above = sideways(load(-1), tile, 1, tiles)[0]
        here = sideways(load(0), tile, 1, tiles)[0]
        for row in range(SUBS):
            below = sideways(load(row + 1), tile, 1, tiles)[0]
            left = factor * z_ref[tile, sub(row), :]
            value, beside, _ = here
            twice = 2.0 * value
            products[0, sub(row), :] = left * value
            products[1, sub(row), :] = left * (twice - beside)
            products[2, sub(row), :] = left * (twice - (above[0] + below[0]))
            products[3, sub(row), :] = (-0.5 * left) * (below[2] - above[2])
            products[4, sub(row), :] = left * pltpu.roll(value, 4, 0)
            above, here = here, below
        cols = pl.ds(pl.multiple_of(index * LANES, LANES), LANES)
        for kind in range(5):
            parts = [products[kind, pl.ds(s, SUBS, stride=SUBS), :] for s in range(SUBS)]
            sums = [(parts[4 * c] + parts[4 * c + 1]) + (parts[4 * c + 2] + parts[4 * c + 3]) for c in range(2)]
            if kind < 4:
                for c in range(2):
                    out_ref[2 * kind + c, :, cols] = sums[c] + data_ref[tile, 2 * kind + c]
            else:
                out_ref[8, :, cols] = (sums[0] + sums[1]) + data_ref[tile, 8]
        return carry

    lax.fori_loop(0, kept, body, 0)


def per_device(observations, coefficients, probes):
    weights = cheb_weights(CHEB, lower_edge, upper_edge)
    f32 = jnp.float32
    columns = probes.shape[3]
    share = columns // lax.axis_size("probe")
    width = share + LANES
    tiles = width // LANES
    seen_tiles = -(-2 * tiles // SUBS)
    rows = lax.axis_size("row")
    down_pairs = [(i, i + 1) for i in range(rows - 1)]
    up_pairs = [(i + 1, i) for i in range(rows - 1)]

    def to_next(edge):
        return lax.ppermute(edge, "row", down_pairs)

    def to_previous(edge):
        return lax.ppermute(edge, "row", up_pairs)

    core = lax.axis_index("probe")
    theirs = lax.dynamic_slice_in_dim(probes, (1 - core) * (columns - width), width, axis=3)
    other = lax.ppermute(theirs, "probe", [(0, 1), (1, 0)])

    expanded = pl.pallas_call(
        functools.partial(prep_kernel, width),
        out_shape=pltpu.VMEM((5, tiles, SUBS * SUBS, LANES), f32),
        in_specs=[any_spec()],
        out_specs=vmem_spec(),
        scratch_shapes=[pltpu.VMEM((9, SUBS, width), f32), pltpu.SemaphoreType.DMA],
        compiler_params=params(),
        cost_estimate=cost(5 * 8 * tiles),
        name="prep",
    )(coefficients)

    message = (tiles + seen_tiles, SUBS, LANES)
    z, top, bottom, seen = pl.pallas_call(
        functools.partial(layout_kernel, width),
        out_shape=[
            pltpu.VMEM((tiles, SUBS * SUBS, LANES), f32),
            pltpu.VMEM(message, f32),
            pltpu.VMEM(message, f32),
            pltpu.VMEM((2, SUBS, width), f32),
        ],
        in_specs=[any_spec(), vmem_spec(), any_spec()],
        out_specs=[vmem_spec()] * 4,
        scratch_shapes=[pltpu.VMEM((2, 2, SUBS, width), f32), pltpu.SemaphoreType.DMA((2,))],
        compiler_params=params(),
        cost_estimate=cost(8 * tiles),
        name="layout",
    )(probes, other, observations)

    def half(upper, constants, own, other_half, halo, before):
        shared = own is z
        offset = (0 if upper else 4) if shared else 0
        other_row = (4 if upper else 3) if shared else (0 if upper else 3)
        operands = [own, other_half, halo, z, expanded]
        if constants[2]:
            operands.append(before)
        return pl.pallas_call(
            functools.partial(step_kernel, upper, constants, offset, other_row, tiles),
            out_shape=[
                pltpu.VMEM((tiles, 4 * SUBS, LANES), f32),
                pltpu.VMEM((tiles, SUBS, LANES), f32),
            ],
            in_specs=[vmem_spec()] * len(operands),
            out_specs=[vmem_spec()] * 2,
            compiler_params=params(),
            cost_estimate=cost(4 * tiles),
            name=("upper" if upper else "lower"),
        )(*operands)

    first_up, first_down = to_next(bottom), to_previous(top)
    up, down = first_up, first_down
    now = (z, z)
    before = (None, None)
    for order in range(CHEB - 1, -1, -1):
        if order == CHEB - 1:
            constants = (weights[order], weights[CHEB], False)
        elif order == CHEB - 2:
            constants = (weights[order] - weights[CHEB], 1.0, False)
        elif order > 0:
            constants = (weights[order], 1.0, True)
        else:
            constants = (weights[0], 0.5, True)
        upper, top = half(True, constants, now[0], now[1], up, before[0])
        next_down = to_previous(top)
        lower, bottom = half(False, constants, now[1], now[0], down, before[1])
        next_up = to_next(bottom)
        before, now = now, (upper, lower)
        up, down = next_up, next_down

    data = pl.pallas_call(
        functools.partial(data_kernel, tiles),
        out_shape=pltpu.VMEM((tiles, 9, SUBS, LANES), f32),
        in_specs=[vmem_spec()] * 3,
        out_specs=vmem_spec(),
        compiler_params=params(),
        cost_estimate=cost(9 * tiles),
        name="data",
    )(seen, first_up, first_down)

    total_probes = probes.shape[0] * lax.axis_size("probe")
    return pl.pallas_call(
        functools.partial(gradient_kernel, tiles, 0.5 / total_probes),
        out_shape=jax.ShapeDtypeStruct((9, SUBS, share), f32),
        in_specs=[vmem_spec()] * 6,
        out_specs=vmem_spec(),
        scratch_shapes=[pltpu.VMEM((5, SUBS * SUBS, LANES), f32)],
        compiler_params=params(),
        cost_estimate=cost(24 * tiles),
        name="gradient",
    )(z, now[0], now[1], up, down, data)


def solution(mesh):
    in_specs = (P("group", "row", None), P("group", "row", None), P("probe", "group", "row", None))
    out_specs = P("group", "row", "probe")
    return jax.shard_map(
        per_device, mesh=mesh, in_specs=in_specs, out_specs=out_specs, check_vma=False
    )
```

time: 146 us -> 82.3 us (0.56)
  other arithmetic: 43.8 us -> 0 us
  waiting for transfers between devices: 44.3 us -> 13.1 us
  Pallas kernels: 0 us -> 27.5 us
  between operations: 13.7 us -> 0.31 us
    pallas_call x0 -> x16, Pallas kernels: none -> 27.5 us  [the longest x12 17.1 us: half(): pl.pallas_call(functools.partial(step_kernel, upper, constants, offset, o...]
    ppermute x14 -> x15, waiting for transfers between devices: 36.7 us -> 13.1 us  [the longest x7 11.5 us: to_previous(): return lax.ppermute(edge, 'row', up_pairs)]
    unnamed x8 -> x0, other arithmetic: 12 us -> none
    sub x5 -> x0, other arithmetic: 9.91 us -> none  [the longest x4 7.14 us: per_device(): following = 2.0 * product(current) - previous]
    concatenate x9 -> x0, other arithmetic: 9.21 us -> none  [the longest x7 7.52 us: extended(): shard = jnp.concatenate([before, shard, after], axis=dim)]
    reduce_scatter x1 -> x0, waiting for transfers between devices: 7.61 us -> none  [per_device(): lax.psum_scatter(probe_sum, 'probe', scatter_dimension=2, tiled=True)]
    reduce_sum x1 -> x0, other arithmetic: 4.38 us -> none  [per_device(): probe_sum = jnp.sum(gradient_terms(probes, series_wide), axis=0)]
    slice x9 -> x0, local copies, waits for them, and re-layouts: 2.91 us -> none  [the longest x7 2.64 us: extended(): last = lax.slice_in_dim(shard, length - width, length, axis=dim)]
  transfers between devices with their start and end apart: 15 -> 15, of which waited for: 13 -> 5; matrix products, arithmetic and copies ran while one was open for 7% -> 0% of each run, Pallas kernels for 0% -> 26%
where the time goes in v1:
time: 82.3 us; the launch traced here: 81.8 us
  starting transfers between devices  37 us (45%)
  Pallas kernels  27.5 us (33%)
  waiting for transfers between devices  13.1 us (16%)
  local copies, waits for them, and re-layouts  3.88 us (5%)
    ppermute x7, starting transfers between devices, to_next(): return lax.ppermute(edge, 'row', down_pairs)  27.4 us
    pallas_call x12, Pallas kernels, half(): pl.pallas_call(functools.partial(step_kernel, upper, constants, offset, o...  17.1 us
    ppermute x7, waiting for transfers between devices, to_previous(): return lax.ppermute(edge, 'row', up_pairs)  11.5 us
    ppermute x7, starting transfers between devices, to_previous(): return lax.ppermute(edge, 'row', up_pairs)  9.04 us
    pallas_call x1, Pallas kernels, per_device(): pl.pallas_call(functools.partial(gradient_kernel, tiles, 0.5 / total_prob...  5.24 us
    pallas_call x1, Pallas kernels, per_device(): pl.pallas_call(functools.partial(data_kernel, tiles), out_shape=pltpu.VME...  3.5 us
    unnamed x6, local copies, waits for them, and re-layouts  2.71 us
  transfers between devices with their start and end apart: 15, of which 5 were waited for; matrix products, arithmetic and copies ran while one was open for 0% of the time, Pallas kernels for 26%

profile of v1, /device:TPU:0, one launch (start us, length us, event | category | flops | bytes accessed | tf_op | source)
XLA Modules:
  0.0 81.8 jit_solution(7388047766402917343)
XLA Ops:
  0.0 1.2 %constant_dynamic-slice_fusion = f32[2,2,8,4224]{3,2,1,0:T(8,128)S(1)} fusion(f32[2,2,8,8192]{3,2,1,0:T(8,128)} %probes_ref.1, s32[]{:T(128)S(6)} %select_n.3), kind=kLoop, calls=%fused_computation | loop fusion | bytes 1081348 | tf_op jit(solution)/shard_map/dynamic_slice | solution.py:305
  1.2 0.5 collective-permute-start
  1.7 1.6 %collective-permute-done.other_ref = f32[2,2,8,4224]{3,2,1,0:T(8,128)S(1)} collective-permute-done((f32[2,2,8,4224]{3,2,1,0:T(8,128)S(1)}, f32[2,2,8,4224]{3,2,1,0:T(8,128)S(1)}, u32[]{:S(2)}, u32[]{:S(2)}) %collective-permute-start) | collective-permute-done | bytes 540704 | tf_op jit(solution)/shard_map/ppermute | solution.py:306
  3.3 1.0 %copy-done.2 = f32[2,8,8192]{2,1,0:T(8,128)S(1)} copy-done((f32[2,8,8192]{2,1,0:T(8,128)S(1)}, f32[2,8,8192]{2,1,0:T(8,128)}, u32[]{:S(2)}) %copy-start.2) | copy-done | bytes 524312
  4.3 0.6 layout.1
  4.9 4.8 %collective-permute-start.1 = (f32[42,8,128]{2,1,0:T(8,128)S(1)}, f32[42,8,128]{2,1,0:T(8,128)S(1)}, u32[]{:S(2)}, u32[]{:S(2)}) collective-permute-start(f32[42,8,128]{2,1,0:T(8,128)S(1)} %get-tuple-element.34), channel_id=1, source_target_pairs={{0,2},{2,4},{4,6},{6,8},{8,10},{10,12},{12,14},{1,3},{3,5},{5,7},{... | collective-permute-start | bytes 516104 | tf_op jit(solution)/shard_map/ppermute | solution.py:299
  9.7 1.3 %collective-permute-start.2 = (f32[42,8,128]{2,1,0:T(8,128)S(1)}, f32[42,8,128]{2,1,0:T(8,128)S(1)}, u32[]{:S(2)}, u32[]{:S(2)}) collective-permute-start(f32[42,8,128]{2,1,0:T(8,128)S(1)} %get-tuple-element.36), channel_id=1, source_target_pairs={{2,0},{4,2},{6,4},{8,6},{10,8},{12,10},{14,12},{3,1},{5,3},{7,5},{... | collective-permute-start | bytes 516104 | tf_op jit(solution)/shard_map/ppermute | solution.py:302
  11.0 0.0 copy-start.1
  11.0 1.7 %copy-done.1 = f32[9,8,8192]{2,1,0:T(8,128)S(1)} copy-done((f32[9,8,8192]{2,1,0:T(8,128)S(1)}, f32[9,8,8192]{2,1,0:T(8,128)}, u32[]{:S(2)}) %copy-start.1) | copy-done | bytes 2359320
  12.7 1.1 %prep.1.refs_4_ = f32[5,33,64,128]{3,2,1,0:T(8,128)S(1)} custom-call(f32[9,8,8192]{2,1,0:T(8,128)S(1)} %copy-done.1), custom_call_target="tpu_custom_call" | custom-call | flops 27033600 | bytes 21626880 | tf_op jit(solution)/shard_map/prep/pallas_call | solution.py:308
  13.7 0.0 collective-permute-done.1.refs_2_.up_ref
  13.7 1.4 %upper.6 = (f32[33,32,128]{2,1,0:T(8,128)S(1)}, f32[33,8,128]{2,1,0:T(8,128)S(1)}) custom-call(f32[33,64,128]{2,1,0:T(8,128)S(1)} %get-tuple-element.33.refs_0_.refs_1_.refs_3_.z_ref, f32[33,64,128]{2,1,0:T(8,128)S(1)} %get-tuple-element.33.refs_0_.refs_1_.refs_3_.z_ref, f32[42,8,128]{2,1,0:T(8,128)S(1)} %collective-permute-done.1.refs_2_.up_ref, ...), custom_call_target="tpu_custom_call" | custom-call | flops 2703360 | bytes 2162688 | tf_op jit(solution)/shard_map/upper/pallas_call | solution.py:343
  15.2 1.3 %collective-permute-start.4 = (f32[33,8,128]{2,1,0:T(8,128)S(1)}, f32[33,8,128]{2,1,0:T(8,128)S(1)}, u32[]{:S(2)}, u32[]{:S(2)}) collective-permute-start(f32[33,8,128]{2,1,0:T(8,128)S(1)} %get-tuple-element.40), channel_id=1, source_target_pairs={{2,0},{4,2},{6,4},{8,6},{10,8},{12,10},{14,12},{3,1},{5,3},{7,5},{... | collective-permute-start | bytes 405512 | tf_op jit(solution)/shard_map/ppermute | solution.py:302
  16.5 1.3 %collective-permute-done.2.refs_2_.down_ref = f32[42,8,128]{2,1,0:T(8,128)S(1)} collective-permute-done((f32[42,8,128]{2,1,0:T(8,128)S(1)}, f32[42,8,128]{2,1,0:T(8,128)S(1)}, u32[]{:S(2)}, u32[]{:S(2)}) %collective-permute-start.2) | collective-permute-done | bytes 172064 | tf_op jit(solution)/shard_map/ppermute | solution.py:302
  17.7 1.4 %lower.6 = (f32[33,32,128]{2,1,0:T(8,128)S(1)}, f32[33,8,128]{2,1,0:T(8,128)S(1)}) custom-call(f32[33,64,128]{2,1,0:T(8,128)S(1)} %get-tuple-element.33.refs_0_.refs_1_.refs_3_.z_ref, f32[33,64,128]{2,1,0:T(8,128)S(1)} %get-tuple-element.33.refs_0_.refs_1_.refs_3_.z_ref, f32[42,8,128]{2,1,0:T(8,128)S(1)} %collective-permute-done.2.refs_2_.down_ref, ...), custom_call_target="tpu_custom_call" | custom-call | flops 2703360 | bytes 2162688 | tf_op jit(solution)/shard_map/lower/pallas_call | solution.py:343
  19.2 4.4 %collective-permute-start.3 = (f32[33,8,128]{2,1,0:T(8,128)S(1)}, f32[33,8,128]{2,1,0:T(8,128)S(1)}, u32[]{:S(2)}, u32[]{:S(2)}) collective-permute-start(f32[33,8,128]{2,1,0:T(8,128)S(1)} %get-tuple-element.38), channel_id=1, source_target_pairs={{0,2},{2,4},{4,6},{6,8},{8,10},{10,12},{12,14},{1,3},{3,5},{5,7},{... | collective-permute-start | bytes 405512 | tf_op jit(solution)/shard_map/ppermute | solution.py:299
  23.5 0.0 collective-permute-done.4.refs_2_
  23.5 1.4 %lower.7 = (f32[33,32,128]{2,1,0:T(8,128)S(1)}, f32[33,8,128]{2,1,0:T(8,128)S(1)}) custom-call(f32[33,32,128]{2,1,0:T(8,128)S(1)} %get-tuple-element.37.refs_1_.refs_0_.refs_5_, f32[33,32,128]{2,1,0:T(8,128)S(1)} %get-tuple-element.35.refs_0_.refs_1_.refs_5_, f32[33,8,128]{2,1,0:T(8,128)S(1)} %collective-permute-done.4.refs_2_, ...), custom_call_target="tpu_custom_call" | custom-call | flops 2703360 | bytes 2162688 | tf_op jit(solution)/shard_map/lower/pallas_call | solution.py:343
  24.9 4.4 %collective-permute-start.5 = (f32[33,8,128]{2,1,0:T(8,128)S(1)}, f32[33,8,128]{2,1,0:T(8,128)S(1)}, u32[]{:S(2)}, u32[]{:S(2)}) collective-permute-start(f32[33,8,128]{2,1,0:T(8,128)S(1)} %get-tuple-element.42), channel_id=1, source_target_pairs={{0,2},{2,4},{4,6},{6,8},{8,10},{10,12},{12,14},{1,3},{3,5},{5,7},{... | collective-permute-start | bytes 405512 | tf_op jit(solution)/shard_map/ppermute | solution.py:299
  29.4 0.0 collective-permute-done.3.refs_2_
  29.4 1.4 %upper.7 = (f32[33,32,128]{2,1,0:T(8,128)S(1)}, f32[33,8,128]{2,1,0:T(8,128)S(1)}) custom-call(f32[33,32,128]{2,1,0:T(8,128)S(1)} %get-tuple-element.35.refs_0_.refs_1_.refs_5_, f32[33,32,128]{2,1,0:T(8,128)S(1)} %get-tuple-element.37.refs_1_.refs_0_.refs_5_, f32[33,8,128]{2,1,0:T(8,128)S(1)} %collective-permute-done.3.refs_2_, ...), custom_call_target="tpu_custom_call" | custom-call | flops 2703360 | bytes 2162688 | tf_op jit(solution)/shard_map/upper/pallas_call | solution.py:343
  30.8 1.3 %collective-permute-start.6 = (f32[33,8,128]{2,1,0:T(8,128)S(1)}, f32[33,8,128]{2,1,0:T(8,128)S(1)}, u32[]{:S(2)}, u32[]{:S(2)}) collective-permute-start(f32[33,8,128]{2,1,0:T(8,128)S(1)} %get-tuple-element.44), channel_id=1, source_target_pairs={{2,0},{4,2},{6,4},{8,6},{10,8},{12,10},{14,12},{3,1},{5,3},{7,5},{... | collective-permute-start | bytes 405512 | tf_op jit(solution)/shard_map/ppermute | solution.py:302
  32.1 0.0 collective-permute-done.5.refs_2_
  32.1 1.4 %upper.8 = (f32[33,32,128]{2,1,0:T(8,128)S(1)}, f32[33,8,128]{2,1,0:T(8,128)S(1)}) custom-call(f32[33,32,128]{2,1,0:T(8,128)S(1)} %get-tuple-element.39.refs_0_.refs_1_.refs_5_, f32[33,32,128]{2,1,0:T(8,128)S(1)} %get-tuple-element.41.refs_1_.refs_0_.refs_5_, f32[33,8,128]{2,1,0:T(8,128)S(1)} %collective-permute-done.5.refs_2_, ...), custom_call_target="tpu_custom_call" | custom-call | flops 2703360 | bytes 2162688 | tf_op jit(solution)/shard_map/upper/pallas_call | solution.py:343
  33.5 1.3 %collective-permute-start.8 = (f32[33,8,128]{2,1,0:T(8,128)S(1)}, f32[33,8,128]{2,1,0:T(8,128)S(1)}, u32[]{:S(2)}, u32[]{:S(2)}) collective-permute-start(f32[33,8,128]{2,1,0:T(8,128)S(1)} %get-tuple-element.48), channel_id=1, source_target_pairs={{2,0},{4,2},{6,4},{8,6},{10,8},{12,10},{14,12},{3,1},{5,3},{7,5},{... | collective-permute-start | bytes 405512 | tf_op jit(solution)/shard_map/ppermute | solution.py:302
  34.8 2.9 %collective-permute-done.6.refs_2_ = f32[33,8,128]{2,1,0:T(8,128)S(1)} collective-permute-done((f32[33,8,128]{2,1,0:T(8,128)S(1)}, f32[33,8,128]{2,1,0:T(8,128)S(1)}, u32[]{:S(2)}, u32[]{:S(2)}) %collective-permute-start.6) | collective-permute-done | bytes 135200 | tf_op jit(solution)/shard_map/ppermute | solution.py:302
  37.7 1.4 %lower.8 = (f32[33,32,128]{2,1,0:T(8,128)S(1)}, f32[33,8,128]{2,1,0:T(8,128)S(1)}) custom-call(f32[33,32,128]{2,1,0:T(8,128)S(1)} %get-tuple-element.41.refs_1_.refs_0_.refs_5_, f32[33,32,128]{2,1,0:T(8,128)S(1)} %get-tuple-element.39.refs_0_.refs_1_.refs_5_, f32[33,8,128]{2,1,0:T(8,128)S(1)} %collective-permute-done.6.refs_2_, ...), custom_call_target="tpu_custom_call" | custom-call | flops 2703360 | bytes 2162688 | tf_op jit(solution)/shard_map/lower/pallas_call | solution.py:343
  39.1 4.3 %collective-permute-start.7 = (f32[33,8,128]{2,1,0:T(8,128)S(1)}, f32[33,8,128]{2,1,0:T(8,128)S(1)}, u32[]{:S(2)}, u32[]{:S(2)}) collective-permute-start(f32[33,8,128]{2,1,0:T(8,128)S(1)} %get-tuple-element.46), channel_id=1, source_target_pairs={{0,2},{2,4},{4,6},{6,8},{8,10},{10,12},{12,14},{1,3},{3,5},{5,7},{... | collective-permute-start | bytes 405512 | tf_op jit(solution)/shard_map/ppermute | solution.py:299
  43.5 0.0 collective-permute-done.8.refs_2_
  43.5 1.4 %lower.9 = (f32[33,32,128]{2,1,0:T(8,128)S(1)}, f32[33,8,128]{2,1,0:T(8,128)S(1)}) custom-call(f32[33,32,128]{2,1,0:T(8,128)S(1)} %get-tuple-element.45.refs_1_.refs_0_.refs_5_, f32[33,32,128]{2,1,0:T(8,128)S(1)} %get-tuple-element.43.refs_0_.refs_1_.refs_5_, f32[33,8,128]{2,1,0:T(8,128)S(1)} %collective-permute-done.8.refs_2_, ...), custom_call_target="tpu_custom_call" | custom-call | flops 2703360 | bytes 2162688 | tf_op jit(solution)/shard_map/lower/pallas_call | solution.py:343
  44.9 2.8 %collective-permute-start.9 = (f32[33,8,128]{2,1,0:T(8,128)S(1)}, f32[33,8,128]{2,1,0:T(8,128)S(1)}, u32[]{:S(2)}, u32[]{:S(2)}) collective-permute-start(f32[33,8,128]{2,1,0:T(8,128)S(1)} %get-tuple-element.50), channel_id=1, source_target_pairs={{0,2},{2,4},{4,6},{6,8},{8,10},{10,12},{12,14},{1,3},{3,5},{5,7},{... | collective-permute-start | bytes 405512 | tf_op jit(solution)/shard_map/ppermute | solution.py:299
  47.7 0.0 collective-permute-done.7.refs_2_
  47.8 1.4 %upper.9 = (f32[33,32,128]{2,1,0:T(8,128)S(1)}, f32[33,8,128]{2,1,0:T(8,128)S(1)}) custom-call(f32[33,32,128]{2,1,0:T(8,128)S(1)} %get-tuple-element.43.refs_0_.refs_1_.refs_5_, f32[33,32,128]{2,1,0:T(8,128)S(1)} %get-tuple-element.45.refs_1_.refs_0_.refs_5_, f32[33,8,128]{2,1,0:T(8,128)S(1)} %collective-permute-done.7.refs_2_, ...), custom_call_target="tpu_custom_call" | custom-call | flops 2703360 | bytes 2162688 | tf_op jit(solution)/shard_map/upper/pallas_call | solution.py:343
  49.2 1.3 %collective-permute-start.10 = (f32[33,8,128]{2,1,0:T(8,128)S(1)}, f32[33,8,128]{2,1,0:T(8,128)S(1)}, u32[]{:S(2)}, u32[]{:S(2)}) collective-permute-start(f32[33,8,128]{2,1,0:T(8,128)S(1)} %get-tuple-element.52), channel_id=1, source_target_pairs={{2,0},{4,2},{6,4},{8,6},{10,8},{12,10},{14,12},{3,1},{5,3},{7,5},{... | collective-permute-start | bytes 405512 | tf_op jit(solution)/shard_map/ppermute | solution.py:302
  50.5 0.0 collective-permute-done.9.refs_2_
  50.5 1.4 %upper.10 = (f32[33,32,128]{2,1,0:T(8,128)S(1)}, f32[33,8,128]{2,1,0:T(8,128)S(1)}) custom-call(f32[33,32,128]{2,1,0:T(8,128)S(1)} %get-tuple-element.47.refs_0_.refs_1_.refs_5_, f32[33,32,128]{2,1,0:T(8,128)S(1)} %get-tuple-element.49.refs_1_.refs_0_.refs_5_, f32[33,8,128]{2,1,0:T(8,128)S(1)} %collective-permute-done.9.refs_2_, ...), custom_call_target="tpu_custom_call" | custom-call | flops 2703360 | bytes 2162688 | tf_op jit(solution)/shard_map/upper/pallas_call | solution.py:343
  51.9 1.3 %collective-permute-start.12 = (f32[33,8,128]{2,1,0:T(8,128)S(1)}, f32[33,8,128]{2,1,0:T(8,128)S(1)}, u32[]{:S(2)}, u32[]{:S(2)}) collective-permute-start(f32[33,8,128]{2,1,0:T(8,128)S(1)} %get-tuple-element.56), channel_id=1, source_target_pairs={{2,0},{4,2},{6,4},{8,6},{10,8},{12,10},{14,12},{3,1},{5,3},{7,5},{... | collective-permute-start | bytes 405512 | tf_op jit(solution)/shard_map/ppermute | solution.py:302
  53.2 4.3 %collective-permute-done.10.refs_2_ = f32[33,8,128]{2,1,0:T(8,128)S(1)} collective-permute-done((f32[33,8,128]{2,1,0:T(8,128)S(1)}, f32[33,8,128]{2,1,0:T(8,128)S(1)}, u32[]{:S(2)}, u32[]{:S(2)}) %collective-permute-start.10) | collective-permute-done | bytes 135200 | tf_op jit(solution)/shard_map/ppermute | solution.py:302
  57.5 1.4 %lower.10 = (f32[33,32,128]{2,1,0:T(8,128)S(1)}, f32[33,8,128]{2,1,0:T(8,128)S(1)}) custom-call(f32[33,32,128]{2,1,0:T(8,128)S(1)} %get-tuple-element.49.refs_1_.refs_0_.refs_5_, f32[33,32,128]{2,1,0:T(8,128)S(1)} %get-tuple-element.47.refs_0_.refs_1_.refs_5_, f32[33,8,128]{2,1,0:T(8,128)S(1)} %collective-permute-done.10.refs_2_, ...), custom_call_target="tpu_custom_call" | custom-call | flops 2703360 | bytes 2162688 | tf_op jit(solution)/shard_map/lower/pallas_call | solution.py:343
  58.9 4.8 %collective-permute-start.11 = (f32[33,8,128]{2,1,0:T(8,128)S(1)}, f32[33,8,128]{2,1,0:T(8,128)S(1)}, u32[]{:S(2)}, u32[]{:S(2)}) collective-permute-start(f32[33,8,128]{2,1,0:T(8,128)S(1)} %get-tuple-element.54), channel_id=1, source_target_pairs={{0,2},{2,4},{4,6},{6,8},{8,10},{10,12},{12,14},{1,3},{3,5},{5,7},{... | collective-permute-start | bytes 405512 | tf_op jit(solution)/shard_map/ppermute | solution.py:299
  63.8 0.0 collective-permute-done.12.refs_2_
  63.8 1.5 %lower.11 = (f32[33,32,128]{2,1,0:T(8,128)S(1)}, f32[33,8,128]{2,1,0:T(8,128)S(1)}) custom-call(f32[33,32,128]{2,1,0:T(8,128)S(1)} %get-tuple-element.53.refs_1_.refs_0_, f32[33,32,128]{2,1,0:T(8,128)S(1)} %get-tuple-element.51.refs_0_.refs_1_, f32[33,8,128]{2,1,0:T(8,128)S(1)} %collective-permute-done.12.refs_2_, ...), custom_call_target="tpu_custom_call" | custom-call | flops 2703360 | bytes 2162688 | tf_op jit(solution)/shard_map/lower/pallas_call | solution.py:343
  65.2 1.9 %collective-permute-start.13 = (f32[33,8,128]{2,1,0:T(8,128)S(1)}, f32[33,8,128]{2,1,0:T(8,128)S(1)}, u32[]{:S(2)}, u32[]{:S(2)}) collective-permute-start(f32[33,8,128]{2,1,0:T(8,128)S(1)} %get-tuple-element.58), channel_id=1, source_target_pairs={{0,2},{2,4},{4,6},{6,8},{8,10},{10,12},{12,14},{1,3},{3,5},{5,7},{... | collective-permute-start | bytes 405512 | tf_op jit(solution)/shard_map/ppermute | solution.py:299
  67.2 1.4 %upper.11 = (f32[33,32,128]{2,1,0:T(8,128)S(1)}, f32[33,8,128]{2,1,0:T(8,128)S(1)}) custom-call(f32[33,32,128]{2,1,0:T(8,128)S(1)} %get-tuple-element.51.refs_0_.refs_1_, f32[33,32,128]{2,1,0:T(8,128)S(1)} %get-tuple-element.53.refs_1_.refs_0_, f32[33,8,128]{2,1,0:T(8,128)S(1)} %collective-permute-done.11.refs_2_, ...), custom_call_target="tpu_custom_call" | custom-call | flops 2703360 | bytes 2162688 | tf_op jit(solution)/shard_map/upper/pallas_call | solution.py:343
  68.6 1.3 %collective-permute-start.14 = (f32[33,8,128]{2,1,0:T(8,128)S(1)}, f32[33,8,128]{2,1,0:T(8,128)S(1)}, u32[]{:S(2)}, u32[]{:S(2)}) collective-permute-start(f32[33,8,128]{2,1,0:T(8,128)S(1)} %get-tuple-element.59), channel_id=1, source_target_pairs={{2,0},{4,2},{6,4},{8,6},{10,8},{12,10},{14,12},{3,1},{5,3},{7,5},{... | collective-permute-start | bytes 405512 | tf_op jit(solution)/shard_map/ppermute | solution.py:302
  69.9 3.5 %data.1.data_ref = f32[33,9,8,128]{3,2,1,0:T(8,128)S(1)} custom-call(f32[2,8,4224]{2,1,0:T(8,128)S(1)} %get-tuple-element.60.seen_ref, f32[42,8,128]{2,1,0:T(8,128)S(1)} %collective-permute-done.1.refs_2_.up_ref, f32[42,8,128]{2,1,0:T(8,128)S(1)} %collective-permute-done.2.refs_2_.down_ref), custom_call_target="tpu_custom_call" | custom-call | flops 6082560 | bytes 4866048 | tf_op jit(solution)/shard_map/data/pallas_call | solution.py:376
  73.4 3.1 %collective-permute-done.14.down_ref = f32[33,8,128]{2,1,0:T(8,128)S(1)} collective-permute-done((f32[33,8,128]{2,1,0:T(8,128)S(1)}, f32[33,8,128]{2,1,0:T(8,128)S(1)}, u32[]{:S(2)}, u32[]{:S(2)}) %collective-permute-start.14) | collective-permute-done | bytes 135200 | tf_op jit(solution)/shard_map/ppermute | solution.py:302
  76.5 5.2 %gradient.1 = f32[9,8,4096]{2,1,0:T(8,128)} custom-call(f32[33,64,128]{2,1,0:T(8,128)S(1)} %get-tuple-element.33.refs_0_.refs_1_.refs_3_.z_ref, f32[33,32,128]{2,1,0:T(8,128)S(1)} %get-tuple-element.55.top_ref, f32[33,32,128]{2,1,0:T(8,128)S(1)} %get-tuple-element.57.bottom_ref, f32[33,8,128]{2,1,0:T(8,128)S(1)} %collective-permute-done.13.up_ref, ...), custom_call_target="tpu_custom_call" | custom-call | flops 16220160 | bytes 12976128 | tf_op jit(solution)/shard_map/gradient/pallas_call | solution.py:387
  (5 shorter events, 0.0 us)
Async XLA Ops:
  0.0 3.3 %copy-start = (f32[2,2,8,8192]{3,2,1,0:T(8,128)S(1)}, f32[2,2,8,8192]{3,2,1,0:T(8,128)}, u32[]{:S(2)}) copy-start(f32[2,2,8,8192]{3,2,1,0:T(8,128)} %probes_ref.1) | copy-start | bytes 3145732
  1.2 2.1 %collective-permute-start = (f32[2,2,8,4224]{3,2,1,0:T(8,128)S(1)}, f32[2,2,8,4224]{3,2,1,0:T(8,128)S(1)}, u32[]{:S(2)}, u32[]{:S(2)}) collective-permute-start(f32[2,2,8,4224]{3,2,1,0:T(8,128)S(1)} %constant_dynamic-slice_fusion), channel_id=1, source_target_pairs={{0,1},{1,0},{2,3},{3,2},{4,5},{5,4},{6,7},{7,6},{8,9},{9,8},{10,11... | collective-permute-start | bytes 1622024 | tf_op jit(solution)/shard_map/ppermute | solution.py:306
  3.3 1.0 %copy-start.2 = (f32[2,8,8192]{2,1,0:T(8,128)S(1)}, f32[2,8,8192]{2,1,0:T(8,128)}, u32[]{:S(2)}) copy-start(f32[2,8,8192]{2,1,0:T(8,128)} %observed_ref.1) | copy-start | bytes 1572868
  4.9 8.8 %collective-permute-start.1 = (f32[42,8,128]{2,1,0:T(8,128)S(1)}, f32[42,8,128]{2,1,0:T(8,128)S(1)}, u32[]{:S(2)}, u32[]{:S(2)}) collective-permute-start(f32[42,8,128]{2,1,0:T(8,128)S(1)} %get-tuple-element.34), channel_id=1, source_target_pairs={{0,2},{2,4},{4,6},{6,8},{8,10},{10,12},{12,14},{1,3},{3,5},{5,7},{... | collective-permute-start | bytes 516104 | tf_op jit(solution)/shard_map/ppermute | solution.py:299
  9.7 8.0 %collective-permute-start.2 = (f32[42,8,128]{2,1,0:T(8,128)S(1)}, f32[42,8,128]{2,1,0:T(8,128)S(1)}, u32[]{:S(2)}, u32[]{:S(2)}) collective-permute-start(f32[42,8,128]{2,1,0:T(8,128)S(1)} %get-tuple-element.36), channel_id=1, source_target_pairs={{2,0},{4,2},{6,4},{8,6},{10,8},{12,10},{14,12},{3,1},{5,3},{7,5},{... | collective-permute-start | bytes 516104 | tf_op jit(solution)/shard_map/ppermute | solution.py:302
  11.0 1.7 %copy-start.1 = (f32[9,8,8192]{2,1,0:T(8,128)S(1)}, f32[9,8,8192]{2,1,0:T(8,128)}, u32[]{:S(2)}) copy-start(f32[9,8,8192]{2,1,0:T(8,128)} %coefficients_ref.1) | copy-start | bytes 7077892
  15.2 8.4 %collective-permute-start.4 = (f32[33,8,128]{2,1,0:T(8,128)S(1)}, f32[33,8,128]{2,1,0:T(8,128)S(1)}, u32[]{:S(2)}, u32[]{:S(2)}) collective-permute-start(f32[33,8,128]{2,1,0:T(8,128)S(1)} %get-tuple-element.40), channel_id=1, source_target_pairs={{2,0},{4,2},{6,4},{8,6},{10,8},{12,10},{14,12},{3,1},{5,3},{7,5},{... | collective-permute-start | bytes 405512 | tf_op jit(solution)/shard_map/ppermute | solution.py:302
  19.2 10.2 %collective-permute-start.3 = (f32[33,8,128]{2,1,0:T(8,128)S(1)}, f32[33,8,128]{2,1,0:T(8,128)S(1)}, u32[]{:S(2)}, u32[]{:S(2)}) collective-permute-start(f32[33,8,128]{2,1,0:T(8,128)S(1)} %get-tuple-element.38), channel_id=1, source_target_pairs={{0,2},{2,4},{4,6},{6,8},{8,10},{10,12},{12,14},{1,3},{3,5},{5,7},{... | collective-permute-start | bytes 405512 | tf_op jit(solution)/shard_map/ppermute | solution.py:299
  24.9 7.1 %collective-permute-start.5 = (f32[33,8,128]{2,1,0:T(8,128)S(1)}, f32[33,8,128]{2,1,0:T(8,128)S(1)}, u32[]{:S(2)}, u32[]{:S(2)}) collective-permute-start(f32[33,8,128]{2,1,0:T(8,128)S(1)} %get-tuple-element.42), channel_id=1, source_target_pairs={{0,2},{2,4},{4,6},{6,8},{8,10},{10,12},{12,14},{1,3},{3,5},{5,7},{... | collective-permute-start | bytes 405512 | tf_op jit(solution)/shard_map/ppermute | solution.py:299
  30.8 6.9 %collective-permute-start.6 = (f32[33,8,128]{2,1,0:T(8,128)S(1)}, f32[33,8,128]{2,1,0:T(8,128)S(1)}, u32[]{:S(2)}, u32[]{:S(2)}) collective-permute-start(f32[33,8,128]{2,1,0:T(8,128)S(1)} %get-tuple-element.44), channel_id=1, source_target_pairs={{2,0},{4,2},{6,4},{8,6},{10,8},{12,10},{14,12},{3,1},{5,3},{7,5},{... | collective-permute-start | bytes 405512 | tf_op jit(solution)/shard_map/ppermute | solution.py:302
  33.5 9.9 %collective-permute-start.8 = (f32[33,8,128]{2,1,0:T(8,128)S(1)}, f32[33,8,128]{2,1,0:T(8,128)S(1)}, u32[]{:S(2)}, u32[]{:S(2)}) collective-permute-start(f32[33,8,128]{2,1,0:T(8,128)S(1)} %get-tuple-element.48), channel_id=1, source_target_pairs={{2,0},{4,2},{6,4},{8,6},{10,8},{12,10},{14,12},{3,1},{5,3},{7,5},{... | collective-permute-start | bytes 405512 | tf_op jit(solution)/shard_map/ppermute | solution.py:302
  39.1 8.6 %collective-permute-start.7 = (f32[33,8,128]{2,1,0:T(8,128)S(1)}, f32[33,8,128]{2,1,0:T(8,128)S(1)}, u32[]{:S(2)}, u32[]{:S(2)}) collective-permute-start(f32[33,8,128]{2,1,0:T(8,128)S(1)} %get-tuple-element.46), channel_id=1, source_target_pairs={{0,2},{2,4},{4,6},{6,8},{8,10},{10,12},{12,14},{1,3},{3,5},{5,7},{... | collective-permute-start | bytes 405512 | tf_op jit(solution)/shard_map/ppermute | solution.py:299
  44.9 5.5 %collective-permute-start.9 = (f32[33,8,128]{2,1,0:T(8,128)S(1)}, f32[33,8,128]{2,1,0:T(8,128)S(1)}, u32[]{:S(2)}, u32[]{:S(2)}) collective-permute-start(f32[33,8,128]{2,1,0:T(8,128)S(1)} %get-tuple-element.50), channel_id=1, source_target_pairs={{0,2},{2,4},{4,6},{6,8},{8,10},{10,12},{12,14},{1,3},{3,5},{5,7},{... | collective-permute-start | bytes 405512 | tf_op jit(solution)/shard_map/ppermute | solution.py:299
  49.2 8.3 %collective-permute-start.10 = (f32[33,8,128]{2,1,0:T(8,128)S(1)}, f32[33,8,128]{2,1,0:T(8,128)S(1)}, u32[]{:S(2)}, u32[]{:S(2)}) collective-permute-start(f32[33,8,128]{2,1,0:T(8,128)S(1)} %get-tuple-element.52), channel_id=1, source_target_pairs={{2,0},{4,2},{6,4},{8,6},{10,8},{12,10},{14,12},{3,1},{5,3},{7,5},{... | collective-permute-start | bytes 405512 | tf_op jit(solution)/shard_map/ppermute | solution.py:302
  51.9 11.9 %collective-permute-start.12 = (f32[33,8,128]{2,1,0:T(8,128)S(1)}, f32[33,8,128]{2,1,0:T(8,128)S(1)}, u32[]{:S(2)}, u32[]{:S(2)}) collective-permute-start(f32[33,8,128]{2,1,0:T(8,128)S(1)} %get-tuple-element.56), channel_id=1, source_target_pairs={{2,0},{4,2},{6,4},{8,6},{10,8},{12,10},{14,12},{3,1},{5,3},{7,5},{... | collective-permute-start | bytes 405512 | tf_op jit(solution)/shard_map/ppermute | solution.py:302
  58.9 8.2 %collective-permute-start.11 = (f32[33,8,128]{2,1,0:T(8,128)S(1)}, f32[33,8,128]{2,1,0:T(8,128)S(1)}, u32[]{:S(2)}, u32[]{:S(2)}) collective-permute-start(f32[33,8,128]{2,1,0:T(8,128)S(1)} %get-tuple-element.54), channel_id=1, source_target_pairs={{0,2},{2,4},{4,6},{6,8},{8,10},{10,12},{12,14},{1,3},{3,5},{5,7},{... | collective-permute-start | bytes 405512 | tf_op jit(solution)/shard_map/ppermute | solution.py:299
  65.2 8.2 %collective-permute-start.13 = (f32[33,8,128]{2,1,0:T(8,128)S(1)}, f32[33,8,128]{2,1,0:T(8,128)S(1)}, u32[]{:S(2)}, u32[]{:S(2)}) collective-permute-start(f32[33,8,128]{2,1,0:T(8,128)S(1)} %get-tuple-element.58), channel_id=1, source_target_pairs={{0,2},{2,4},{4,6},{6,8},{8,10},{10,12},{12,14},{1,3},{3,5},{5,7},{... | collective-permute-start | bytes 405512 | tf_op jit(solution)/shard_map/ppermute | solution.py:299
  68.6 7.9 %collective-permute-start.14 = (f32[33,8,128]{2,1,0:T(8,128)S(1)}, f32[33,8,128]{2,1,0:T(8,128)S(1)}, u32[]{:S(2)}, u32[]{:S(2)}) collective-permute-start(f32[33,8,128]{2,1,0:T(8,128)S(1)} %get-tuple-element.59), channel_id=1, source_target_pairs={{2,0},{4,2},{6,4},{8,6},{10,8},{12,10},{14,12},{3,1},{5,3},{7,5},{... | collective-permute-start | bytes 405512 | tf_op jit(solution)/shard_map/ppermute | solution.py:302

commit v2 on v0

v2 whole, which is shorter than its diff:
```python
import functools
import math

import jax
import jax.numpy as jnp
from jax import lax
from jax.experimental import pallas as pl
from jax.experimental.pallas import tpu as pltpu
from jax.sharding import PartitionSpec as P

CHEB = 6
LANES = 128
SUBS = 8

lower_edge = 0.25
upper_edge = 12.0


def cheb_weights(degree, low_end, high_end):
    count = degree + 1
    values = []
    for order in range(count):
        accum = 0.0
        for node in range(count):
            angle = math.pi * (node + 0.5) / count
            point = 0.5 * (high_end - low_end) * math.cos(angle) + 0.5 * (high_end + low_end)
            accum += math.cos(order * angle) / point
        accum = accum * 2.0 / count
        if order == 0:
            accum = accum * 0.5
        values.append(accum)
    return values


def vmem_spec():
    return pl.BlockSpec(memory_space=pltpu.VMEM)


def params():
    return pltpu.CompilerParams(vmem_limit_bytes=40 * 1024 * 1024)


def cost(vregs):
    return pl.CostEstimate(flops=vregs * 1024 * 20, bytes_accessed=vregs * 4096 * 4, transcendentals=0)


def masks():
    lane = lax.broadcasted_iota(jnp.int32, (SUBS, LANES), 1)
    return lane == 0, lane == LANES - 1


def window_tiles(load, first, count, total):
    before = jnp.where(first > 0, load(jnp.maximum(first - 1, 0)), 0.0)
    after = jnp.where(first + count < total, load(jnp.minimum(first + count, total - 1)), 0.0)
    return [before] + [load(first + k) for k in range(count)] + [after]


def beside(before, here, after, edges):
    left = pltpu.roll(jnp.where(edges[1], before, here), 1, 1)
    right = pltpu.roll(jnp.where(edges[0], after, here), LANES - 1, 1)
    return left, right


def sub(row):
    return pl.ds(row * SUBS, SUBS)


def tile_columns(tile):
    return pl.ds(pl.multiple_of(tile * LANES, LANES), LANES)


def chunk_of(tiles):
    return max(count for count in range(1, 12) if tiles % count == 0)


def load_kernel(width, probes_ref, observed_ref, coefficients_ref, theirs_ref, own_ref, seen_ref, window_ref, sem):
    core = lax.axis_index("probe")
    move = probes_ref.shape[3] - width
    mine = pl.ds(pl.multiple_of(core * move, LANES), width)
    other = pl.ds(pl.multiple_of((1 - core) * move, LANES), width)
    copies = [
        pltpu.make_async_copy(probes_ref.at[:, :, :, other], theirs_ref, sem.at[0]),
        pltpu.make_async_copy(probes_ref.at[:, :, :, mine], own_ref, sem.at[1]),
        pltpu.make_async_copy(coefficients_ref.at[:, :, mine], window_ref, sem.at[2]),
        pltpu.make_async_copy(observed_ref.at[:, :, mine], seen_ref, sem.at[3]),
    ]
    for copy in copies:
        copy.start()
    for copy in copies:
        copy.wait()


def prep_kernel(window_ref, expanded_ref):
    tiles = expanded_ref.shape[1]
    chunk = chunk_of(tiles)
    scale = 4.0 / (upper_edge - lower_edge)
    shift = 2.0 * (upper_edge + lower_edge) / (upper_edge - lower_edge)

    def body(step, carry):
        for k in range(chunk):
            tile = step * chunk + k
            cols = tile_columns(tile)
            kappa, across, along, skew = [
                [window_ref[2 * kind + c, :, cols] for c in range(2)] for kind in range(4)
            ]
            coupling = scale * window_ref[8, :, cols]
            for c in range(2):
                values = (
                    scale * (kappa[c] + 2.0 * (across[c] + along[c])) - shift,
                    -scale * across[c],
                    -scale * along[c],
                    -0.5 * scale * skew[c],
                    coupling,
                )
                for kind, value in enumerate(values):
                    for probe in range(4):
                        expanded_ref[kind, tile, pl.ds(4 * c + probe, SUBS, stride=SUBS), :] = value
        return carry

    lax.fori_loop(0, tiles // chunk, body, 0)


def layout_kernel(own_ref, other_ref, seen_ref, z_ref, top_ref, bottom_ref):
    tiles = z_ref.shape[0]
    chunk = chunk_of(tiles)

    def body(step, carry):
        for k in range(chunk):
            tile = step * chunk + k
            cols = tile_columns(tile)
            for c in range(2):
                for probe in range(2):
                    z_ref[tile, pl.ds(4 * c + probe, SUBS, stride=SUBS), :] = own_ref[probe, c, :, cols]
                    z_ref[tile, pl.ds(4 * c + 2 + probe, SUBS, stride=SUBS), :] = other_ref[probe, c, :, cols]
        return carry

    lax.fori_loop(0, tiles // chunk, body, 0)
    for tile in range(tiles):
        top_ref[tile] = z_ref[tile, sub(0), :]
        bottom_ref[tile] = z_ref[tile, sub(SUBS - 1), :]
    for c in range(2):
        for tile in range(tiles):
            place = c * tiles + tile
            cols = pl.ds(tile * LANES, LANES)
            at = (tiles + place // SUBS, pl.ds(place % SUBS, 1))
            top_ref[at[0], at[1], :] = seen_ref[c, 0:1, cols]
            bottom_ref[at[0], at[1], :] = seen_ref[c, SUBS - 1 : SUBS, cols]


def step_kernel(upper, constants, offset, other_row, tiles, *refs):
    weight, scale, subtract = constants
    own_ref, other_ref, halo_ref, z_ref, coefficients_ref = refs[:5]
    rest = refs[5:]
    before_ref = None
    if subtract:
        before_ref, rest = rest[0], rest[1:]
    out_ref, edge_ref = rest
    first_row = 0 if upper else 4
    chunk = chunk_of(tiles)

    def load(row):
        if row == (-1 if upper else 4):
            return lambda tile: halo_ref[tile]
        if row == (4 if upper else -1):
            return lambda tile: other_ref[tile, sub(other_row), :]
        return lambda tile: own_ref[tile, sub(offset + row), :]

    def body(step, carry):
        edges = masks()
        first = step * chunk
        for k in range(chunk):
            tile = first + k
            values, sums, slopes = [], [], []
            for row in range(-1, 5):
                loader = load(row)
                here = loader(tile)
                if k == 0:
                    before = jnp.where(first > 0, loader(jnp.maximum(first - 1, 0)), 0.0)
                else:
                    before = loader(tile - 1)
                if k == chunk - 1:
                    last = first + chunk < tiles
                    after = jnp.where(last, loader(jnp.minimum(first + chunk, tiles - 1)), 0.0)
                else:
                    after = loader(tile + 1)
                left, right = beside(before, here, after, edges)
                values.append(here)
                sums.append(left + right)
                slopes.append(right - left)
            for row in range(4):
                rows = sub(first_row + row)
                coefs = [coefficients_ref[kind, tile, rows, :] for kind in range(5)]
                total = (
                    coefs[0] * values[row + 1]
                    + coefs[1] * sums[row + 1]
                    + coefs[2] * (values[row] + values[row + 2])
                    + coefs[3] * (slopes[row + 2] - slopes[row])
                    + coefs[4] * pltpu.roll(values[row + 1], 4, 0)
                )
                if scale != 1.0:
                    total = scale * total
                total = total + weight * z_ref[tile, rows, :]
                if subtract:
                    total = total - before_ref[tile, sub(row), :]
                out_ref[tile, sub(row), :] = total
                if row == (0 if upper else 3):
                    edge_ref[tile] = total
        return carry

    lax.fori_loop(0, tiles // chunk, body, 0)


def data_kernel(tiles, seen_ref, up_ref, down_ref, out_ref):
    chunk = chunk_of(tiles)

    def halo(ref, c, tile):
        place = c * tiles + tile
        return jnp.broadcast_to(ref[tiles + place // SUBS, pl.ds(place % SUBS, 1), :], (SUBS, LANES))

    def body(step, carry):
        edges = masks()
        row = lax.broadcasted_iota(jnp.int32, (SUBS, LANES), 0)
        first = step * chunk
        kept = [[], []]
        for c in range(2):
            values = window_tiles(lambda tile: seen_ref[c, :, tile_columns(tile)], first, chunk, tiles)
            ups = window_tiles(lambda tile: halo(up_ref, c, tile), first, chunk, tiles)
            downs = window_tiles(lambda tile: halo(down_ref, c, tile), first, chunk, tiles)
            aboves = [jnp.where(row == 0, u, pltpu.roll(v, 1, 0)) for u, v in zip(ups, values)]
            belows = [jnp.where(row == SUBS - 1, d, pltpu.roll(v, SUBS - 1, 0)) for d, v in zip(downs, values)]
            tilts = [b - a for a, b in zip(aboves, belows)]
            for k in range(chunk):
                tile = first + k
                value = values[k + 1]
                left, right = beside(values[k], value, values[k + 2], edges)
                low, high = beside(tilts[k], tilts[k + 1], tilts[k + 2], edges)
                half = -0.5 * value
                out_ref[tile, c] = half * value
                out_ref[tile, 2 + c] = half * (2.0 * value - (left + right))
                out_ref[tile, 4 + c] = half * (2.0 * value - (aboves[k + 1] + belows[k + 1]))
                out_ref[tile, 6 + c] = (-0.5 * half) * (high - low)
                kept[c].append(value)
        for k in range(chunk):
            out_ref[first + k, 8] = -(kept[0][k] * kept[1][k])
        return carry

    lax.fori_loop(0, tiles // chunk, body, 0)


def gradient_kernel(tiles, factor, z_ref, top_ref, bottom_ref, data_ref, out_ref, products):
    kept = out_ref.shape[2] // LANES
    offset = lax.axis_index("probe") * (tiles - kept)
    count = products.shape[0]

    def load(row):
        if row < 4:
            return lambda tile: top_ref[tile, sub(row), :]
        return lambda tile: bottom_ref[tile, sub(row - 4), :]

    def body(step, carry):
        edges = masks()
        for k in range(count):
            index = step * count + k
            tile = index + offset
            values, sums, slopes = [], [], []
            for row in range(SUBS):
                loader = load(row)
                before, here, after = window_tiles(loader, tile, 1, tiles)
                left, right = beside(before, here, after, edges)
                values.append(here)
                sums.append(left + right)
                slopes.append(right - left)
            for row in range(SUBS):
                left = factor * z_ref[tile, sub(row), :]
                value = values[row]
                twice = 2.0 * value
                if row == 0:
                    along, skew = values[1], slopes[1]
                elif row == SUBS - 1:
                    along, skew = values[row - 1], -slopes[row - 1]
                else:
                    along, skew = values[row - 1] + values[row + 1], slopes[row + 1] - slopes[row - 1]
                products[k, 0, sub(row), :] = left * value
                products[k, 1, sub(row), :] = left * (twice - sums[row])
                products[k, 2, sub(row), :] = left * (twice - along)
                products[k, 3, sub(row), :] = (-0.5 * left) * skew
                products[k, 4, sub(row), :] = left * pltpu.roll(value, 4, 0)
        for k in range(count):
            index = step * count + k
            tile = index + offset
            cols = tile_columns(index)
            for kind in range(5):
                parts = [products[k, kind, pl.ds(s, SUBS, stride=SUBS), :] for s in range(SUBS)]
                sums = [(parts[4 * c] + parts[4 * c + 1]) + (parts[4 * c + 2] + parts[4 * c + 3]) for c in range(2)]
                if kind < 4:
                    for c in range(2):
                        out_ref[2 * kind + c, :, cols] = sums[c] + data_ref[tile, 2 * kind + c]
                else:
                    out_ref[8, :, cols] = (sums[0] + sums[1]) + data_ref[tile, 8]
        return carry

    lax.fori_loop(0, kept // count, body, 0)


def finish_kernel(tiles, factor, part_ref, z_ref, up_ref, down_ref, out_ref, fixed, sem):
    kept = out_ref.shape[2] // LANES
    offset = lax.axis_index("probe") * (tiles - kept)
    count = max(n for n in range(1, 9) if kept % n == 0)
    early = [
        pltpu.make_async_copy(part_ref.at[pl.ds(0, 4)], out_ref.at[pl.ds(0, 4)], sem.at[0]),
        pltpu.make_async_copy(part_ref.at[pl.ds(8, 1)], out_ref.at[pl.ds(8, 1)], sem.at[1]),
    ]
    for copy in early:
        copy.start()

    def body(step, carry):
        edges = masks()
        row = lax.broadcasted_iota(jnp.int32, (SUBS, LANES), 0)
        for k in range(count):
            index = step * count + k
            tile = index + offset
            cols = tile_columns(index)
            adds = []
            for ref, z_row, sign in ((up_ref, 0, 0.5), (down_ref, SUBS - 1, -0.5)):
                before, here, after = window_tiles(lambda at: ref[at], tile, 1, tiles)
                left, right = beside(before, here, after, edges)
                z = factor * z_ref[tile, sub(z_row), :]
                pair = []
                for term in (-z * here, (sign * z) * (right - left)):
                    term = term + pltpu.roll(term, 1, 0)
                    pair.append(term + pltpu.roll(term, 2, 0))
                adds.append(pair)
            for kind in range(2):
                for c in range(2):
                    at = 4 * c + 3
                    channel = 2 * kind + c
                    top = jnp.broadcast_to(adds[0][kind][at : at + 1, :], (SUBS, LANES))
                    bottom = jnp.broadcast_to(adds[1][kind][at : at + 1, :], (SUBS, LANES))
                    more = jnp.where(row == 0, top, jnp.where(row == SUBS - 1, bottom, 0.0))
                    fixed[channel, :, cols] = part_ref[4 + channel, :, cols] + more
        return carry

    lax.fori_loop(0, kept // count, body, 0)
    late = pltpu.make_async_copy(fixed, out_ref.at[pl.ds(4, 4)], sem.at[2])
    late.start()
    late.wait()
    for copy in early:
        copy.wait()


def per_device(observations, coefficients, probes):
    weights = cheb_weights(CHEB, lower_edge, upper_edge)
    f32 = jnp.float32
    columns = probes.shape[3]
    share = columns // lax.axis_size("probe")
    width = share + LANES
    tiles = width // LANES
    kept = share // LANES
    seen_tiles = -(-2 * tiles // SUBS)
    rows = lax.axis_size("row")
    down_pairs = [(i, i + 1) for i in range(rows - 1)]
    up_pairs = [(i + 1, i) for i in range(rows - 1)]

    def to_next(edge):
        return lax.ppermute(edge, "row", down_pairs)

    def to_previous(edge):
        return lax.ppermute(edge, "row", up_pairs)

    def call(kernel, name, vregs, operands, outs, scratch=(), in_specs=None, out_specs=None):
        return pl.pallas_call(
            kernel,
            out_shape=outs,
            in_specs=in_specs or [vmem_spec()] * len(operands),
            out_specs=out_specs or jax.tree.map(lambda _: vmem_spec(), outs),
            scratch_shapes=scratch,
            compiler_params=params(),
            cost_estimate=cost(vregs),
            name=name,
        )(*operands)

    theirs, own, seen, window = call(
        functools.partial(load_kernel, width),
        "load",
        100,
        [
            pltpu.with_memory_space_constraint(array, pltpu.HBM)
            for array in (probes, observations, coefficients)
        ],
        [
            pltpu.VMEM((2, 2, SUBS, width), f32),
            pltpu.VMEM((2, 2, SUBS, width), f32),
            pltpu.VMEM((2, SUBS, width), f32),
            pltpu.VMEM((9, SUBS, width), f32),
        ],
        [pltpu.SemaphoreType.DMA((4,))],
        [pl.BlockSpec(memory_space=pltpu.HBM)] * 3,
    )
    other = lax.ppermute(theirs, "probe", [(0, 1), (1, 0)])
    expanded = call(
        prep_kernel, "prep", 5 * 8 * tiles, (window,), pltpu.VMEM((5, tiles, SUBS * SUBS, LANES), f32)
    )
    own, expanded = lax.optimization_barrier((own, expanded))
    message = (tiles + seen_tiles, SUBS, LANES)
    z, top, bottom = call(
        layout_kernel,
        "layout",
        8 * tiles,
        (own, other, seen),
        [pltpu.VMEM((tiles, SUBS * SUBS, LANES), f32), pltpu.VMEM(message, f32), pltpu.VMEM(message, f32)],
    )

    def half(upper, constants, own, other_half, halo, before):
        shared = own is z
        offset = (0 if upper else 4) if shared else 0
        other_row = (4 if upper else 3) if shared else (0 if upper else 3)
        operands = [own, other_half, halo, z, expanded]
        if constants[2]:
            operands.append(before)
        return call(
            functools.partial(step_kernel, upper, constants, offset, other_row, tiles),
            "upper" if upper else "lower",
            4 * tiles,
            operands,
            [pltpu.VMEM((tiles, 4 * SUBS, LANES), f32), pltpu.VMEM((tiles, SUBS, LANES), f32)],
        )

    first_up, first_down = to_next(bottom), to_previous(top)
    up, down = first_up, first_down
    now = (z, z)
    before = (None, None)
    for order in range(CHEB - 1, -1, -1):
        if order == CHEB - 1:
            constants = (weights[order], weights[CHEB], False)
        elif order == CHEB - 2:
            constants = (weights[order] - weights[CHEB], 1.0, False)
        elif order > 0:
            constants = (weights[order], 1.0, True)
        else:
            constants = (weights[0], 0.5, True)
        upper, top = half(True, constants, now[0], now[1], up, before[0])
        next_down = to_previous(top)
        lower, bottom = half(False, constants, now[1], now[0], down, before[1])
        next_up = to_next(bottom)
        before, now = now, (upper, lower)
        up, down = next_up, next_down

    data = call(
        functools.partial(data_kernel, tiles),
        "data",
        9 * tiles,
        (seen, first_up, first_down),
        pltpu.VMEM((tiles, 9, SUBS, LANES), f32),
    )
    factor = 0.5 / (probes.shape[0] * lax.axis_size("probe"))
    count = max(n for n in range(1, 5) if kept % n == 0)
    part = call(
        functools.partial(gradient_kernel, tiles, factor),
        "gradient",
        24 * tiles,
        (z, now[0], now[1], data),
        pltpu.VMEM((9, SUBS, share), f32),
        [pltpu.VMEM((count, 5, SUBS * SUBS, LANES), f32)],
    )
    return call(
        functools.partial(finish_kernel, tiles, factor),
        "finish",
        8 * tiles,
        (part, z, up, down),
        jax.ShapeDtypeStruct((9, SUBS, share), f32),
        [pltpu.VMEM((4, SUBS, share), f32), pltpu.SemaphoreType.DMA((3,))],
        None,
        pl.BlockSpec(memory_space=pltpu.HBM),
    )


def solution(mesh):
    in_specs = (P("group", "row", None), P("group", "row", None), P("probe", "group", "row", None))
    out_specs = P("group", "row", "probe")
    return jax.shard_map(
        per_device, mesh=mesh, in_specs=in_specs, out_specs=out_specs, check_vma=False
    )
```

time: 146 us -> 71.3 us (0.49)
  other arithmetic: 43.8 us -> 0 us
  waiting for transfers between devices: 44.3 us -> 15.8 us
  Pallas kernels: 0 us -> 15 us
  between operations: 13.7 us -> 0.28 us
  local copies, waits for them, and re-layouts: 5.26 us -> 0 us
  starting transfers between devices: 37.9 us -> 39.7 us
    ppermute x14 -> x15, waiting for transfers between devices: 36.7 us -> 15.8 us  [the longest x7 9.83 us: to_previous(): return lax.ppermute(edge, 'row', up_pairs)]
    pallas_call x0 -> x18, Pallas kernels: none -> 15 us  [call(): pl.pallas_call(kernel, out_shape=outs, in_specs=in_specs or [vmem_spec()]...]
    unnamed x8 -> x0, other arithmetic: 12 us -> none
    sub x5 -> x0, other arithmetic: 9.91 us -> none  [the longest x4 7.14 us: per_device(): following = 2.0 * product(current) - previous]
    concatenate x9 -> x0, other arithmetic: 9.21 us -> none  [the longest x7 7.52 us: extended(): shard = jnp.concatenate([before, shard, after], axis=dim)]
    reduce_scatter x1 -> x0, waiting for transfers between devices: 7.61 us -> none  [per_device(): lax.psum_scatter(probe_sum, 'probe', scatter_dimension=2, tiled=True)]
    reduce_sum x1 -> x0, other arithmetic: 4.38 us -> none  [per_device(): probe_sum = jnp.sum(gradient_terms(probes, series_wide), axis=0)]
    slice x9 -> x0, local copies, waits for them, and re-layouts: 2.91 us -> none  [the longest x7 2.64 us: extended(): last = lax.slice_in_dim(shard, length - width, length, axis=dim)]
  transfers between devices with their start and end apart: 15 -> 15, of which waited for: 13 -> 8; matrix products, arithmetic and copies ran while one was open for 7% -> 0% of each run, Pallas kernels for 0% -> 17%
where the time goes in v2:
time: 71.3 us; the launch traced here: 70.8 us
  starting transfers between devices  39.7 us (56%)
  waiting for transfers between devices  15.8 us (22%)
  Pallas kernels  15 us (21%)
    ppermute x7, starting transfers between devices, to_next(): return lax.ppermute(edge, 'row', down_pairs)  30.1 us
    pallas_call x18, Pallas kernels, call(): pl.pallas_call(kernel, out_shape=outs, in_specs=in_specs or [vmem_spec()]...  15 us
    ppermute x7, waiting for transfers between devices, to_previous(): return lax.ppermute(edge, 'row', up_pairs)  9.83 us
    ppermute x7, starting transfers between devices, to_previous(): return lax.ppermute(edge, 'row', up_pairs)  9.04 us
    ppermute x7, waiting for transfers between devices, to_next(): return lax.ppermute(edge, 'row', down_pairs)  5.26 us
  transfers between devices with their start and end apart: 15, of which 8 were waited for; matrix products, arithmetic and copies ran while one was open for 0% of the time, Pallas kernels for 17%

profile of v2, /device:TPU:0, one launch (start us, length us, event | category | flops | bytes accessed | tf_op | source)
XLA Modules:
  0.0 70.8 jit_solution(1914763427254183489)
XLA Ops:
  0.0 1.7 %load.1 = (f32[2,2,8,4224]{3,2,1,0:T(8,128)S(1)}, f32[2,2,8,4224]{3,2,1,0:T(8,128)S(1)}, f32[2,8,4224]{2,1,0:T(8,128)S(1)}, f32[9,8,4224]{2,1,0:T(8,128)S(1)}) custom-call(f32[2,2,8,8192]{3,2,1,0:T(8,128)} %probes_ref.1, f32[2,8,8192]{2,1,0:T(8,128)} %observed_ref.1, f32[9,8,8192]{2,1,0:T(8,128)} %coefficients_ref.1), custom_call_target="tpu_custom_call" | custom-call | flops 2048000 | bytes 1638400 | tf_op jit(solution)/shard_map/load/pallas_call | solution.py:371
  1.7 0.5 collective-permute-start
  2.2 0.8 %prep.1.refs_4_ = f32[5,33,64,128]{3,2,1,0:T(8,128)S(1)} custom-call(f32[9,8,4224]{2,1,0:T(8,128)S(1)} %get-tuple-element.39.window_ref), custom_call_target="tpu_custom_call" | custom-call | flops 27033600 | bytes 21626880 | tf_op jit(solution)/shard_map/prep/pallas_call | solution.py:371
  3.0 0.7 %collective-permute-done.other_ref = f32[2,2,8,4224]{3,2,1,0:T(8,128)S(1)} collective-permute-done((f32[2,2,8,4224]{3,2,1,0:T(8,128)S(1)}, f32[2,2,8,4224]{3,2,1,0:T(8,128)S(1)}, u32[]{:S(2)}, u32[]{:S(2)}) %collective-permute-start) | collective-permute-done | bytes 540704 | tf_op jit(solution)/shard_map/ppermute | solution.py:399
  3.8 0.3 layout.1
  4.0 4.8 %collective-permute-start.1 = (f32[42,8,128]{2,1,0:T(8,128)S(1)}, f32[42,8,128]{2,1,0:T(8,128)S(1)}, u32[]{:S(2)}, u32[]{:S(2)}) collective-permute-start(f32[42,8,128]{2,1,0:T(8,128)S(1)} %get-tuple-element.44), channel_id=1, source_target_pairs={{0,2},{2,4},{4,6},{6,8},{8,10},{10,12},{12,14},{1,3},{3,5},{5,7},{... | collective-permute-start | bytes 516104 | tf_op jit(solution)/shard_map/ppermute | solution.py:365
  8.8 1.3 %collective-permute-start.2 = (f32[42,8,128]{2,1,0:T(8,128)S(1)}, f32[42,8,128]{2,1,0:T(8,128)S(1)}, u32[]{:S(2)}, u32[]{:S(2)}) collective-permute-start(f32[42,8,128]{2,1,0:T(8,128)S(1)} %get-tuple-element.47), channel_id=1, source_target_pairs={{2,0},{4,2},{6,4},{8,6},{10,8},{12,10},{14,12},{3,1},{5,3},{7,5},{... | collective-permute-start | bytes 516104 | tf_op jit(solution)/shard_map/ppermute | solution.py:368
  10.1 2.6 %collective-permute-done.1.refs_2_.up_ref = f32[42,8,128]{2,1,0:T(8,128)S(1)} collective-permute-done((f32[42,8,128]{2,1,0:T(8,128)S(1)}, f32[42,8,128]{2,1,0:T(8,128)S(1)}, u32[]{:S(2)}, u32[]{:S(2)}) %collective-permute-start.1) | collective-permute-done | bytes 172064 | tf_op jit(solution)/shard_map/ppermute | solution.py:365
  12.7 0.7 upper.6
  13.4 1.3 %collective-permute-start.4 = (f32[33,8,128]{2,1,0:T(8,128)S(1)}, f32[33,8,128]{2,1,0:T(8,128)S(1)}, u32[]{:S(2)}, u32[]{:S(2)}) collective-permute-start(f32[33,8,128]{2,1,0:T(8,128)S(1)} %get-tuple-element.51), channel_id=1, source_target_pairs={{2,0},{4,2},{6,4},{8,6},{10,8},{12,10},{14,12},{3,1},{5,3},{7,5},{... | collective-permute-start | bytes 405512 | tf_op jit(solution)/shard_map/ppermute | solution.py:368
  14.7 2.1 %collective-permute-done.2.refs_2_.down_ref = f32[42,8,128]{2,1,0:T(8,128)S(1)} collective-permute-done((f32[42,8,128]{2,1,0:T(8,128)S(1)}, f32[42,8,128]{2,1,0:T(8,128)S(1)}, u32[]{:S(2)}, u32[]{:S(2)}) %collective-permute-start.2) | collective-permute-done | bytes 172064 | tf_op jit(solution)/shard_map/ppermute | solution.py:368
  16.8 0.7 lower.6
  17.5 4.4 %collective-permute-start.3 = (f32[33,8,128]{2,1,0:T(8,128)S(1)}, f32[33,8,128]{2,1,0:T(8,128)S(1)}, u32[]{:S(2)}, u32[]{:S(2)}) collective-permute-start(f32[33,8,128]{2,1,0:T(8,128)S(1)} %get-tuple-element.49), channel_id=1, source_target_pairs={{0,2},{2,4},{4,6},{6,8},{8,10},{10,12},{12,14},{1,3},{3,5},{5,7},{... | collective-permute-start | bytes 405512 | tf_op jit(solution)/shard_map/ppermute | solution.py:365
  21.9 0.0 collective-permute-done.4.refs_2_
  21.9 0.7 lower.7
  22.6 4.0 %collective-permute-start.5 = (f32[33,8,128]{2,1,0:T(8,128)S(1)}, f32[33,8,128]{2,1,0:T(8,128)S(1)}, u32[]{:S(2)}, u32[]{:S(2)}) collective-permute-start(f32[33,8,128]{2,1,0:T(8,128)S(1)} %get-tuple-element.53), channel_id=1, source_target_pairs={{0,2},{2,4},{4,6},{6,8},{8,10},{10,12},{12,14},{1,3},{3,5},{5,7},{... | collective-permute-start | bytes 405512 | tf_op jit(solution)/shard_map/ppermute | solution.py:365
  26.6 0.0 collective-permute-done.3.refs_2_
  26.6 0.7 upper.7
  27.3 1.3 %collective-permute-start.6 = (f32[33,8,128]{2,1,0:T(8,128)S(1)}, f32[33,8,128]{2,1,0:T(8,128)S(1)}, u32[]{:S(2)}, u32[]{:S(2)}) collective-permute-start(f32[33,8,128]{2,1,0:T(8,128)S(1)} %get-tuple-element.55), channel_id=1, source_target_pairs={{2,0},{4,2},{6,4},{8,6},{10,8},{12,10},{14,12},{3,1},{5,3},{7,5},{... | collective-permute-start | bytes 405512 | tf_op jit(solution)/shard_map/ppermute | solution.py:368
  28.6 0.7 %collective-permute-done.5.refs_2_ = f32[33,8,128]{2,1,0:T(8,128)S(1)} collective-permute-done((f32[33,8,128]{2,1,0:T(8,128)S(1)}, f32[33,8,128]{2,1,0:T(8,128)S(1)}, u32[]{:S(2)}, u32[]{:S(2)}) %collective-permute-start.5) | collective-permute-done | bytes 135200 | tf_op jit(solution)/shard_map/ppermute | solution.py:365
  29.3 0.7 upper.8
  30.0 1.3 %collective-permute-start.8 = (f32[33,8,128]{2,1,0:T(8,128)S(1)}, f32[33,8,128]{2,1,0:T(8,128)S(1)}, u32[]{:S(2)}, u32[]{:S(2)}) collective-permute-start(f32[33,8,128]{2,1,0:T(8,128)S(1)} %get-tuple-element.59), channel_id=1, source_target_pairs={{2,0},{4,2},{6,4},{8,6},{10,8},{12,10},{14,12},{3,1},{5,3},{7,5},{... | collective-permute-start | bytes 405512 | tf_op jit(solution)/shard_map/ppermute | solution.py:368
  31.3 2.9 %collective-permute-done.6.refs_2_ = f32[33,8,128]{2,1,0:T(8,128)S(1)} collective-permute-done((f32[33,8,128]{2,1,0:T(8,128)S(1)}, f32[33,8,128]{2,1,0:T(8,128)S(1)}, u32[]{:S(2)}, u32[]{:S(2)}) %collective-permute-start.6) | collective-permute-done | bytes 135200 | tf_op jit(solution)/shard_map/ppermute | solution.py:368
  34.2 0.7 %lower.8 = (f32[33,32,128]{2,1,0:T(8,128)S(1)}, f32[33,8,128]{2,1,0:T(8,128)S(1)}) custom-call(f32[33,32,128]{2,1,0:T(8,128)S(1)} %get-tuple-element.52.refs_1_.refs_0_.refs_5_, f32[33,32,128]{2,1,0:T(8,128)S(1)} %get-tuple-element.50.refs_0_.refs_1_.refs_5_, f32[33,8,128]{2,1,0:T(8,128)S(1)} %collective-permute-done.6.refs_2_, ...), custom_call_target="tpu_custom_call" | custom-call | flops 2703360 | bytes 2162688 | tf_op jit(solution)/shard_map/lower/pallas_call | solution.py:371
  35.0 4.1 %collective-permute-start.7 = (f32[33,8,128]{2,1,0:T(8,128)S(1)}, f32[33,8,128]{2,1,0:T(8,128)S(1)}, u32[]{:S(2)}, u32[]{:S(2)}) collective-permute-start(f32[33,8,128]{2,1,0:T(8,128)S(1)} %get-tuple-element.57), channel_id=1, source_target_pairs={{0,2},{2,4},{4,6},{6,8},{8,10},{10,12},{12,14},{1,3},{3,5},{5,7},{... | collective-permute-start | bytes 405512 | tf_op jit(solution)/shard_map/ppermute | solution.py:365
  39.1 0.0 collective-permute-done.8.refs_2_
  39.1 0.7 lower.9
  39.8 4.4 %collective-permute-start.9 = (f32[33,8,128]{2,1,0:T(8,128)S(1)}, f32[33,8,128]{2,1,0:T(8,128)S(1)}, u32[]{:S(2)}, u32[]{:S(2)}) collective-permute-start(f32[33,8,128]{2,1,0:T(8,128)S(1)} %get-tuple-element.61), channel_id=1, source_target_pairs={{0,2},{2,4},{4,6},{6,8},{8,10},{10,12},{12,14},{1,3},{3,5},{5,7},{... | collective-permute-start | bytes 405512 | tf_op jit(solution)/shard_map/ppermute | solution.py:365
  44.2 0.0 collective-permute-done.7.refs_2_
  44.2 0.7 %upper.9 = (f32[33,32,128]{2,1,0:T(8,128)S(1)}, f32[33,8,128]{2,1,0:T(8,128)S(1)}) custom-call(f32[33,32,128]{2,1,0:T(8,128)S(1)} %get-tuple-element.54.refs_0_.refs_1_.refs_5_, f32[33,32,128]{2,1,0:T(8,128)S(1)} %get-tuple-element.56.refs_1_.refs_0_.refs_5_, f32[33,8,128]{2,1,0:T(8,128)S(1)} %collective-permute-done.7.refs_2_, ...), custom_call_target="tpu_custom_call" | custom-call | flops 2703360 | bytes 2162688 | tf_op jit(solution)/shard_map/upper/pallas_call | solution.py:371
  44.9 1.3 %collective-permute-start.10 = (f32[33,8,128]{2,1,0:T(8,128)S(1)}, f32[33,8,128]{2,1,0:T(8,128)S(1)}, u32[]{:S(2)}, u32[]{:S(2)}) collective-permute-start(f32[33,8,128]{2,1,0:T(8,128)S(1)} %get-tuple-element.63), channel_id=1, source_target_pairs={{2,0},{4,2},{6,4},{8,6},{10,8},{12,10},{14,12},{3,1},{5,3},{7,5},{... | collective-permute-start | bytes 405512 | tf_op jit(solution)/shard_map/ppermute | solution.py:368
  46.2 1.9 %collective-permute-done.9.refs_2_ = f32[33,8,128]{2,1,0:T(8,128)S(1)} collective-permute-done((f32[33,8,128]{2,1,0:T(8,128)S(1)}, f32[33,8,128]{2,1,0:T(8,128)S(1)}, u32[]{:S(2)}, u32[]{:S(2)}) %collective-permute-start.9) | collective-permute-done | bytes 135200 | tf_op jit(solution)/shard_map/ppermute | solution.py:365
  48.2 0.7 %upper.10 = (f32[33,32,128]{2,1,0:T(8,128)S(1)}, f32[33,8,128]{2,1,0:T(8,128)S(1)}) custom-call(f32[33,32,128]{2,1,0:T(8,128)S(1)} %get-tuple-element.58.refs_0_.refs_1_.refs_5_, f32[33,32,128]{2,1,0:T(8,128)S(1)} %get-tuple-element.60.refs_1_.refs_0_.refs_5_, f32[33,8,128]{2,1,0:T(8,128)S(1)} %collective-permute-done.9.refs_2_, ...), custom_call_target="tpu_custom_call" | custom-call | flops 2703360 | bytes 2162688 | tf_op jit(solution)/shard_map/upper/pallas_call | solution.py:371
  48.9 1.3 %collective-permute-start.12 = (f32[33,8,128]{2,1,0:T(8,128)S(1)}, f32[33,8,128]{2,1,0:T(8,128)S(1)}, u32[]{:S(2)}, u32[]{:S(2)}) collective-permute-start(f32[33,8,128]{2,1,0:T(8,128)S(1)} %get-tuple-element.67), channel_id=1, source_target_pairs={{2,0},{4,2},{6,4},{8,6},{10,8},{12,10},{14,12},{3,1},{5,3},{7,5},{... | collective-permute-start | bytes 405512 | tf_op jit(solution)/shard_map/ppermute | solution.py:368
  50.2 1.7 %collective-permute-done.10.refs_2_ = f32[33,8,128]{2,1,0:T(8,128)S(1)} collective-permute-done((f32[33,8,128]{2,1,0:T(8,128)S(1)}, f32[33,8,128]{2,1,0:T(8,128)S(1)}, u32[]{:S(2)}, u32[]{:S(2)}) %collective-permute-start.10) | collective-permute-done | bytes 135200 | tf_op jit(solution)/shard_map/ppermute | solution.py:368
  51.9 0.7 lower.10
  52.6 4.8 %collective-permute-start.11 = (f32[33,8,128]{2,1,0:T(8,128)S(1)}, f32[33,8,128]{2,1,0:T(8,128)S(1)}, u32[]{:S(2)}, u32[]{:S(2)}) collective-permute-start(f32[33,8,128]{2,1,0:T(8,128)S(1)} %get-tuple-element.65), channel_id=1, source_target_pairs={{0,2},{2,4},{4,6},{6,8},{8,10},{10,12},{12,14},{1,3},{3,5},{5,7},{... | collective-permute-start | bytes 405512 | tf_op jit(solution)/shard_map/ppermute | solution.py:365
  57.4 0.0 collective-permute-done.12.refs_2_
  57.4 0.7 %lower.11 = (f32[33,32,128]{2,1,0:T(8,128)S(1)}, f32[33,8,128]{2,1,0:T(8,128)S(1)}) custom-call(f32[33,32,128]{2,1,0:T(8,128)S(1)} %get-tuple-element.64.refs_1_.refs_0_, f32[33,32,128]{2,1,0:T(8,128)S(1)} %get-tuple-element.62.refs_0_.refs_1_, f32[33,8,128]{2,1,0:T(8,128)S(1)} %collective-permute-done.12.refs_2_, ...), custom_call_target="tpu_custom_call" | custom-call | flops 2703360 | bytes 2162688 | tf_op jit(solution)/shard_map/lower/pallas_call | solution.py:371
  58.1 3.7 %collective-permute-start.13 = (f32[33,8,128]{2,1,0:T(8,128)S(1)}, f32[33,8,128]{2,1,0:T(8,128)S(1)}, u32[]{:S(2)}, u32[]{:S(2)}) collective-permute-start(f32[33,8,128]{2,1,0:T(8,128)S(1)} %get-tuple-element.69), channel_id=1, source_target_pairs={{0,2},{2,4},{4,6},{6,8},{8,10},{10,12},{12,14},{1,3},{3,5},{5,7},{... | collective-permute-start | bytes 405512 | tf_op jit(solution)/shard_map/ppermute | solution.py:365
  61.8 0.0 collective-permute-done.11.refs_2_
  61.8 0.7 upper.11
  62.5 1.3 %collective-permute-start.14 = (f32[33,8,128]{2,1,0:T(8,128)S(1)}, f32[33,8,128]{2,1,0:T(8,128)S(1)}, u32[]{:S(2)}, u32[]{:S(2)}) collective-permute-start(f32[33,8,128]{2,1,0:T(8,128)S(1)} %get-tuple-element.70), channel_id=1, source_target_pairs={{2,0},{4,2},{6,4},{8,6},{10,8},{12,10},{14,12},{3,1},{5,3},{7,5},{... | collective-permute-start | bytes 405512 | tf_op jit(solution)/shard_map/ppermute | solution.py:368
  63.8 0.8 %data.1.data_ref = f32[33,9,8,128]{3,2,1,0:T(8,128)S(1)} custom-call(f32[2,8,4224]{2,1,0:T(8,128)S(1)} %get-tuple-element.42.seen_ref, f32[42,8,128]{2,1,0:T(8,128)S(1)} %collective-permute-done.1.refs_2_.up_ref, f32[42,8,128]{2,1,0:T(8,128)S(1)} %collective-permute-done.2.refs_2_.down_ref), custom_call_target="tpu_custom_call" | custom-call | flops 6082560 | bytes 4866048 | tf_op jit(solution)/shard_map/data/pallas_call | solution.py:371
  64.6 1.7 %gradient.1.part_ref = f32[9,8,4096]{2,1,0:T(8,128)S(1)} custom-call(f32[33,64,128]{2,1,0:T(8,128)S(1)} %get-tuple-element.43.refs_0_.refs_1_.refs_3_.z_ref, f32[33,32,128]{2,1,0:T(8,128)S(1)} %get-tuple-element.66.top_ref, f32[33,32,128]{2,1,0:T(8,128)S(1)} %get-tuple-element.68.bottom_ref, f32[33,9,8,128]{3,2,1,0:T(8,128)S(1)} %data.1.data_ref), custom_call_target="tpu_custom_call" | custom-call | flops 16220160 | bytes 12976128 | tf_op jit(solution)/shard_map/gradient/pallas_call | solution.py:371
  66.3 0.0 collective-permute-done.13.up_ref
  66.3 3.1 %collective-permute-done.14.down_ref = f32[33,8,128]{2,1,0:T(8,128)S(1)} collective-permute-done((f32[33,8,128]{2,1,0:T(8,128)S(1)}, f32[33,8,128]{2,1,0:T(8,128)S(1)}, u32[]{:S(2)}, u32[]{:S(2)}) %collective-permute-start.14) | collective-permute-done | bytes 135200 | tf_op jit(solution)/shard_map/ppermute | solution.py:368
  69.5 1.4 %finish.1 = f32[9,8,4096]{2,1,0:T(8,128)} custom-call(f32[9,8,4096]{2,1,0:T(8,128)S(1)} %gradient.1.part_ref, f32[33,64,128]{2,1,0:T(8,128)S(1)} %get-tuple-element.43.refs_0_.refs_1_.refs_3_.z_ref, f32[33,8,128]{2,1,0:T(8,128)S(1)} %collective-permute-done.13.up_ref, f32[33,8,128]{2,1,0:T(8,128)S(1)} %collective-permute-done.14.down_ref), custom_call_target="tpu_custom_call" | custom-call | flops 5406720 | bytes 4325376 | tf_op jit(solution)/shard_map/finish/pallas_call | solution.py:371
Async XLA Ops:
  1.7 2.1 %collective-permute-start = (f32[2,2,8,4224]{3,2,1,0:T(8,128)S(1)}, f32[2,2,8,4224]{3,2,1,0:T(8,128)S(1)}, u32[]{:S(2)}, u32[]{:S(2)}) collective-permute-start(f32[2,2,8,4224]{3,2,1,0:T(8,128)S(1)} %get-tuple-element.41), channel_id=1, source_target_pairs={{0,1},{1,0},{2,3},{3,2},{4,5},{5,4},{6,7},{7,6},{8,9},{9,8},{10,11... | collective-permute-start | bytes 1622024 | tf_op jit(solution)/shard_map/ppermute | solution.py:399
  4.0 8.7 %collective-permute-start.1 = (f32[42,8,128]{2,1,0:T(8,128)S(1)}, f32[42,8,128]{2,1,0:T(8,128)S(1)}, u32[]{:S(2)}, u32[]{:S(2)}) collective-permute-start(f32[42,8,128]{2,1,0:T(8,128)S(1)} %get-tuple-element.44), channel_id=1, source_target_pairs={{0,2},{2,4},{4,6},{6,8},{8,10},{10,12},{12,14},{1,3},{3,5},{5,7},{... | collective-permute-start | bytes 516104 | tf_op jit(solution)/shard_map/ppermute | solution.py:365
  8.8 8.0 %collective-permute-start.2 = (f32[42,8,128]{2,1,0:T(8,128)S(1)}, f32[42,8,128]{2,1,0:T(8,128)S(1)}, u32[]{:S(2)}, u32[]{:S(2)}) collective-permute-start(f32[42,8,128]{2,1,0:T(8,128)S(1)} %get-tuple-element.47), channel_id=1, source_target_pairs={{2,0},{4,2},{6,4},{8,6},{10,8},{12,10},{14,12},{3,1},{5,3},{7,5},{... | collective-permute-start | bytes 516104 | tf_op jit(solution)/shard_map/ppermute | solution.py:368
  13.4 8.5 %collective-permute-start.4 = (f32[33,8,128]{2,1,0:T(8,128)S(1)}, f32[33,8,128]{2,1,0:T(8,128)S(1)}, u32[]{:S(2)}, u32[]{:S(2)}) collective-permute-start(f32[33,8,128]{2,1,0:T(8,128)S(1)} %get-tuple-element.51), channel_id=1, source_target_pairs={{2,0},{4,2},{6,4},{8,6},{10,8},{12,10},{14,12},{3,1},{5,3},{7,5},{... | collective-permute-start | bytes 405512 | tf_op jit(solution)/shard_map/ppermute | solution.py:368
  17.5 9.0 %collective-permute-start.3 = (f32[33,8,128]{2,1,0:T(8,128)S(1)}, f32[33,8,128]{2,1,0:T(8,128)S(1)}, u32[]{:S(2)}, u32[]{:S(2)}) collective-permute-start(f32[33,8,128]{2,1,0:T(8,128)S(1)} %get-tuple-element.49), channel_id=1, source_target_pairs={{0,2},{2,4},{4,6},{6,8},{8,10},{10,12},{12,14},{1,3},{3,5},{5,7},{... | collective-permute-start | bytes 405512 | tf_op jit(solution)/shard_map/ppermute | solution.py:365
  22.6 6.7 %collective-permute-start.5 = (f32[33,8,128]{2,1,0:T(8,128)S(1)}, f32[33,8,128]{2,1,0:T(8,128)S(1)}, u32[]{:S(2)}, u32[]{:S(2)}) collective-permute-start(f32[33,8,128]{2,1,0:T(8,128)S(1)} %get-tuple-element.53), channel_id=1, source_target_pairs={{0,2},{2,4},{4,6},{6,8},{8,10},{10,12},{12,14},{1,3},{3,5},{5,7},{... | collective-permute-start | bytes 405512 | tf_op jit(solution)/shard_map/ppermute | solution.py:365
  27.3 7.0 %collective-permute-start.6 = (f32[33,8,128]{2,1,0:T(8,128)S(1)}, f32[33,8,128]{2,1,0:T(8,128)S(1)}, u32[]{:S(2)}, u32[]{:S(2)}) collective-permute-start(f32[33,8,128]{2,1,0:T(8,128)S(1)} %get-tuple-element.55), channel_id=1, source_target_pairs={{2,0},{4,2},{6,4},{8,6},{10,8},{12,10},{14,12},{3,1},{5,3},{7,5},{... | collective-permute-start | bytes 405512 | tf_op jit(solution)/shard_map/ppermute | solution.py:368
  30.0 9.1 %collective-permute-start.8 = (f32[33,8,128]{2,1,0:T(8,128)S(1)}, f32[33,8,128]{2,1,0:T(8,128)S(1)}, u32[]{:S(2)}, u32[]{:S(2)}) collective-permute-start(f32[33,8,128]{2,1,0:T(8,128)S(1)} %get-tuple-element.59), channel_id=1, source_target_pairs={{2,0},{4,2},{6,4},{8,6},{10,8},{12,10},{14,12},{3,1},{5,3},{7,5},{... | collective-permute-start | bytes 405512 | tf_op jit(solution)/shard_map/ppermute | solution.py:368
  35.0 9.3 %collective-permute-start.7 = (f32[33,8,128]{2,1,0:T(8,128)S(1)}, f32[33,8,128]{2,1,0:T(8,128)S(1)}, u32[]{:S(2)}, u32[]{:S(2)}) collective-permute-start(f32[33,8,128]{2,1,0:T(8,128)S(1)} %get-tuple-element.57), channel_id=1, source_target_pairs={{0,2},{2,4},{4,6},{6,8},{8,10},{10,12},{12,14},{1,3},{3,5},{5,7},{... | collective-permute-start | bytes 405512 | tf_op jit(solution)/shard_map/ppermute | solution.py:365
  39.8 8.4 %collective-permute-start.9 = (f32[33,8,128]{2,1,0:T(8,128)S(1)}, f32[33,8,128]{2,1,0:T(8,128)S(1)}, u32[]{:S(2)}, u32[]{:S(2)}) collective-permute-start(f32[33,8,128]{2,1,0:T(8,128)S(1)} %get-tuple-element.61), channel_id=1, source_target_pairs={{0,2},{2,4},{4,6},{6,8},{8,10},{10,12},{12,14},{1,3},{3,5},{5,7},{... | collective-permute-start | bytes 405512 | tf_op jit(solution)/shard_map/ppermute | solution.py:365
  44.9 6.9 %collective-permute-start.10 = (f32[33,8,128]{2,1,0:T(8,128)S(1)}, f32[33,8,128]{2,1,0:T(8,128)S(1)}, u32[]{:S(2)}, u32[]{:S(2)}) collective-permute-start(f32[33,8,128]{2,1,0:T(8,128)S(1)} %get-tuple-element.63), channel_id=1, source_target_pairs={{2,0},{4,2},{6,4},{8,6},{10,8},{12,10},{14,12},{3,1},{5,3},{7,5},{... | collective-permute-start | bytes 405512 | tf_op jit(solution)/shard_map/ppermute | solution.py:368
  48.9 8.5 %collective-permute-start.12 = (f32[33,8,128]{2,1,0:T(8,128)S(1)}, f32[33,8,128]{2,1,0:T(8,128)S(1)}, u32[]{:S(2)}, u32[]{:S(2)}) collective-permute-start(f32[33,8,128]{2,1,0:T(8,128)S(1)} %get-tuple-element.67), channel_id=1, source_target_pairs={{2,0},{4,2},{6,4},{8,6},{10,8},{12,10},{14,12},{3,1},{5,3},{7,5},{... | collective-permute-start | bytes 405512 | tf_op jit(solution)/shard_map/ppermute | solution.py:368
  52.6 9.3 %collective-permute-start.11 = (f32[33,8,128]{2,1,0:T(8,128)S(1)}, f32[33,8,128]{2,1,0:T(8,128)S(1)}, u32[]{:S(2)}, u32[]{:S(2)}) collective-permute-start(f32[33,8,128]{2,1,0:T(8,128)S(1)} %get-tuple-element.65), channel_id=1, source_target_pairs={{0,2},{2,4},{4,6},{6,8},{8,10},{10,12},{12,14},{1,3},{3,5},{5,7},{... | collective-permute-start | bytes 405512 | tf_op jit(solution)/shard_map/ppermute | solution.py:365
  58.1 8.2 %collective-permute-start.13 = (f32[33,8,128]{2,1,0:T(8,128)S(1)}, f32[33,8,128]{2,1,0:T(8,128)S(1)}, u32[]{:S(2)}, u32[]{:S(2)}) collective-permute-start(f32[33,8,128]{2,1,0:T(8,128)S(1)} %get-tuple-element.69), channel_id=1, source_target_pairs={{0,2},{2,4},{4,6},{6,8},{8,10},{10,12},{12,14},{1,3},{3,5},{5,7},{... | collective-permute-start | bytes 405512 | tf_op jit(solution)/shard_map/ppermute | solution.py:365
  62.5 6.9 %collective-permute-start.14 = (f32[33,8,128]{2,1,0:T(8,128)S(1)}, f32[33,8,128]{2,1,0:T(8,128)S(1)}, u32[]{:S(2)}, u32[]{:S(2)}) collective-permute-start(f32[33,8,128]{2,1,0:T(8,128)S(1)} %get-tuple-element.70), channel_id=1, source_target_pairs={{2,0},{4,2},{6,4},{8,6},{10,8},{12,10},{14,12},{3,1},{5,3},{7,5},{... | collective-permute-start | bytes 405512 | tf_op jit(solution)/shard_map/ppermute | solution.py:368

commit v3 on v2

--- a/solution.py
+++ b/solution.py
@@ -90,37 +90,50 @@
         copy.wait()
 
 
-def prep_kernel(window_ref, expanded_ref):
+def combine(kappa, across, along, skew, coupling):
+    scale = 4.0 / (upper_edge - lower_edge)
+    shift = 2.0 * (upper_edge + lower_edge) / (upper_edge - lower_edge)
+    return (
+        scale * (kappa + 2.0 * (across + along)) - shift,
+        -scale * across,
+        -scale * along,
+        -0.5 * scale * skew,
+        scale * coupling,
+    )
+
+
+def prep_kernel(window_ref, seen_ref, expanded_ref, top_ref, bottom_ref, eight, rest):
     tiles = expanded_ref.shape[1]
     chunk = chunk_of(tiles)
-    scale = 4.0 / (upper_edge - lower_edge)
-    shift = 2.0 * (upper_edge + lower_edge) / (upper_edge - lower_edge)
+    rest[...] = jnp.zeros_like(rest)
 
     def body(step, carry):
         for k in range(chunk):
             tile = step * chunk + k
             cols = tile_columns(tile)
-            kappa, across, along, skew = [
-                [window_ref[2 * kind + c, :, cols] for c in range(2)] for kind in range(4)
-            ]
-            coupling = scale * window_ref[8, :, cols]
+            raw = [window_ref[channel, :, cols] for channel in range(9)]
             for c in range(2):
-                values = (
-                    scale * (kappa[c] + 2.0 * (across[c] + along[c])) - shift,
-                    -scale * across[c],
-                    -scale * along[c],
-                    -0.5 * scale * skew[c],
-                    coupling,
-                )
+                values = combine(raw[c], raw[2 + c], raw[4 + c], raw[6 + c], raw[8])
                 for kind, value in enumerate(values):
                     for probe in range(4):
                         expanded_ref[kind, tile, pl.ds(4 * c + probe, SUBS, stride=SUBS), :] = value
+            for channel in range(8):
+                eight[tile, pl.ds(channel, SUBS, stride=SUBS), :] = raw[channel]
+            top_ref[tile] = eight[tile, sub(0), :]
+            bottom_ref[tile] = eight[tile, sub(SUBS - 1), :]
         return carry
 
     lax.fori_loop(0, tiles // chunk, body, 0)
-
-
-def layout_kernel(own_ref, other_ref, seen_ref, z_ref, top_ref, bottom_ref):
+    for tile in range(tiles):
+        cols = pl.ds(tile * LANES, LANES)
+        for slot, row in enumerate((window_ref[8, :, cols], seen_ref[0, :, cols], seen_ref[1, :, cols])):
+            rest[tile // 2, pl.ds(4 * (tile % 2) + slot, SUBS, stride=SUBS), :] = row
+    for pair in range(rest.shape[0]):
+        top_ref[tiles + pair] = rest[pair, sub(0), :]
+        bottom_ref[tiles + pair] = rest[pair, sub(SUBS - 1), :]
+
+
+def layout_kernel(own_ref, other_ref, more_top_ref, more_bottom_ref, z_ref, top_ref, bottom_ref):
     tiles = z_ref.shape[0]
     chunk = chunk_of(tiles)
 
@@ -136,34 +149,39 @@
 
     lax.fori_loop(0, tiles // chunk, body, 0)
     for tile in range(tiles):
-        top_ref[tile] = z_ref[tile, sub(0), :]
-        bottom_ref[tile] = z_ref[tile, sub(SUBS - 1), :]
-    for c in range(2):
-        for tile in range(tiles):
-            place = c * tiles + tile
-            cols = pl.ds(tile * LANES, LANES)
-            at = (tiles + place // SUBS, pl.ds(place % SUBS, 1))
-            top_ref[at[0], at[1], :] = seen_ref[c, 0:1, cols]
-            bottom_ref[at[0], at[1], :] = seen_ref[c, SUBS - 1 : SUBS, cols]
-
-
-def step_kernel(upper, constants, offset, other_row, tiles, *refs):
-    weight, scale, subtract = constants
-    own_ref, other_ref, halo_ref, z_ref, coefficients_ref = refs[:5]
-    rest = refs[5:]
-    before_ref = None
-    if subtract:
-        before_ref, rest = rest[0], rest[1:]
-    out_ref, edge_ref = rest
-    first_row = 0 if upper else 4
+        for row in range(2):
+            top_ref[2 * tile + row] = z_ref[tile, sub(row), :]
+            bottom_ref[2 * tile + row] = z_ref[tile, sub(SUBS - 2 + row), :]
+    for index in range(more_top_ref.shape[0]):
+        top_ref[2 * tiles + index] = more_top_ref[index]
+        bottom_ref[2 * tiles + index] = more_bottom_ref[index]
+
+
+def rim(halo_ref, rim_ref, tiles):
     chunk = chunk_of(tiles)
 
-    def load(row):
-        if row == (-1 if upper else 4):
-            return lambda tile: halo_ref[tile]
-        if row == (4 if upper else -1):
-            return lambda tile: other_ref[tile, sub(other_row), :]
-        return lambda tile: own_ref[tile, sub(offset + row), :]
+    def spread(ref, index, row):
+        return jnp.broadcast_to(ref[index, pl.ds(row, 1), :], (SUBS, LANES))
+
+    def body(step, carry):
+        low = lax.broadcasted_iota(jnp.int32, (SUBS, LANES), 0) < 4
+        for k in range(chunk):
+            tile = step * chunk + k
+            pairs = [
+                jnp.where(low, spread(halo_ref, 2 * tiles + tile, 2 * kind), spread(halo_ref, 2 * tiles + tile, 2 * kind + 1))
+                for kind in range(4)
+            ]
+            coupling = spread(halo_ref, 3 * tiles + tile // 2, 4 * (tile % 2))
+            for kind, value in enumerate(combine(*pairs, coupling)):
+                rim_ref[kind, tile] = value
+        return carry
+
+    lax.fori_loop(0, tiles // chunk, body, 0)
+
+
+def sweep(tiles, low, count, load, factor, z_row, before, constants, store):
+    weight, scale = constants
+    chunk = chunk_of(tiles)
 
     def body(step, carry):
         edges = masks()
@@ -171,51 +189,129 @@
         for k in range(chunk):
             tile = first + k
             values, sums, slopes = [], [], []
-            for row in range(-1, 5):
-                loader = load(row)
-                here = loader(tile)
+            for row in range(low - 1, low + count + 1):
+                here = load(row, tile)
                 if k == 0:
-                    before = jnp.where(first > 0, loader(jnp.maximum(first - 1, 0)), 0.0)
+                    last = jnp.where(first > 0, load(row, jnp.maximum(first - 1, 0)), 0.0)
                 else:
-                    before = loader(tile - 1)
+                    last = load(row, tile - 1)
                 if k == chunk - 1:
-                    last = first + chunk < tiles
-                    after = jnp.where(last, loader(jnp.minimum(first + chunk, tiles - 1)), 0.0)
+                    more = first + chunk < tiles
+                    after = jnp.where(more, load(row, jnp.minimum(first + chunk, tiles - 1)), 0.0)
                 else:
-                    after = loader(tile + 1)
-                left, right = beside(before, here, after, edges)
+                    after = load(row, tile + 1)
+                left, right = beside(last, here, after, edges)
                 values.append(here)
                 sums.append(left + right)
                 slopes.append(right - left)
-            for row in range(4):
-                rows = sub(first_row + row)
-                coefs = [coefficients_ref[kind, tile, rows, :] for kind in range(5)]
+            for at in range(count):
+                row = low + at
                 total = (
-                    coefs[0] * values[row + 1]
-                    + coefs[1] * sums[row + 1]
-                    + coefs[2] * (values[row] + values[row + 2])
-                    + coefs[3] * (slopes[row + 2] - slopes[row])
-                    + coefs[4] * pltpu.roll(values[row + 1], 4, 0)
+                    factor(0, row, tile) * values[at + 1]
+                    + factor(1, row, tile) * sums[at + 1]
+                    + factor(2, row, tile) * (values[at] + values[at + 2])
+                    + factor(3, row, tile) * (slopes[at + 2] - slopes[at])
+                    + factor(4, row, tile) * pltpu.roll(values[at + 1], 4, 0)
                 )
                 if scale != 1.0:
                     total = scale * total
-                total = total + weight * z_ref[tile, rows, :]
-                if subtract:
-                    total = total - before_ref[tile, sub(row), :]
-                out_ref[tile, sub(row), :] = total
-                if row == (0 if upper else 3):
-                    edge_ref[tile] = total
+                total = total + weight * z_row(row, tile)
+                if before is not None:
+                    total = total - before(row, tile)
+                store(row, tile, total)
         return carry
 
     lax.fori_loop(0, tiles // chunk, body, 0)
+
+
+def middle_kernel(steps, tiles, first_round, *refs):
+    if first_round:
+        z_ref, expanded_ref, once_ref, twice_ref = refs
+    else:
+        z_ref, expanded_ref, top_ref, inner_ref, bottom_ref, older_ref, once_ref, twice_ref = refs
+
+    def now(row, tile):
+        if first_round:
+            return z_ref[tile, sub(row), :]
+        if row < 2:
+            return top_ref[2 * tile + row]
+        if row < 6:
+            return inner_ref[tile, sub(row - 2), :]
+        return bottom_ref[2 * tile + row - 6]
+
+    def factor(kind, row, tile):
+        return expanded_ref[kind, tile, sub(row), :]
+
+    def z_row(row, tile):
+        return z_ref[tile, sub(row), :]
+
+    def once(row, tile):
+        return once_ref[tile, sub(row - 1), :]
+
+    def store_once(row, tile, value):
+        once_ref[tile, sub(row - 1), :] = value
+
+    def store_twice(row, tile, value):
+        twice_ref[tile, sub(row - 2), :] = value
+
+    older = None if first_round else (lambda row, tile: older_ref[tile, sub(row - 1), :])
+    sweep(tiles, 1, 6, now, factor, z_row, older, steps[0], store_once)
+    sweep(tiles, 2, 4, once, factor, z_row, None if first_round else now, steps[1], store_twice)
+
+
+def edge_kernel(upper, steps, tiles, first_round, last_round, *refs):
+    halo_ref, z_halo_ref, z_ref, expanded_ref, inner_ref = refs[:5]
+    refs = refs[5:]
+    if first_round:
+        once_ref, twice_ref, rim_ref = refs[:3]
+        rim(halo_ref, rim_ref, tiles)
+    else:
+        rim_ref, top_ref, older_ref, once_ref, twice_ref = refs[:5]
+    row_ref = refs[-1]
+    base = 0 if upper else 6
+    low = -1 if upper else 7
+
+    def now(row, tile):
+        if row < 0 or row > 7:
+            return halo_ref[2 * tile + (row + 2 if upper else row - 8)]
+        if first_round:
+            return z_ref[tile, sub(row), :]
+        return top_ref[2 * tile + row - base]
+
+    def factor(kind, row, tile):
+        if row < 0 or row > 7:
+            return rim_ref[kind, tile]
+        return expanded_ref[kind, tile, sub(row), :]
+
+    def z_row(row, tile):
+        if row < 0 or row > 7:
+            return z_halo_ref[2 * tile + (1 if upper else 0)]
+        return z_ref[tile, sub(row), :]
+
+    def once(row, tile):
+        if 1 <= row <= 6:
+            return inner_ref[tile, sub(row - 1), :]
+        return once_ref[tile, sub(row - low), :]
+
+    def store_once(row, tile, value):
+        once_ref[tile, sub(row - low), :] = value
+
+    def store_twice(row, tile, value):
+        twice_ref[2 * tile + row - base] = value
+        if last_round and row == (0 if upper else 7):
+            row_ref[tile] = value
+
+    older = None if first_round else (lambda row, tile: older_ref[tile, sub(row - low), :])
+    sweep(tiles, low, 2, now, factor, z_row, older, steps[0], store_once)
+    sweep(tiles, base, 2, once, factor, z_row, None if first_round else now, steps[1], store_twice)
 
 
 def data_kernel(tiles, seen_ref, up_ref, down_ref, out_ref):
     chunk = chunk_of(tiles)
 
     def halo(ref, c, tile):
-        place = c * tiles + tile
-        return jnp.broadcast_to(ref[tiles + place // SUBS, pl.ds(place % SUBS, 1), :], (SUBS, LANES))
+        row = ref[3 * tiles + tile // 2, pl.ds(4 * (tile % 2) + 1 + c, 1), :]
+        return jnp.broadcast_to(row, (SUBS, LANES))
 
     def body(step, carry):
         edges = masks()
@@ -247,15 +343,17 @@
     lax.fori_loop(0, tiles // chunk, body, 0)
 
 
-def gradient_kernel(tiles, factor, z_ref, top_ref, bottom_ref, data_ref, out_ref, products):
+def gradient_kernel(tiles, factor, z_ref, top_ref, inner_ref, bottom_ref, data_ref, out_ref, products):
     kept = out_ref.shape[2] // LANES
     offset = lax.axis_index("probe") * (tiles - kept)
     count = products.shape[0]
 
     def load(row):
-        if row < 4:
-            return lambda tile: top_ref[tile, sub(row), :]
-        return lambda tile: bottom_ref[tile, sub(row - 4), :]
+        if row < 2:
+            return lambda tile: top_ref[2 * tile + row]
+        if row < 6:
+            return lambda tile: inner_ref[tile, sub(row - 2), :]
+        return lambda tile: bottom_ref[2 * tile + row - 6]
 
     def body(step, carry):
         edges = masks()
@@ -356,7 +454,6 @@
     width = share + LANES
     tiles = width // LANES
     kept = share // LANES
-    seen_tiles = -(-2 * tiles // SUBS)
     rows = lax.axis_size("row")
     down_pairs = [(i, i + 1) for i in range(rows - 1)]
     up_pairs = [(i + 1, i) for i in range(rows - 1)]
@@ -397,53 +494,76 @@
         [pl.BlockSpec(memory_space=pltpu.HBM)] * 3,
     )
     other = lax.ppermute(theirs, "probe", [(0, 1), (1, 0)])
-    expanded = call(
-        prep_kernel, "prep", 5 * 8 * tiles, (window,), pltpu.VMEM((5, tiles, SUBS * SUBS, LANES), f32)
+    pairs = -(-tiles // 2)
+    more = (tiles + pairs, SUBS, LANES)
+    expanded, more_top, more_bottom = call(
+        prep_kernel,
+        "prep",
+        5 * 8 * tiles,
+        (window, seen),
+        [pltpu.VMEM((5, tiles, SUBS * SUBS, LANES), f32), pltpu.VMEM(more, f32), pltpu.VMEM(more, f32)],
+        [pltpu.VMEM((tiles, SUBS * SUBS, LANES), f32), pltpu.VMEM((pairs, SUBS * SUBS, LANES), f32)],
     )
     own, expanded = lax.optimization_barrier((own, expanded))
-    message = (tiles + seen_tiles, SUBS, LANES)
+    message = (2 * tiles + more[0], SUBS, LANES)
     z, top, bottom = call(
         layout_kernel,
         "layout",
         8 * tiles,
-        (own, other, seen),
+        (own, other, more_top, more_bottom),
         [pltpu.VMEM((tiles, SUBS * SUBS, LANES), f32), pltpu.VMEM(message, f32), pltpu.VMEM(message, f32)],
     )
-
-    def half(upper, constants, own, other_half, halo, before):
-        shared = own is z
-        offset = (0 if upper else 4) if shared else 0
-        other_row = (4 if upper else 3) if shared else (0 if upper else 3)
-        operands = [own, other_half, halo, z, expanded]
-        if constants[2]:
-            operands.append(before)
-        return call(
-            functools.partial(step_kernel, upper, constants, offset, other_row, tiles),
-            "upper" if upper else "lower",
-            4 * tiles,
-            operands,
-            [pltpu.VMEM((tiles, 4 * SUBS, LANES), f32), pltpu.VMEM((tiles, SUBS, LANES), f32)],
-        )
 
     first_up, first_down = to_next(bottom), to_previous(top)
     up, down = first_up, first_down
-    now = (z, z)
-    before = (None, None)
-    for order in range(CHEB - 1, -1, -1):
-        if order == CHEB - 1:
-            constants = (weights[order], weights[CHEB], False)
-        elif order == CHEB - 2:
-            constants = (weights[order] - weights[CHEB], 1.0, False)
-        elif order > 0:
-            constants = (weights[order], 1.0, True)
+    rounds = CHEB // 2
+    inner = once = rims = None
+    for index in range(rounds):
+        first_round, last_round = index == 0, index == rounds - 1
+        high = CHEB - 1 - 2 * index
+        if first_round:
+            steps = ((weights[high], weights[CHEB]), (weights[high - 1] - weights[CHEB], 1.0))
         else:
-            constants = (weights[0], 0.5, True)
-        upper, top = half(True, constants, now[0], now[1], up, before[0])
-        next_down = to_previous(top)
-        lower, bottom = half(False, constants, now[1], now[0], down, before[1])
-        next_up = to_next(bottom)
-        before, now = now, (upper, lower)
-        up, down = next_up, next_down
+            steps = ((weights[high], 1.0), (weights[high - 1], 0.5 if last_round else 1.0))
+        operands = [z, expanded]
+        if not first_round:
+            operands += [top, inner, bottom, once[1]]
+        inner_once, inner_twice = call(
+            functools.partial(middle_kernel, steps, tiles, first_round),
+            "middle",
+            10 * tiles,
+            operands,
+            [pltpu.VMEM((tiles, 6 * SUBS, LANES), f32), pltpu.VMEM((tiles, 4 * SUBS, LANES), f32)],
+        )
+        results = []
+        for upper in (True, False):
+            halo, z_halo = (up, first_up) if upper else (down, first_down)
+            operands = [halo, z_halo, z, expanded, inner_once]
+            outs = [pltpu.VMEM((tiles, 2 * SUBS, LANES), f32), pltpu.VMEM((2 * tiles, SUBS, LANES), f32)]
+            if first_round:
+                outs.append(pltpu.VMEM((5, tiles, SUBS, LANES), f32))
+            else:
+                operands += [rims[0 if upper else 1], top if upper else bottom, once[0 if upper else 2]]
+            if last_round:
+                outs.append(pltpu.VMEM((tiles, SUBS, LANES), f32))
+            results.append(
+                call(
+                    functools.partial(edge_kernel, upper, steps, tiles, first_round, last_round),
+                    "upper" if upper else "lower",
+                    4 * tiles,
+                    operands,
+                    outs,
+                )
+            )
+        over, under = results
+        once = (over[0], inner_once, under[0])
+        top, inner, bottom = over[1], inner_twice, under[1]
+        if first_round:
+            rims = (over[2], under[2])
+        if last_round:
+            down, up = to_previous(over[-1]), to_next(under[-1])
+        else:
+            down, up = to_previous(top), to_next(bottom)
 
     data = call(
         functools.partial(data_kernel, tiles),
@@ -458,7 +578,7 @@
         functools.partial(gradient_kernel, tiles, factor),
         "gradient",
         24 * tiles,
-        (z, now[0], now[1], data),
+        (z, top, inner, bottom, data),
         pltpu.VMEM((9, SUBS, share), f32),
         [pltpu.VMEM((count, 5, SUBS * SUBS, LANES), f32)],
     )

time: 71.3 us -> 69.6 us (0.976)
  starting transfers between devices: 39.7 us -> 24 us
  waiting for transfers between devices: 15.8 us -> 25.6 us
  Pallas kernels: 15 us -> 19.5 us
    ppermute x7 -> x4, starting transfers between devices: 30.1 us -> 18.3 us  [to_next(): return lax.ppermute(edge, 'row', down_pairs)]
    ppermute x7 -> x4, waiting for transfers between devices: 9.83 us -> 19 us  [to_previous(): return lax.ppermute(edge, 'row', up_pairs)]
    pallas_call x18 -> x15, Pallas kernels: 15 us -> 19.5 us  [call(): pl.pallas_call(kernel, out_shape=outs, in_specs=in_specs or [vmem_spec()]...]
    ppermute x7 -> x4, starting transfers between devices: 9.04 us -> 5.16 us  [to_previous(): return lax.ppermute(edge, 'row', up_pairs)]
    ppermute x7 -> x4, waiting for transfers between devices: 5.26 us -> 6.07 us  [to_next(): return lax.ppermute(edge, 'row', down_pairs)]
  transfers between devices with their start and end apart: 15 -> 9, of which waited for: 8 -> 6; matrix products, arithmetic and copies ran while one was open for 0% -> 0% of each run, Pallas kernels for 17% -> 23%
where the time goes in v3:
time: 69.6 us; the launch traced here: 69.3 us
  waiting for transfers between devices  25.6 us (37%)
  starting transfers between devices  24 us (34%)
  Pallas kernels  19.5 us (28%)
    pallas_call x15, Pallas kernels, call(): pl.pallas_call(kernel, out_shape=outs, in_specs=in_specs or [vmem_spec()]...  19.5 us
    ppermute x4, waiting for transfers between devices, to_previous(): return lax.ppermute(edge, 'row', up_pairs)  19 us
    ppermute x4, starting transfers between devices, to_next(): return lax.ppermute(edge, 'row', down_pairs)  18.3 us
    ppermute x4, waiting for transfers between devices, to_next(): return lax.ppermute(edge, 'row', down_pairs)  6.07 us
    ppermute x4, starting transfers between devices, to_previous(): return lax.ppermute(edge, 'row', up_pairs)  5.16 us
  transfers between devices with their start and end apart: 9, of which 6 were waited for; matrix products, arithmetic and copies ran while one was open for 0% of the time, Pallas kernels for 23%

profile of v3, /device:TPU:0, one launch (start us, length us, event | category | flops | bytes accessed | tf_op | source)
XLA Modules:
  0.0 69.3 jit_solution(15043149551315844234)
XLA Ops:
  0.0 1.7 %load.1 = (f32[2,2,8,4224]{3,2,1,0:T(8,128)S(1)}, f32[2,2,8,4224]{3,2,1,0:T(8,128)S(1)}, f32[2,8,4224]{2,1,0:T(8,128)S(1)}, f32[9,8,4224]{2,1,0:T(8,128)S(1)}) custom-call(f32[2,2,8,8192]{3,2,1,0:T(8,128)} %probes_ref.1, f32[2,8,8192]{2,1,0:T(8,128)} %observed_ref.1, f32[9,8,8192]{2,1,0:T(8,128)} %coefficients_ref.1), custom_call_target="tpu_custom_call" | custom-call | flops 2048000 | bytes 1638400 | tf_op jit(solution)/shard_map/load/pallas_call | solution.py:468
  1.7 0.5 collective-permute-start
  2.2 1.1 %prep.1 = (f32[5,33,64,128]{3,2,1,0:T(8,128)S(1)}, f32[50,8,128]{2,1,0:T(8,128)S(1)}, f32[50,8,128]{2,1,0:T(8,128)S(1)}) custom-call(f32[9,8,4224]{2,1,0:T(8,128)S(1)} %get-tuple-element.38.window_ref, f32[2,8,4224]{2,1,0:T(8,128)S(1)} %get-tuple-element.39.seen_ref), custom_call_target="tpu_custom_call" | custom-call | flops 27033600 | bytes 21626880 | tf_op jit(solution)/shard_map/prep/pallas_call | solution.py:468
  3.3 0.5 collective-permute-done.other_ref
  3.8 0.2 layout.1
  4.0 1.3 %collective-permute-start.3 = (f32[116,8,128]{2,1,0:T(8,128)S(1)}, f32[116,8,128]{2,1,0:T(8,128)S(1)}, u32[]{:S(2)}, u32[]{:S(2)}) collective-permute-start(f32[116,8,128]{2,1,0:T(8,128)S(1)} %get-tuple-element.50), channel_id=1, source_target_pairs={{2,0},{4,2},{6,4},{8,6},{10,8},{12,10},{14,12},{3,1},{5,3},{7,5},{... | collective-permute-start | bytes 1425416 | tf_op jit(solution)/shard_map/ppermute | solution.py:465
  5.3 5.4 %collective-permute-start.1 = (f32[116,8,128]{2,1,0:T(8,128)S(1)}, f32[116,8,128]{2,1,0:T(8,128)S(1)}, u32[]{:S(2)}, u32[]{:S(2)}) collective-permute-start(f32[116,8,128]{2,1,0:T(8,128)S(1)} %get-tuple-element.46), channel_id=1, source_target_pairs={{0,2},{2,4},{4,6},{6,8},{8,10},{10,12},{12,14},{1,3},{3,5},{5,7},{... | collective-permute-start | bytes 1425416 | tf_op jit(solution)/shard_map/ppermute | solution.py:462
  10.7 1.5 %middle.3 = (f32[33,48,128]{2,1,0:T(8,128)S(1)}, f32[33,32,128]{2,1,0:T(8,128)S(1)}) custom-call(f32[33,64,128]{2,1,0:T(8,128)S(1)} %get-tuple-element.45.refs_0_.refs_2_.z_ref, f32[5,33,64,128]{3,2,1,0:T(8,128)S(1)} %get-tuple-element.47.refs_1_.refs_3_), custom_call_target="tpu_custom_call" | custom-call | flops 6758400 | bytes 5406720 | tf_op jit(solution)/shard_map/middle/pallas_call | solution.py:468
  12.2 7.7 %collective-permute-done.3.refs_0_.refs_1_.down_ref = f32[116,8,128]{2,1,0:T(8,128)S(1)} collective-permute-done((f32[116,8,128]{2,1,0:T(8,128)S(1)}, f32[116,8,128]{2,1,0:T(8,128)S(1)}, u32[]{:S(2)}, u32[]{:S(2)}) %collective-permute-start.3) | collective-permute-done | bytes 475168 | tf_op jit(solution)/shard_map/ppermute | solution.py:465
  19.9 1.3 %lower.3 = (f32[33,16,128]{2,1,0:T(8,128)S(1)}, f32[66,8,128]{2,1,0:T(8,128)S(1)}, f32[5,33,8,128]{3,2,1,0:T(8,128)S(1)}) custom-call(f32[116,8,128]{2,1,0:T(8,128)S(1)} %collective-permute-done.3.refs_0_.refs_1_.down_ref, f32[116,8,128]{2,1,0:T(8,128)S(1)} %collective-permute-done.3.refs_0_.refs_1_.down_ref, ...), custom_call_target="tpu_custom_call" | custom-call | flops 2703360 | bytes 2162688 | tf_op jit(solution)/shard_map/lower/pallas_call | solution.py:468
  21.2 4.7 %collective-permute-start.5 = (f32[66,8,128]{2,1,0:T(8,128)S(1)}, f32[66,8,128]{2,1,0:T(8,128)S(1)}, u32[]{:S(2)}, u32[]{:S(2)}) collective-permute-start(f32[66,8,128]{2,1,0:T(8,128)S(1)} %get-tuple-element.52.refs_4_.refs_6_), channel_id=1, source_target_pairs={{0,2},{2,4},{4,6},{6,8},{8,10},{10,12},{12,14},{1,3},{3,5},{5,7},{... | collective-permute-start | bytes 811016 | tf_op jit(solution)/shard_map/ppermute | solution.py:462
  25.9 4.5 %collective-permute-done.1.refs_0_.refs_1_.up_ref = f32[116,8,128]{2,1,0:T(8,128)S(1)} collective-permute-done((f32[116,8,128]{2,1,0:T(8,128)S(1)}, f32[116,8,128]{2,1,0:T(8,128)S(1)}, u32[]{:S(2)}, u32[]{:S(2)}) %collective-permute-start.1) | collective-permute-done | bytes 475168 | tf_op jit(solution)/shard_map/ppermute | solution.py:462
  30.4 1.3 %upper.3 = (f32[33,16,128]{2,1,0:T(8,128)S(1)}, f32[66,8,128]{2,1,0:T(8,128)S(1)}, f32[5,33,8,128]{3,2,1,0:T(8,128)S(1)}) custom-call(f32[116,8,128]{2,1,0:T(8,128)S(1)} %collective-permute-done.1.refs_0_.refs_1_.up_ref, f32[116,8,128]{2,1,0:T(8,128)S(1)} %collective-permute-done.1.refs_0_.refs_1_.up_ref, ...), custom_call_target="tpu_custom_call" | custom-call | flops 2703360 | bytes 2162688 | tf_op jit(solution)/shard_map/upper/pallas_call | solution.py:468
  31.6 1.3 %collective-permute-start.2 = (f32[66,8,128]{2,1,0:T(8,128)S(1)}, f32[66,8,128]{2,1,0:T(8,128)S(1)}, u32[]{:S(2)}, u32[]{:S(2)}) collective-permute-start(f32[66,8,128]{2,1,0:T(8,128)S(1)} %get-tuple-element.49.refs_2_.refs_6_), channel_id=1, source_target_pairs={{2,0},{4,2},{6,4},{8,6},{10,8},{12,10},{14,12},{3,1},{5,3},{7,5},{... | collective-permute-start | bytes 811016 | tf_op jit(solution)/shard_map/ppermute | solution.py:465
  32.9 1.6 %middle.4 = (f32[33,48,128]{2,1,0:T(8,128)S(1)}, f32[33,32,128]{2,1,0:T(8,128)S(1)}) custom-call(f32[33,64,128]{2,1,0:T(8,128)S(1)} %get-tuple-element.45.refs_0_.refs_2_.z_ref, f32[5,33,64,128]{3,2,1,0:T(8,128)S(1)} %get-tuple-element.47.refs_1_.refs_3_, f32[66,8,128]{2,1,0:T(8,128)S(1)} %get-tuple-element.49.refs_2_.refs_6_, ...), custom_call_target="tpu_custom_call" | custom-call | flops 6758400 | bytes 5406720 | tf_op jit(solution)/shard_map/middle/pallas_call | solution.py:468
  34.5 1.6 %collective-permute-done.5.refs_0_ = f32[66,8,128]{2,1,0:T(8,128)S(1)} collective-permute-done((f32[66,8,128]{2,1,0:T(8,128)S(1)}, f32[66,8,128]{2,1,0:T(8,128)S(1)}, u32[]{:S(2)}, u32[]{:S(2)}) %collective-permute-start.5) | collective-permute-done | bytes 270368 | tf_op jit(solution)/shard_map/ppermute | solution.py:462
  36.1 1.1 %upper.4 = (f32[33,16,128]{2,1,0:T(8,128)S(1)}, f32[66,8,128]{2,1,0:T(8,128)S(1)}) custom-call(f32[66,8,128]{2,1,0:T(8,128)S(1)} %collective-permute-done.5.refs_0_, f32[116,8,128]{2,1,0:T(8,128)S(1)} %collective-permute-done.1.refs_0_.refs_1_.up_ref, f32[33,64,128]{2,1,0:T(8,128)S(1)} %get-tuple-element.45.refs_0_.refs_2_.z_ref, ...), custom_call_target="tpu_custom_call" | custom-call | flops 2703360 | bytes 2162688 | tf_op jit(solution)/shard_map/upper/pallas_call | solution.py:468
  37.1 1.3 %collective-permute-start.6 = (f32[66,8,128]{2,1,0:T(8,128)S(1)}, f32[66,8,128]{2,1,0:T(8,128)S(1)}, u32[]{:S(2)}, u32[]{:S(2)}) collective-permute-start(f32[66,8,128]{2,1,0:T(8,128)S(1)} %get-tuple-element.59.refs_2_.refs_6_), channel_id=1, source_target_pairs={{2,0},{4,2},{6,4},{8,6},{10,8},{12,10},{14,12},{3,1},{5,3},{7,5},{... | collective-permute-start | bytes 811016 | tf_op jit(solution)/shard_map/ppermute | solution.py:465
  38.4 8.2 %collective-permute-done.2.refs_0_ = f32[66,8,128]{2,1,0:T(8,128)S(1)} collective-permute-done((f32[66,8,128]{2,1,0:T(8,128)S(1)}, f32[66,8,128]{2,1,0:T(8,128)S(1)}, u32[]{:S(2)}, u32[]{:S(2)}) %collective-permute-start.2) | collective-permute-done | bytes 270368 | tf_op jit(solution)/shard_map/ppermute | solution.py:465
  46.6 1.0 %lower.4 = (f32[33,16,128]{2,1,0:T(8,128)S(1)}, f32[66,8,128]{2,1,0:T(8,128)S(1)}) custom-call(f32[66,8,128]{2,1,0:T(8,128)S(1)} %collective-permute-done.2.refs_0_, f32[116,8,128]{2,1,0:T(8,128)S(1)} %collective-permute-done.3.refs_0_.refs_1_.down_ref, f32[33,64,128]{2,1,0:T(8,128)S(1)} %get-tuple-element.45.refs_0_.refs_2_.z_ref, ...), custom_call_target="tpu_custom_call" | custom-call | flops 2703360 | bytes 2162688 | tf_op jit(solution)/shard_map/lower/pallas_call | solution.py:468
  47.7 4.0 %collective-permute-start.4 = (f32[66,8,128]{2,1,0:T(8,128)S(1)}, f32[66,8,128]{2,1,0:T(8,128)S(1)}, u32[]{:S(2)}, u32[]{:S(2)}) collective-permute-start(f32[66,8,128]{2,1,0:T(8,128)S(1)} %get-tuple-element.56.refs_4_.refs_6_), channel_id=1, source_target_pairs={{0,2},{2,4},{4,6},{6,8},{8,10},{10,12},{12,14},{1,3},{3,5},{5,7},{... | collective-permute-start | bytes 811016 | tf_op jit(solution)/shard_map/ppermute | solution.py:462
  51.7 1.6 %middle.5 = (f32[33,48,128]{2,1,0:T(8,128)S(1)}, f32[33,32,128]{2,1,0:T(8,128)S(1)}) custom-call(f32[33,64,128]{2,1,0:T(8,128)S(1)} %get-tuple-element.45.refs_0_.refs_2_.z_ref, f32[5,33,64,128]{3,2,1,0:T(8,128)S(1)} %get-tuple-element.47.refs_1_.refs_3_, f32[66,8,128]{2,1,0:T(8,128)S(1)} %get-tuple-element.59.refs_2_.refs_6_, ...), custom_call_target="tpu_custom_call" | custom-call | flops 6758400 | bytes 5406720 | tf_op jit(solution)/shard_map/middle/pallas_call | solution.py:468
  53.3 0.0 collective-permute-done.6.refs_0_
  53.3 1.8 %lower.5 = (f32[33,16,128]{2,1,0:T(8,128)}, f32[66,8,128]{2,1,0:T(8,128)S(1)}, f32[33,8,128]{2,1,0:T(8,128)S(1)}) custom-call(f32[66,8,128]{2,1,0:T(8,128)S(1)} %collective-permute-done.6.refs_0_, f32[116,8,128]{2,1,0:T(8,128)S(1)} %collective-permute-done.3.refs_0_.refs_1_.down_ref, f32[33,64,128]{2,1,0:T(8,128)S(1)} %get-tuple-element.45.refs_0_.refs_2_.z_ref, ...), custom_call_target="tpu_custom_call" | custom-call | flops 2703360 | bytes 2162688 | tf_op jit(solution)/shard_map/lower/pallas_call | solution.py:468
  55.1 4.2 %collective-permute-start.7 = (f32[33,8,128]{2,1,0:T(8,128)S(1)}, f32[33,8,128]{2,1,0:T(8,128)S(1)}, u32[]{:S(2)}, u32[]{:S(2)}) collective-permute-start(f32[33,8,128]{2,1,0:T(8,128)S(1)} %get-tuple-element.67), channel_id=1, source_target_pairs={{0,2},{2,4},{4,6},{6,8},{8,10},{10,12},{12,14},{1,3},{3,5},{5,7},{... | collective-permute-start | bytes 405512 | tf_op jit(solution)/shard_map/ppermute | solution.py:462
  59.3 0.0 collective-permute-done.4.refs_0_
  59.3 1.8 %upper.5 = (f32[33,16,128]{2,1,0:T(8,128)}, f32[66,8,128]{2,1,0:T(8,128)S(1)}, f32[33,8,128]{2,1,0:T(8,128)S(1)}) custom-call(f32[66,8,128]{2,1,0:T(8,128)S(1)} %collective-permute-done.4.refs_0_, f32[116,8,128]{2,1,0:T(8,128)S(1)} %collective-permute-done.1.refs_0_.refs_1_.up_ref, f32[33,64,128]{2,1,0:T(8,128)S(1)} %get-tuple-element.45.refs_0_.refs_2_.z_ref, ...), custom_call_target="tpu_custom_call" | custom-call | flops 2703360 | bytes 2162688 | tf_op jit(solution)/shard_map/upper/pallas_call | solution.py:468
  61.0 1.3 %collective-permute-start.8 = (f32[33,8,128]{2,1,0:T(8,128)S(1)}, f32[33,8,128]{2,1,0:T(8,128)S(1)}, u32[]{:S(2)}, u32[]{:S(2)}) collective-permute-start(f32[33,8,128]{2,1,0:T(8,128)S(1)} %get-tuple-element.68), channel_id=1, source_target_pairs={{2,0},{4,2},{6,4},{8,6},{10,8},{12,10},{14,12},{3,1},{5,3},{7,5},{... | collective-permute-start | bytes 405512 | tf_op jit(solution)/shard_map/ppermute | solution.py:465
  62.3 0.7 %data.1.data_ref = f32[33,9,8,128]{3,2,1,0:T(8,128)S(1)} custom-call(f32[2,8,4224]{2,1,0:T(8,128)S(1)} %get-tuple-element.39.seen_ref, f32[116,8,128]{2,1,0:T(8,128)S(1)} %collective-permute-done.1.refs_0_.refs_1_.up_ref, f32[116,8,128]{2,1,0:T(8,128)S(1)} %collective-permute-done.3.refs_0_.refs_1_.down_ref), custom_call_target="tpu_custom_call" | custom-call | flops 6082560 | bytes 4866048 | tf_op jit(solution)/shard_map/data/pallas_call | solution.py:468
  63.0 1.8 %gradient.1.part_ref = f32[9,8,4096]{2,1,0:T(8,128)S(1)} custom-call(f32[33,64,128]{2,1,0:T(8,128)S(1)} %get-tuple-element.45.refs_0_.refs_2_.z_ref, f32[66,8,128]{2,1,0:T(8,128)S(1)} %get-tuple-element.63.top_ref, f32[33,32,128]{2,1,0:T(8,128)S(1)} %get-tuple-element.64.inner_ref, f32[66,8,128]{2,1,0:T(8,128)S(1)} %get-tuple-element.66.bottom_ref, ...), custom_call_target="tpu_custom_call" | custom-call | flops 16220160 | bytes 12976128 | tf_op jit(solution)/shard_map/gradient/pallas_call | solution.py:468
  64.8 0.0 collective-permute-done.7.up_ref
  64.8 3.1 %collective-permute-done.8.down_ref = f32[33,8,128]{2,1,0:T(8,128)S(1)} collective-permute-done((f32[33,8,128]{2,1,0:T(8,128)S(1)}, f32[33,8,128]{2,1,0:T(8,128)S(1)}, u32[]{:S(2)}, u32[]{:S(2)}) %collective-permute-start.8) | collective-permute-done | bytes 135200 | tf_op jit(solution)/shard_map/ppermute | solution.py:465
  67.9 1.4 %finish.1 = f32[9,8,4096]{2,1,0:T(8,128)} custom-call(f32[9,8,4096]{2,1,0:T(8,128)S(1)} %gradient.1.part_ref, f32[33,64,128]{2,1,0:T(8,128)S(1)} %get-tuple-element.45.refs_0_.refs_2_.z_ref, f32[33,8,128]{2,1,0:T(8,128)S(1)} %collective-permute-done.7.up_ref, f32[33,8,128]{2,1,0:T(8,128)S(1)} %collective-permute-done.8.down_ref), custom_call_target="tpu_custom_call" | custom-call | flops 5406720 | bytes 4325376 | tf_op jit(solution)/shard_map/finish/pallas_call | solution.py:468
Async XLA Ops:
  1.7 2.1 %collective-permute-start = (f32[2,2,8,4224]{3,2,1,0:T(8,128)S(1)}, f32[2,2,8,4224]{3,2,1,0:T(8,128)S(1)}, u32[]{:S(2)}, u32[]{:S(2)}) collective-permute-start(f32[2,2,8,4224]{3,2,1,0:T(8,128)S(1)} %get-tuple-element.42), channel_id=1, source_target_pairs={{0,1},{1,0},{2,3},{3,2},{4,5},{5,4},{6,7},{7,6},{8,9},{9,8},{10,11... | collective-permute-start | bytes 1622024 | tf_op jit(solution)/shard_map/ppermute | solution.py:496
  4.0 15.9 %collective-permute-start.3 = (f32[116,8,128]{2,1,0:T(8,128)S(1)}, f32[116,8,128]{2,1,0:T(8,128)S(1)}, u32[]{:S(2)}, u32[]{:S(2)}) collective-permute-start(f32[116,8,128]{2,1,0:T(8,128)S(1)} %get-tuple-element.50), channel_id=1, source_target_pairs={{2,0},{4,2},{6,4},{8,6},{10,8},{12,10},{14,12},{3,1},{5,3},{7,5},{... | collective-permute-start | bytes 1425416 | tf_op jit(solution)/shard_map/ppermute | solution.py:465
  5.3 25.0 %collective-permute-start.1 = (f32[116,8,128]{2,1,0:T(8,128)S(1)}, f32[116,8,128]{2,1,0:T(8,128)S(1)}, u32[]{:S(2)}, u32[]{:S(2)}) collective-permute-start(f32[116,8,128]{2,1,0:T(8,128)S(1)} %get-tuple-element.46), channel_id=1, source_target_pairs={{0,2},{2,4},{4,6},{6,8},{8,10},{10,12},{12,14},{1,3},{3,5},{5,7},{... | collective-permute-start | bytes 1425416 | tf_op jit(solution)/shard_map/ppermute | solution.py:462
  21.2 14.8 %collective-permute-start.5 = (f32[66,8,128]{2,1,0:T(8,128)S(1)}, f32[66,8,128]{2,1,0:T(8,128)S(1)}, u32[]{:S(2)}, u32[]{:S(2)}) collective-permute-start(f32[66,8,128]{2,1,0:T(8,128)S(1)} %get-tuple-element.52.refs_4_.refs_6_), channel_id=1, source_target_pairs={{0,2},{2,4},{4,6},{6,8},{8,10},{10,12},{12,14},{1,3},{3,5},{5,7},{... | collective-permute-start | bytes 811016 | tf_op jit(solution)/shard_map/ppermute | solution.py:462
  31.6 15.0 %collective-permute-start.2 = (f32[66,8,128]{2,1,0:T(8,128)S(1)}, f32[66,8,128]{2,1,0:T(8,128)S(1)}, u32[]{:S(2)}, u32[]{:S(2)}) collective-permute-start(f32[66,8,128]{2,1,0:T(8,128)S(1)} %get-tuple-element.49.refs_2_.refs_6_), channel_id=1, source_target_pairs={{2,0},{4,2},{6,4},{8,6},{10,8},{12,10},{14,12},{3,1},{5,3},{7,5},{... | collective-permute-start | bytes 811016 | tf_op jit(solution)/shard_map/ppermute | solution.py:465
  37.1 16.2 %collective-permute-start.6 = (f32[66,8,128]{2,1,0:T(8,128)S(1)}, f32[66,8,128]{2,1,0:T(8,128)S(1)}, u32[]{:S(2)}, u32[]{:S(2)}) collective-permute-start(f32[66,8,128]{2,1,0:T(8,128)S(1)} %get-tuple-element.59.refs_2_.refs_6_), channel_id=1, source_target_pairs={{2,0},{4,2},{6,4},{8,6},{10,8},{12,10},{14,12},{3,1},{5,3},{7,5},{... | collective-permute-start | bytes 811016 | tf_op jit(solution)/shard_map/ppermute | solution.py:465
  47.7 11.6 %collective-permute-start.4 = (f32[66,8,128]{2,1,0:T(8,128)S(1)}, f32[66,8,128]{2,1,0:T(8,128)S(1)}, u32[]{:S(2)}, u32[]{:S(2)}) collective-permute-start(f32[66,8,128]{2,1,0:T(8,128)S(1)} %get-tuple-element.56.refs_4_.refs_6_), channel_id=1, source_target_pairs={{0,2},{2,4},{4,6},{6,8},{8,10},{10,12},{12,14},{1,3},{3,5},{5,7},{... | collective-permute-start | bytes 811016 | tf_op jit(solution)/shard_map/ppermute | solution.py:462
  55.1 9.8 %collective-permute-start.7 = (f32[33,8,128]{2,1,0:T(8,128)S(1)}, f32[33,8,128]{2,1,0:T(8,128)S(1)}, u32[]{:S(2)}, u32[]{:S(2)}) collective-permute-start(f32[33,8,128]{2,1,0:T(8,128)S(1)} %get-tuple-element.67), channel_id=1, source_target_pairs={{0,2},{2,4},{4,6},{6,8},{8,10},{10,12},{12,14},{1,3},{3,5},{5,7},{... | collective-permute-start | bytes 405512 | tf_op jit(solution)/shard_map/ppermute | solution.py:462
  61.0 6.9 %collective-permute-start.8 = (f32[33,8,128]{2,1,0:T(8,128)S(1)}, f32[33,8,128]{2,1,0:T(8,128)S(1)}, u32[]{:S(2)}, u32[]{:S(2)}) collective-permute-start(f32[33,8,128]{2,1,0:T(8,128)S(1)} %get-tuple-element.68), channel_id=1, source_target_pairs={{2,0},{4,2},{6,4},{8,6},{10,8},{12,10},{14,12},{3,1},{5,3},{7,5},{... | collective-permute-start | bytes 405512 | tf_op jit(solution)/shard_map/ppermute | solution.py:465

commit v4 on v2

--- a/solution.py
+++ b/solution.py
@@ -63,6 +63,18 @@
 
 def sub(row):
     return pl.ds(row * SUBS, SUBS)
+
+
+def upside_down():
+    return 1 - lax.axis_index("row") % 2
+
+
+def place(row, flip):
+    return row + flip * (SUBS - 1 - 2 * row)
+
+
+def placed(row, flip):
+    return pl.ds(pl.multiple_of(place(row, flip) * SUBS, SUBS), SUBS)
 
 
 def tile_columns(tile):
@@ -95,6 +107,7 @@
     chunk = chunk_of(tiles)
     scale = 4.0 / (upper_edge - lower_edge)
     shift = 2.0 * (upper_edge + lower_edge) / (upper_edge - lower_edge)
+    tilt = (upside_down().astype(jnp.float32) - 0.5) * scale
 
     def body(step, carry):
         for k in range(chunk):
@@ -109,7 +122,7 @@
                     scale * (kappa[c] + 2.0 * (across[c] + along[c])) - shift,
                     -scale * across[c],
                     -scale * along[c],
-                    -0.5 * scale * skew[c],
+                    tilt * skew[c],
                     coupling,
                 )
                 for kind, value in enumerate(values):
@@ -120,9 +133,10 @@
     lax.fori_loop(0, tiles // chunk, body, 0)
 
 
-def layout_kernel(own_ref, other_ref, seen_ref, z_ref, top_ref, bottom_ref):
+def layout_kernel(own_ref, other_ref, seen_ref, z_ref, top_ref, bottom_ref, natural):
     tiles = z_ref.shape[0]
     chunk = chunk_of(tiles)
+    flip = upside_down()
 
     def body(step, carry):
         for k in range(chunk):
@@ -130,21 +144,28 @@
             cols = tile_columns(tile)
             for c in range(2):
                 for probe in range(2):
-                    z_ref[tile, pl.ds(4 * c + probe, SUBS, stride=SUBS), :] = own_ref[probe, c, :, cols]
-                    z_ref[tile, pl.ds(4 * c + 2 + probe, SUBS, stride=SUBS), :] = other_ref[probe, c, :, cols]
+                    natural[tile, pl.ds(4 * c + probe, SUBS, stride=SUBS), :] = own_ref[probe, c, :, cols]
+                    natural[tile, pl.ds(4 * c + 2 + probe, SUBS, stride=SUBS), :] = other_ref[probe, c, :, cols]
+        for k in range(chunk):
+            tile = step * chunk + k
+            for row in range(SUBS):
+                value = natural[tile, placed(row, flip), :]
+                z_ref[tile, sub(row), :] = value
+                if row == 0:
+                    top_ref[tile] = value
+                if row == SUBS - 1:
+                    bottom_ref[tile] = value
         return carry
 
     lax.fori_loop(0, tiles // chunk, body, 0)
-    for tile in range(tiles):
-        top_ref[tile] = z_ref[tile, sub(0), :]
-        bottom_ref[tile] = z_ref[tile, sub(SUBS - 1), :]
     for c in range(2):
         for tile in range(tiles):
-            place = c * tiles + tile
+            index = c * tiles + tile
             cols = pl.ds(tile * LANES, LANES)
-            at = (tiles + place // SUBS, pl.ds(place % SUBS, 1))
-            top_ref[at[0], at[1], :] = seen_ref[c, 0:1, cols]
-            bottom_ref[at[0], at[1], :] = seen_ref[c, SUBS - 1 : SUBS, cols]
+            at = (tiles + index // SUBS, pl.ds(index % SUBS, 1))
+            first, last = seen_ref[c, 0:1, cols], seen_ref[c, SUBS - 1 : SUBS, cols]
+            top_ref[at[0], at[1], :] = jnp.where(flip == 1, last, first)
+            bottom_ref[at[0], at[1], :] = jnp.where(flip == 1, first, last)
 
 
 def step_kernel(upper, constants, offset, other_row, tiles, *refs):
@@ -157,6 +178,8 @@
     out_ref, edge_ref = rest
     first_row = 0 if upper else 4
     chunk = chunk_of(tiles)
+
+    flip = upside_down()
 
     def load(row):
         if row == (-1 if upper else 4):
@@ -189,7 +212,8 @@
                 slopes.append(right - left)
             for row in range(4):
                 rows = sub(first_row + row)
-                coefs = [coefficients_ref[kind, tile, rows, :] for kind in range(5)]
+                at = placed(first_row + row, flip)
+                coefs = [coefficients_ref[kind, tile, at, :] for kind in range(5)]
                 total = (
                     coefs[0] * values[row + 1]
                     + coefs[1] * sums[row + 1]
@@ -213,9 +237,12 @@
 def data_kernel(tiles, seen_ref, up_ref, down_ref, out_ref):
     chunk = chunk_of(tiles)
 
-    def halo(ref, c, tile):
-        place = c * tiles + tile
-        return jnp.broadcast_to(ref[tiles + place // SUBS, pl.ds(place % SUBS, 1), :], (SUBS, LANES))
+    flip = upside_down()
+
+    def halo(near, far, c, tile):
+        index = c * tiles + tile
+        at = (tiles + index // SUBS, pl.ds(index % SUBS, 1), slice(None))
+        return jnp.broadcast_to(jnp.where(flip == 1, far[at], near[at]), (SUBS, LANES))
 
     def body(step, carry):
         edges = masks()
@@ -224,8 +251,8 @@
         kept = [[], []]
         for c in range(2):
             values = window_tiles(lambda tile: seen_ref[c, :, tile_columns(tile)], first, chunk, tiles)
-            ups = window_tiles(lambda tile: halo(up_ref, c, tile), first, chunk, tiles)
-            downs = window_tiles(lambda tile: halo(down_ref, c, tile), first, chunk, tiles)
+            ups = window_tiles(lambda tile: halo(up_ref, down_ref, c, tile), first, chunk, tiles)
+            downs = window_tiles(lambda tile: halo(down_ref, up_ref, c, tile), first, chunk, tiles)
             aboves = [jnp.where(row == 0, u, pltpu.roll(v, 1, 0)) for u, v in zip(ups, values)]
             belows = [jnp.where(row == SUBS - 1, d, pltpu.roll(v, SUBS - 1, 0)) for d, v in zip(downs, values)]
             tilts = [b - a for a, b in zip(aboves, belows)]
@@ -251,6 +278,8 @@
     kept = out_ref.shape[2] // LANES
     offset = lax.axis_index("probe") * (tiles - kept)
     count = products.shape[0]
+    flip = upside_down()
+    tilt = flip.astype(jnp.float32) - 0.5
 
     def load(row):
         if row < 4:
@@ -273,6 +302,7 @@
             for row in range(SUBS):
                 left = factor * z_ref[tile, sub(row), :]
                 value = values[row]
+                at = placed(row, flip)
                 twice = 2.0 * value
                 if row == 0:
                     along, skew = values[1], slopes[1]
@@ -280,11 +310,11 @@
                     along, skew = values[row - 1], -slopes[row - 1]
                 else:
                     along, skew = values[row - 1] + values[row + 1], slopes[row + 1] - slopes[row - 1]
-                products[k, 0, sub(row), :] = left * value
-                products[k, 1, sub(row), :] = left * (twice - sums[row])
-                products[k, 2, sub(row), :] = left * (twice - along)
-                products[k, 3, sub(row), :] = (-0.5 * left) * skew
-                products[k, 4, sub(row), :] = left * pltpu.roll(value, 4, 0)
+                products[k, 0, at, :] = left * value
+                products[k, 1, at, :] = left * (twice - sums[row])
+                products[k, 2, at, :] = left * (twice - along)
+                products[k, 3, at, :] = (tilt * left) * skew
+                products[k, 4, at, :] = left * pltpu.roll(value, 4, 0)
         for k in range(count):
             index = step * count + k
             tile = index + offset
@@ -312,16 +342,18 @@
     ]
     for copy in early:
         copy.start()
+    flip = upside_down()
+    tilt = 0.5 - flip.astype(jnp.float32)
 
     def body(step, carry):
         edges = masks()
-        row = lax.broadcasted_iota(jnp.int32, (SUBS, LANES), 0)
+        row = place(lax.broadcasted_iota(jnp.int32, (SUBS, LANES), 0), flip)
         for k in range(count):
             index = step * count + k
             tile = index + offset
             cols = tile_columns(index)
             adds = []
-            for ref, z_row, sign in ((up_ref, 0, 0.5), (down_ref, SUBS - 1, -0.5)):
+            for ref, z_row, sign in ((up_ref, 0, tilt), (down_ref, SUBS - 1, -tilt)):
                 before, here, after = window_tiles(lambda at: ref[at], tile, 1, tiles)
                 left, right = beside(before, here, after, edges)
                 z = factor * z_ref[tile, sub(z_row), :]
@@ -358,14 +390,14 @@
     kept = share // LANES
     seen_tiles = -(-2 * tiles // SUBS)
     rows = lax.axis_size("row")
-    down_pairs = [(i, i + 1) for i in range(rows - 1)]
-    up_pairs = [(i + 1, i) for i in range(rows - 1)]
-
-    def to_next(edge):
-        return lax.ppermute(edge, "row", down_pairs)
-
-    def to_previous(edge):
-        return lax.ppermute(edge, "row", up_pairs)
+    near_pairs = [pair for i in range(0, rows - 1, 2) for pair in ((i, i + 1), (i + 1, i))]
+    far_pairs = [pair for i in range(1, rows - 1, 2) for pair in ((i, i + 1), (i + 1, i))]
+
+    def near(edge):
+        return lax.ppermute(edge, "row", near_pairs)
+
+    def far(edge):
+        return lax.ppermute(edge, "row", far_pairs)
 
     def call(kernel, name, vregs, operands, outs, scratch=(), in_specs=None, out_specs=None):
         return pl.pallas_call(
@@ -408,6 +440,7 @@
         8 * tiles,
         (own, other, seen),
         [pltpu.VMEM((tiles, SUBS * SUBS, LANES), f32), pltpu.VMEM(message, f32), pltpu.VMEM(message, f32)],
+        [pltpu.VMEM((tiles, SUBS * SUBS, LANES), f32)],
     )
 
     def half(upper, constants, own, other_half, halo, before):
@@ -425,7 +458,7 @@
             [pltpu.VMEM((tiles, 4 * SUBS, LANES), f32), pltpu.VMEM((tiles, SUBS, LANES), f32)],
         )
 
-    first_up, first_down = to_next(bottom), to_previous(top)
+    first_up, first_down = near(top), far(bottom)
     up, down = first_up, first_down
     now = (z, z)
     before = (None, None)
@@ -439,9 +472,9 @@
         else:
             constants = (weights[0], 0.5, True)
         upper, top = half(True, constants, now[0], now[1], up, before[0])
-        next_down = to_previous(top)
+        next_up = near(top)
         lower, bottom = half(False, constants, now[1], now[0], down, before[1])
-        next_up = to_next(bottom)
+        next_down = far(bottom)
         before, now = now, (upper, lower)
         up, down = next_up, next_down
 

time: 71.3 us -> 72.1 us (1.011)
  the two profiles are of different devices: /device:TPU:0 before, /device:TPU:16 now
where the time goes in v4:
time: 72.1 us; the launch traced here: 71.8 us
  waiting for transfers between devices  31.1 us (43%)
  starting transfers between devices  24.2 us (34%)
  Pallas kernels  16.3 us (23%)
    ppermute x7, waiting for transfers between devices, far(): return lax.ppermute(edge, 'row', far_pairs)  19 us
    pallas_call x18, Pallas kernels, call(): pl.pallas_call(kernel, out_shape=outs, in_specs=in_specs or [vmem_spec()]...  16.3 us
    ppermute x7, starting transfers between devices, far(): return lax.ppermute(edge, 'row', far_pairs)  14.2 us
    ppermute x7, waiting for transfers between devices, near(): return lax.ppermute(edge, 'row', near_pairs)  11.1 us
    ppermute x7, starting transfers between devices, near(): return lax.ppermute(edge, 'row', near_pairs)  9.97 us
  transfers between devices with their start and end apart: 15, of which 13 were waited for; matrix products, arithmetic and copies ran while one was open for 0% of the time, Pallas kernels for 18%

profile of v4, /device:TPU:16, one launch (start us, length us, event | category | flops | bytes accessed | tf_op | source)
XLA Modules:
  0.0 71.8 jit_solution(11250082460112234963)
XLA Ops:
  0.0 1.7 %load.1 = (f32[2,2,8,4224]{3,2,1,0:T(8,128)S(1)}, f32[2,2,8,4224]{3,2,1,0:T(8,128)S(1)}, f32[2,8,4224]{2,1,0:T(8,128)S(1)}, f32[9,8,4224]{2,1,0:T(8,128)S(1)}) custom-call(f32[2,2,8,8192]{3,2,1,0:T(8,128)} %probes_ref.1, f32[2,8,8192]{2,1,0:T(8,128)} %observed_ref.1, f32[9,8,8192]{2,1,0:T(8,128)} %coefficients_ref.1), custom_call_target="tpu_custom_call" | custom-call | flops 2048000 | bytes 1638400 | tf_op jit(solution)/shard_map/load/pallas_call | solution.py:403
  1.7 0.1 collective-permute-start
  1.8 0.8 %prep.1.refs_4_ = f32[5,33,64,128]{3,2,1,0:T(8,128)S(1)} custom-call(f32[9,8,4224]{2,1,0:T(8,128)S(1)} %get-tuple-element.39.window_ref), custom_call_target="tpu_custom_call" | custom-call | flops 27033600 | bytes 21626880 | tf_op jit(solution)/shard_map/prep/pallas_call | solution.py:403
  2.6 1.1 %collective-permute-done.other_ref = f32[2,2,8,4224]{3,2,1,0:T(8,128)S(1)} collective-permute-done((f32[2,2,8,4224]{3,2,1,0:T(8,128)S(1)}, f32[2,2,8,4224]{3,2,1,0:T(8,128)S(1)}, u32[]{:S(2)}, u32[]{:S(2)}) %collective-permute-start) | collective-permute-done | bytes 540704 | tf_op jit(solution)/shard_map/ppermute | solution.py:431
  3.7 0.3 layout.1
  4.0 1.6 %collective-permute-start.1 = (f32[42,8,128]{2,1,0:T(8,128)S(1)}, f32[42,8,128]{2,1,0:T(8,128)S(1)}, u32[]{:S(2)}, u32[]{:S(2)}) collective-permute-start(f32[42,8,128]{2,1,0:T(8,128)S(1)} %get-tuple-element.44), channel_id=1, source_target_pairs={{0,2},{2,0},{4,6},{6,4},{8,10},{10,8},{12,14},{14,12},{1,3},{3,1},... | collective-permute-start | bytes 516104 | tf_op jit(solution)/shard_map/ppermute | solution.py:397
  5.6 2.3 %collective-permute-start.2 = (f32[42,8,128]{2,1,0:T(8,128)S(1)}, f32[42,8,128]{2,1,0:T(8,128)S(1)}, u32[]{:S(2)}, u32[]{:S(2)}) collective-permute-start(f32[42,8,128]{2,1,0:T(8,128)S(1)} %get-tuple-element.47), channel_id=1, source_target_pairs={{2,4},{4,2},{6,8},{8,6},{10,12},{12,10},{3,5},{5,3},{7,9},{9,7},{1... | collective-permute-start | bytes 516104 | tf_op jit(solution)/shard_map/ppermute | solution.py:400
  7.9 5.8 %collective-permute-done.1.refs_2_.up_ref = f32[42,8,128]{2,1,0:T(8,128)S(1)} collective-permute-done((f32[42,8,128]{2,1,0:T(8,128)S(1)}, f32[42,8,128]{2,1,0:T(8,128)S(1)}, u32[]{:S(2)}, u32[]{:S(2)}) %collective-permute-start.1) | collective-permute-done | bytes 172064 | tf_op jit(solution)/shard_map/ppermute | solution.py:397
  13.7 0.7 upper.6
  14.4 2.6 %collective-permute-start.3 = (f32[33,8,128]{2,1,0:T(8,128)S(1)}, f32[33,8,128]{2,1,0:T(8,128)S(1)}, u32[]{:S(2)}, u32[]{:S(2)}) collective-permute-start(f32[33,8,128]{2,1,0:T(8,128)S(1)} %get-tuple-element.49), channel_id=1, source_target_pairs={{0,2},{2,0},{4,6},{6,4},{8,10},{10,8},{12,14},{14,12},{1,3},{3,1},... | collective-permute-start | bytes 405512 | tf_op jit(solution)/shard_map/ppermute | solution.py:397
  16.9 0.0 collective-permute-done.2.refs_2_.down_ref
  16.9 0.7 lower.6
  17.6 1.9 %collective-permute-start.4 = (f32[33,8,128]{2,1,0:T(8,128)S(1)}, f32[33,8,128]{2,1,0:T(8,128)S(1)}, u32[]{:S(2)}, u32[]{:S(2)}) collective-permute-start(f32[33,8,128]{2,1,0:T(8,128)S(1)} %get-tuple-element.51), channel_id=1, source_target_pairs={{2,4},{4,2},{6,8},{8,6},{10,12},{12,10},{3,5},{5,3},{7,9},{9,7},{1... | collective-permute-start | bytes 405512 | tf_op jit(solution)/shard_map/ppermute | solution.py:400
  19.6 2.0 %collective-permute-done.3.refs_2_ = f32[33,8,128]{2,1,0:T(8,128)S(1)} collective-permute-done((f32[33,8,128]{2,1,0:T(8,128)S(1)}, f32[33,8,128]{2,1,0:T(8,128)S(1)}, u32[]{:S(2)}, u32[]{:S(2)}) %collective-permute-start.3) | collective-permute-done | bytes 135200 | tf_op jit(solution)/shard_map/ppermute | solution.py:397
  21.5 0.7 upper.7
  22.2 2.4 %collective-permute-start.5 = (f32[33,8,128]{2,1,0:T(8,128)S(1)}, f32[33,8,128]{2,1,0:T(8,128)S(1)}, u32[]{:S(2)}, u32[]{:S(2)}) collective-permute-start(f32[33,8,128]{2,1,0:T(8,128)S(1)} %get-tuple-element.53), channel_id=1, source_target_pairs={{0,2},{2,0},{4,6},{6,4},{8,10},{10,8},{12,14},{14,12},{1,3},{3,1},... | collective-permute-start | bytes 405512 | tf_op jit(solution)/shard_map/ppermute | solution.py:397
  24.6 0.8 %collective-permute-done.4.refs_2_ = f32[33,8,128]{2,1,0:T(8,128)S(1)} collective-permute-done((f32[33,8,128]{2,1,0:T(8,128)S(1)}, f32[33,8,128]{2,1,0:T(8,128)S(1)}, u32[]{:S(2)}, u32[]{:S(2)}) %collective-permute-start.4) | collective-permute-done | bytes 135200 | tf_op jit(solution)/shard_map/ppermute | solution.py:400
  25.4 0.7 lower.7
  26.1 2.0 %collective-permute-start.6 = (f32[33,8,128]{2,1,0:T(8,128)S(1)}, f32[33,8,128]{2,1,0:T(8,128)S(1)}, u32[]{:S(2)}, u32[]{:S(2)}) collective-permute-start(f32[33,8,128]{2,1,0:T(8,128)S(1)} %get-tuple-element.55), channel_id=1, source_target_pairs={{2,4},{4,2},{6,8},{8,6},{10,12},{12,10},{3,5},{5,3},{7,9},{9,7},{1... | collective-permute-start | bytes 405512 | tf_op jit(solution)/shard_map/ppermute | solution.py:400
  28.2 1.3 %collective-permute-done.5.refs_2_ = f32[33,8,128]{2,1,0:T(8,128)S(1)} collective-permute-done((f32[33,8,128]{2,1,0:T(8,128)S(1)}, f32[33,8,128]{2,1,0:T(8,128)S(1)}, u32[]{:S(2)}, u32[]{:S(2)}) %collective-permute-start.5) | collective-permute-done | bytes 135200 | tf_op jit(solution)/shard_map/ppermute | solution.py:397
  29.5 0.7 upper.8
  30.2 2.0 %collective-permute-start.7 = (f32[33,8,128]{2,1,0:T(8,128)S(1)}, f32[33,8,128]{2,1,0:T(8,128)S(1)}, u32[]{:S(2)}, u32[]{:S(2)}) collective-permute-start(f32[33,8,128]{2,1,0:T(8,128)S(1)} %get-tuple-element.57), channel_id=1, source_target_pairs={{0,2},{2,0},{4,6},{6,4},{8,10},{10,8},{12,14},{14,12},{1,3},{3,1},... | collective-permute-start | bytes 405512 | tf_op jit(solution)/shard_map/ppermute | solution.py:397
  32.1 1.8 %collective-permute-done.6.refs_2_ = f32[33,8,128]{2,1,0:T(8,128)S(1)} collective-permute-done((f32[33,8,128]{2,1,0:T(8,128)S(1)}, f32[33,8,128]{2,1,0:T(8,128)S(1)}, u32[]{:S(2)}, u32[]{:S(2)}) %collective-permute-start.6) | collective-permute-done | bytes 135200 | tf_op jit(solution)/shard_map/ppermute | solution.py:400
  33.9 0.7 lower.8
  34.7 2.0 %collective-permute-start.8 = (f32[33,8,128]{2,1,0:T(8,128)S(1)}, f32[33,8,128]{2,1,0:T(8,128)S(1)}, u32[]{:S(2)}, u32[]{:S(2)}) collective-permute-start(f32[33,8,128]{2,1,0:T(8,128)S(1)} %get-tuple-element.59), channel_id=1, source_target_pairs={{2,4},{4,2},{6,8},{8,6},{10,12},{12,10},{3,5},{5,3},{7,9},{9,7},{1... | collective-permute-start | bytes 405512 | tf_op jit(solution)/shard_map/ppermute | solution.py:400
  36.7 0.8 %collective-permute-done.7.refs_2_ = f32[33,8,128]{2,1,0:T(8,128)S(1)} collective-permute-done((f32[33,8,128]{2,1,0:T(8,128)S(1)}, f32[33,8,128]{2,1,0:T(8,128)S(1)}, u32[]{:S(2)}, u32[]{:S(2)}) %collective-permute-start.7) | collective-permute-done | bytes 135200 | tf_op jit(solution)/shard_map/ppermute | solution.py:397
  37.5 0.7 upper.9
  38.3 1.4 %collective-permute-start.9 = (f32[33,8,128]{2,1,0:T(8,128)S(1)}, f32[33,8,128]{2,1,0:T(8,128)S(1)}, u32[]{:S(2)}, u32[]{:S(2)}) collective-permute-start(f32[33,8,128]{2,1,0:T(8,128)S(1)} %get-tuple-element.61), channel_id=1, source_target_pairs={{0,2},{2,0},{4,6},{6,4},{8,10},{10,8},{12,14},{14,12},{1,3},{3,1},... | collective-permute-start | bytes 405512 | tf_op jit(solution)/shard_map/ppermute | solution.py:397
  39.6 3.4 %collective-permute-done.8.refs_2_ = f32[33,8,128]{2,1,0:T(8,128)S(1)} collective-permute-done((f32[33,8,128]{2,1,0:T(8,128)S(1)}, f32[33,8,128]{2,1,0:T(8,128)S(1)}, u32[]{:S(2)}, u32[]{:S(2)}) %collective-permute-start.8) | collective-permute-done | bytes 135200 | tf_op jit(solution)/shard_map/ppermute | solution.py:400
  43.0 0.7 lower.9
  43.8 1.9 %collective-permute-start.10 = (f32[33,8,128]{2,1,0:T(8,128)S(1)}, f32[33,8,128]{2,1,0:T(8,128)S(1)}, u32[]{:S(2)}, u32[]{:S(2)}) collective-permute-start(f32[33,8,128]{2,1,0:T(8,128)S(1)} %get-tuple-element.63), channel_id=1, source_target_pairs={{2,4},{4,2},{6,8},{8,6},{10,12},{12,10},{3,5},{5,3},{7,9},{9,7},{1... | collective-permute-start | bytes 405512 | tf_op jit(solution)/shard_map/ppermute | solution.py:400
  45.7 1.0 %collective-permute-done.9.refs_2_ = f32[33,8,128]{2,1,0:T(8,128)S(1)} collective-permute-done((f32[33,8,128]{2,1,0:T(8,128)S(1)}, f32[33,8,128]{2,1,0:T(8,128)S(1)}, u32[]{:S(2)}, u32[]{:S(2)}) %collective-permute-start.9) | collective-permute-done | bytes 135200 | tf_op jit(solution)/shard_map/ppermute | solution.py:397
  46.7 0.7 upper.10
  47.4 0.1 collective-permute-start.11
  47.5 5.5 %collective-permute-done.10.refs_2_ = f32[33,8,128]{2,1,0:T(8,128)S(1)} collective-permute-done((f32[33,8,128]{2,1,0:T(8,128)S(1)}, f32[33,8,128]{2,1,0:T(8,128)S(1)}, u32[]{:S(2)}, u32[]{:S(2)}) %collective-permute-start.10) | collective-permute-done | bytes 135200 | tf_op jit(solution)/shard_map/ppermute | solution.py:400
  53.0 0.7 lower.10
  53.7 1.9 %collective-permute-start.12 = (f32[33,8,128]{2,1,0:T(8,128)S(1)}, f32[33,8,128]{2,1,0:T(8,128)S(1)}, u32[]{:S(2)}, u32[]{:S(2)}) collective-permute-start(f32[33,8,128]{2,1,0:T(8,128)S(1)} %get-tuple-element.67), channel_id=1, source_target_pairs={{2,4},{4,2},{6,8},{8,6},{10,12},{12,10},{3,5},{5,3},{7,9},{9,7},{1... | collective-permute-start | bytes 405512 | tf_op jit(solution)/shard_map/ppermute | solution.py:400
  55.6 0.1 collective-permute-done.11.refs_2_
  55.8 0.7 upper.11
  56.5 0.1 collective-permute-start.13
  56.5 5.4 %collective-permute-done.12.refs_2_ = f32[33,8,128]{2,1,0:T(8,128)S(1)} collective-permute-done((f32[33,8,128]{2,1,0:T(8,128)S(1)}, f32[33,8,128]{2,1,0:T(8,128)S(1)}, u32[]{:S(2)}, u32[]{:S(2)}) %collective-permute-start.12) | collective-permute-done | bytes 135200 | tf_op jit(solution)/shard_map/ppermute | solution.py:400
  62.0 0.7 lower.11
  62.7 2.1 %collective-permute-start.14 = (f32[33,8,128]{2,1,0:T(8,128)S(1)}, f32[33,8,128]{2,1,0:T(8,128)S(1)}, u32[]{:S(2)}, u32[]{:S(2)}) collective-permute-start(f32[33,8,128]{2,1,0:T(8,128)S(1)} %get-tuple-element.70), channel_id=1, source_target_pairs={{2,4},{4,2},{6,8},{8,6},{10,12},{12,10},{3,5},{5,3},{7,9},{9,7},{1... | collective-permute-start | bytes 405512 | tf_op jit(solution)/shard_map/ppermute | solution.py:400
  64.8 0.8 %data.1.data_ref = f32[33,9,8,128]{3,2,1,0:T(8,128)S(1)} custom-call(f32[2,8,4224]{2,1,0:T(8,128)S(1)} %get-tuple-element.42.seen_ref, f32[42,8,128]{2,1,0:T(8,128)S(1)} %collective-permute-done.1.refs_2_.up_ref, f32[42,8,128]{2,1,0:T(8,128)S(1)} %collective-permute-done.2.refs_2_.down_ref), custom_call_target="tpu_custom_call" | custom-call | flops 6082560 | bytes 4866048 | tf_op jit(solution)/shard_map/data/pallas_call | solution.py:403
  65.6 2.9 %gradient.1.part_ref = f32[9,8,4096]{2,1,0:T(8,128)S(1)} custom-call(f32[33,64,128]{2,1,0:T(8,128)S(1)} %get-tuple-element.43.refs_0_.refs_1_.refs_3_.z_ref, f32[33,32,128]{2,1,0:T(8,128)S(1)} %get-tuple-element.66.top_ref, f32[33,32,128]{2,1,0:T(8,128)S(1)} %get-tuple-element.68.bottom_ref, f32[33,9,8,128]{3,2,1,0:T(8,128)S(1)} %data.1.data_ref), custom_call_target="tpu_custom_call" | custom-call | flops 16220160 | bytes 12976128 | tf_op jit(solution)/shard_map/gradient/pallas_call | solution.py:403
  68.5 0.0 collective-permute-done.13.up_ref
  68.5 2.0 %collective-permute-done.14.down_ref = f32[33,8,128]{2,1,0:T(8,128)S(1)} collective-permute-done((f32[33,8,128]{2,1,0:T(8,128)S(1)}, f32[33,8,128]{2,1,0:T(8,128)S(1)}, u32[]{:S(2)}, u32[]{:S(2)}) %collective-permute-start.14) | collective-permute-done | bytes 135200 | tf_op jit(solution)/shard_map/ppermute | solution.py:400
  70.5 1.4 %finish.1 = f32[9,8,4096]{2,1,0:T(8,128)} custom-call(f32[9,8,4096]{2,1,0:T(8,128)S(1)} %gradient.1.part_ref, f32[33,64,128]{2,1,0:T(8,128)S(1)} %get-tuple-element.43.refs_0_.refs_1_.refs_3_.z_ref, f32[33,8,128]{2,1,0:T(8,128)S(1)} %collective-permute-done.13.up_ref, f32[33,8,128]{2,1,0:T(8,128)S(1)} %collective-permute-done.14.down_ref), custom_call_target="tpu_custom_call" | custom-call | flops 5406720 | bytes 4325376 | tf_op jit(solution)/shard_map/finish/pallas_call | solution.py:403
Async XLA Ops:
  1.7 2.0 %collective-permute-start = (f32[2,2,8,4224]{3,2,1,0:T(8,128)S(1)}, f32[2,2,8,4224]{3,2,1,0:T(8,128)S(1)}, u32[]{:S(2)}, u32[]{:S(2)}) collective-permute-start(f32[2,2,8,4224]{3,2,1,0:T(8,128)S(1)} %get-tuple-element.41), channel_id=1, source_target_pairs={{0,1},{1,0},{2,3},{3,2},{4,5},{5,4},{6,7},{7,6},{8,9},{9,8},{10,11... | collective-permute-start | bytes 1622024 | tf_op jit(solution)/shard_map/ppermute | solution.py:431
  4.0 9.7 %collective-permute-start.1 = (f32[42,8,128]{2,1,0:T(8,128)S(1)}, f32[42,8,128]{2,1,0:T(8,128)S(1)}, u32[]{:S(2)}, u32[]{:S(2)}) collective-permute-start(f32[42,8,128]{2,1,0:T(8,128)S(1)} %get-tuple-element.44), channel_id=1, source_target_pairs={{0,2},{2,0},{4,6},{6,4},{8,10},{10,8},{12,14},{14,12},{1,3},{3,1},... | collective-permute-start | bytes 516104 | tf_op jit(solution)/shard_map/ppermute | solution.py:397
  5.6 11.3 %collective-permute-start.2 = (f32[42,8,128]{2,1,0:T(8,128)S(1)}, f32[42,8,128]{2,1,0:T(8,128)S(1)}, u32[]{:S(2)}, u32[]{:S(2)}) collective-permute-start(f32[42,8,128]{2,1,0:T(8,128)S(1)} %get-tuple-element.47), channel_id=1, source_target_pairs={{2,4},{4,2},{6,8},{8,6},{10,12},{12,10},{3,5},{5,3},{7,9},{9,7},{1... | collective-permute-start | bytes 516104 | tf_op jit(solution)/shard_map/ppermute | solution.py:400
  14.4 7.2 %collective-permute-start.3 = (f32[33,8,128]{2,1,0:T(8,128)S(1)}, f32[33,8,128]{2,1,0:T(8,128)S(1)}, u32[]{:S(2)}, u32[]{:S(2)}) collective-permute-start(f32[33,8,128]{2,1,0:T(8,128)S(1)} %get-tuple-element.49), channel_id=1, source_target_pairs={{0,2},{2,0},{4,6},{6,4},{8,10},{10,8},{12,14},{14,12},{1,3},{3,1},... | collective-permute-start | bytes 405512 | tf_op jit(solution)/shard_map/ppermute | solution.py:397
  17.6 7.8 %collective-permute-start.4 = (f32[33,8,128]{2,1,0:T(8,128)S(1)}, f32[33,8,128]{2,1,0:T(8,128)S(1)}, u32[]{:S(2)}, u32[]{:S(2)}) collective-permute-start(f32[33,8,128]{2,1,0:T(8,128)S(1)} %get-tuple-element.51), channel_id=1, source_target_pairs={{2,4},{4,2},{6,8},{8,6},{10,12},{12,10},{3,5},{5,3},{7,9},{9,7},{1... | collective-permute-start | bytes 405512 | tf_op jit(solution)/shard_map/ppermute | solution.py:400
  22.2 7.2 %collective-permute-start.5 = (f32[33,8,128]{2,1,0:T(8,128)S(1)}, f32[33,8,128]{2,1,0:T(8,128)S(1)}, u32[]{:S(2)}, u32[]{:S(2)}) collective-permute-start(f32[33,8,128]{2,1,0:T(8,128)S(1)} %get-tuple-element.53), channel_id=1, source_target_pairs={{0,2},{2,0},{4,6},{6,4},{8,10},{10,8},{12,14},{14,12},{1,3},{3,1},... | collective-permute-start | bytes 405512 | tf_op jit(solution)/shard_map/ppermute | solution.py:397
  26.1 7.8 %collective-permute-start.6 = (f32[33,8,128]{2,1,0:T(8,128)S(1)}, f32[33,8,128]{2,1,0:T(8,128)S(1)}, u32[]{:S(2)}, u32[]{:S(2)}) collective-permute-start(f32[33,8,128]{2,1,0:T(8,128)S(1)} %get-tuple-element.55), channel_id=1, source_target_pairs={{2,4},{4,2},{6,8},{8,6},{10,12},{12,10},{3,5},{5,3},{7,9},{9,7},{1... | collective-permute-start | bytes 405512 | tf_op jit(solution)/shard_map/ppermute | solution.py:400
  30.2 7.4 %collective-permute-start.7 = (f32[33,8,128]{2,1,0:T(8,128)S(1)}, f32[33,8,128]{2,1,0:T(8,128)S(1)}, u32[]{:S(2)}, u32[]{:S(2)}) collective-permute-start(f32[33,8,128]{2,1,0:T(8,128)S(1)} %get-tuple-element.57), channel_id=1, source_target_pairs={{0,2},{2,0},{4,6},{6,4},{8,10},{10,8},{12,14},{14,12},{1,3},{3,1},... | collective-permute-start | bytes 405512 | tf_op jit(solution)/shard_map/ppermute | solution.py:397
  34.7 8.4 %collective-permute-start.8 = (f32[33,8,128]{2,1,0:T(8,128)S(1)}, f32[33,8,128]{2,1,0:T(8,128)S(1)}, u32[]{:S(2)}, u32[]{:S(2)}) collective-permute-start(f32[33,8,128]{2,1,0:T(8,128)S(1)} %get-tuple-element.59), channel_id=1, source_target_pairs={{2,4},{4,2},{6,8},{8,6},{10,12},{12,10},{3,5},{5,3},{7,9},{9,7},{1... | collective-permute-start | bytes 405512 | tf_op jit(solution)/shard_map/ppermute | solution.py:400
  38.3 8.5 %collective-permute-start.9 = (f32[33,8,128]{2,1,0:T(8,128)S(1)}, f32[33,8,128]{2,1,0:T(8,128)S(1)}, u32[]{:S(2)}, u32[]{:S(2)}) collective-permute-start(f32[33,8,128]{2,1,0:T(8,128)S(1)} %get-tuple-element.61), channel_id=1, source_target_pairs={{0,2},{2,0},{4,6},{6,4},{8,10},{10,8},{12,14},{14,12},{1,3},{3,1},... | collective-permute-start | bytes 405512 | tf_op jit(solution)/shard_map/ppermute | solution.py:397
  43.8 9.2 %collective-permute-start.10 = (f32[33,8,128]{2,1,0:T(8,128)S(1)}, f32[33,8,128]{2,1,0:T(8,128)S(1)}, u32[]{:S(2)}, u32[]{:S(2)}) collective-permute-start(f32[33,8,128]{2,1,0:T(8,128)S(1)} %get-tuple-element.63), channel_id=1, source_target_pairs={{2,4},{4,2},{6,8},{8,6},{10,12},{12,10},{3,5},{5,3},{7,9},{9,7},{1... | collective-permute-start | bytes 405512 | tf_op jit(solution)/shard_map/ppermute | solution.py:400
  47.4 8.3 %collective-permute-start.11 = (f32[33,8,128]{2,1,0:T(8,128)S(1)}, f32[33,8,128]{2,1,0:T(8,128)S(1)}, u32[]{:S(2)}, u32[]{:S(2)}) collective-permute-start(f32[33,8,128]{2,1,0:T(8,128)S(1)} %get-tuple-element.65), channel_id=1, source_target_pairs={{0,2},{2,0},{4,6},{6,4},{8,10},{10,8},{12,14},{14,12},{1,3},{3,1},... | collective-permute-start | bytes 405512 | tf_op jit(solution)/shard_map/ppermute | solution.py:397
  53.7 8.3 %collective-permute-start.12 = (f32[33,8,128]{2,1,0:T(8,128)S(1)}, f32[33,8,128]{2,1,0:T(8,128)S(1)}, u32[]{:S(2)}, u32[]{:S(2)}) collective-permute-start(f32[33,8,128]{2,1,0:T(8,128)S(1)} %get-tuple-element.67), channel_id=1, source_target_pairs={{2,4},{4,2},{6,8},{8,6},{10,12},{12,10},{3,5},{5,3},{7,9},{9,7},{1... | collective-permute-start | bytes 405512 | tf_op jit(solution)/shard_map/ppermute | solution.py:400
  56.5 12.0 %collective-permute-start.13 = (f32[33,8,128]{2,1,0:T(8,128)S(1)}, f32[33,8,128]{2,1,0:T(8,128)S(1)}, u32[]{:S(2)}, u32[]{:S(2)}) collective-permute-start(f32[33,8,128]{2,1,0:T(8,128)S(1)} %get-tuple-element.69), channel_id=1, source_target_pairs={{0,2},{2,0},{4,6},{6,4},{8,10},{10,8},{12,14},{14,12},{1,3},{3,1},... | collective-permute-start | bytes 405512 | tf_op jit(solution)/shard_map/ppermute | solution.py:397
  62.7 7.8 %collective-permute-start.14 = (f32[33,8,128]{2,1,0:T(8,128)S(1)}, f32[33,8,128]{2,1,0:T(8,128)S(1)}, u32[]{:S(2)}, u32[]{:S(2)}) collective-permute-start(f32[33,8,128]{2,1,0:T(8,128)S(1)} %get-tuple-element.70), channel_id=1, source_target_pairs={{2,4},{4,2},{6,8},{8,6},{10,12},{12,10},{3,5},{5,3},{7,9},{9,7},{1... | collective-permute-start | bytes 405512 | tf_op jit(solution)/shard_map/ppermute | solution.py:400

commit v5 on v3

--- a/solution.py
+++ b/solution.py
@@ -63,6 +63,23 @@
 
 def sub(row):
     return pl.ds(row * SUBS, SUBS)
+
+
+def upside_down():
+    return 1 - lax.axis_index("row") % 2
+
+
+def place(row, flip):
+    return row + flip * (SUBS - 1 - 2 * row)
+
+
+def placed(row, flip):
+    at = place(row, flip) * SUBS
+    return pl.ds(at if isinstance(at, int) else pl.multiple_of(at, SUBS), SUBS)
+
+
+def tilt_sign():
+    return 1.0 - 2.0 * upside_down().astype(jnp.float32)
 
 
 def tile_columns(tile):
@@ -90,22 +107,25 @@
         copy.wait()
 
 
-def combine(kappa, across, along, skew, coupling):
+def combine(kappa, across, along, skew, coupling, sign):
     scale = 4.0 / (upper_edge - lower_edge)
     shift = 2.0 * (upper_edge + lower_edge) / (upper_edge - lower_edge)
     return (
         scale * (kappa + 2.0 * (across + along)) - shift,
         -scale * across,
         -scale * along,
-        -0.5 * scale * skew,
+        (-0.5 * scale * sign) * skew,
         scale * coupling,
     )
 
 
-def prep_kernel(window_ref, seen_ref, expanded_ref, top_ref, bottom_ref, eight, rest):
+def prep_kernel(window_ref, seen_ref, expanded_ref, near_ref, far_ref, eight, rest, observed):
     tiles = expanded_ref.shape[1]
     chunk = chunk_of(tiles)
+    flip = upside_down()
+    sign = tilt_sign()
     rest[...] = jnp.zeros_like(rest)
+    observed[...] = jnp.zeros_like(observed)
 
     def body(step, carry):
         for k in range(chunk):
@@ -113,29 +133,34 @@
             cols = tile_columns(tile)
             raw = [window_ref[channel, :, cols] for channel in range(9)]
             for c in range(2):
-                values = combine(raw[c], raw[2 + c], raw[4 + c], raw[6 + c], raw[8])
+                values = combine(raw[c], raw[2 + c], raw[4 + c], raw[6 + c], raw[8], sign)
                 for kind, value in enumerate(values):
                     for probe in range(4):
                         expanded_ref[kind, tile, pl.ds(4 * c + probe, SUBS, stride=SUBS), :] = value
             for channel in range(8):
                 eight[tile, pl.ds(channel, SUBS, stride=SUBS), :] = raw[channel]
-            top_ref[tile] = eight[tile, sub(0), :]
-            bottom_ref[tile] = eight[tile, sub(SUBS - 1), :]
         return carry
 
     lax.fori_loop(0, tiles // chunk, body, 0)
     for tile in range(tiles):
         cols = pl.ds(tile * LANES, LANES)
-        for slot, row in enumerate((window_ref[8, :, cols], seen_ref[0, :, cols], seen_ref[1, :, cols])):
-            rest[tile // 2, pl.ds(4 * (tile % 2) + slot, SUBS, stride=SUBS), :] = row
-    for pair in range(rest.shape[0]):
-        top_ref[tiles + pair] = rest[pair, sub(0), :]
-        bottom_ref[tiles + pair] = rest[pair, sub(SUBS - 1), :]
-
-
-def layout_kernel(own_ref, other_ref, more_top_ref, more_bottom_ref, z_ref, top_ref, bottom_ref):
+        rest[tile // 8, pl.ds(tile % 8, SUBS, stride=SUBS), :] = window_ref[8, :, cols]
+        for c in range(2):
+            observed[tile // 4, pl.ds(2 * (tile % 4) + c, SUBS, stride=SUBS), :] = seen_ref[c, :, cols]
+    first, last = placed(0, flip), placed(SUBS - 1, flip)
+    for tile in range(tiles):
+        far_ref[tile] = eight[tile, last, :]
+    for index in range(rest.shape[0]):
+        far_ref[tiles + index] = rest[index, last, :]
+    for index in range(observed.shape[0]):
+        near_ref[index] = observed[index, first, :]
+        far_ref[tiles + rest.shape[0] + index] = observed[index, last, :]
+
+
+def layout_kernel(own_ref, other_ref, more_near_ref, more_far_ref, z_ref, near_ref, far_ref, natural):
     tiles = z_ref.shape[0]
     chunk = chunk_of(tiles)
+    flip = upside_down()
 
     def body(step, carry):
         for k in range(chunk):
@@ -143,36 +168,43 @@
             cols = tile_columns(tile)
             for c in range(2):
                 for probe in range(2):
-                    z_ref[tile, pl.ds(4 * c + probe, SUBS, stride=SUBS), :] = own_ref[probe, c, :, cols]
-                    z_ref[tile, pl.ds(4 * c + 2 + probe, SUBS, stride=SUBS), :] = other_ref[probe, c, :, cols]
+                    natural[tile, pl.ds(4 * c + probe, SUBS, stride=SUBS), :] = own_ref[probe, c, :, cols]
+                    natural[tile, pl.ds(4 * c + 2 + probe, SUBS, stride=SUBS), :] = other_ref[probe, c, :, cols]
+        for k in range(chunk):
+            tile = step * chunk + k
+            for row in range(SUBS):
+                value = natural[tile, placed(row, flip), :]
+                z_ref[tile, sub(row), :] = value
+                if row == 0:
+                    near_ref[tile] = value
+                if row >= SUBS - 2:
+                    far_ref[2 * tile + row - SUBS + 2] = value
         return carry
 
     lax.fori_loop(0, tiles // chunk, body, 0)
-    for tile in range(tiles):
-        for row in range(2):
-            top_ref[2 * tile + row] = z_ref[tile, sub(row), :]
-            bottom_ref[2 * tile + row] = z_ref[tile, sub(SUBS - 2 + row), :]
-    for index in range(more_top_ref.shape[0]):
-        top_ref[2 * tiles + index] = more_top_ref[index]
-        bottom_ref[2 * tiles + index] = more_bottom_ref[index]
+    for index in range(more_near_ref.shape[0]):
+        near_ref[tiles + index] = more_near_ref[index]
+    for index in range(more_far_ref.shape[0]):
+        far_ref[2 * tiles + index] = more_far_ref[index]
 
 
 def rim(halo_ref, rim_ref, tiles):
     chunk = chunk_of(tiles)
-
-    def spread(ref, index, row):
-        return jnp.broadcast_to(ref[index, pl.ds(row, 1), :], (SUBS, LANES))
+    sign = tilt_sign()
+
+    def spread(index, row):
+        return jnp.broadcast_to(halo_ref[index, pl.ds(row, 1), :], (SUBS, LANES))
 
     def body(step, carry):
         low = lax.broadcasted_iota(jnp.int32, (SUBS, LANES), 0) < 4
         for k in range(chunk):
             tile = step * chunk + k
             pairs = [
-                jnp.where(low, spread(halo_ref, 2 * tiles + tile, 2 * kind), spread(halo_ref, 2 * tiles + tile, 2 * kind + 1))
+                jnp.where(low, spread(2 * tiles + tile, 2 * kind), spread(2 * tiles + tile, 2 * kind + 1))
                 for kind in range(4)
             ]
-            coupling = spread(halo_ref, 3 * tiles + tile // 2, 4 * (tile % 2))
-            for kind, value in enumerate(combine(*pairs, coupling)):
+            coupling = spread(3 * tiles + tile // 8, tile % 8)
+            for kind, value in enumerate(combine(*pairs, coupling, sign)):
                 rim_ref[kind, tile] = value
         return carry
 
@@ -228,19 +260,20 @@
     if first_round:
         z_ref, expanded_ref, once_ref, twice_ref = refs
     else:
-        z_ref, expanded_ref, top_ref, inner_ref, bottom_ref, older_ref, once_ref, twice_ref = refs
+        z_ref, expanded_ref, top_ref, second_ref, inner_ref, bottom_ref, older_ref, once_ref, twice_ref = refs
+    flip = upside_down()
 
     def now(row, tile):
         if first_round:
             return z_ref[tile, sub(row), :]
         if row < 2:
-            return top_ref[2 * tile + row]
+            return (top_ref, second_ref)[row][tile]
         if row < 6:
             return inner_ref[tile, sub(row - 2), :]
         return bottom_ref[2 * tile + row - 6]
 
     def factor(kind, row, tile):
-        return expanded_ref[kind, tile, sub(row), :]
+        return expanded_ref[kind, tile, placed(row, flip), :]
 
     def z_row(row, tile):
         return z_ref[tile, sub(row), :]
@@ -259,58 +292,110 @@
     sweep(tiles, 2, 4, once, factor, z_row, None if first_round else now, steps[1], store_twice)
 
 
-def edge_kernel(upper, steps, tiles, first_round, last_round, *refs):
+def near_once_kernel(constants, tiles, first_round, *refs):
+    if first_round:
+        halo_ref, z_ref, expanded_ref, out_ref = refs
+    else:
+        halo_ref, z_ref, expanded_ref, top_ref, second_ref, older_ref, out_ref = refs
+    flip = upside_down()
+
+    def now(row, tile):
+        if row < 0:
+            return halo_ref[tile]
+        if first_round:
+            return z_ref[tile, sub(row), :]
+        return (top_ref, second_ref)[row][tile]
+
+    def factor(kind, row, tile):
+        return expanded_ref[kind, tile, placed(row, flip), :]
+
+    def store(row, tile, value):
+        out_ref[tile] = value
+
+    older = None if first_round else (lambda row, tile: older_ref[tile])
+    sweep(tiles, 0, 1, now, factor, lambda row, tile: z_ref[tile, sub(row), :], older, constants, store)
+
+
+def near_twice_kernel(constants, tiles, first_round, *refs):
+    if first_round:
+        halo_ref, z_ref, expanded_ref, once_ref, inner_ref, out_ref, second_out_ref = refs
+    else:
+        halo_ref, z_ref, expanded_ref, once_ref, inner_ref, top_ref, second_ref, out_ref, second_out_ref = refs
+    flip = upside_down()
+
+    def once(row, tile):
+        if row < 0:
+            return halo_ref[tile]
+        if row == 0:
+            return once_ref[tile]
+        return inner_ref[tile, sub(row - 1), :]
+
+    def factor(kind, row, tile):
+        return expanded_ref[kind, tile, placed(row, flip), :]
+
+    def store(row, tile, value):
+        (out_ref, second_out_ref)[row][tile] = value
+
+    older = None if first_round else (lambda row, tile: (top_ref, second_ref)[row][tile])
+    sweep(tiles, 0, 2, once, factor, lambda row, tile: z_ref[tile, sub(row), :], older, constants, store)
+
+
+def far_kernel(steps, tiles, first_round, last_round, *refs):
     halo_ref, z_halo_ref, z_ref, expanded_ref, inner_ref = refs[:5]
     refs = refs[5:]
     if first_round:
         once_ref, twice_ref, rim_ref = refs[:3]
         rim(halo_ref, rim_ref, tiles)
     else:
-        rim_ref, top_ref, older_ref, once_ref, twice_ref = refs[:5]
+        rim_ref, bottom_ref, older_ref, once_ref, twice_ref = refs[:5]
     row_ref = refs[-1]
-    base = 0 if upper else 6
-    low = -1 if upper else 7
+    flip = upside_down()
 
     def now(row, tile):
-        if row < 0 or row > 7:
-            return halo_ref[2 * tile + (row + 2 if upper else row - 8)]
+        if row > 7:
+            return halo_ref[2 * tile + 9 - row]
         if first_round:
             return z_ref[tile, sub(row), :]
-        return top_ref[2 * tile + row - base]
+        return bottom_ref[2 * tile + row - 6]
 
     def factor(kind, row, tile):
-        if row < 0 or row > 7:
+        if row > 7:
             return rim_ref[kind, tile]
-        return expanded_ref[kind, tile, sub(row), :]
+        return expanded_ref[kind, tile, placed(row, flip), :]
 
     def z_row(row, tile):
-        if row < 0 or row > 7:
-            return z_halo_ref[2 * tile + (1 if upper else 0)]
+        if row > 7:
+            return z_halo_ref[2 * tile + 1]
         return z_ref[tile, sub(row), :]
 
     def once(row, tile):
-        if 1 <= row <= 6:
+        if row <= 6:
             return inner_ref[tile, sub(row - 1), :]
-        return once_ref[tile, sub(row - low), :]
+        return once_ref[tile, sub(row - 7), :]
 
     def store_once(row, tile, value):
-        once_ref[tile, sub(row - low), :] = value
+        once_ref[tile, sub(row - 7), :] = value
 
     def store_twice(row, tile, value):
-        twice_ref[2 * tile + row - base] = value
-        if last_round and row == (0 if upper else 7):
+        twice_ref[2 * tile + row - 6] = value
+        if last_round and row == 7:
             row_ref[tile] = value
 
-    older = None if first_round else (lambda row, tile: older_ref[tile, sub(row - low), :])
-    sweep(tiles, low, 2, now, factor, z_row, older, steps[0], store_once)
-    sweep(tiles, base, 2, once, factor, z_row, None if first_round else now, steps[1], store_twice)
-
-
-def data_kernel(tiles, seen_ref, up_ref, down_ref, out_ref):
+    older = None if first_round else (lambda row, tile: older_ref[tile, sub(row - 7), :])
+    sweep(tiles, 7, 2, now, factor, z_row, older, steps[0], store_once)
+    sweep(tiles, 6, 2, once, factor, z_row, None if first_round else now, steps[1], store_twice)
+
+
+def data_kernel(tiles, seen_ref, near_ref, far_ref, out_ref):
     chunk = chunk_of(tiles)
 
-    def halo(ref, c, tile):
-        row = ref[3 * tiles + tile // 2, pl.ds(4 * (tile % 2) + 1 + c, 1), :]
+    flip = upside_down()
+    far_base = far_ref.shape[0] - (near_ref.shape[0] - tiles)
+
+    def halo(above, c, tile):
+        at = pl.ds(2 * (tile % 4) + c, 1)
+        near, far = near_ref[tiles + tile // 4, at, :], far_ref[far_base + tile // 4, at, :]
+        row = jnp.where(flip == 1, far, near) if above else jnp.where(flip == 1, near, far)
         return jnp.broadcast_to(row, (SUBS, LANES))
 
     def body(step, carry):
@@ -320,8 +405,8 @@
         kept = [[], []]
         for c in range(2):
             values = window_tiles(lambda tile: seen_ref[c, :, tile_columns(tile)], first, chunk, tiles)
-            ups = window_tiles(lambda tile: halo(up_ref, c, tile), first, chunk, tiles)
-            downs = window_tiles(lambda tile: halo(down_ref, c, tile), first, chunk, tiles)
+            ups = window_tiles(lambda tile: halo(True, c, tile), first, chunk, tiles)
+            downs = window_tiles(lambda tile: halo(False, c, tile), first, chunk, tiles)
             aboves = [jnp.where(row == 0, u, pltpu.roll(v, 1, 0)) for u, v in zip(ups, values)]
             belows = [jnp.where(row == SUBS - 1, d, pltpu.roll(v, SUBS - 1, 0)) for d, v in zip(downs, values)]
             tilts = [b - a for a, b in zip(aboves, belows)]
@@ -343,19 +428,19 @@
     lax.fori_loop(0, tiles // chunk, body, 0)
 
 
-def gradient_kernel(tiles, factor, z_ref, top_ref, inner_ref, bottom_ref, data_ref, out_ref, products):
+def gradient_kernel(tiles, factor, z_ref, top_ref, second_ref, inner_ref, bottom_ref, data_ref, out_ref, products):
     kept = out_ref.shape[2] // LANES
     offset = lax.axis_index("probe") * (tiles - kept)
     count = products.shape[0]
 
     def load(row):
         if row < 2:
-            return lambda tile: top_ref[2 * tile + row]
+            return lambda tile: (top_ref, second_ref)[row][tile]
         if row < 6:
             return lambda tile: inner_ref[tile, sub(row - 2), :]
         return lambda tile: bottom_ref[2 * tile + row - 6]
 
-    def body(step, carry):
+    def body(flip, step, carry):
         edges = masks()
         for k in range(count):
             index = step * count + k
@@ -371,6 +456,7 @@
             for row in range(SUBS):
                 left = factor * z_ref[tile, sub(row), :]
                 value = values[row]
+                at = placed(row, flip)
                 twice = 2.0 * value
                 if row == 0:
                     along, skew = values[1], slopes[1]
@@ -378,11 +464,11 @@
                     along, skew = values[row - 1], -slopes[row - 1]
                 else:
                     along, skew = values[row - 1] + values[row + 1], slopes[row + 1] - slopes[row - 1]
-                products[k, 0, sub(row), :] = left * value
-                products[k, 1, sub(row), :] = left * (twice - sums[row])
-                products[k, 2, sub(row), :] = left * (twice - along)
-                products[k, 3, sub(row), :] = (-0.5 * left) * skew
-                products[k, 4, sub(row), :] = left * pltpu.roll(value, 4, 0)
+                products[k, 0, at, :] = left * value
+                products[k, 1, at, :] = left * (twice - sums[row])
+                products[k, 2, at, :] = left * (twice - along)
+                products[k, 3, at, :] = ((flip - 0.5) * left) * skew
+                products[k, 4, at, :] = left * pltpu.roll(value, 4, 0)
         for k in range(count):
             index = step * count + k
             tile = index + offset
@@ -397,7 +483,11 @@
                     out_ref[8, :, cols] = (sums[0] + sums[1]) + data_ref[tile, 8]
         return carry
 
-    lax.fori_loop(0, kept // count, body, 0)
+    for flip in range(2):
+
+        @pl.when(upside_down() == flip)
+        def _():
+            lax.fori_loop(0, kept // count, functools.partial(body, flip), 0)
 
 
 def finish_kernel(tiles, factor, part_ref, z_ref, up_ref, down_ref, out_ref, fixed, sem):
@@ -410,21 +500,23 @@
     ]
     for copy in early:
         copy.start()
+    flip = upside_down()
+    sign = 0.5 * tilt_sign()
 
     def body(step, carry):
         edges = masks()
-        row = lax.broadcasted_iota(jnp.int32, (SUBS, LANES), 0)
+        row = place(lax.broadcasted_iota(jnp.int32, (SUBS, LANES), 0), flip)
         for k in range(count):
             index = step * count + k
             tile = index + offset
             cols = tile_columns(index)
             adds = []
-            for ref, z_row, sign in ((up_ref, 0, 0.5), (down_ref, SUBS - 1, -0.5)):
+            for ref, z_row, slant in ((up_ref, 0, sign), (down_ref, SUBS - 1, -sign)):
                 before, here, after = window_tiles(lambda at: ref[at], tile, 1, tiles)
                 left, right = beside(before, here, after, edges)
                 z = factor * z_ref[tile, sub(z_row), :]
                 pair = []
-                for term in (-z * here, (sign * z) * (right - left)):
+                for term in (-z * here, (slant * z) * (right - left)):
                     term = term + pltpu.roll(term, 1, 0)
                     pair.append(term + pltpu.roll(term, 2, 0))
                 adds.append(pair)
@@ -455,14 +547,14 @@
     tiles = width // LANES
     kept = share // LANES
     rows = lax.axis_size("row")
-    down_pairs = [(i, i + 1) for i in range(rows - 1)]
-    up_pairs = [(i + 1, i) for i in range(rows - 1)]
-
-    def to_next(edge):
-        return lax.ppermute(edge, "row", down_pairs)
-
-    def to_previous(edge):
-        return lax.ppermute(edge, "row", up_pairs)
+    near_pairs = [pair for i in range(0, rows - 1, 2) for pair in ((i, i + 1), (i + 1, i))]
+    far_pairs = [pair for i in range(1, rows - 1, 2) for pair in ((i, i + 1), (i + 1, i))]
+
+    def near(edge):
+        return lax.ppermute(edge, "row", near_pairs)
+
+    def far(edge):
+        return lax.ppermute(edge, "row", far_pairs)
 
     def call(kernel, name, vregs, operands, outs, scratch=(), in_specs=None, out_specs=None):
         return pl.pallas_call(
@@ -494,30 +586,47 @@
         [pl.BlockSpec(memory_space=pltpu.HBM)] * 3,
     )
     other = lax.ppermute(theirs, "probe", [(0, 1), (1, 0)])
-    pairs = -(-tiles // 2)
-    more = (tiles + pairs, SUBS, LANES)
-    expanded, more_top, more_bottom = call(
+    eights, fours = -(-tiles // 8), -(-tiles // 4)
+    expanded, more_near, more_far = call(
         prep_kernel,
         "prep",
         5 * 8 * tiles,
         (window, seen),
-        [pltpu.VMEM((5, tiles, SUBS * SUBS, LANES), f32), pltpu.VMEM(more, f32), pltpu.VMEM(more, f32)],
-        [pltpu.VMEM((tiles, SUBS * SUBS, LANES), f32), pltpu.VMEM((pairs, SUBS * SUBS, LANES), f32)],
+        [
+            pltpu.VMEM((5, tiles, SUBS * SUBS, LANES), f32),
+            pltpu.VMEM((fours, SUBS, LANES), f32),
+            pltpu.VMEM((tiles + eights + fours, SUBS, LANES), f32),
+        ],
+        [pltpu.VMEM((count, SUBS * SUBS, LANES), f32) for count in (tiles, eights, fours)],
     )
     own, expanded = lax.optimization_barrier((own, expanded))
-    message = (2 * tiles + more[0], SUBS, LANES)
     z, top, bottom = call(
         layout_kernel,
         "layout",
         8 * tiles,
-        (own, other, more_top, more_bottom),
-        [pltpu.VMEM((tiles, SUBS * SUBS, LANES), f32), pltpu.VMEM(message, f32), pltpu.VMEM(message, f32)],
+        (own, other, more_near, more_far),
+        [
+            pltpu.VMEM((tiles, SUBS * SUBS, LANES), f32),
+            pltpu.VMEM((tiles + fours, SUBS, LANES), f32),
+            pltpu.VMEM((3 * tiles + eights + fours, SUBS, LANES), f32),
+        ],
+        [pltpu.VMEM((tiles, SUBS * SUBS, LANES), f32)],
     )
 
-    first_up, first_down = to_next(bottom), to_previous(top)
+    def rows_of(count):
+        return pltpu.VMEM((tiles, count * SUBS, LANES), f32)
+
+    first_up, first_down = near(top), far(bottom)
     up, down = first_up, first_down
+    data = call(
+        functools.partial(data_kernel, tiles),
+        "data",
+        9 * tiles,
+        (seen, first_up, first_down),
+        pltpu.VMEM((tiles, 9, SUBS, LANES), f32),
+    )
     rounds = CHEB // 2
-    inner = once = rims = None
+    second = inner = once = rim_factors = None
     for index in range(rounds):
         first_round, last_round = index == 0, index == rounds - 1
         high = CHEB - 1 - 2 * index
@@ -525,60 +634,55 @@
             steps = ((weights[high], weights[CHEB]), (weights[high - 1] - weights[CHEB], 1.0))
         else:
             steps = ((weights[high], 1.0), (weights[high - 1], 0.5 if last_round else 1.0))
-        operands = [z, expanded]
-        if not first_round:
-            operands += [top, inner, bottom, once[1]]
+        if index == 1:
+            inner, data = lax.optimization_barrier((inner, data))
+        near_once = call(
+            functools.partial(near_once_kernel, steps[0], tiles, first_round),
+            "near_once",
+            tiles,
+            [up, z, expanded] + ([] if first_round else [top, second, once[0]]),
+            rows_of(1),
+        )
+        up = near(near_once)
         inner_once, inner_twice = call(
             functools.partial(middle_kernel, steps, tiles, first_round),
             "middle",
             10 * tiles,
-            operands,
-            [pltpu.VMEM((tiles, 6 * SUBS, LANES), f32), pltpu.VMEM((tiles, 4 * SUBS, LANES), f32)],
+            [z, expanded] + ([] if first_round else [top, second, inner, bottom, once[1]]),
+            [rows_of(6), rows_of(4)],
         )
-        results = []
-        for upper in (True, False):
-            halo, z_halo = (up, first_up) if upper else (down, first_down)
-            operands = [halo, z_halo, z, expanded, inner_once]
-            outs = [pltpu.VMEM((tiles, 2 * SUBS, LANES), f32), pltpu.VMEM((2 * tiles, SUBS, LANES), f32)]
-            if first_round:
-                outs.append(pltpu.VMEM((5, tiles, SUBS, LANES), f32))
-            else:
-                operands += [rims[0 if upper else 1], top if upper else bottom, once[0 if upper else 2]]
-            if last_round:
-                outs.append(pltpu.VMEM((tiles, SUBS, LANES), f32))
-            results.append(
-                call(
-                    functools.partial(edge_kernel, upper, steps, tiles, first_round, last_round),
-                    "upper" if upper else "lower",
-                    4 * tiles,
-                    operands,
-                    outs,
-                )
-            )
-        over, under = results
-        once = (over[0], inner_once, under[0])
-        top, inner, bottom = over[1], inner_twice, under[1]
+        outs = [rows_of(2), pltpu.VMEM((2 * tiles, SUBS, LANES), f32)]
         if first_round:
-            rims = (over[2], under[2])
+            outs.append(pltpu.VMEM((5, tiles, SUBS, LANES), f32))
         if last_round:
-            down, up = to_previous(over[-1]), to_next(under[-1])
-        else:
-            down, up = to_previous(top), to_next(bottom)
-
-    data = call(
-        functools.partial(data_kernel, tiles),
-        "data",
-        9 * tiles,
-        (seen, first_up, first_down),
-        pltpu.VMEM((tiles, 9, SUBS, LANES), f32),
-    )
+            outs.append(rows_of(1))
+        under = call(
+            functools.partial(far_kernel, steps, tiles, first_round, last_round),
+            "far",
+            4 * tiles,
+            [down, first_down, z, expanded, inner_once] + ([] if first_round else [rim_factors, bottom, once[2]]),
+            outs,
+        )
+        over = call(
+            functools.partial(near_twice_kernel, steps[1], tiles, first_round),
+            "near_twice",
+            2 * tiles,
+            [up, z, expanded, near_once, inner_once] + ([] if first_round else [top, second]),
+            [rows_of(1), rows_of(1)],
+        )
+        once = (near_once, inner_once, under[0])
+        top, second, inner, bottom = over[0], over[1], inner_twice, under[1]
+        if first_round:
+            rim_factors = under[2]
+        up, down = near(top), far(under[-1] if last_round else bottom)
+
     factor = 0.5 / (probes.shape[0] * lax.axis_size("probe"))
     count = max(n for n in range(1, 5) if kept % n == 0)
     part = call(
         functools.partial(gradient_kernel, tiles, factor),
         "gradient",
         24 * tiles,
-        (z, top, inner, bottom, data),
+        (z, top, second, inner, bottom, data),
         pltpu.VMEM((9, SUBS, share), f32),
         [pltpu.VMEM((count, 5, SUBS * SUBS, LANES), f32)],
     )

time: 69.6 us -> 74.9 us (1.076)
  the two profiles are of different devices: /device:TPU:0 before, /device:TPU:8 now
where the time goes in v5:
time: 74.9 us; the launch traced here: 74.7 us
  waiting for transfers between devices  35.8 us (48%)
  starting transfers between devices  20.2 us (27%)
  Pallas kernels  18.6 us (25%)
    ppermute x7, waiting for transfers between devices, near(): return lax.ppermute(edge, 'row', near_pairs)  30.6 us
    pallas_call x18, Pallas kernels, call(): pl.pallas_call(kernel, out_shape=outs, in_specs=in_specs or [vmem_spec()]...  18.6 us
    ppermute x7, starting transfers between devices, near(): return lax.ppermute(edge, 'row', near_pairs)  11 us
    ppermute x4, starting transfers between devices, far(): return lax.ppermute(edge, 'row', far_pairs)  9.2 us
    ppermute x4, waiting for transfers between devices, far(): return lax.ppermute(edge, 'row', far_pairs)  4.29 us
  transfers between devices with their start and end apart: 12, of which 8 were waited for; matrix products, arithmetic and copies ran while one was open for 0% of the time, Pallas kernels for 20%

profile of v5, /device:TPU:8, one launch (start us, length us, event | category | flops | bytes accessed | tf_op | source)
XLA Modules:
  0.0 74.7 jit_solution(8076478837723898722)
XLA Ops:
  0.0 1.7 %load.1 = (f32[2,2,8,4224]{3,2,1,0:T(8,128)S(1)}, f32[2,2,8,4224]{3,2,1,0:T(8,128)S(1)}, f32[2,8,4224]{2,1,0:T(8,128)S(1)}, f32[9,8,4224]{2,1,0:T(8,128)S(1)}) custom-call(f32[2,2,8,8192]{3,2,1,0:T(8,128)} %probes_ref.1, f32[2,8,8192]{2,1,0:T(8,128)} %observed_ref.1, f32[9,8,8192]{2,1,0:T(8,128)} %coefficients_ref.1), custom_call_target="tpu_custom_call" | custom-call | flops 2048000 | bytes 1638400 | tf_op jit(solution)/shard_map/load/pallas_call | solution.py:560
  1.7 0.1 collective-permute-start
  1.8 1.1 %prep.1 = (f32[5,33,64,128]{3,2,1,0:T(8,128)S(1)}, f32[9,8,128]{2,1,0:T(8,128)S(1)}, f32[47,8,128]{2,1,0:T(8,128)S(1)}) custom-call(f32[9,8,4224]{2,1,0:T(8,128)S(1)} %get-tuple-element.39.window_ref, f32[2,8,4224]{2,1,0:T(8,128)S(1)} %get-tuple-element.40.seen_ref), custom_call_target="tpu_custom_call" | custom-call | flops 27033600 | bytes 21626880 | tf_op jit(solution)/shard_map/prep/pallas_call | solution.py:560
  2.8 0.8 %collective-permute-done.other_ref = f32[2,2,8,4224]{3,2,1,0:T(8,128)S(1)} collective-permute-done((f32[2,2,8,4224]{3,2,1,0:T(8,128)S(1)}, f32[2,2,8,4224]{3,2,1,0:T(8,128)S(1)}, u32[]{:S(2)}, u32[]{:S(2)}) %collective-permute-start) | collective-permute-done | bytes 540704 | tf_op jit(solution)/shard_map/ppermute | solution.py:588
  3.7 0.3 layout.1
  4.0 3.3 %collective-permute-start.5 = (f32[113,8,128]{2,1,0:T(8,128)S(1)}, f32[113,8,128]{2,1,0:T(8,128)S(1)}, u32[]{:S(2)}, u32[]{:S(2)}) collective-permute-start(f32[113,8,128]{2,1,0:T(8,128)S(1)} %get-tuple-element.53), channel_id=1, source_target_pairs={{2,4},{4,2},{6,8},{8,6},{10,12},{12,10},{3,5},{5,3},{7,9},{9,7},{1... | collective-permute-start | bytes 1388552 | tf_op jit(solution)/shard_map/ppermute | solution.py:557
  7.3 1.7 %collective-permute-start.1 = (f32[42,8,128]{2,1,0:T(8,128)S(1)}, f32[42,8,128]{2,1,0:T(8,128)S(1)}, u32[]{:S(2)}, u32[]{:S(2)}) collective-permute-start(f32[42,8,128]{2,1,0:T(8,128)S(1)} %get-tuple-element.47), channel_id=1, source_target_pairs={{0,2},{2,0},{4,6},{6,4},{8,10},{10,8},{12,14},{14,12},{1,3},{3,1},... | collective-permute-start | bytes 516104 | tf_op jit(solution)/shard_map/ppermute | solution.py:554
  9.0 14.1 %collective-permute-done.1.refs_0_.near_ref = f32[42,8,128]{2,1,0:T(8,128)S(1)} collective-permute-done((f32[42,8,128]{2,1,0:T(8,128)S(1)}, f32[42,8,128]{2,1,0:T(8,128)S(1)}, u32[]{:S(2)}, u32[]{:S(2)}) %collective-permute-start.1) | collective-permute-done | bytes 172064 | tf_op jit(solution)/shard_map/ppermute | solution.py:554
  23.1 0.4 near_once.3.refs_3_.refs_5_
  23.6 1.6 %collective-permute-start.2 = (f32[33,8,128]{2,1,0:T(8,128)S(1)}, f32[33,8,128]{2,1,0:T(8,128)S(1)}, u32[]{:S(2)}, u32[]{:S(2)}) collective-permute-start(f32[33,8,128]{2,1,0:T(8,128)S(1)} %near_once.3.refs_3_.refs_5_), channel_id=1, source_target_pairs={{0,2},{2,0},{4,6},{6,4},{8,10},{10,8},{12,14},{14,12},{1,3},{3,1},... | collective-permute-start | bytes 405512 | tf_op jit(solution)/shard_map/ppermute | solution.py:554
  25.1 1.5 %middle.3 = (f32[33,48,128]{2,1,0:T(8,128)S(1)}, f32[33,32,128]{2,1,0:T(8,128)S(1)}) custom-call(f32[33,64,128]{2,1,0:T(8,128)S(1)} %get-tuple-element.46.refs_1_.refs_0_.refs_2_.z_ref, f32[5,33,64,128]{3,2,1,0:T(8,128)S(1)} %get-tuple-element.48.refs_2_.refs_1_.refs_3_), custom_call_target="tpu_custom_call" | custom-call | flops 6758400 | bytes 5406720 | tf_op jit(solution)/shard_map/middle/pallas_call | solution.py:560
  26.7 2.5 %collective-permute-done.2.refs_0_ = f32[33,8,128]{2,1,0:T(8,128)S(1)} collective-permute-done((f32[33,8,128]{2,1,0:T(8,128)S(1)}, f32[33,8,128]{2,1,0:T(8,128)S(1)}, u32[]{:S(2)}, u32[]{:S(2)}) %collective-permute-start.2) | collective-permute-done | bytes 135200 | tf_op jit(solution)/shard_map/ppermute | solution.py:554
  29.2 0.5 near_twice.3
  29.7 1.6 %collective-permute-start.3 = (f32[33,8,128]{2,1,0:T(8,128)S(1)}, f32[33,8,128]{2,1,0:T(8,128)S(1)}, u32[]{:S(2)}, u32[]{:S(2)}) collective-permute-start(f32[33,8,128]{2,1,0:T(8,128)S(1)} %get-tuple-element.50.refs_3_.refs_2_.refs_5_), channel_id=1, source_target_pairs={{0,2},{2,0},{4,6},{6,4},{8,10},{10,8},{12,14},{14,12},{1,3},{3,1},... | collective-permute-start | bytes 405512 | tf_op jit(solution)/shard_map/ppermute | solution.py:554
  31.2 0.0 collective-permute-done.5.far_ref.refs_0_.refs_1_
  31.2 1.3 %far.3 = (f32[33,16,128]{2,1,0:T(8,128)S(1)}, f32[66,8,128]{2,1,0:T(8,128)S(1)}, f32[5,33,8,128]{3,2,1,0:T(8,128)S(1)}) custom-call(f32[113,8,128]{2,1,0:T(8,128)S(1)} %collective-permute-done.5.far_ref.refs_0_.refs_1_, f32[113,8,128]{2,1,0:T(8,128)S(1)} %collective-permute-done.5.far_ref.refs_0_.refs_1_, ...), custom_call_target="tpu_custom_call" | custom-call | flops 2703360 | bytes 2162688 | tf_op jit(solution)/shard_map/far/pallas_call | solution.py:560
  32.5 2.1 %collective-permute-start.8 = (f32[66,8,128]{2,1,0:T(8,128)S(1)}, f32[66,8,128]{2,1,0:T(8,128)S(1)}, u32[]{:S(2)}, u32[]{:S(2)}) collective-permute-start(f32[66,8,128]{2,1,0:T(8,128)S(1)} %get-tuple-element.55.refs_5_.refs_6_), channel_id=1, source_target_pairs={{2,4},{4,2},{6,8},{8,6},{10,12},{12,10},{3,5},{5,3},{7,9},{9,7},{1... | collective-permute-start | bytes 811016 | tf_op jit(solution)/shard_map/ppermute | solution.py:557
  34.6 0.2 collective-permute-done.3.refs_0_
  34.8 0.4 near_once.4.refs_3_.refs_5_
  35.2 2.8 %collective-permute-start.4 = (f32[33,8,128]{2,1,0:T(8,128)S(1)}, f32[33,8,128]{2,1,0:T(8,128)S(1)}, u32[]{:S(2)}, u32[]{:S(2)}) collective-permute-start(f32[33,8,128]{2,1,0:T(8,128)S(1)} %near_once.4.refs_3_.refs_5_), channel_id=1, source_target_pairs={{0,2},{2,0},{4,6},{6,4},{8,10},{10,8},{12,14},{14,12},{1,3},{3,1},... | collective-permute-start | bytes 405512 | tf_op jit(solution)/shard_map/ppermute | solution.py:554
  38.0 0.7 data.1.data_ref
  38.7 1.6 %middle.4 = (f32[33,48,128]{2,1,0:T(8,128)S(1)}, f32[33,32,128]{2,1,0:T(8,128)S(1)}) custom-call(f32[33,64,128]{2,1,0:T(8,128)S(1)} %get-tuple-element.46.refs_1_.refs_0_.refs_2_.z_ref, f32[5,33,64,128]{3,2,1,0:T(8,128)S(1)} %get-tuple-element.48.refs_2_.refs_1_.refs_3_, f32[33,8,128]{2,1,0:T(8,128)S(1)} %get-tuple-element.50.refs_3_.refs_2_.refs_5_, ...), custom_call_target="tpu_custom_call" | custom-call | flops 6758400 | bytes 5406720 | tf_op jit(solution)/shard_map/middle/pallas_call | solution.py:560
  40.3 5.1 %collective-permute-done.4.refs_0_ = f32[33,8,128]{2,1,0:T(8,128)S(1)} collective-permute-done((f32[33,8,128]{2,1,0:T(8,128)S(1)}, f32[33,8,128]{2,1,0:T(8,128)S(1)}, u32[]{:S(2)}, u32[]{:S(2)}) %collective-permute-start.4) | collective-permute-done | bytes 135200 | tf_op jit(solution)/shard_map/ppermute | solution.py:554
  45.5 0.5 near_twice.4
  46.0 0.6 collective-permute-start.6
  46.6 0.0 collective-permute-done.8.refs_0_
  46.6 1.1 %far.4 = (f32[33,16,128]{2,1,0:T(8,128)S(1)}, f32[66,8,128]{2,1,0:T(8,128)S(1)}) custom-call(f32[66,8,128]{2,1,0:T(8,128)S(1)} %collective-permute-done.8.refs_0_, f32[113,8,128]{2,1,0:T(8,128)S(1)} %collective-permute-done.5.far_ref.refs_0_.refs_1_, f32[33,64,128]{2,1,0:T(8,128)S(1)} %get-tuple-element.46.refs_1_.refs_0_.refs_2_.z_ref, ...), custom_call_target="tpu_custom_call" | custom-call | flops 2703360 | bytes 2162688 | tf_op jit(solution)/shard_map/far/pallas_call | solution.py:560
  47.7 1.9 %collective-permute-start.9 = (f32[66,8,128]{2,1,0:T(8,128)S(1)}, f32[66,8,128]{2,1,0:T(8,128)S(1)}, u32[]{:S(2)}, u32[]{:S(2)}) collective-permute-start(f32[66,8,128]{2,1,0:T(8,128)S(1)} %get-tuple-element.62.refs_5_.refs_6_), channel_id=1, source_target_pairs={{2,4},{4,2},{6,8},{8,6},{10,12},{12,10},{3,5},{5,3},{7,9},{9,7},{1... | collective-permute-start | bytes 811016 | tf_op jit(solution)/shard_map/ppermute | solution.py:557
  49.6 2.0 %collective-permute-done.6.refs_0_ = f32[33,8,128]{2,1,0:T(8,128)S(1)} collective-permute-done((f32[33,8,128]{2,1,0:T(8,128)S(1)}, f32[33,8,128]{2,1,0:T(8,128)S(1)}, u32[]{:S(2)}, u32[]{:S(2)}) %collective-permute-start.6) | collective-permute-done | bytes 135200 | tf_op jit(solution)/shard_map/ppermute | solution.py:554
  51.6 0.4 near_once.5.refs_3_
  52.0 1.2 %collective-permute-start.7 = (f32[33,8,128]{2,1,0:T(8,128)S(1)}, f32[33,8,128]{2,1,0:T(8,128)S(1)}, u32[]{:S(2)}, u32[]{:S(2)}) collective-permute-start(f32[33,8,128]{2,1,0:T(8,128)S(1)} %near_once.5.refs_3_), channel_id=1, source_target_pairs={{0,2},{2,0},{4,6},{6,4},{8,10},{10,8},{12,14},{14,12},{1,3},{3,1},... | collective-permute-start | bytes 405512 | tf_op jit(solution)/shard_map/ppermute | solution.py:554
  53.2 1.6 %middle.5 = (f32[33,48,128]{2,1,0:T(8,128)S(1)}, f32[33,32,128]{2,1,0:T(8,128)S(1)}) custom-call(f32[33,64,128]{2,1,0:T(8,128)S(1)} %get-tuple-element.46.refs_1_.refs_0_.refs_2_.z_ref, f32[5,33,64,128]{3,2,1,0:T(8,128)S(1)} %get-tuple-element.48.refs_2_.refs_1_.refs_3_, f32[33,8,128]{2,1,0:T(8,128)S(1)} %get-tuple-element.57.refs_3_.refs_2_.refs_5_, ...), custom_call_target="tpu_custom_call" | custom-call | flops 6758400 | bytes 5406720 | tf_op jit(solution)/shard_map/middle/pallas_call | solution.py:560
  54.8 6.7 %collective-permute-done.7.refs_0_ = f32[33,8,128]{2,1,0:T(8,128)S(1)} collective-permute-done((f32[33,8,128]{2,1,0:T(8,128)S(1)}, f32[33,8,128]{2,1,0:T(8,128)S(1)}, u32[]{:S(2)}, u32[]{:S(2)}) %collective-permute-start.7) | collective-permute-done | bytes 135200 | tf_op jit(solution)/shard_map/ppermute | solution.py:554
  61.5 0.5 near_twice.5
  62.1 1.5 %collective-permute-start.10 = (f32[33,8,128]{2,1,0:T(8,128)S(1)}, f32[33,8,128]{2,1,0:T(8,128)S(1)}, u32[]{:S(2)}, u32[]{:S(2)}) collective-permute-start(f32[33,8,128]{2,1,0:T(8,128)S(1)} %get-tuple-element.64.top_ref), channel_id=1, source_target_pairs={{0,2},{2,0},{4,6},{6,4},{8,10},{10,8},{12,14},{14,12},{1,3},{3,1},... | collective-permute-start | bytes 405512 | tf_op jit(solution)/shard_map/ppermute | solution.py:554
  63.6 0.0 collective-permute-done.9.refs_0_
  63.6 1.8 %far.5 = (f32[33,16,128]{2,1,0:T(8,128)}, f32[66,8,128]{2,1,0:T(8,128)S(1)}, f32[33,8,128]{2,1,0:T(8,128)S(1)}) custom-call(f32[66,8,128]{2,1,0:T(8,128)S(1)} %collective-permute-done.9.refs_0_, f32[113,8,128]{2,1,0:T(8,128)S(1)} %collective-permute-done.5.far_ref.refs_0_.refs_1_, f32[33,64,128]{2,1,0:T(8,128)S(1)} %get-tuple-element.46.refs_1_.refs_0_.refs_2_.z_ref, ...), custom_call_target="tpu_custom_call" | custom-call | flops 2703360 | bytes 2162688 | tf_op jit(solution)/shard_map/far/pallas_call | solution.py:560
  65.4 1.9 %collective-permute-start.11 = (f32[33,8,128]{2,1,0:T(8,128)S(1)}, f32[33,8,128]{2,1,0:T(8,128)S(1)}, u32[]{:S(2)}, u32[]{:S(2)}) collective-permute-start(f32[33,8,128]{2,1,0:T(8,128)S(1)} %get-tuple-element.70), channel_id=1, source_target_pairs={{2,4},{4,2},{6,8},{8,6},{10,12},{12,10},{3,5},{5,3},{7,9},{9,7},{1... | collective-permute-start | bytes 405512 | tf_op jit(solution)/shard_map/ppermute | solution.py:557
  67.3 1.8 %gradient.1.part_ref = f32[9,8,4096]{2,1,0:T(8,128)S(1)} custom-call(f32[33,64,128]{2,1,0:T(8,128)S(1)} %get-tuple-element.46.refs_1_.refs_0_.refs_2_.z_ref, f32[33,8,128]{2,1,0:T(8,128)S(1)} %get-tuple-element.64.top_ref, f32[33,8,128]{2,1,0:T(8,128)S(1)} %get-tuple-element.65.second_ref, f32[33,32,128]{2,1,0:T(8,128)S(1)} %get-tuple-element.66.inner_ref, ...), custom_call_target="tpu_custom_call" | custom-call | flops 16220160 | bytes 12976128 | tf_op jit(solution)/shard_map/gradient/pallas_call | solution.py:560
  69.1 0.0 collective-permute-done.10.up_ref
  69.1 4.3 %collective-permute-done.11.down_ref = f32[33,8,128]{2,1,0:T(8,128)S(1)} collective-permute-done((f32[33,8,128]{2,1,0:T(8,128)S(1)}, f32[33,8,128]{2,1,0:T(8,128)S(1)}, u32[]{:S(2)}, u32[]{:S(2)}) %collective-permute-start.11) | collective-permute-done | bytes 135200 | tf_op jit(solution)/shard_map/ppermute | solution.py:557
  73.4 1.4 %finish.1 = f32[9,8,4096]{2,1,0:T(8,128)} custom-call(f32[9,8,4096]{2,1,0:T(8,128)S(1)} %gradient.1.part_ref, f32[33,64,128]{2,1,0:T(8,128)S(1)} %get-tuple-element.46.refs_1_.refs_0_.refs_2_.z_ref, f32[33,8,128]{2,1,0:T(8,128)S(1)} %collective-permute-done.10.up_ref, f32[33,8,128]{2,1,0:T(8,128)S(1)} %collective-permute-done.11.down_ref), custom_call_target="tpu_custom_call" | custom-call | flops 5406720 | bytes 4325376 | tf_op jit(solution)/shard_map/finish/pallas_call | solution.py:560
Async XLA Ops:
  1.7 2.0 %collective-permute-start = (f32[2,2,8,4224]{3,2,1,0:T(8,128)S(1)}, f32[2,2,8,4224]{3,2,1,0:T(8,128)S(1)}, u32[]{:S(2)}, u32[]{:S(2)}) collective-permute-start(f32[2,2,8,4224]{3,2,1,0:T(8,128)S(1)} %get-tuple-element.43), channel_id=1, source_target_pairs={{0,1},{1,0},{2,3},{3,2},{4,5},{5,4},{6,7},{7,6},{8,9},{9,8},{10,11... | collective-permute-start | bytes 1622024 | tf_op jit(solution)/shard_map/ppermute | solution.py:588
  4.0 27.2 %collective-permute-start.5 = (f32[113,8,128]{2,1,0:T(8,128)S(1)}, f32[113,8,128]{2,1,0:T(8,128)S(1)}, u32[]{:S(2)}, u32[]{:S(2)}) collective-permute-start(f32[113,8,128]{2,1,0:T(8,128)S(1)} %get-tuple-element.53), channel_id=1, source_target_pairs={{2,4},{4,2},{6,8},{8,6},{10,12},{12,10},{3,5},{5,3},{7,9},{9,7},{1... | collective-permute-start | bytes 1388552 | tf_op jit(solution)/shard_map/ppermute | solution.py:557
  7.3 15.8 %collective-permute-start.1 = (f32[42,8,128]{2,1,0:T(8,128)S(1)}, f32[42,8,128]{2,1,0:T(8,128)S(1)}, u32[]{:S(2)}, u32[]{:S(2)}) collective-permute-start(f32[42,8,128]{2,1,0:T(8,128)S(1)} %get-tuple-element.47), channel_id=1, source_target_pairs={{0,2},{2,0},{4,6},{6,4},{8,10},{10,8},{12,14},{14,12},{1,3},{3,1},... | collective-permute-start | bytes 516104 | tf_op jit(solution)/shard_map/ppermute | solution.py:554
  23.6 5.6 %collective-permute-start.2 = (f32[33,8,128]{2,1,0:T(8,128)S(1)}, f32[33,8,128]{2,1,0:T(8,128)S(1)}, u32[]{:S(2)}, u32[]{:S(2)}) collective-permute-start(f32[33,8,128]{2,1,0:T(8,128)S(1)} %near_once.3.refs_3_.refs_5_), channel_id=1, source_target_pairs={{0,2},{2,0},{4,6},{6,4},{8,10},{10,8},{12,14},{14,12},{1,3},{3,1},... | collective-permute-start | bytes 405512 | tf_op jit(solution)/shard_map/ppermute | solution.py:554
  29.7 5.1 %collective-permute-start.3 = (f32[33,8,128]{2,1,0:T(8,128)S(1)}, f32[33,8,128]{2,1,0:T(8,128)S(1)}, u32[]{:S(2)}, u32[]{:S(2)}) collective-permute-start(f32[33,8,128]{2,1,0:T(8,128)S(1)} %get-tuple-element.50.refs_3_.refs_2_.refs_5_), channel_id=1, source_target_pairs={{0,2},{2,0},{4,6},{6,4},{8,10},{10,8},{12,14},{14,12},{1,3},{3,1},... | collective-permute-start | bytes 405512 | tf_op jit(solution)/shard_map/ppermute | solution.py:554
  32.5 14.1 %collective-permute-start.8 = (f32[66,8,128]{2,1,0:T(8,128)S(1)}, f32[66,8,128]{2,1,0:T(8,128)S(1)}, u32[]{:S(2)}, u32[]{:S(2)}) collective-permute-start(f32[66,8,128]{2,1,0:T(8,128)S(1)} %get-tuple-element.55.refs_5_.refs_6_), channel_id=1, source_target_pairs={{2,4},{4,2},{6,8},{8,6},{10,12},{12,10},{3,5},{5,3},{7,9},{9,7},{1... | collective-permute-start | bytes 811016 | tf_op jit(solution)/shard_map/ppermute | solution.py:557
  35.2 10.3 %collective-permute-start.4 = (f32[33,8,128]{2,1,0:T(8,128)S(1)}, f32[33,8,128]{2,1,0:T(8,128)S(1)}, u32[]{:S(2)}, u32[]{:S(2)}) collective-permute-start(f32[33,8,128]{2,1,0:T(8,128)S(1)} %near_once.4.refs_3_.refs_5_), channel_id=1, source_target_pairs={{0,2},{2,0},{4,6},{6,4},{8,10},{10,8},{12,14},{14,12},{1,3},{3,1},... | collective-permute-start | bytes 405512 | tf_op jit(solution)/shard_map/ppermute | solution.py:554
  46.0 5.6 %collective-permute-start.6 = (f32[33,8,128]{2,1,0:T(8,128)S(1)}, f32[33,8,128]{2,1,0:T(8,128)S(1)}, u32[]{:S(2)}, u32[]{:S(2)}) collective-permute-start(f32[33,8,128]{2,1,0:T(8,128)S(1)} %get-tuple-element.57.refs_3_.refs_2_.refs_5_), channel_id=1, source_target_pairs={{0,2},{2,0},{4,6},{6,4},{8,10},{10,8},{12,14},{14,12},{1,3},{3,1},... | collective-permute-start | bytes 405512 | tf_op jit(solution)/shard_map/ppermute | solution.py:554
  47.7 15.9 %collective-permute-start.9 = (f32[66,8,128]{2,1,0:T(8,128)S(1)}, f32[66,8,128]{2,1,0:T(8,128)S(1)}, u32[]{:S(2)}, u32[]{:S(2)}) collective-permute-start(f32[66,8,128]{2,1,0:T(8,128)S(1)} %get-tuple-element.62.refs_5_.refs_6_), channel_id=1, source_target_pairs={{2,4},{4,2},{6,8},{8,6},{10,12},{12,10},{3,5},{5,3},{7,9},{9,7},{1... | collective-permute-start | bytes 811016 | tf_op jit(solution)/shard_map/ppermute | solution.py:557
  52.0 9.5 %collective-permute-start.7 = (f32[33,8,128]{2,1,0:T(8,128)S(1)}, f32[33,8,128]{2,1,0:T(8,128)S(1)}, u32[]{:S(2)}, u32[]{:S(2)}) collective-permute-start(f32[33,8,128]{2,1,0:T(8,128)S(1)} %near_once.5.refs_3_), channel_id=1, source_target_pairs={{0,2},{2,0},{4,6},{6,4},{8,10},{10,8},{12,14},{14,12},{1,3},{3,1},... | collective-permute-start | bytes 405512 | tf_op jit(solution)/shard_map/ppermute | solution.py:554
  62.1 7.0 %collective-permute-start.10 = (f32[33,8,128]{2,1,0:T(8,128)S(1)}, f32[33,8,128]{2,1,0:T(8,128)S(1)}, u32[]{:S(2)}, u32[]{:S(2)}) collective-permute-start(f32[33,8,128]{2,1,0:T(8,128)S(1)} %get-tuple-element.64.top_ref), channel_id=1, source_target_pairs={{0,2},{2,0},{4,6},{6,4},{8,10},{10,8},{12,14},{14,12},{1,3},{3,1},... | collective-permute-start | bytes 405512 | tf_op jit(solution)/shard_map/ppermute | solution.py:554
  65.4 8.0 %collective-permute-start.11 = (f32[33,8,128]{2,1,0:T(8,128)S(1)}, f32[33,8,128]{2,1,0:T(8,128)S(1)}, u32[]{:S(2)}, u32[]{:S(2)}) collective-permute-start(f32[33,8,128]{2,1,0:T(8,128)S(1)} %get-tuple-element.70), channel_id=1, source_target_pairs={{2,4},{4,2},{6,8},{8,6},{10,12},{12,10},{3,5},{5,3},{7,9},{9,7},{1... | collective-permute-start | bytes 405512 | tf_op jit(solution)/shard_map/ppermute | solution.py:557

commit v6 on v3

v6 whole, which is shorter than its diff:
```python
import functools
import math

import jax
import jax.numpy as jnp
from jax import lax
from jax.experimental import pallas as pl
from jax.experimental.pallas import tpu as pltpu
from jax.sharding import PartitionSpec as P

CHEB = 6
LANES = 128
SUBS = 8

lower_edge = 0.25
upper_edge = 12.0


def cheb_weights(degree, low_end, high_end):
    count = degree + 1
    values = []
    for order in range(count):
        accum = 0.0
        for node in range(count):
            angle = math.pi * (node + 0.5) / count
            point = 0.5 * (high_end - low_end) * math.cos(angle) + 0.5 * (high_end + low_end)
            accum += math.cos(order * angle) / point
        accum = accum * 2.0 / count
        if order == 0:
            accum = accum * 0.5
        values.append(accum)
    return values


def vmem_spec():
    return pl.BlockSpec(memory_space=pltpu.VMEM)


def params():
    return pltpu.CompilerParams(vmem_limit_bytes=40 * 1024 * 1024)


def cost(vregs):
    return pl.CostEstimate(flops=vregs * 1024 * 20, bytes_accessed=vregs * 4096 * 4, transcendentals=0)


def masks():
    lane = lax.broadcasted_iota(jnp.int32, (SUBS, LANES), 1)
    return lane == 0, lane == LANES - 1


def window_tiles(load, first, count, total):
    before = jnp.where(first > 0, load(jnp.maximum(first - 1, 0)), 0.0)
    after = jnp.where(first + count < total, load(jnp.minimum(first + count, total - 1)), 0.0)
    return [before] + [load(first + k) for k in range(count)] + [after]


def beside(before, here, after, edges):
    left = pltpu.roll(jnp.where(edges[1], before, here), 1, 1)
    right = pltpu.roll(jnp.where(edges[0], after, here), LANES - 1, 1)
    return left, right


def sub(row):
    return pl.ds(row * SUBS, SUBS)


def tile_columns(tile):
    return pl.ds(pl.multiple_of(tile * LANES, LANES), LANES)


def chunk_of(tiles):
    return max(count for count in range(1, 12) if tiles % count == 0)


def load_kernel(width, probes_ref, observed_ref, coefficients_ref, theirs_ref, own_ref, seen_ref, window_ref, sem):
    core = lax.axis_index("probe")
    move = probes_ref.shape[3] - width
    mine = pl.ds(pl.multiple_of(core * move, LANES), width)
    other = pl.ds(pl.multiple_of((1 - core) * move, LANES), width)
    copies = [
        pltpu.make_async_copy(probes_ref.at[:, :, :, other], theirs_ref, sem.at[0]),
        pltpu.make_async_copy(probes_ref.at[:, :, :, mine], own_ref, sem.at[1]),
        pltpu.make_async_copy(coefficients_ref.at[:, :, mine], window_ref, sem.at[2]),
        pltpu.make_async_copy(observed_ref.at[:, :, mine], seen_ref, sem.at[3]),
    ]
    for copy in copies:
        copy.start()
    for copy in copies:
        copy.wait()


def combine(kappa, across, along, skew, coupling):
    scale = 4.0 / (upper_edge - lower_edge)
    shift = 2.0 * (upper_edge + lower_edge) / (upper_edge - lower_edge)
    return (
        scale * (kappa + 2.0 * (across + along)) - shift,
        -scale * across,
        -scale * along,
        -0.5 * scale * skew,
        scale * coupling,
    )


def prep_kernel(window_ref, seen_ref, expanded_ref, top_ref, bottom_ref, eight, rest, observed):
    tiles = expanded_ref.shape[1]
    chunk = chunk_of(tiles)
    rest[...] = jnp.zeros_like(rest)
    observed[...] = jnp.zeros_like(observed)

    def body(step, carry):
        for k in range(chunk):
            tile = step * chunk + k
            cols = tile_columns(tile)
            raw = [window_ref[channel, :, cols] for channel in range(9)]
            for c in range(2):
                values = combine(raw[c], raw[2 + c], raw[4 + c], raw[6 + c], raw[8])
                for kind, value in enumerate(values):
                    for probe in range(4):
                        expanded_ref[kind, tile, pl.ds(4 * c + probe, SUBS, stride=SUBS), :] = value
            for channel in range(8):
                eight[tile, pl.ds(channel, SUBS, stride=SUBS), :] = raw[channel]
            top_ref[tile] = eight[tile, sub(0), :]
            bottom_ref[tile] = eight[tile, sub(SUBS - 1), :]
        return carry

    lax.fori_loop(0, tiles // chunk, body, 0)
    for tile in range(tiles):
        cols = pl.ds(tile * LANES, LANES)
        rest[tile // 8, pl.ds(tile % 8, SUBS, stride=SUBS), :] = window_ref[8, :, cols]
        for c in range(2):
            observed[tile // 4, pl.ds(2 * (tile % 4) + c, SUBS, stride=SUBS), :] = seen_ref[c, :, cols]
    base = tiles
    for source in (rest, observed):
        for index in range(source.shape[0]):
            top_ref[base + index] = source[index, sub(0), :]
            bottom_ref[base + index] = source[index, sub(SUBS - 1), :]
        base += source.shape[0]


def layout_kernel(own_ref, other_ref, z_ref, top_ref, bottom_ref):
    tiles = z_ref.shape[0]
    chunk = chunk_of(tiles)

    def body(step, carry):
        for k in range(chunk):
            tile = step * chunk + k
            cols = tile_columns(tile)
            for c in range(2):
                for probe in range(2):
                    z_ref[tile, pl.ds(4 * c + probe, SUBS, stride=SUBS), :] = own_ref[probe, c, :, cols]
                    z_ref[tile, pl.ds(4 * c + 2 + probe, SUBS, stride=SUBS), :] = other_ref[probe, c, :, cols]
            top_ref[tile] = z_ref[tile, sub(0), :]
            bottom_ref[tile] = z_ref[tile, sub(SUBS - 1), :]
        return carry

    lax.fori_loop(0, tiles // chunk, body, 0)


def rim(edge_ref, rim_ref, tiles):
    chunk = chunk_of(tiles)

    def spread(index, row):
        return jnp.broadcast_to(edge_ref[index, pl.ds(row, 1), :], (SUBS, LANES))

    def body(step, carry):
        low = lax.broadcasted_iota(jnp.int32, (SUBS, LANES), 0) < 4
        for k in range(chunk):
            tile = step * chunk + k
            pairs = [jnp.where(low, spread(tile, 2 * kind), spread(tile, 2 * kind + 1)) for kind in range(4)]
            coupling = spread(tiles + tile // 8, tile % 8)
            for kind, value in enumerate(combine(*pairs, coupling)):
                rim_ref[kind, tile] = value
        return carry

    lax.fori_loop(0, tiles // chunk, body, 0)


def sweep(tiles, low, count, load, factor, z_row, before, constants, store):
    weight, scale = constants
    chunk = chunk_of(tiles)

    def body(step, carry):
        edges = masks()
        first = step * chunk
        for k in range(chunk):
            tile = first + k
            values, sums, slopes = [], [], []
            for row in range(low - 1, low + count + 1):
                here = load(row, tile)
                if k == 0:
                    last = jnp.where(first > 0, load(row, jnp.maximum(first - 1, 0)), 0.0)
                else:
                    last = load(row, tile - 1)
                if k == chunk - 1:
                    more = first + chunk < tiles
                    after = jnp.where(more, load(row, jnp.minimum(first + chunk, tiles - 1)), 0.0)
                else:
                    after = load(row, tile + 1)
                left, right = beside(last, here, after, edges)
                values.append(here)
                sums.append(left + right)
                slopes.append(right - left)
            for at in range(count):
                row = low + at
                total = (
                    factor(0, row, tile) * values[at + 1]
                    + factor(1, row, tile) * sums[at + 1]
                    + factor(2, row, tile) * (values[at] + values[at + 2])
                    + factor(3, row, tile) * (slopes[at + 2] - slopes[at])
                    + factor(4, row, tile) * pltpu.roll(values[at + 1], 4, 0)
                )
                if scale != 1.0:
                    total = scale * total
                total = total + weight * z_row(row, tile)
                if before is not None:
                    total = total - before(row, tile)
                store(row, tile, total)
        return carry

    lax.fori_loop(0, tiles // chunk, body, 0)


def first_kernel(part, constants, tiles, *refs):
    halo_ref = None
    if part != 1:
        halo_ref, refs = refs[0], refs[1:]
    z_ref, expanded_ref, out_ref = refs
    low, count = ((0, 2), (2, 4), (6, 2))[part]

    def now(row, tile):
        if row < 0 or row > 7:
            return halo_ref[tile]
        return z_ref[tile, sub(row), :]

    def store(row, tile, value):
        if part == 1:
            out_ref[tile, sub(row - low), :] = value
        else:
            out_ref[2 * tile + row - low] = value

    def factor(kind, row, tile):
        return expanded_ref[kind, tile, sub(row), :]

    sweep(tiles, low, count, now, factor, lambda row, tile: z_ref[tile, sub(row), :], None, constants, store)


def inner_rows(top_ref, inner_ref, bottom_ref):
    def now(row, tile):
        if row < 2:
            return top_ref[2 * tile + row]
        if row < 6:
            return inner_ref[tile, sub(row - 2), :]
        return bottom_ref[2 * tile + row - 6]

    return now


def middle_kernel(steps, tiles, *refs):
    z_ref, expanded_ref, top_ref, inner_ref, bottom_ref = refs[:5]
    once_ref, twice_ref = refs[-2:]
    now = inner_rows(top_ref, inner_ref, bottom_ref)

    def factor(kind, row, tile):
        return expanded_ref[kind, tile, sub(row), :]

    def z_row(row, tile):
        return z_ref[tile, sub(row), :]

    def once(row, tile):
        return once_ref[tile, sub(row - 1), :]

    def store_once(row, tile, value):
        once_ref[tile, sub(row - 1), :] = value

    def store_twice(row, tile, value):
        twice_ref[tile, sub(row - 2), :] = value

    older = None
    if len(refs) > 7:
        older = lambda row, tile: refs[5][tile, sub(row - 1), :]
    sweep(tiles, 1, 6, now, factor, z_row, older, steps[0], store_once)
    sweep(tiles, 2, 4, once, factor, z_row, now, steps[1], store_twice)


def edge_product(upper, constants, tiles, halo_ref, z_halo_ref, z_ref, expanded_ref, rim_ref, edge_ref, older_ref, once_ref):
    base = 0 if upper else 6
    low = -1 if upper else 7

    def now(row, tile):
        if row < 0 or row > 7:
            return halo_ref[2 * tile + (row + 2 if upper else row - 8)]
        return edge_ref[2 * tile + row - base]

    def factor(kind, row, tile):
        if row < 0 or row > 7:
            return rim_ref[kind, tile]
        return expanded_ref[kind, tile, sub(row), :]

    def z_row(row, tile):
        if row < 0 or row > 7:
            return z_halo_ref[tile]
        return z_ref[tile, sub(row), :]

    def store(row, tile, value):
        once_ref[tile, sub(row - low), :] = value

    older = None if older_ref is None else (lambda row, tile: older_ref[tile, sub(row - low), :])
    sweep(tiles, low, 2, now, factor, z_row, older, constants, store)
    return now, factor, z_row


def edge_kernel(upper, steps, tiles, *refs):
    halo_ref, z_halo_ref, z_ref, expanded_ref, rim_ref, edge_ref, inner_ref = refs[:7]
    once_ref, twice_ref = refs[-2:]
    older_ref = refs[7] if len(refs) > 9 else None
    now, factor, z_row = edge_product(
        upper, steps[0], tiles, halo_ref, z_halo_ref, z_ref, expanded_ref, rim_ref, edge_ref, older_ref, once_ref
    )
    base = 0 if upper else 6
    low = -1 if upper else 7

    def once(row, tile):
        if 1 <= row <= 6:
            return inner_ref[tile, sub(row - 1), :]
        return once_ref[tile, sub(row - low), :]

    def store_twice(row, tile, value):
        twice_ref[2 * tile + row - base] = value

    sweep(tiles, base, 2, once, factor, z_row, now, steps[1], store_twice)


def gradient_rows(low, count, tile, slot, load, z_ref, factor, tiles, products):
    edges = masks()
    values, sums, slopes = [], [], []
    for row in range(low - 1, low + count + 1):
        before, here, after = window_tiles(lambda at: load(row, at), tile, 1, tiles)
        left, right = beside(before, here, after, edges)
        values.append(here)
        sums.append(left + right)
        slopes.append(right - left)
    for at in range(count):
        row = low + at
        left = factor * z_ref[tile, sub(row), :]
        value = values[at + 1]
        twice = 2.0 * value
        products[slot, 0, sub(row), :] = left * value
        products[slot, 1, sub(row), :] = left * (twice - sums[at + 1])
        products[slot, 2, sub(row), :] = left * (twice - (values[at] + values[at + 2]))
        products[slot, 3, sub(row), :] = (-0.5 * left) * (slopes[at + 2] - slopes[at])
        products[slot, 4, sub(row), :] = left * pltpu.roll(value, 4, 0)


def gradient_sums(slot, products, start, store):
    for kind in range(5):
        parts = [products[slot, kind, pl.ds(s, SUBS, stride=SUBS), :] for s in range(SUBS)]
        sums = [(parts[4 * c] + parts[4 * c + 1]) + (parts[4 * c + 2] + parts[4 * c + 3]) for c in range(2)]
        if kind < 4:
            for c in range(2):
                store(2 * kind + c, sums[c] + start(2 * kind + c))
        else:
            store(8, (sums[0] + sums[1]) + start(8))


def gradient_kernel(constants, tiles, factor, *refs):
    z_ref, expanded_ref, top_ref, inner_ref, bottom_ref, older_ref, data_ref, series_ref, out_ref, products = refs
    now = inner_rows(top_ref, inner_ref, bottom_ref)

    def coefficient(kind, row, tile):
        return expanded_ref[kind, tile, sub(row), :]

    def store(row, tile, value):
        series_ref[tile, sub(row - 1), :] = value

    def series(row, tile):
        return series_ref[tile, sub(row - 1), :]

    sweep(
        tiles,
        1,
        6,
        now,
        coefficient,
        lambda row, tile: z_ref[tile, sub(row), :],
        lambda row, tile: older_ref[tile, sub(row - 1), :],
        constants,
        store,
    )
    kept = out_ref.shape[2] // LANES
    offset = lax.axis_index("probe") * (tiles - kept)
    count = products.shape[0]
    products[...] = jnp.zeros_like(products)

    def body(step, carry):
        for k in range(count):
            gradient_rows(2, 4, step * count + k + offset, k, series, z_ref, factor, tiles, products)
        for k in range(count):
            index = step * count + k
            cols = tile_columns(index)

            def put(channel, value):
                out_ref[channel, :, cols] = value

            gradient_sums(k, products, lambda channel: data_ref[index + offset, channel], put)
        return carry

    lax.fori_loop(0, kept // count, body, 0)


def end_kernel(upper, constants, tiles, factor, *refs):
    halo_ref, z_halo_ref, z_ref, expanded_ref, rim_ref, edge_ref, inner_ref, older_ref, part_ref = refs[:9]
    if upper:
        out_ref, once_ref, products = refs[9:]
        target = out_ref
    else:
        out_ref, once_ref, products, target, sem = refs[9:]
    edge_product(
        upper, constants, tiles, halo_ref, z_halo_ref, z_ref, expanded_ref, rim_ref, edge_ref, older_ref, once_ref
    )
    low = -1 if upper else 7

    def series(row, tile):
        if 1 <= row <= 6:
            return inner_ref[tile, sub(row - 1), :]
        return once_ref[tile, sub(row - low), :]

    kept = target.shape[2] // LANES
    offset = lax.axis_index("probe") * (tiles - kept)
    count = products.shape[0]
    products[...] = jnp.zeros_like(products)

    def body(step, carry):
        for k in range(count):
            tile = step * count + k + offset
            gradient_rows(0 if upper else 6, 2, tile, k, series, z_ref, factor, tiles, products)
        for k in range(count):
            cols = tile_columns(step * count + k)

            def put(channel, value):
                target[channel, :, cols] = value

            gradient_sums(k, products, lambda channel: part_ref[channel, :, cols], put)
        return carry

    steps = kept // count
    if upper:
        lax.fori_loop(0, steps, body, 0)
        return
    groups = sem.shape[0]
    copies = []
    for group in range(groups):
        lax.fori_loop(group * steps // groups, (group + 1) * steps // groups, body, 0)
        cols = pl.ds(group * kept // groups * LANES, kept // groups * LANES)
        copies.append(pltpu.make_async_copy(target.at[:, :, cols], out_ref.at[:, :, cols], sem.at[group]))
        copies[-1].start()
    for copy in copies:
        copy.wait()


def border_kernel(tiles, seen_ref, up_ref, down_ref, out_ref, rim_up_ref, rim_down_ref):
    rim(up_ref, rim_up_ref, tiles)
    rim(down_ref, rim_down_ref, tiles)
    chunk = chunk_of(tiles)

    base = tiles + -(-tiles // 8)

    def halo(ref, c, tile):
        row = ref[base + tile // 4, pl.ds(2 * (tile % 4) + c, 1), :]
        return jnp.broadcast_to(row, (SUBS, LANES))

    def body(step, carry):
        edges = masks()
        row = lax.broadcasted_iota(jnp.int32, (SUBS, LANES), 0)
        first = step * chunk
        kept = [[], []]
        for c in range(2):
            values = window_tiles(lambda tile: seen_ref[c, :, tile_columns(tile)], first, chunk, tiles)
            ups = window_tiles(lambda tile: halo(up_ref, c, tile), first, chunk, tiles)
            downs = window_tiles(lambda tile: halo(down_ref, c, tile), first, chunk, tiles)
            aboves = [jnp.where(row == 0, u, pltpu.roll(v, 1, 0)) for u, v in zip(ups, values)]
            belows = [jnp.where(row == SUBS - 1, d, pltpu.roll(v, SUBS - 1, 0)) for d, v in zip(downs, values)]
            tilts = [b - a for a, b in zip(aboves, belows)]
            for k in range(chunk):
                tile = first + k
                value = values[k + 1]
                left, right = beside(values[k], value, values[k + 2], edges)
                low, high = beside(tilts[k], tilts[k + 1], tilts[k + 2], edges)
                half = -0.5 * value
                out_ref[tile, c] = half * value
                out_ref[tile, 2 + c] = half * (2.0 * value - (left + right))
                out_ref[tile, 4 + c] = half * (2.0 * value - (aboves[k + 1] + belows[k + 1]))
                out_ref[tile, 6 + c] = (-0.5 * half) * (high - low)
                kept[c].append(value)
        for k in range(chunk):
            out_ref[first + k, 8] = -(kept[0][k] * kept[1][k])
        return carry

    lax.fori_loop(0, tiles // chunk, body, 0)


def per_device(observations, coefficients, probes):
    weights = cheb_weights(CHEB, lower_edge, upper_edge)
    f32 = jnp.float32
    columns = probes.shape[3]
    share = columns // lax.axis_size("probe")
    width = share + LANES
    tiles = width // LANES
    kept = share // LANES
    rows = lax.axis_size("row")
    down_pairs = [(i, i + 1) for i in range(rows - 1)]
    up_pairs = [(i + 1, i) for i in range(rows - 1)]

    def to_next(edge):
        return lax.ppermute(edge, "row", down_pairs)

    def to_previous(edge):
        return lax.ppermute(edge, "row", up_pairs)

    def call(kernel, name, vregs, operands, outs, scratch=(), in_specs=None, out_specs=None):
        return pl.pallas_call(
            kernel,
            out_shape=outs,
            in_specs=in_specs or [vmem_spec()] * len(operands),
            out_specs=out_specs or jax.tree.map(lambda _: vmem_spec(), outs),
            scratch_shapes=scratch,
            compiler_params=params(),
            cost_estimate=cost(vregs),
            name=name,
        )(*operands)

    theirs, own, seen, window = call(
        functools.partial(load_kernel, width),
        "load",
        100,
        [
            pltpu.with_memory_space_constraint(array, pltpu.HBM)
            for array in (probes, observations, coefficients)
        ],
        [
            pltpu.VMEM((2, 2, SUBS, width), f32),
            pltpu.VMEM((2, 2, SUBS, width), f32),
            pltpu.VMEM((2, SUBS, width), f32),
            pltpu.VMEM((9, SUBS, width), f32),
        ],
        [pltpu.SemaphoreType.DMA((4,))],
        [pl.BlockSpec(memory_space=pltpu.HBM)] * 3,
    )
    other = lax.ppermute(theirs, "probe", [(0, 1), (1, 0)])
    eights, fours = -(-tiles // 8), -(-tiles // 4)
    edge_shape = pltpu.VMEM((tiles + eights + fours, SUBS, LANES), f32)
    expanded, edge_top, edge_bottom = call(
        prep_kernel,
        "prep",
        5 * 8 * tiles,
        (window, seen),
        [pltpu.VMEM((5, tiles, SUBS * SUBS, LANES), f32), edge_shape, edge_shape],
        [pltpu.VMEM((count, SUBS * SUBS, LANES), f32) for count in (tiles, eights, fours)],
    )
    edges_down, edges_up = to_previous(edge_top), to_next(edge_bottom)
    own, expanded = lax.optimization_barrier((own, expanded))
    def rows_of(count):
        return pltpu.VMEM((tiles, count * SUBS, LANES), f32)

    z, top, bottom = call(
        layout_kernel,
        "layout",
        8 * tiles,
        (own, other),
        [rows_of(SUBS), rows_of(1), rows_of(1)],
    )
    z_down, z_up = to_previous(top), to_next(bottom)
    edge_rows = pltpu.VMEM((2 * tiles, SUBS, LANES), f32)
    constants = (weights[CHEB - 1], weights[CHEB])

    def first(part, halos, out):
        return call(
            functools.partial(first_kernel, part, constants, tiles),
            "first",
            (2 + part % 2 * 2) * tiles,
            [*halos, z, expanded],
            out,
        )

    rim_shape = pltpu.VMEM((5, tiles, SUBS, LANES), f32)
    data, rim_up, rim_down = call(
        functools.partial(border_kernel, tiles),
        "border",
        9 * tiles,
        (seen, edges_up, edges_down),
        [pltpu.VMEM((tiles, 9, SUBS, LANES), f32), rim_shape, rim_shape],
    )
    expanded, data = lax.optimization_barrier((expanded, data))
    inner = first(1, [], rows_of(4))
    bottom = first(2, [z_down], edge_rows)
    up = to_next(bottom)
    top = first(0, [z_up], edge_rows)
    down = to_previous(top)
    once = None
    for order in range(CHEB - 2, 0, -2):
        opening = weights[order] - (weights[CHEB] if order == CHEB - 2 else 0.0)
        steps = ((opening, 1.0), (weights[order - 1], 1.0))
        inner_once, inner_twice = call(
            functools.partial(middle_kernel, steps, tiles),
            "middle",
            10 * tiles,
            [z, expanded, top, inner, bottom] + ([once[1]] if once else []),
            [rows_of(6), rows_of(4)],
        )

        def edge(upper):
            operands = [up if upper else down, z_up if upper else z_down, z, expanded, rim_up if upper else rim_down]
            operands += [top if upper else bottom, inner_once]
            return call(
                functools.partial(edge_kernel, upper, steps, tiles),
                "upper" if upper else "lower",
                4 * tiles,
                operands + ([once[0 if upper else 2]] if once else []),
                [rows_of(2), edge_rows],
            )

        over, under = edge(True), edge(False)
        once = (over[0], inner_once, under[0])
        top, inner, bottom = over[1], inner_twice, under[1]
        down, up = to_previous(top), to_next(bottom)

    factor = 0.5 / (probes.shape[0] * lax.axis_size("probe"))
    count = max(n for n in range(1, 5) if kept % n == 0)
    constants = (weights[0], 0.5)
    products = pltpu.VMEM((count, 5, SUBS * SUBS, LANES), f32)
    whole = (9, SUBS, share)
    series, part = call(
        functools.partial(gradient_kernel, constants, tiles, factor),
        "gradient",
        24 * tiles,
        (z, expanded, top, inner, bottom, once[1], data),
        [rows_of(6), pltpu.VMEM(whole, f32)],
        [products],
    )
    part = call(
        functools.partial(end_kernel, True, constants, tiles, factor),
        "upper_end",
        8 * tiles,
        (up, z_up, z, expanded, rim_up, top, series, once[0], part),
        pltpu.VMEM(whole, f32),
        [rows_of(2), products],
    )
    groups = max(n for n in range(1, 5) if kept // count % n == 0)
    return call(
        functools.partial(end_kernel, False, constants, tiles, factor),
        "lower_end",
        8 * tiles,
        (down, z_down, z, expanded, rim_down, bottom, series, once[2], part),
        jax.ShapeDtypeStruct(whole, f32),
        [rows_of(2), products, pltpu.VMEM(whole, f32), pltpu.SemaphoreType.DMA((groups,))],
        None,
        pl.BlockSpec(memory_space=pltpu.HBM),
    )


def solution(mesh):
    in_specs = (P("group", "row", None), P("group", "row", None), P("probe", "group", "row", None))
    out_specs = P("group", "row", "probe")
    return jax.shard_map(
        per_device, mesh=mesh, in_specs=in_specs, out_specs=out_specs, check_vma=False
    )
```

time: 69.6 us -> 68.9 us (0.990)
  waiting for transfers between devices: 25.6 us -> 16.8 us
  starting transfers between devices: 24 us -> 31.2 us
  Pallas kernels: 19.5 us -> 20.2 us
    ppermute x4 -> x5, waiting for transfers between devices: 19 us -> 9.1 us  [to_previous(): return lax.ppermute(edge, 'row', up_pairs)]
    ppermute x4 -> x5, starting transfers between devices: 18.3 us -> 24.2 us  [to_next(): return lax.ppermute(edge, 'row', down_pairs)]
    ppermute x4 -> x5, waiting for transfers between devices: 6.07 us -> 7.74 us  [to_next(): return lax.ppermute(edge, 'row', down_pairs)]
    ppermute x4 -> x5, starting transfers between devices: 5.16 us -> 6.46 us  [to_previous(): return lax.ppermute(edge, 'row', up_pairs)]
    pallas_call x15 -> x16, Pallas kernels: 19.5 us -> 20.2 us  [call(): pl.pallas_call(kernel, out_shape=outs, in_specs=in_specs or [vmem_spec()]...]
  transfers between devices with their start and end apart: 9 -> 11, of which waited for: 6 -> 5; matrix products, arithmetic and copies ran while one was open for 0% -> 0% of each run, Pallas kernels for 23% -> 23%
where the time goes in v6:
time: 68.9 us; the launch traced here: 68.5 us
  starting transfers between devices  31.2 us (45%)
  Pallas kernels  20.2 us (29%)
  waiting for transfers between devices  16.8 us (24%)
    ppermute x5, starting transfers between devices, to_next(): return lax.ppermute(edge, 'row', down_pairs)  24.2 us
    pallas_call x16, Pallas kernels, call(): pl.pallas_call(kernel, out_shape=outs, in_specs=in_specs or [vmem_spec()]...  20.2 us
    ppermute x5, waiting for transfers between devices, to_previous(): return lax.ppermute(edge, 'row', up_pairs)  9.1 us
    ppermute x5, waiting for transfers between devices, to_next(): return lax.ppermute(edge, 'row', down_pairs)  7.74 us
    ppermute x5, starting transfers between devices, to_previous(): return lax.ppermute(edge, 'row', up_pairs)  6.46 us
  transfers between devices with their start and end apart: 11, of which 5 were waited for; matrix products, arithmetic and copies ran while one was open for 0% of the time, Pallas kernels for 23%

profile of v6, /device:TPU:0, one launch (start us, length us, event | category | flops | bytes accessed | tf_op | source)
XLA Modules:
  0.0 68.5 jit_solution(4808455340695007445)
XLA Ops:
  0.0 1.7 %load.1 = (f32[2,2,8,4224]{3,2,1,0:T(8,128)S(1)}, f32[2,2,8,4224]{3,2,1,0:T(8,128)S(1)}, f32[2,8,4224]{2,1,0:T(8,128)S(1)}, f32[9,8,4224]{2,1,0:T(8,128)S(1)}) custom-call(f32[2,2,8,8192]{3,2,1,0:T(8,128)} %probes_ref.1, f32[2,8,8192]{2,1,0:T(8,128)} %observed_ref.1, f32[9,8,8192]{2,1,0:T(8,128)} %coefficients_ref.1), custom_call_target="tpu_custom_call" | custom-call | flops 2048000 | bytes 1638400 | tf_op jit(solution)/shard_map/load/pallas_call | solution.py:521
  1.7 0.5 collective-permute-start
  2.2 1.0 %prep.1 = (f32[5,33,64,128]{3,2,1,0:T(8,128)S(1)}, f32[47,8,128]{2,1,0:T(8,128)S(1)}, f32[47,8,128]{2,1,0:T(8,128)S(1)}) custom-call(f32[9,8,4224]{2,1,0:T(8,128)S(1)} %get-tuple-element.37.window_ref, f32[2,8,4224]{2,1,0:T(8,128)S(1)} %get-tuple-element.38.seen_ref), custom_call_target="tpu_custom_call" | custom-call | flops 27033600 | bytes 21626880 | tf_op jit(solution)/shard_map/prep/pallas_call | solution.py:521
  3.3 4.4 %collective-permute-start.2 = (f32[47,8,128]{2,1,0:T(8,128)S(1)}, f32[47,8,128]{2,1,0:T(8,128)S(1)}, u32[]{:S(2)}, u32[]{:S(2)}) collective-permute-start(f32[47,8,128]{2,1,0:T(8,128)S(1)} %get-tuple-element.45), channel_id=1, source_target_pairs={{0,2},{2,4},{4,6},{6,8},{8,10},{10,12},{12,14},{1,3},{3,5},{5,7},{... | collective-permute-start | bytes 577544 | tf_op jit(solution)/shard_map/ppermute | solution.py:515
  7.7 1.3 %collective-permute-start.3 = (f32[47,8,128]{2,1,0:T(8,128)S(1)}, f32[47,8,128]{2,1,0:T(8,128)S(1)}, u32[]{:S(2)}, u32[]{:S(2)}) collective-permute-start(f32[47,8,128]{2,1,0:T(8,128)S(1)} %get-tuple-element.46), channel_id=1, source_target_pairs={{2,0},{4,2},{6,4},{8,6},{10,8},{12,10},{14,12},{3,1},{5,3},{7,5},{... | collective-permute-start | bytes 577544 | tf_op jit(solution)/shard_map/ppermute | solution.py:518
  9.0 0.0 collective-permute-done.other_ref
  9.0 0.2 layout.1
  9.2 1.3 %collective-permute-start.5 = (f32[33,8,128]{2,1,0:T(8,128)S(1)}, f32[33,8,128]{2,1,0:T(8,128)S(1)}, u32[]{:S(2)}, u32[]{:S(2)}) collective-permute-start(f32[33,8,128]{2,1,0:T(8,128)S(1)} %get-tuple-element.49), channel_id=1, source_target_pairs={{2,0},{4,2},{6,4},{8,6},{10,8},{12,10},{14,12},{3,1},{5,3},{7,5},{... | collective-permute-start | bytes 405512 | tf_op jit(solution)/shard_map/ppermute | solution.py:518
  10.5 5.2 %collective-permute-start.1 = (f32[33,8,128]{2,1,0:T(8,128)S(1)}, f32[33,8,128]{2,1,0:T(8,128)S(1)}, u32[]{:S(2)}, u32[]{:S(2)}) collective-permute-start(f32[33,8,128]{2,1,0:T(8,128)S(1)} %get-tuple-element.42), channel_id=1, source_target_pairs={{0,2},{2,4},{4,6},{6,8},{8,10},{10,12},{12,14},{1,3},{3,5},{5,7},{... | collective-permute-start | bytes 405512 | tf_op jit(solution)/shard_map/ppermute | solution.py:515
  15.7 0.0 collective-permute-done.2.up_ref
  15.7 1.5 %collective-permute-done.3.down_ref = f32[47,8,128]{2,1,0:T(8,128)S(1)} collective-permute-done((f32[47,8,128]{2,1,0:T(8,128)S(1)}, f32[47,8,128]{2,1,0:T(8,128)S(1)}, u32[]{:S(2)}, u32[]{:S(2)}) %collective-permute-start.3) | collective-permute-done | bytes 192544 | tf_op jit(solution)/shard_map/ppermute | solution.py:518
  17.2 1.1 %border.1 = (f32[33,9,8,128]{3,2,1,0:T(8,128)S(1)}, f32[5,33,8,128]{3,2,1,0:T(8,128)S(1)}, f32[5,33,8,128]{3,2,1,0:T(8,128)S(1)}) custom-call(f32[2,8,4224]{2,1,0:T(8,128)S(1)} %get-tuple-element.38.seen_ref, f32[47,8,128]{2,1,0:T(8,128)S(1)} %collective-permute-done.2.up_ref, f32[47,8,128]{2,1,0:T(8,128)S(1)} %collective-permute-done.3.down_ref), custom_call_target="tpu_custom_call" | custom-call | flops 6082560 | bytes 4866048 | tf_op jit(solution)/shard_map/border/pallas_call | solution.py:521
  18.4 1.0 %collective-permute-done.5.refs_0_.refs_1_ = f32[33,8,128]{2,1,0:T(8,128)S(1)} collective-permute-done((f32[33,8,128]{2,1,0:T(8,128)S(1)}, f32[33,8,128]{2,1,0:T(8,128)S(1)}, u32[]{:S(2)}, u32[]{:S(2)}) %collective-permute-start.5) | collective-permute-done | bytes 135200 | tf_op jit(solution)/shard_map/ppermute | solution.py:518
  19.4 0.5 first.4.refs_4_.refs_5_
  19.9 4.5 %collective-permute-start.7 = (f32[66,8,128]{2,1,0:T(8,128)S(1)}, f32[66,8,128]{2,1,0:T(8,128)S(1)}, u32[]{:S(2)}, u32[]{:S(2)}) collective-permute-start(f32[66,8,128]{2,1,0:T(8,128)S(1)} %first.4.refs_4_.refs_5_), channel_id=1, source_target_pairs={{0,2},{2,4},{4,6},{6,8},{8,10},{10,12},{12,14},{1,3},{3,5},{5,7},{... | collective-permute-start | bytes 811016 | tf_op jit(solution)/shard_map/ppermute | solution.py:515
  24.4 0.0 collective-permute-done.1.refs_0_.refs_1_
  24.4 0.5 first.3.refs_2_.refs_5_
  24.9 1.3 %collective-permute-start.4 = (f32[66,8,128]{2,1,0:T(8,128)S(1)}, f32[66,8,128]{2,1,0:T(8,128)S(1)}, u32[]{:S(2)}, u32[]{:S(2)}) collective-permute-start(f32[66,8,128]{2,1,0:T(8,128)S(1)} %first.3.refs_2_.refs_5_), channel_id=1, source_target_pairs={{2,0},{4,2},{6,4},{8,6},{10,8},{12,10},{14,12},{3,1},{5,3},{7,5},{... | collective-permute-start | bytes 811016 | tf_op jit(solution)/shard_map/ppermute | solution.py:518
  26.2 0.7 first.5.refs_3_
  26.9 1.5 %middle.2 = (f32[33,48,128]{2,1,0:T(8,128)S(1)}, f32[33,32,128]{2,1,0:T(8,128)S(1)}) custom-call(f32[33,64,128]{2,1,0:T(8,128)S(1)} %get-tuple-element.43.refs_1_.refs_0_.refs_2_, f32[5,33,64,128]{3,2,1,0:T(8,128)S(1)} %get-tuple-element.48.refs_2_.refs_1_.refs_3_, f32[66,8,128]{2,1,0:T(8,128)S(1)} %first.3.refs_2_.refs_5_, ...), custom_call_target="tpu_custom_call" | custom-call | flops 6758400 | bytes 5406720 | tf_op jit(solution)/shard_map/middle/pallas_call | solution.py:521
  28.5 1.1 %collective-permute-done.7.refs_0_ = f32[66,8,128]{2,1,0:T(8,128)S(1)} collective-permute-done((f32[66,8,128]{2,1,0:T(8,128)S(1)}, f32[66,8,128]{2,1,0:T(8,128)S(1)}, u32[]{:S(2)}, u32[]{:S(2)}) %collective-permute-start.7) | collective-permute-done | bytes 270368 | tf_op jit(solution)/shard_map/ppermute | solution.py:515
  29.6 1.0 %upper.2 = (f32[33,16,128]{2,1,0:T(8,128)S(1)}, f32[66,8,128]{2,1,0:T(8,128)S(1)}) custom-call(f32[66,8,128]{2,1,0:T(8,128)S(1)} %collective-permute-done.7.refs_0_, f32[33,8,128]{2,1,0:T(8,128)S(1)} %collective-permute-done.1.refs_0_.refs_1_, f32[33,64,128]{2,1,0:T(8,128)S(1)} %get-tuple-element.43.refs_1_.refs_0_.refs_2_, ...), custom_call_target="tpu_custom_call" | custom-call | flops 2703360 | bytes 2162688 | tf_op jit(solution)/shard_map/upper/pallas_call | solution.py:521
  30.6 1.3 %collective-permute-start.9 = (f32[66,8,128]{2,1,0:T(8,128)S(1)}, f32[66,8,128]{2,1,0:T(8,128)S(1)}, u32[]{:S(2)}, u32[]{:S(2)}) collective-permute-start(f32[66,8,128]{2,1,0:T(8,128)S(1)} %get-tuple-element.54.refs_2_.refs_5_), channel_id=1, source_target_pairs={{2,0},{4,2},{6,4},{8,6},{10,8},{12,10},{14,12},{3,1},{5,3},{7,5},{... | collective-permute-start | bytes 811016 | tf_op jit(solution)/shard_map/ppermute | solution.py:518
  31.9 6.6 %collective-permute-done.4.refs_0_ = f32[66,8,128]{2,1,0:T(8,128)S(1)} collective-permute-done((f32[66,8,128]{2,1,0:T(8,128)S(1)}, f32[66,8,128]{2,1,0:T(8,128)S(1)}, u32[]{:S(2)}, u32[]{:S(2)}) %collective-permute-start.4) | collective-permute-done | bytes 270368 | tf_op jit(solution)/shard_map/ppermute | solution.py:518
  38.5 1.0 %lower.2 = (f32[33,16,128]{2,1,0:T(8,128)S(1)}, f32[66,8,128]{2,1,0:T(8,128)S(1)}) custom-call(f32[66,8,128]{2,1,0:T(8,128)S(1)} %collective-permute-done.4.refs_0_, f32[33,8,128]{2,1,0:T(8,128)S(1)} %collective-permute-done.5.refs_0_.refs_1_, f32[33,64,128]{2,1,0:T(8,128)S(1)} %get-tuple-element.43.refs_1_.refs_0_.refs_2_, ...), custom_call_target="tpu_custom_call" | custom-call | flops 2703360 | bytes 2162688 | tf_op jit(solution)/shard_map/lower/pallas_call | solution.py:521
  39.6 4.6 %collective-permute-start.6 = (f32[66,8,128]{2,1,0:T(8,128)S(1)}, f32[66,8,128]{2,1,0:T(8,128)S(1)}, u32[]{:S(2)}, u32[]{:S(2)}) collective-permute-start(f32[66,8,128]{2,1,0:T(8,128)S(1)} %get-tuple-element.52.refs_4_.refs_5_), channel_id=1, source_target_pairs={{0,2},{2,4},{4,6},{6,8},{8,10},{10,12},{12,14},{1,3},{3,5},{5,7},{... | collective-permute-start | bytes 811016 | tf_op jit(solution)/shard_map/ppermute | solution.py:515
  44.1 1.6 %middle.3 = (f32[33,48,128]{2,1,0:T(8,128)S(1)}, f32[33,32,128]{2,1,0:T(8,128)S(1)}) custom-call(f32[33,64,128]{2,1,0:T(8,128)S(1)} %get-tuple-element.43.refs_1_.refs_0_.refs_2_, f32[5,33,64,128]{3,2,1,0:T(8,128)S(1)} %get-tuple-element.48.refs_2_.refs_1_.refs_3_, f32[66,8,128]{2,1,0:T(8,128)S(1)} %get-tuple-element.54.refs_2_.refs_5_, ...), custom_call_target="tpu_custom_call" | custom-call | flops 6758400 | bytes 5406720 | tf_op jit(solution)/shard_map/middle/pallas_call | solution.py:521
  45.7 0.0 collective-permute-done.9.refs_0_
  45.7 1.1 %lower.3 = (f32[33,16,128]{2,1,0:T(8,128)S(1)}, f32[66,8,128]{2,1,0:T(8,128)S(1)}) custom-call(f32[66,8,128]{2,1,0:T(8,128)S(1)} %collective-permute-done.9.refs_0_, f32[33,8,128]{2,1,0:T(8,128)S(1)} %collective-permute-done.5.refs_0_.refs_1_, f32[33,64,128]{2,1,0:T(8,128)S(1)} %get-tuple-element.43.refs_1_.refs_0_.refs_2_, ...), custom_call_target="tpu_custom_call" | custom-call | flops 2703360 | bytes 2162688 | tf_op jit(solution)/shard_map/lower/pallas_call | solution.py:521
  46.8 5.6 %collective-permute-start.10 = (f32[66,8,128]{2,1,0:T(8,128)S(1)}, f32[66,8,128]{2,1,0:T(8,128)S(1)}, u32[]{:S(2)}, u32[]{:S(2)}) collective-permute-start(f32[66,8,128]{2,1,0:T(8,128)S(1)} %get-tuple-element.60.refs_4_.refs_5_), channel_id=1, source_target_pairs={{0,2},{2,4},{4,6},{6,8},{8,10},{10,12},{12,14},{1,3},{3,5},{5,7},{... | collective-permute-start | bytes 811016 | tf_op jit(solution)/shard_map/ppermute | solution.py:515
  52.4 0.0 collective-permute-done.6.refs_0_
  52.4 1.1 %upper.3 = (f32[33,16,128]{2,1,0:T(8,128)S(1)}, f32[66,8,128]{2,1,0:T(8,128)S(1)}) custom-call(f32[66,8,128]{2,1,0:T(8,128)S(1)} %collective-permute-done.6.refs_0_, f32[33,8,128]{2,1,0:T(8,128)S(1)} %collective-permute-done.1.refs_0_.refs_1_, f32[33,64,128]{2,1,0:T(8,128)S(1)} %get-tuple-element.43.refs_1_.refs_0_.refs_2_, ...), custom_call_target="tpu_custom_call" | custom-call | flops 2703360 | bytes 2162688 | tf_op jit(solution)/shard_map/upper/pallas_call | solution.py:521
  53.5 1.3 %collective-permute-start.8 = (f32[66,8,128]{2,1,0:T(8,128)S(1)}, f32[66,8,128]{2,1,0:T(8,128)S(1)}, u32[]{:S(2)}, u32[]{:S(2)}) collective-permute-start(f32[66,8,128]{2,1,0:T(8,128)S(1)} %get-tuple-element.58.refs_2_.refs_5_), channel_id=1, source_target_pairs={{2,0},{4,2},{6,4},{8,6},{10,8},{12,10},{14,12},{3,1},{5,3},{7,5},{... | collective-permute-start | bytes 811016 | tf_op jit(solution)/shard_map/ppermute | solution.py:518
  54.8 2.4 %gradient.1 = (f32[33,48,128]{2,1,0:T(8,128)S(1)}, f32[9,8,4096]{2,1,0:T(8,128)S(1)}) custom-call(f32[33,64,128]{2,1,0:T(8,128)S(1)} %get-tuple-element.43.refs_1_.refs_0_.refs_2_, f32[5,33,64,128]{3,2,1,0:T(8,128)S(1)} %get-tuple-element.48.refs_2_.refs_1_.refs_3_, f32[66,8,128]{2,1,0:T(8,128)S(1)} %get-tuple-element.58.refs_2_.refs_5_, ...), custom_call_target="tpu_custom_call" | custom-call | flops 16220160 | bytes 12976128 | tf_op jit(solution)/shard_map/gradient/pallas_call | solution.py:521
  57.2 6.6 %collective-permute-done.10.refs_0_ = f32[66,8,128]{2,1,0:T(8,128)S(1)} collective-permute-done((f32[66,8,128]{2,1,0:T(8,128)S(1)}, f32[66,8,128]{2,1,0:T(8,128)S(1)}, u32[]{:S(2)}, u32[]{:S(2)}) %collective-permute-start.10) | collective-permute-done | bytes 270368 | tf_op jit(solution)/shard_map/ppermute | solution.py:515
  63.8 2.0 %upper_end.1.refs_8_ = f32[9,8,4096]{2,1,0:T(8,128)S(1)} custom-call(f32[66,8,128]{2,1,0:T(8,128)S(1)} %collective-permute-done.10.refs_0_, f32[33,8,128]{2,1,0:T(8,128)S(1)} %collective-permute-done.1.refs_0_.refs_1_, f32[33,64,128]{2,1,0:T(8,128)S(1)} %get-tuple-element.43.refs_1_.refs_0_.refs_2_, ...), custom_call_target="tpu_custom_call" | custom-call | flops 5406720 | bytes 4325376 | tf_op jit(solution)/shard_map/upper_end/pallas_call | solution.py:521
  65.7 0.0 collective-permute-done.8.refs_0_
  65.7 2.8 %lower_end.1 = f32[9,8,4096]{2,1,0:T(8,128)} custom-call(f32[66,8,128]{2,1,0:T(8,128)S(1)} %collective-permute-done.8.refs_0_, f32[33,8,128]{2,1,0:T(8,128)S(1)} %collective-permute-done.5.refs_0_.refs_1_, f32[33,64,128]{2,1,0:T(8,128)S(1)} %get-tuple-element.43.refs_1_.refs_0_.refs_2_, f32[5,33,64,128]{3,2,1,0:T(8,128)S(1)} %get-tuple-element.48.refs_2_.refs_1_.refs_3_, ...), custom_call_target="tpu_custom_call" | custom-call | flops 5406720 | bytes 4325376 | tf_op jit(solution)/shard_map/lower_end/pallas_call | solution.py:521
Async XLA Ops:
  1.7 7.3 %collective-permute-start = (f32[2,2,8,4224]{3,2,1,0:T(8,128)S(1)}, f32[2,2,8,4224]{3,2,1,0:T(8,128)S(1)}, u32[]{:S(2)}, u32[]{:S(2)}) collective-permute-start(f32[2,2,8,4224]{3,2,1,0:T(8,128)S(1)} %get-tuple-element.41), channel_id=1, source_target_pairs={{0,1},{1,0},{2,3},{3,2},{4,5},{5,4},{6,7},{7,6},{8,9},{9,8},{10,11... | collective-permute-start | bytes 1622024 | tf_op jit(solution)/shard_map/ppermute | solution.py:549
  3.3 12.5 %collective-permute-start.2 = (f32[47,8,128]{2,1,0:T(8,128)S(1)}, f32[47,8,128]{2,1,0:T(8,128)S(1)}, u32[]{:S(2)}, u32[]{:S(2)}) collective-permute-start(f32[47,8,128]{2,1,0:T(8,128)S(1)} %get-tuple-element.45), channel_id=1, source_target_pairs={{0,2},{2,4},{4,6},{6,8},{8,10},{10,12},{12,14},{1,3},{3,5},{5,7},{... | collective-permute-start | bytes 577544 | tf_op jit(solution)/shard_map/ppermute | solution.py:515
  7.7 9.5 %collective-permute-start.3 = (f32[47,8,128]{2,1,0:T(8,128)S(1)}, f32[47,8,128]{2,1,0:T(8,128)S(1)}, u32[]{:S(2)}, u32[]{:S(2)}) collective-permute-start(f32[47,8,128]{2,1,0:T(8,128)S(1)} %get-tuple-element.46), channel_id=1, source_target_pairs={{2,0},{4,2},{6,4},{8,6},{10,8},{12,10},{14,12},{3,1},{5,3},{7,5},{... | collective-permute-start | bytes 577544 | tf_op jit(solution)/shard_map/ppermute | solution.py:518
  9.2 10.2 %collective-permute-start.5 = (f32[33,8,128]{2,1,0:T(8,128)S(1)}, f32[33,8,128]{2,1,0:T(8,128)S(1)}, u32[]{:S(2)}, u32[]{:S(2)}) collective-permute-start(f32[33,8,128]{2,1,0:T(8,128)S(1)} %get-tuple-element.49), channel_id=1, source_target_pairs={{2,0},{4,2},{6,4},{8,6},{10,8},{12,10},{14,12},{3,1},{5,3},{7,5},{... | collective-permute-start | bytes 405512 | tf_op jit(solution)/shard_map/ppermute | solution.py:518
  10.5 13.9 %collective-permute-start.1 = (f32[33,8,128]{2,1,0:T(8,128)S(1)}, f32[33,8,128]{2,1,0:T(8,128)S(1)}, u32[]{:S(2)}, u32[]{:S(2)}) collective-permute-start(f32[33,8,128]{2,1,0:T(8,128)S(1)} %get-tuple-element.42), channel_id=1, source_target_pairs={{0,2},{2,4},{4,6},{6,8},{8,10},{10,12},{12,14},{1,3},{3,5},{5,7},{... | collective-permute-start | bytes 405512 | tf_op jit(solution)/shard_map/ppermute | solution.py:515
  19.9 9.7 %collective-permute-start.7 = (f32[66,8,128]{2,1,0:T(8,128)S(1)}, f32[66,8,128]{2,1,0:T(8,128)S(1)}, u32[]{:S(2)}, u32[]{:S(2)}) collective-permute-start(f32[66,8,128]{2,1,0:T(8,128)S(1)} %first.4.refs_4_.refs_5_), channel_id=1, source_target_pairs={{0,2},{2,4},{4,6},{6,8},{8,10},{10,12},{12,14},{1,3},{3,5},{5,7},{... | collective-permute-start | bytes 811016 | tf_op jit(solution)/shard_map/ppermute | solution.py:515
  24.9 13.6 %collective-permute-start.4 = (f32[66,8,128]{2,1,0:T(8,128)S(1)}, f32[66,8,128]{2,1,0:T(8,128)S(1)}, u32[]{:S(2)}, u32[]{:S(2)}) collective-permute-start(f32[66,8,128]{2,1,0:T(8,128)S(1)} %first.3.refs_2_.refs_5_), channel_id=1, source_target_pairs={{2,0},{4,2},{6,4},{8,6},{10,8},{12,10},{14,12},{3,1},{5,3},{7,5},{... | collective-permute-start | bytes 811016 | tf_op jit(solution)/shard_map/ppermute | solution.py:518
  30.6 15.0 %collective-permute-start.9 = (f32[66,8,128]{2,1,0:T(8,128)S(1)}, f32[66,8,128]{2,1,0:T(8,128)S(1)}, u32[]{:S(2)}, u32[]{:S(2)}) collective-permute-start(f32[66,8,128]{2,1,0:T(8,128)S(1)} %get-tuple-element.54.refs_2_.refs_5_), channel_id=1, source_target_pairs={{2,0},{4,2},{6,4},{8,6},{10,8},{12,10},{14,12},{3,1},{5,3},{7,5},{... | collective-permute-start | bytes 811016 | tf_op jit(solution)/shard_map/ppermute | solution.py:518
  39.6 12.8 %collective-permute-start.6 = (f32[66,8,128]{2,1,0:T(8,128)S(1)}, f32[66,8,128]{2,1,0:T(8,128)S(1)}, u32[]{:S(2)}, u32[]{:S(2)}) collective-permute-start(f32[66,8,128]{2,1,0:T(8,128)S(1)} %get-tuple-element.52.refs_4_.refs_5_), channel_id=1, source_target_pairs={{0,2},{2,4},{4,6},{6,8},{8,10},{10,12},{12,14},{1,3},{3,5},{5,7},{... | collective-permute-start | bytes 811016 | tf_op jit(solution)/shard_map/ppermute | solution.py:515
  46.8 17.0 %collective-permute-start.10 = (f32[66,8,128]{2,1,0:T(8,128)S(1)}, f32[66,8,128]{2,1,0:T(8,128)S(1)}, u32[]{:S(2)}, u32[]{:S(2)}) collective-permute-start(f32[66,8,128]{2,1,0:T(8,128)S(1)} %get-tuple-element.60.refs_4_.refs_5_), channel_id=1, source_target_pairs={{0,2},{2,4},{4,6},{6,8},{8,10},{10,12},{12,14},{1,3},{3,5},{5,7},{... | collective-permute-start | bytes 811016 | tf_op jit(solution)/shard_map/ppermute | solution.py:515
  53.5 12.3 %collective-permute-start.8 = (f32[66,8,128]{2,1,0:T(8,128)S(1)}, f32[66,8,128]{2,1,0:T(8,128)S(1)}, u32[]{:S(2)}, u32[]{:S(2)}) collective-permute-start(f32[66,8,128]{2,1,0:T(8,128)S(1)} %get-tuple-element.58.refs_2_.refs_5_), channel_id=1, source_target_pairs={{2,0},{4,2},{6,4},{8,6},{10,8},{12,10},{14,12},{3,1},{5,3},{7,5},{... | collective-permute-start | bytes 811016 | tf_op jit(solution)/shard_map/ppermute | solution.py:518

commit v7 on v6

--- a/solution.py
+++ b/solution.py
@@ -73,21 +73,40 @@
     return max(count for count in range(1, 12) if tiles % count == 0)
 
 
-def load_kernel(width, probes_ref, observed_ref, coefficients_ref, theirs_ref, own_ref, seen_ref, window_ref, sem):
+def load_kernel(width, probes_ref, observed_ref, coefficients_ref, *refs):
+    theirs_ref, own_ref, seen_ref, window_ref, top_ref, bottom_ref, eight, rest, observed, sem = refs
     core = lax.axis_index("probe")
     move = probes_ref.shape[3] - width
     mine = pl.ds(pl.multiple_of(core * move, LANES), width)
     other = pl.ds(pl.multiple_of((1 - core) * move, LANES), width)
     copies = [
-        pltpu.make_async_copy(probes_ref.at[:, :, :, other], theirs_ref, sem.at[0]),
-        pltpu.make_async_copy(probes_ref.at[:, :, :, mine], own_ref, sem.at[1]),
-        pltpu.make_async_copy(coefficients_ref.at[:, :, mine], window_ref, sem.at[2]),
-        pltpu.make_async_copy(observed_ref.at[:, :, mine], seen_ref, sem.at[3]),
+        pltpu.make_async_copy(coefficients_ref.at[:, :, mine], window_ref, sem.at[0]),
+        pltpu.make_async_copy(observed_ref.at[:, :, mine], seen_ref, sem.at[1]),
+        pltpu.make_async_copy(probes_ref.at[:, :, :, other], theirs_ref, sem.at[2]),
+        pltpu.make_async_copy(probes_ref.at[:, :, :, mine], own_ref, sem.at[3]),
     ]
     for copy in copies:
         copy.start()
-    for copy in copies:
-        copy.wait()
+    rest[...] = jnp.zeros_like(rest)
+    observed[...] = jnp.zeros_like(observed)
+    copies[0].wait()
+    copies[1].wait()
+    tiles = width // LANES
+    for tile in range(tiles):
+        cols = pl.ds(tile * LANES, LANES)
+        for channel in range(8):
+            eight[tile, pl.ds(channel, SUBS, stride=SUBS), :] = window_ref[channel, :, cols]
+        rest[tile // 8, pl.ds(tile % 8, SUBS, stride=SUBS), :] = window_ref[8, :, cols]
+        for c in range(2):
+            observed[tile // 4, pl.ds(2 * (tile % 4) + c, SUBS, stride=SUBS), :] = seen_ref[c, :, cols]
+    base = 0
+    for source in (eight, rest, observed):
+        for index in range(source.shape[0]):
+            top_ref[base + index] = source[index, sub(0), :]
+            bottom_ref[base + index] = source[index, sub(SUBS - 1), :]
+        base += source.shape[0]
+    copies[2].wait()
+    copies[3].wait()
 
 
 def combine(kappa, across, along, skew, coupling):
@@ -102,11 +121,9 @@
     )
 
 
-def prep_kernel(window_ref, seen_ref, expanded_ref, top_ref, bottom_ref, eight, rest, observed):
+def prep_kernel(window_ref, expanded_ref):
     tiles = expanded_ref.shape[1]
     chunk = chunk_of(tiles)
-    rest[...] = jnp.zeros_like(rest)
-    observed[...] = jnp.zeros_like(observed)
 
     def body(step, carry):
         for k in range(chunk):
@@ -118,24 +135,9 @@
                 for kind, value in enumerate(values):
                     for probe in range(4):
                         expanded_ref[kind, tile, pl.ds(4 * c + probe, SUBS, stride=SUBS), :] = value
-            for channel in range(8):
-                eight[tile, pl.ds(channel, SUBS, stride=SUBS), :] = raw[channel]
-            top_ref[tile] = eight[tile, sub(0), :]
-            bottom_ref[tile] = eight[tile, sub(SUBS - 1), :]
         return carry
 
     lax.fori_loop(0, tiles // chunk, body, 0)
-    for tile in range(tiles):
-        cols = pl.ds(tile * LANES, LANES)
-        rest[tile // 8, pl.ds(tile % 8, SUBS, stride=SUBS), :] = window_ref[8, :, cols]
-        for c in range(2):
-            observed[tile // 4, pl.ds(2 * (tile % 4) + c, SUBS, stride=SUBS), :] = seen_ref[c, :, cols]
-    base = tiles
-    for source in (rest, observed):
-        for index in range(source.shape[0]):
-            top_ref[base + index] = source[index, sub(0), :]
-            bottom_ref[base + index] = source[index, sub(SUBS - 1), :]
-        base += source.shape[0]
 
 
 def layout_kernel(own_ref, other_ref, z_ref, top_ref, bottom_ref):
@@ -408,22 +410,17 @@
     lax.fori_loop(0, kept // count, body, 0)
 
 
-def end_kernel(upper, constants, tiles, factor, *refs):
-    halo_ref, z_halo_ref, z_ref, expanded_ref, rim_ref, edge_ref, inner_ref, older_ref, part_ref = refs[:9]
-    if upper:
-        out_ref, once_ref, products = refs[9:]
-        target = out_ref
-    else:
-        out_ref, once_ref, products, target, sem = refs[9:]
-    edge_product(
-        upper, constants, tiles, halo_ref, z_halo_ref, z_ref, expanded_ref, rim_ref, edge_ref, older_ref, once_ref
-    )
-    low = -1 if upper else 7
-
+def end_kernel(upper, constants, tiles, *refs):
+    edge_product(upper, constants, tiles, *refs)
+
+
+def finish_kernel(tiles, factor, z_ref, over_ref, inner_ref, under_ref, part_ref, out_ref, products, target, sem):
     def series(row, tile):
-        if 1 <= row <= 6:
-            return inner_ref[tile, sub(row - 1), :]
-        return once_ref[tile, sub(row - low), :]
+        if row < 1:
+            return over_ref[tile, sub(row + 1), :]
+        if row > 6:
+            return under_ref[tile, sub(row - 7), :]
+        return inner_ref[tile, sub(row - 1), :]
 
     kept = target.shape[2] // LANES
     offset = lax.axis_index("probe") * (tiles - kept)
@@ -433,7 +430,8 @@
     def body(step, carry):
         for k in range(count):
             tile = step * count + k + offset
-            gradient_rows(0 if upper else 6, 2, tile, k, series, z_ref, factor, tiles, products)
+            for low in (0, 6):
+                gradient_rows(low, 2, tile, k, series, z_ref, factor, tiles, products)
         for k in range(count):
             cols = tile_columns(step * count + k)
 
@@ -444,9 +442,6 @@
         return carry
 
     steps = kept // count
-    if upper:
-        lax.fori_loop(0, steps, body, 0)
-        return
     groups = sem.shape[0]
     copies = []
     for group in range(groups):
@@ -529,7 +524,9 @@
             name=name,
         )(*operands)
 
-    theirs, own, seen, window = call(
+    eights, fours = -(-tiles // 8), -(-tiles // 4)
+    edge_shape = pltpu.VMEM((tiles + eights + fours, SUBS, LANES), f32)
+    theirs, own, seen, window, edge_top, edge_bottom = call(
         functools.partial(load_kernel, width),
         "load",
         100,
@@ -542,22 +539,18 @@
             pltpu.VMEM((2, 2, SUBS, width), f32),
             pltpu.VMEM((2, SUBS, width), f32),
             pltpu.VMEM((9, SUBS, width), f32),
+            edge_shape,
+            edge_shape,
         ],
-        [pltpu.SemaphoreType.DMA((4,))],
+        [pltpu.VMEM((count, SUBS * SUBS, LANES), f32) for count in (tiles, eights, fours)]
+        + [pltpu.SemaphoreType.DMA((4,))],
         [pl.BlockSpec(memory_space=pltpu.HBM)] * 3,
     )
     other = lax.ppermute(theirs, "probe", [(0, 1), (1, 0)])
-    eights, fours = -(-tiles // 8), -(-tiles // 4)
-    edge_shape = pltpu.VMEM((tiles + eights + fours, SUBS, LANES), f32)
-    expanded, edge_top, edge_bottom = call(
-        prep_kernel,
-        "prep",
-        5 * 8 * tiles,
-        (window, seen),
-        [pltpu.VMEM((5, tiles, SUBS * SUBS, LANES), f32), edge_shape, edge_shape],
-        [pltpu.VMEM((count, SUBS * SUBS, LANES), f32) for count in (tiles, eights, fours)],
-    )
     edges_down, edges_up = to_previous(edge_top), to_next(edge_bottom)
+    expanded = call(
+        prep_kernel, "prep", 5 * 8 * tiles, (window,), pltpu.VMEM((5, tiles, SUBS * SUBS, LANES), f32)
+    )
     own, expanded = lax.optimization_barrier((own, expanded))
     def rows_of(count):
         return pltpu.VMEM((tiles, count * SUBS, LANES), f32)
@@ -637,22 +630,27 @@
         [rows_of(6), pltpu.VMEM(whole, f32)],
         [products],
     )
-    part = call(
-        functools.partial(end_kernel, True, constants, tiles, factor),
-        "upper_end",
-        8 * tiles,
-        (up, z_up, z, expanded, rim_up, top, series, once[0], part),
-        pltpu.VMEM(whole, f32),
-        [rows_of(2), products],
-    )
+    ends = [
+        call(
+            functools.partial(end_kernel, upper, constants, tiles),
+            "upper_end" if upper else "lower_end",
+            2 * tiles,
+            operands,
+            rows_of(2),
+        )
+        for upper, operands in (
+            (True, (up, z_up, z, expanded, rim_up, top, once[0])),
+            (False, (down, z_down, z, expanded, rim_down, bottom, once[2])),
+        )
+    ]
     groups = max(n for n in range(1, 5) if kept // count % n == 0)
     return call(
-        functools.partial(end_kernel, False, constants, tiles, factor),
-        "lower_end",
-        8 * tiles,
-        (down, z_down, z, expanded, rim_down, bottom, series, once[2], part),
+        functools.partial(finish_kernel, tiles, factor),
+        "finish",
+        16 * tiles,
+        (z, ends[0], series, ends[1], part),
         jax.ShapeDtypeStruct(whole, f32),
-        [rows_of(2), products, pltpu.VMEM(whole, f32), pltpu.SemaphoreType.DMA((groups,))],
+        [products, pltpu.VMEM(whole, f32), pltpu.SemaphoreType.DMA((groups,))],
         None,
         pl.BlockSpec(memory_space=pltpu.HBM),
     )

time: 68.9 us -> 69.3 us (level)
  the two profiles are of different devices: /device:TPU:0 before, /device:TPU:8 now
where the time goes in v7:
time: 69.3 us; the launch traced here: 69 us
  starting transfers between devices  30.5 us (44%)
  waiting for transfers between devices  19.3 us (28%)
  Pallas kernels  18.9 us (27%)
    pallas_call x17, Pallas kernels, call(): pl.pallas_call(kernel, out_shape=outs, in_specs=in_specs or [vmem_spec()]...  18.9 us
    ppermute x5, starting transfers between devices, to_previous(): return lax.ppermute(edge, 'row', up_pairs)  16.2 us
    ppermute x5, starting transfers between devices, to_next(): return lax.ppermute(edge, 'row', down_pairs)  14.1 us
    ppermute x5, waiting for transfers between devices, to_previous(): return lax.ppermute(edge, 'row', up_pairs)  12.6 us
    ppermute x5, waiting for transfers between devices, to_next(): return lax.ppermute(edge, 'row', down_pairs)  6.69 us
  transfers between devices with their start and end apart: 11, of which 5 were waited for; matrix products, arithmetic and copies ran while one was open for 0% of the time, Pallas kernels for 21%

profile of v7, /device:TPU:8, one launch (start us, length us, event | category | flops | bytes accessed | tf_op | source)
XLA Modules:
  0.0 69.0 jit_solution(6211860505998203024)
XLA Ops:
  0.0 1.7 %load.1 = (f32[2,2,8,4224]{3,2,1,0:T(8,128)S(1)}, f32[2,2,8,4224]{3,2,1,0:T(8,128)S(1)}, f32[2,8,4224]{2,1,0:T(8,128)S(1)}, f32[9,8,4224]{2,1,0:T(8,128)S(1)}, f...) custom-call(f32[2,2,8,8192]{3,2,1,0:T(8,128)} %probes_ref.1, f32[2,8,8192]{2,1,0:T(8,128)} %observed_ref.1, ...), custom_call_target="tpu_custom_call" | custom-call | flops 2048000 | bytes 1638400 | tf_op jit(solution)/shard_map/load/pallas_call | solution.py:516
  1.7 0.1 collective-permute-start
  1.8 3.4 %collective-permute-start.2 = (f32[47,8,128]{2,1,0:T(8,128)S(1)}, f32[47,8,128]{2,1,0:T(8,128)S(1)}, u32[]{:S(2)}, u32[]{:S(2)}) collective-permute-start(f32[47,8,128]{2,1,0:T(8,128)S(1)} %get-tuple-element.43), channel_id=1, source_target_pairs={{0,2},{2,4},{4,6},{6,8},{8,10},{10,12},{12,14},{1,3},{3,5},{5,7},{... | collective-permute-start | bytes 577544 | tf_op jit(solution)/shard_map/ppermute | solution.py:510
  5.2 3.3 %collective-permute-start.3 = (f32[47,8,128]{2,1,0:T(8,128)S(1)}, f32[47,8,128]{2,1,0:T(8,128)S(1)}, u32[]{:S(2)}, u32[]{:S(2)}) collective-permute-start(f32[47,8,128]{2,1,0:T(8,128)S(1)} %get-tuple-element.44), channel_id=1, source_target_pairs={{2,0},{4,2},{6,4},{8,6},{10,8},{12,10},{14,12},{3,1},{5,3},{7,5},{... | collective-permute-start | bytes 577544 | tf_op jit(solution)/shard_map/ppermute | solution.py:513
  8.5 0.8 %prep.1.refs_2_.refs_1_.refs_3_ = f32[5,33,64,128]{3,2,1,0:T(8,128)S(1)} custom-call(f32[9,8,4224]{2,1,0:T(8,128)S(1)} %get-tuple-element.36.window_ref), custom_call_target="tpu_custom_call" | custom-call | flops 27033600 | bytes 21626880 | tf_op jit(solution)/shard_map/prep/pallas_call | solution.py:516
  9.4 0.0 collective-permute-done.other_ref
  9.4 0.2 layout.1
  9.6 2.5 %collective-permute-start.5 = (f32[33,8,128]{2,1,0:T(8,128)S(1)}, f32[33,8,128]{2,1,0:T(8,128)S(1)}, u32[]{:S(2)}, u32[]{:S(2)}) collective-permute-start(f32[33,8,128]{2,1,0:T(8,128)S(1)} %get-tuple-element.47), channel_id=1, source_target_pairs={{0,2},{2,4},{4,6},{6,8},{8,10},{10,12},{12,14},{1,3},{3,5},{5,7},{... | collective-permute-start | bytes 405512 | tf_op jit(solution)/shard_map/ppermute | solution.py:510
  12.1 4.2 %collective-permute-start.1 = (f32[33,8,128]{2,1,0:T(8,128)S(1)}, f32[33,8,128]{2,1,0:T(8,128)S(1)}, u32[]{:S(2)}, u32[]{:S(2)}) collective-permute-start(f32[33,8,128]{2,1,0:T(8,128)S(1)} %get-tuple-element.40), channel_id=1, source_target_pairs={{2,0},{4,2},{6,4},{8,6},{10,8},{12,10},{14,12},{3,1},{5,3},{7,5},{... | collective-permute-start | bytes 405512 | tf_op jit(solution)/shard_map/ppermute | solution.py:513
  16.4 0.0 collective-permute-done.2.up_ref
  16.4 2.5 %collective-permute-done.3.down_ref = f32[47,8,128]{2,1,0:T(8,128)S(1)} collective-permute-done((f32[47,8,128]{2,1,0:T(8,128)S(1)}, f32[47,8,128]{2,1,0:T(8,128)S(1)}, u32[]{:S(2)}, u32[]{:S(2)}) %collective-permute-start.3) | collective-permute-done | bytes 192544 | tf_op jit(solution)/shard_map/ppermute | solution.py:513
  18.9 1.1 %border.1 = (f32[33,9,8,128]{3,2,1,0:T(8,128)S(1)}, f32[5,33,8,128]{3,2,1,0:T(8,128)S(1)}, f32[5,33,8,128]{3,2,1,0:T(8,128)S(1)}) custom-call(f32[2,8,4224]{2,1,0:T(8,128)S(1)} %get-tuple-element.42.seen_ref, f32[47,8,128]{2,1,0:T(8,128)S(1)} %collective-permute-done.2.up_ref, f32[47,8,128]{2,1,0:T(8,128)S(1)} %collective-permute-done.3.down_ref), custom_call_target="tpu_custom_call" | custom-call | flops 6082560 | bytes 4866048 | tf_op jit(solution)/shard_map/border/pallas_call | solution.py:516
  20.0 0.0 collective-permute-done.5.refs_0_.refs_1_
  20.0 0.5 first.4.refs_2_.refs_5_
  20.5 1.9 %collective-permute-start.7 = (f32[66,8,128]{2,1,0:T(8,128)S(1)}, f32[66,8,128]{2,1,0:T(8,128)S(1)}, u32[]{:S(2)}, u32[]{:S(2)}) collective-permute-start(f32[66,8,128]{2,1,0:T(8,128)S(1)} %first.4.refs_2_.refs_5_), channel_id=1, source_target_pairs={{2,0},{4,2},{6,4},{8,6},{10,8},{12,10},{14,12},{3,1},{5,3},{7,5},{... | collective-permute-start | bytes 811016 | tf_op jit(solution)/shard_map/ppermute | solution.py:513
  22.5 0.0 collective-permute-done.1.refs_0_.refs_1_
  22.5 0.5 first.3.refs_4_.refs_5_
  23.0 3.9 %collective-permute-start.4 = (f32[66,8,128]{2,1,0:T(8,128)S(1)}, f32[66,8,128]{2,1,0:T(8,128)S(1)}, u32[]{:S(2)}, u32[]{:S(2)}) collective-permute-start(f32[66,8,128]{2,1,0:T(8,128)S(1)} %first.3.refs_4_.refs_5_), channel_id=1, source_target_pairs={{0,2},{2,4},{4,6},{6,8},{8,10},{10,12},{12,14},{1,3},{3,5},{5,7},{... | collective-permute-start | bytes 811016 | tf_op jit(solution)/shard_map/ppermute | solution.py:510
  26.9 0.7 %first.5.refs_3_ = f32[33,32,128]{2,1,0:T(8,128)S(1)} custom-call(f32[33,64,128]{2,1,0:T(8,128)S(1)} %get-tuple-element.39.refs_1_.refs_0_.refs_2_.z_ref, f32[5,33,64,128]{3,2,1,0:T(8,128)S(1)} %prep.1.refs_2_.refs_1_.refs_3_), custom_call_target="tpu_custom_call" | custom-call | flops 2703360 | bytes 2162688 | tf_op jit(solution)/shard_map/first/pallas_call | solution.py:516
  27.7 1.6 %middle.2 = (f32[33,48,128]{2,1,0:T(8,128)S(1)}, f32[33,32,128]{2,1,0:T(8,128)S(1)}) custom-call(f32[33,64,128]{2,1,0:T(8,128)S(1)} %get-tuple-element.39.refs_1_.refs_0_.refs_2_.z_ref, f32[5,33,64,128]{3,2,1,0:T(8,128)S(1)} %prep.1.refs_2_.refs_1_.refs_3_, f32[66,8,128]{2,1,0:T(8,128)S(1)} %first.4.refs_2_.refs_5_, f32[33,32,128]{2,1,0:T(8,128)S(1)} %first.5.refs_3_, ...), custom_call_target="tpu_custom_call" | custom-call | flops 6758400 | bytes 5406720 | tf_op jit(solution)/shard_map/middle/pallas_call | solution.py:516
  29.2 7.4 %collective-permute-done.7.refs_0_ = f32[66,8,128]{2,1,0:T(8,128)S(1)} collective-permute-done((f32[66,8,128]{2,1,0:T(8,128)S(1)}, f32[66,8,128]{2,1,0:T(8,128)S(1)}, u32[]{:S(2)}, u32[]{:S(2)}) %collective-permute-start.7) | collective-permute-done | bytes 270368 | tf_op jit(solution)/shard_map/ppermute | solution.py:513
  36.6 1.1 %lower.2 = (f32[33,16,128]{2,1,0:T(8,128)S(1)}, f32[66,8,128]{2,1,0:T(8,128)S(1)}) custom-call(f32[66,8,128]{2,1,0:T(8,128)S(1)} %collective-permute-done.7.refs_0_, f32[33,8,128]{2,1,0:T(8,128)S(1)} %collective-permute-done.1.refs_0_.refs_1_, f32[33,64,128]{2,1,0:T(8,128)S(1)} %get-tuple-element.39.refs_1_.refs_0_.refs_2_.z_ref, ...), custom_call_target="tpu_custom_call" | custom-call | flops 2703360 | bytes 2162688 | tf_op jit(solution)/shard_map/lower/pallas_call | solution.py:516
  37.7 1.9 %collective-permute-start.9 = (f32[66,8,128]{2,1,0:T(8,128)S(1)}, f32[66,8,128]{2,1,0:T(8,128)S(1)}, u32[]{:S(2)}, u32[]{:S(2)}) collective-permute-start(f32[66,8,128]{2,1,0:T(8,128)S(1)} %get-tuple-element.52.refs_4_.refs_5_), channel_id=1, source_target_pairs={{0,2},{2,4},{4,6},{6,8},{8,10},{10,12},{12,14},{1,3},{3,5},{5,7},{... | collective-permute-start | bytes 811016 | tf_op jit(solution)/shard_map/ppermute | solution.py:510
  39.6 0.0 collective-permute-done.4.refs_0_
  39.6 1.1 %upper.2 = (f32[33,16,128]{2,1,0:T(8,128)S(1)}, f32[66,8,128]{2,1,0:T(8,128)S(1)}) custom-call(f32[66,8,128]{2,1,0:T(8,128)S(1)} %collective-permute-done.4.refs_0_, f32[33,8,128]{2,1,0:T(8,128)S(1)} %collective-permute-done.5.refs_0_.refs_1_, f32[33,64,128]{2,1,0:T(8,128)S(1)} %get-tuple-element.39.refs_1_.refs_0_.refs_2_.z_ref, ...), custom_call_target="tpu_custom_call" | custom-call | flops 2703360 | bytes 2162688 | tf_op jit(solution)/shard_map/upper/pallas_call | solution.py:516
  40.7 4.8 %collective-permute-start.6 = (f32[66,8,128]{2,1,0:T(8,128)S(1)}, f32[66,8,128]{2,1,0:T(8,128)S(1)}, u32[]{:S(2)}, u32[]{:S(2)}) collective-permute-start(f32[66,8,128]{2,1,0:T(8,128)S(1)} %get-tuple-element.50.refs_2_.refs_5_), channel_id=1, source_target_pairs={{2,0},{4,2},{6,4},{8,6},{10,8},{12,10},{14,12},{3,1},{5,3},{7,5},{... | collective-permute-start | bytes 811016 | tf_op jit(solution)/shard_map/ppermute | solution.py:513
  45.5 1.6 %middle.3 = (f32[33,48,128]{2,1,0:T(8,128)S(1)}, f32[33,32,128]{2,1,0:T(8,128)S(1)}) custom-call(f32[33,64,128]{2,1,0:T(8,128)S(1)} %get-tuple-element.39.refs_1_.refs_0_.refs_2_.z_ref, f32[5,33,64,128]{3,2,1,0:T(8,128)S(1)} %prep.1.refs_2_.refs_1_.refs_3_, f32[66,8,128]{2,1,0:T(8,128)S(1)} %get-tuple-element.50.refs_2_.refs_5_, ...), custom_call_target="tpu_custom_call" | custom-call | flops 6758400 | bytes 5406720 | tf_op jit(solution)/shard_map/middle/pallas_call | solution.py:516
  47.1 0.9 %collective-permute-done.9.refs_0_ = f32[66,8,128]{2,1,0:T(8,128)S(1)} collective-permute-done((f32[66,8,128]{2,1,0:T(8,128)S(1)}, f32[66,8,128]{2,1,0:T(8,128)S(1)}, u32[]{:S(2)}, u32[]{:S(2)}) %collective-permute-start.9) | collective-permute-done | bytes 270368 | tf_op jit(solution)/shard_map/ppermute | solution.py:510
  48.1 1.1 %upper.3 = (f32[33,16,128]{2,1,0:T(8,128)S(1)}, f32[66,8,128]{2,1,0:T(8,128)S(1)}) custom-call(f32[66,8,128]{2,1,0:T(8,128)S(1)} %collective-permute-done.9.refs_0_, f32[33,8,128]{2,1,0:T(8,128)S(1)} %collective-permute-done.5.refs_0_.refs_1_, f32[33,64,128]{2,1,0:T(8,128)S(1)} %get-tuple-element.39.refs_1_.refs_0_.refs_2_.z_ref, ...), custom_call_target="tpu_custom_call" | custom-call | flops 2703360 | bytes 2162688 | tf_op jit(solution)/shard_map/upper/pallas_call | solution.py:516
  49.2 1.9 %collective-permute-start.10 = (f32[66,8,128]{2,1,0:T(8,128)S(1)}, f32[66,8,128]{2,1,0:T(8,128)S(1)}, u32[]{:S(2)}, u32[]{:S(2)}) collective-permute-start(f32[66,8,128]{2,1,0:T(8,128)S(1)} %get-tuple-element.58.refs_5_.refs_2_), channel_id=1, source_target_pairs={{2,0},{4,2},{6,4},{8,6},{10,8},{12,10},{14,12},{3,1},{5,3},{7,5},{... | collective-permute-start | bytes 811016 | tf_op jit(solution)/shard_map/ppermute | solution.py:513
  51.1 2.8 %collective-permute-done.6.refs_0_ = f32[66,8,128]{2,1,0:T(8,128)S(1)} collective-permute-done((f32[66,8,128]{2,1,0:T(8,128)S(1)}, f32[66,8,128]{2,1,0:T(8,128)S(1)}, u32[]{:S(2)}, u32[]{:S(2)}) %collective-permute-start.6) | collective-permute-done | bytes 270368 | tf_op jit(solution)/shard_map/ppermute | solution.py:513
  53.9 1.1 %lower.3 = (f32[33,16,128]{2,1,0:T(8,128)S(1)}, f32[66,8,128]{2,1,0:T(8,128)S(1)}) custom-call(f32[66,8,128]{2,1,0:T(8,128)S(1)} %collective-permute-done.6.refs_0_, f32[33,8,128]{2,1,0:T(8,128)S(1)} %collective-permute-done.1.refs_0_.refs_1_, f32[33,64,128]{2,1,0:T(8,128)S(1)} %get-tuple-element.39.refs_1_.refs_0_.refs_2_.z_ref, ...), custom_call_target="tpu_custom_call" | custom-call | flops 2703360 | bytes 2162688 | tf_op jit(solution)/shard_map/lower/pallas_call | solution.py:516
  54.9 2.4 %collective-permute-start.8 = (f32[66,8,128]{2,1,0:T(8,128)S(1)}, f32[66,8,128]{2,1,0:T(8,128)S(1)}, u32[]{:S(2)}, u32[]{:S(2)}) collective-permute-start(f32[66,8,128]{2,1,0:T(8,128)S(1)} %get-tuple-element.56.refs_4_.refs_5_), channel_id=1, source_target_pairs={{0,2},{2,4},{4,6},{6,8},{8,10},{10,12},{12,14},{1,3},{3,5},{5,7},{... | collective-permute-start | bytes 811016 | tf_op jit(solution)/shard_map/ppermute | solution.py:510
  57.3 2.4 %gradient.1 = (f32[33,48,128]{2,1,0:T(8,128)S(1)}, f32[9,8,4096]{2,1,0:T(8,128)S(1)}) custom-call(f32[33,64,128]{2,1,0:T(8,128)S(1)} %get-tuple-element.39.refs_1_.refs_0_.refs_2_.z_ref, f32[5,33,64,128]{3,2,1,0:T(8,128)S(1)} %prep.1.refs_2_.refs_1_.refs_3_, f32[66,8,128]{2,1,0:T(8,128)S(1)} %get-tuple-element.58.refs_5_.refs_2_, ...), custom_call_target="tpu_custom_call" | custom-call | flops 16220160 | bytes 12976128 | tf_op jit(solution)/shard_map/gradient/pallas_call | solution.py:516
  59.7 0.0 collective-permute-done.10.refs_0_
  59.8 0.5 lower_end.1.under_ref
  60.3 5.7 %collective-permute-done.8.refs_0_ = f32[66,8,128]{2,1,0:T(8,128)S(1)} collective-permute-done((f32[66,8,128]{2,1,0:T(8,128)S(1)}, f32[66,8,128]{2,1,0:T(8,128)S(1)}, u32[]{:S(2)}, u32[]{:S(2)}) %collective-permute-start.8) | collective-permute-done | bytes 270368 | tf_op jit(solution)/shard_map/ppermute | solution.py:510
  66.0 0.5 upper_end.1.over_ref
  66.6 2.4 %finish.1 = f32[9,8,4096]{2,1,0:T(8,128)} custom-call(f32[33,64,128]{2,1,0:T(8,128)S(1)} %get-tuple-element.39.refs_1_.refs_0_.refs_2_.z_ref, f32[33,16,128]{2,1,0:T(8,128)S(1)} %upper_end.1.over_ref, f32[33,48,128]{2,1,0:T(8,128)S(1)} %get-tuple-element.62.inner_ref, f32[33,16,128]{2,1,0:T(8,128)S(1)} %lower_end.1.under_ref, ...), custom_call_target="tpu_custom_call" | custom-call | flops 10813440 | bytes 8650752 | tf_op jit(solution)/shard_map/finish/pallas_call | solution.py:516
Async XLA Ops:
  1.7 7.7 %collective-permute-start = (f32[2,2,8,4224]{3,2,1,0:T(8,128)S(1)}, f32[2,2,8,4224]{3,2,1,0:T(8,128)S(1)}, u32[]{:S(2)}, u32[]{:S(2)}) collective-permute-start(f32[2,2,8,4224]{3,2,1,0:T(8,128)S(1)} %get-tuple-element.38), channel_id=1, source_target_pairs={{0,1},{1,0},{2,3},{3,2},{4,5},{5,4},{6,7},{7,6},{8,9},{9,8},{10,11... | collective-permute-start | bytes 1622024 | tf_op jit(solution)/shard_map/ppermute | solution.py:549
  1.8 14.6 %collective-permute-start.2 = (f32[47,8,128]{2,1,0:T(8,128)S(1)}, f32[47,8,128]{2,1,0:T(8,128)S(1)}, u32[]{:S(2)}, u32[]{:S(2)}) collective-permute-start(f32[47,8,128]{2,1,0:T(8,128)S(1)} %get-tuple-element.43), channel_id=1, source_target_pairs={{0,2},{2,4},{4,6},{6,8},{8,10},{10,12},{12,14},{1,3},{3,5},{5,7},{... | collective-permute-start | bytes 577544 | tf_op jit(solution)/shard_map/ppermute | solution.py:510
  5.2 13.7 %collective-permute-start.3 = (f32[47,8,128]{2,1,0:T(8,128)S(1)}, f32[47,8,128]{2,1,0:T(8,128)S(1)}, u32[]{:S(2)}, u32[]{:S(2)}) collective-permute-start(f32[47,8,128]{2,1,0:T(8,128)S(1)} %get-tuple-element.44), channel_id=1, source_target_pairs={{2,0},{4,2},{6,4},{8,6},{10,8},{12,10},{14,12},{3,1},{5,3},{7,5},{... | collective-permute-start | bytes 577544 | tf_op jit(solution)/shard_map/ppermute | solution.py:513
  9.6 10.4 %collective-permute-start.5 = (f32[33,8,128]{2,1,0:T(8,128)S(1)}, f32[33,8,128]{2,1,0:T(8,128)S(1)}, u32[]{:S(2)}, u32[]{:S(2)}) collective-permute-start(f32[33,8,128]{2,1,0:T(8,128)S(1)} %get-tuple-element.47), channel_id=1, source_target_pairs={{0,2},{2,4},{4,6},{6,8},{8,10},{10,12},{12,14},{1,3},{3,5},{5,7},{... | collective-permute-start | bytes 405512 | tf_op jit(solution)/shard_map/ppermute | solution.py:510
  12.1 10.4 %collective-permute-start.1 = (f32[33,8,128]{2,1,0:T(8,128)S(1)}, f32[33,8,128]{2,1,0:T(8,128)S(1)}, u32[]{:S(2)}, u32[]{:S(2)}) collective-permute-start(f32[33,8,128]{2,1,0:T(8,128)S(1)} %get-tuple-element.40), channel_id=1, source_target_pairs={{2,0},{4,2},{6,4},{8,6},{10,8},{12,10},{14,12},{3,1},{5,3},{7,5},{... | collective-permute-start | bytes 405512 | tf_op jit(solution)/shard_map/ppermute | solution.py:513
  20.5 16.1 %collective-permute-start.7 = (f32[66,8,128]{2,1,0:T(8,128)S(1)}, f32[66,8,128]{2,1,0:T(8,128)S(1)}, u32[]{:S(2)}, u32[]{:S(2)}) collective-permute-start(f32[66,8,128]{2,1,0:T(8,128)S(1)} %first.4.refs_2_.refs_5_), channel_id=1, source_target_pairs={{2,0},{4,2},{6,4},{8,6},{10,8},{12,10},{14,12},{3,1},{5,3},{7,5},{... | collective-permute-start | bytes 811016 | tf_op jit(solution)/shard_map/ppermute | solution.py:513
  23.0 16.6 %collective-permute-start.4 = (f32[66,8,128]{2,1,0:T(8,128)S(1)}, f32[66,8,128]{2,1,0:T(8,128)S(1)}, u32[]{:S(2)}, u32[]{:S(2)}) collective-permute-start(f32[66,8,128]{2,1,0:T(8,128)S(1)} %first.3.refs_4_.refs_5_), channel_id=1, source_target_pairs={{0,2},{2,4},{4,6},{6,8},{8,10},{10,12},{12,14},{1,3},{3,5},{5,7},{... | collective-permute-start | bytes 811016 | tf_op jit(solution)/shard_map/ppermute | solution.py:510
  37.7 10.4 %collective-permute-start.9 = (f32[66,8,128]{2,1,0:T(8,128)S(1)}, f32[66,8,128]{2,1,0:T(8,128)S(1)}, u32[]{:S(2)}, u32[]{:S(2)}) collective-permute-start(f32[66,8,128]{2,1,0:T(8,128)S(1)} %get-tuple-element.52.refs_4_.refs_5_), channel_id=1, source_target_pairs={{0,2},{2,4},{4,6},{6,8},{8,10},{10,12},{12,14},{1,3},{3,5},{5,7},{... | collective-permute-start | bytes 811016 | tf_op jit(solution)/shard_map/ppermute | solution.py:510
  40.7 13.2 %collective-permute-start.6 = (f32[66,8,128]{2,1,0:T(8,128)S(1)}, f32[66,8,128]{2,1,0:T(8,128)S(1)}, u32[]{:S(2)}, u32[]{:S(2)}) collective-permute-start(f32[66,8,128]{2,1,0:T(8,128)S(1)} %get-tuple-element.50.refs_2_.refs_5_), channel_id=1, source_target_pairs={{2,0},{4,2},{6,4},{8,6},{10,8},{12,10},{14,12},{3,1},{5,3},{7,5},{... | collective-permute-start | bytes 811016 | tf_op jit(solution)/shard_map/ppermute | solution.py:513
  49.2 10.6 %collective-permute-start.10 = (f32[66,8,128]{2,1,0:T(8,128)S(1)}, f32[66,8,128]{2,1,0:T(8,128)S(1)}, u32[]{:S(2)}, u32[]{:S(2)}) collective-permute-start(f32[66,8,128]{2,1,0:T(8,128)S(1)} %get-tuple-element.58.refs_5_.refs_2_), channel_id=1, source_target_pairs={{2,0},{4,2},{6,4},{8,6},{10,8},{12,10},{14,12},{3,1},{5,3},{7,5},{... | collective-permute-start | bytes 811016 | tf_op jit(solution)/shard_map/ppermute | solution.py:513
  54.9 11.1 %collective-permute-start.8 = (f32[66,8,128]{2,1,0:T(8,128)S(1)}, f32[66,8,128]{2,1,0:T(8,128)S(1)}, u32[]{:S(2)}, u32[]{:S(2)}) collective-permute-start(f32[66,8,128]{2,1,0:T(8,128)S(1)} %get-tuple-element.56.refs_4_.refs_5_), channel_id=1, source_target_pairs={{0,2},{2,4},{4,6},{6,8},{8,10},{10,12},{12,14},{1,3},{3,5},{5,7},{... | collective-permute-start | bytes 811016 | tf_op jit(solution)/shard_map/ppermute | solution.py:510

commit v8 on v7

--- a/solution.py
+++ b/solution.py
@@ -63,6 +63,19 @@
 
 def sub(row):
     return pl.ds(row * SUBS, SUBS)
+
+
+def upside_down():
+    return 1 - lax.axis_index("row") % 2
+
+
+def place(row, flip):
+    return row + flip * (SUBS - 1 - 2 * row)
+
+
+def placed(row, flip):
+    at = place(row, flip) * SUBS
+    return pl.ds(at if isinstance(at, int) else pl.multiple_of(at, SUBS), SUBS)
 
 
 def tile_columns(tile):
@@ -99,24 +112,26 @@
         rest[tile // 8, pl.ds(tile % 8, SUBS, stride=SUBS), :] = window_ref[8, :, cols]
         for c in range(2):
             observed[tile // 4, pl.ds(2 * (tile % 4) + c, SUBS, stride=SUBS), :] = seen_ref[c, :, cols]
+    flip = upside_down()
+    first, last = placed(0, flip), placed(SUBS - 1, flip)
     base = 0
     for source in (eight, rest, observed):
         for index in range(source.shape[0]):
-            top_ref[base + index] = source[index, sub(0), :]
-            bottom_ref[base + index] = source[index, sub(SUBS - 1), :]
+            top_ref[base + index] = source[index, first, :]
+            bottom_ref[base + index] = source[index, last, :]
         base += source.shape[0]
     copies[2].wait()
     copies[3].wait()
 
 
-def combine(kappa, across, along, skew, coupling):
+def combine(kappa, across, along, skew, coupling, sign):
     scale = 4.0 / (upper_edge - lower_edge)
     shift = 2.0 * (upper_edge + lower_edge) / (upper_edge - lower_edge)
     return (
         scale * (kappa + 2.0 * (across + along)) - shift,
         -scale * across,
         -scale * along,
-        -0.5 * scale * skew,
+        (-0.5 * scale * sign) * skew,
         scale * coupling,
     )
 
@@ -124,6 +139,7 @@
 def prep_kernel(window_ref, expanded_ref):
     tiles = expanded_ref.shape[1]
     chunk = chunk_of(tiles)
+    sign = 1.0 - 2.0 * upside_down().astype(jnp.float32)
 
     def body(step, carry):
         for k in range(chunk):
@@ -131,7 +147,7 @@
             cols = tile_columns(tile)
             raw = [window_ref[channel, :, cols] for channel in range(9)]
             for c in range(2):
-                values = combine(raw[c], raw[2 + c], raw[4 + c], raw[6 + c], raw[8])
+                values = combine(raw[c], raw[2 + c], raw[4 + c], raw[6 + c], raw[8], sign)
                 for kind, value in enumerate(values):
                     for probe in range(4):
                         expanded_ref[kind, tile, pl.ds(4 * c + probe, SUBS, stride=SUBS), :] = value
@@ -140,9 +156,10 @@
     lax.fori_loop(0, tiles // chunk, body, 0)
 
 
-def layout_kernel(own_ref, other_ref, z_ref, top_ref, bottom_ref):
+def layout_kernel(own_ref, other_ref, z_ref, top_ref, bottom_ref, natural):
     tiles = z_ref.shape[0]
     chunk = chunk_of(tiles)
+    flip = upside_down()
 
     def body(step, carry):
         for k in range(chunk):
@@ -150,10 +167,17 @@
             cols = tile_columns(tile)
             for c in range(2):
                 for probe in range(2):
-                    z_ref[tile, pl.ds(4 * c + probe, SUBS, stride=SUBS), :] = own_ref[probe, c, :, cols]
-                    z_ref[tile, pl.ds(4 * c + 2 + probe, SUBS, stride=SUBS), :] = other_ref[probe, c, :, cols]
-            top_ref[tile] = z_ref[tile, sub(0), :]
-            bottom_ref[tile] = z_ref[tile, sub(SUBS - 1), :]
+                    natural[tile, pl.ds(4 * c + probe, SUBS, stride=SUBS), :] = own_ref[probe, c, :, cols]
+                    natural[tile, pl.ds(4 * c + 2 + probe, SUBS, stride=SUBS), :] = other_ref[probe, c, :, cols]
+        for k in range(chunk):
+            tile = step * chunk + k
+            for row in range(SUBS):
+                value = natural[tile, placed(row, flip), :]
+                z_ref[tile, sub(row), :] = value
+                if row == 0:
+                    top_ref[tile] = value
+                if row == SUBS - 1:
+                    bottom_ref[tile] = value
         return carry
 
     lax.fori_loop(0, tiles // chunk, body, 0)
@@ -161,6 +185,8 @@
 
 def rim(edge_ref, rim_ref, tiles):
     chunk = chunk_of(tiles)
+
+    sign = 1.0 - 2.0 * upside_down().astype(jnp.float32)
 
     def spread(index, row):
         return jnp.broadcast_to(edge_ref[index, pl.ds(row, 1), :], (SUBS, LANES))
@@ -171,7 +197,7 @@
             tile = step * chunk + k
             pairs = [jnp.where(low, spread(tile, 2 * kind), spread(tile, 2 * kind + 1)) for kind in range(4)]
             coupling = spread(tiles + tile // 8, tile % 8)
-            for kind, value in enumerate(combine(*pairs, coupling)):
+            for kind, value in enumerate(combine(*pairs, coupling, sign)):
                 rim_ref[kind, tile] = value
         return carry
 
@@ -229,6 +255,7 @@
         halo_ref, refs = refs[0], refs[1:]
     z_ref, expanded_ref, out_ref = refs
     low, count = ((0, 2), (2, 4), (6, 2))[part]
+    flip = upside_down()
 
     def now(row, tile):
         if row < 0 or row > 7:
@@ -242,7 +269,7 @@
             out_ref[2 * tile + row - low] = value
 
     def factor(kind, row, tile):
-        return expanded_ref[kind, tile, sub(row), :]
+        return expanded_ref[kind, tile, placed(row, flip), :]
 
     sweep(tiles, low, count, now, factor, lambda row, tile: z_ref[tile, sub(row), :], None, constants, store)
 
@@ -262,9 +289,10 @@
     z_ref, expanded_ref, top_ref, inner_ref, bottom_ref = refs[:5]
     once_ref, twice_ref = refs[-2:]
     now = inner_rows(top_ref, inner_ref, bottom_ref)
+    flip = upside_down()
 
     def factor(kind, row, tile):
-        return expanded_ref[kind, tile, sub(row), :]
+        return expanded_ref[kind, tile, placed(row, flip), :]
 
     def z_row(row, tile):
         return z_ref[tile, sub(row), :]
@@ -287,17 +315,18 @@
 
 def edge_product(upper, constants, tiles, halo_ref, z_halo_ref, z_ref, expanded_ref, rim_ref, edge_ref, older_ref, once_ref):
     base = 0 if upper else 6
+    flip = upside_down()
     low = -1 if upper else 7
 
     def now(row, tile):
         if row < 0 or row > 7:
-            return halo_ref[2 * tile + (row + 2 if upper else row - 8)]
+            return halo_ref[2 * tile + (-1 - row if upper else 9 - row)]
         return edge_ref[2 * tile + row - base]
 
     def factor(kind, row, tile):
         if row < 0 or row > 7:
             return rim_ref[kind, tile]
-        return expanded_ref[kind, tile, sub(row), :]
+        return expanded_ref[kind, tile, placed(row, flip), :]
 
     def z_row(row, tile):
         if row < 0 or row > 7:
@@ -333,7 +362,7 @@
     sweep(tiles, base, 2, once, factor, z_row, now, steps[1], store_twice)
 
 
-def gradient_rows(low, count, tile, slot, load, z_ref, factor, tiles, products):
+def gradient_rows(low, count, tile, slot, load, z_ref, factor, tiles, products, flip):
     edges = masks()
     values, sums, slopes = [], [], []
     for row in range(low - 1, low + count + 1):
@@ -347,11 +376,12 @@
         left = factor * z_ref[tile, sub(row), :]
         value = values[at + 1]
         twice = 2.0 * value
-        products[slot, 0, sub(row), :] = left * value
-        products[slot, 1, sub(row), :] = left * (twice - sums[at + 1])
-        products[slot, 2, sub(row), :] = left * (twice - (values[at] + values[at + 2]))
-        products[slot, 3, sub(row), :] = (-0.5 * left) * (slopes[at + 2] - slopes[at])
-        products[slot, 4, sub(row), :] = left * pltpu.roll(value, 4, 0)
+        rows = placed(row, flip)
+        products[slot, 0, rows, :] = left * value
+        products[slot, 1, rows, :] = left * (twice - sums[at + 1])
+        products[slot, 2, rows, :] = left * (twice - (values[at] + values[at + 2]))
+        products[slot, 3, rows, :] = ((flip - 0.5) * left) * (slopes[at + 2] - slopes[at])
+        products[slot, 4, rows, :] = left * pltpu.roll(value, 4, 0)
 
 
 def gradient_sums(slot, products, start, store):
@@ -368,9 +398,10 @@
 def gradient_kernel(constants, tiles, factor, *refs):
     z_ref, expanded_ref, top_ref, inner_ref, bottom_ref, older_ref, data_ref, series_ref, out_ref, products = refs
     now = inner_rows(top_ref, inner_ref, bottom_ref)
+    flip = upside_down()
 
     def coefficient(kind, row, tile):
-        return expanded_ref[kind, tile, sub(row), :]
+        return expanded_ref[kind, tile, placed(row, flip), :]
 
     def store(row, tile, value):
         series_ref[tile, sub(row - 1), :] = value
@@ -394,9 +425,9 @@
     count = products.shape[0]
     products[...] = jnp.zeros_like(products)
 
-    def body(step, carry):
+    def body(turned, step, carry):
         for k in range(count):
-            gradient_rows(2, 4, step * count + k + offset, k, series, z_ref, factor, tiles, products)
+            gradient_rows(2, 4, step * count + k + offset, k, series, z_ref, factor, tiles, products, turned)
         for k in range(count):
             index = step * count + k
             cols = tile_columns(index)
@@ -407,7 +438,11 @@
             gradient_sums(k, products, lambda channel: data_ref[index + offset, channel], put)
         return carry
 
-    lax.fori_loop(0, kept // count, body, 0)
+    for turned in range(2):
+
+        @pl.when(flip == turned)
+        def _():
+            lax.fori_loop(0, kept // count, functools.partial(body, turned), 0)
 
 
 def end_kernel(upper, constants, tiles, *refs):
@@ -427,11 +462,11 @@
     count = products.shape[0]
     products[...] = jnp.zeros_like(products)
 
-    def body(step, carry):
+    def body(turned, step, carry):
         for k in range(count):
             tile = step * count + k + offset
             for low in (0, 6):
-                gradient_rows(low, 2, tile, k, series, z_ref, factor, tiles, products)
+                gradient_rows(low, 2, tile, k, series, z_ref, factor, tiles, products, turned)
         for k in range(count):
             cols = tile_columns(step * count + k)
 
@@ -443,14 +478,20 @@
 
     steps = kept // count
     groups = sem.shape[0]
-    copies = []
-    for group in range(groups):
-        lax.fori_loop(group * steps // groups, (group + 1) * steps // groups, body, 0)
-        cols = pl.ds(group * kept // groups * LANES, kept // groups * LANES)
-        copies.append(pltpu.make_async_copy(target.at[:, :, cols], out_ref.at[:, :, cols], sem.at[group]))
-        copies[-1].start()
-    for copy in copies:
-        copy.wait()
+
+    def run(turned):
+        copies = []
+        for group in range(groups):
+            span = (group * steps // groups, (group + 1) * steps // groups)
+            lax.fori_loop(*span, functools.partial(body, turned), 0)
+            cols = pl.ds(group * kept // groups * LANES, kept // groups * LANES)
+            copies.append(pltpu.make_async_copy(target.at[:, :, cols], out_ref.at[:, :, cols], sem.at[group]))
+            copies[-1].start()
+        for copy in copies:
+            copy.wait()
+
+    for turned in range(2):
+        pl.when(upside_down() == turned)(functools.partial(run, turned))
 
 
 def border_kernel(tiles, seen_ref, up_ref, down_ref, out_ref, rim_up_ref, rim_down_ref):
@@ -459,9 +500,11 @@
     chunk = chunk_of(tiles)
 
     base = tiles + -(-tiles // 8)
-
-    def halo(ref, c, tile):
-        row = ref[base + tile // 4, pl.ds(2 * (tile % 4) + c, 1), :]
+    flip = upside_down()
+
+    def halo(near, far, c, tile):
+        at = (base + tile // 4, pl.ds(2 * (tile % 4) + c, 1), slice(None))
+        row = jnp.where(flip == 1, far[at], near[at])
         return jnp.broadcast_to(row, (SUBS, LANES))
 
     def body(step, carry):
@@ -471,8 +514,8 @@
         kept = [[], []]
         for c in range(2):
             values = window_tiles(lambda tile: seen_ref[c, :, tile_columns(tile)], first, chunk, tiles)
-            ups = window_tiles(lambda tile: halo(up_ref, c, tile), first, chunk, tiles)
-            downs = window_tiles(lambda tile: halo(down_ref, c, tile), first, chunk, tiles)
+            ups = window_tiles(lambda tile: halo(up_ref, down_ref, c, tile), first, chunk, tiles)
+            downs = window_tiles(lambda tile: halo(down_ref, up_ref, c, tile), first, chunk, tiles)
             aboves = [jnp.where(row == 0, u, pltpu.roll(v, 1, 0)) for u, v in zip(ups, values)]
             belows = [jnp.where(row == SUBS - 1, d, pltpu.roll(v, SUBS - 1, 0)) for d, v in zip(downs, values)]
             tilts = [b - a for a, b in zip(aboves, belows)]
@@ -503,14 +546,14 @@
     tiles = width // LANES
     kept = share // LANES
     rows = lax.axis_size("row")
-    down_pairs = [(i, i + 1) for i in range(rows - 1)]
-    up_pairs = [(i + 1, i) for i in range(rows - 1)]
-
-    def to_next(edge):
-        return lax.ppermute(edge, "row", down_pairs)
-
-    def to_previous(edge):
-        return lax.ppermute(edge, "row", up_pairs)
+    near_pairs = [pair for i in range(0, rows - 1, 2) for pair in ((i, i + 1), (i + 1, i))]
+    far_pairs = [pair for i in range(1, rows - 1, 2) for pair in ((i, i + 1), (i + 1, i))]
+
+    def near(edge):
+        return lax.ppermute(edge, "row", near_pairs)
+
+    def far(edge):
+        return lax.ppermute(edge, "row", far_pairs)
 
     def call(kernel, name, vregs, operands, outs, scratch=(), in_specs=None, out_specs=None):
         return pl.pallas_call(
@@ -547,7 +590,7 @@
         [pl.BlockSpec(memory_space=pltpu.HBM)] * 3,
     )
     other = lax.ppermute(theirs, "probe", [(0, 1), (1, 0)])
-    edges_down, edges_up = to_previous(edge_top), to_next(edge_bottom)
+    edges_up, edges_down = near(edge_top), far(edge_bottom)
     expanded = call(
         prep_kernel, "prep", 5 * 8 * tiles, (window,), pltpu.VMEM((5, tiles, SUBS * SUBS, LANES), f32)
     )
@@ -561,8 +604,9 @@
         8 * tiles,
         (own, other),
         [rows_of(SUBS), rows_of(1), rows_of(1)],
-    )
-    z_down, z_up = to_previous(top), to_next(bottom)
+        [rows_of(SUBS)],
+    )
+    z_up, z_down = near(top), far(bottom)
     edge_rows = pltpu.VMEM((2 * tiles, SUBS, LANES), f32)
     constants = (weights[CHEB - 1], weights[CHEB])
 
@@ -586,9 +630,9 @@
     expanded, data = lax.optimization_barrier((expanded, data))
     inner = first(1, [], rows_of(4))
     bottom = first(2, [z_down], edge_rows)
-    up = to_next(bottom)
+    down = far(bottom)
     top = first(0, [z_up], edge_rows)
-    down = to_previous(top)
+    up = near(top)
     once = None
     for order in range(CHEB - 2, 0, -2):
         opening = weights[order] - (weights[CHEB] if order == CHEB - 2 else 0.0)
@@ -615,7 +659,7 @@
         over, under = edge(True), edge(False)
         once = (over[0], inner_once, under[0])
         top, inner, bottom = over[1], inner_twice, under[1]
-        down, up = to_previous(top), to_next(bottom)
+        up, down = near(top), far(bottom)
 
     factor = 0.5 / (probes.shape[0] * lax.axis_size("probe"))
     count = max(n for n in range(1, 5) if kept % n == 0)

time: 69.3 us -> 65.7 us (0.948)
  the two profiles are of different devices: /device:TPU:8 before, /device:TPU:24 now
where the time goes in v8:
time: 65.7 us; the launch traced here: 65.5 us
  waiting for transfers between devices  24.9 us (38%)
  starting transfers between devices  21.5 us (33%)
  Pallas kernels  18.9 us (29%)
    ppermute x5, waiting for transfers between devices, near(): return lax.ppermute(edge, 'row', near_pairs)  24.9 us
    ppermute x5, starting transfers between devices, far(): return lax.ppermute(edge, 'row', far_pairs)  19.6 us
    pallas_call x17, Pallas kernels, call(): pl.pallas_call(kernel, out_shape=outs, in_specs=in_specs or [vmem_spec()]...  18.9 us
    ppermute x5, starting transfers between devices, near(): return lax.ppermute(edge, 'row', near_pairs)  1.84 us
  transfers between devices with their start and end apart: 11, of which 5 were waited for; matrix products, arithmetic and copies ran while one was open for 0% of the time, Pallas kernels for 22%

profile of v8, /device:TPU:24, one launch (start us, length us, event | category | flops | bytes accessed | tf_op | source)
XLA Modules:
  0.0 65.5 jit_solution(8625208987451258862)
XLA Ops:
  0.0 1.7 %load.1 = (f32[2,2,8,4224]{3,2,1,0:T(8,128)S(1)}, f32[2,2,8,4224]{3,2,1,0:T(8,128)S(1)}, f32[2,8,4224]{2,1,0:T(8,128)S(1)}, f32[9,8,4224]{2,1,0:T(8,128)S(1)}, f...) custom-call(f32[2,2,8,8192]{3,2,1,0:T(8,128)} %probes_ref.1, f32[2,8,8192]{2,1,0:T(8,128)} %observed_ref.1, ...), custom_call_target="tpu_custom_call" | custom-call | flops 2048000 | bytes 1638400 | tf_op jit(solution)/shard_map/load/pallas_call | solution.py:559
  1.7 0.1 collective-permute-start
  1.8 1.6 %collective-permute-start.2 = (f32[47,8,128]{2,1,0:T(8,128)S(1)}, f32[47,8,128]{2,1,0:T(8,128)S(1)}, u32[]{:S(2)}, u32[]{:S(2)}) collective-permute-start(f32[47,8,128]{2,1,0:T(8,128)S(1)} %get-tuple-element.43), channel_id=1, source_target_pairs={{0,2},{2,0},{4,6},{6,4},{8,10},{10,8},{12,14},{14,12},{1,3},{3,1},... | collective-permute-start | bytes 577544 | tf_op jit(solution)/shard_map/ppermute | solution.py:553
  3.3 2.3 %collective-permute-start.3 = (f32[47,8,128]{2,1,0:T(8,128)S(1)}, f32[47,8,128]{2,1,0:T(8,128)S(1)}, u32[]{:S(2)}, u32[]{:S(2)}) collective-permute-start(f32[47,8,128]{2,1,0:T(8,128)S(1)} %get-tuple-element.44), channel_id=1, source_target_pairs={{2,4},{4,2},{6,8},{8,6},{10,12},{12,10},{3,5},{5,3},{7,9},{9,7},{1... | collective-permute-start | bytes 577544 | tf_op jit(solution)/shard_map/ppermute | solution.py:556
  5.7 0.8 %prep.1.refs_2_.refs_1_.refs_3_ = f32[5,33,64,128]{3,2,1,0:T(8,128)S(1)} custom-call(f32[9,8,4224]{2,1,0:T(8,128)S(1)} %get-tuple-element.36.window_ref), custom_call_target="tpu_custom_call" | custom-call | flops 27033600 | bytes 21626880 | tf_op jit(solution)/shard_map/prep/pallas_call | solution.py:559
  6.5 0.0 collective-permute-done.other_ref
  6.5 0.3 layout.1
  6.8 0.1 collective-permute-start.1
  6.9 4.4 %collective-permute-start.5 = (f32[33,8,128]{2,1,0:T(8,128)S(1)}, f32[33,8,128]{2,1,0:T(8,128)S(1)}, u32[]{:S(2)}, u32[]{:S(2)}) collective-permute-start(f32[33,8,128]{2,1,0:T(8,128)S(1)} %get-tuple-element.48), channel_id=1, source_target_pairs={{2,4},{4,2},{6,8},{8,6},{10,12},{12,10},{3,5},{5,3},{7,9},{9,7},{1... | collective-permute-start | bytes 405512 | tf_op jit(solution)/shard_map/ppermute | solution.py:556
  11.3 4.7 %collective-permute-done.2.up_ref = f32[47,8,128]{2,1,0:T(8,128)S(1)} collective-permute-done((f32[47,8,128]{2,1,0:T(8,128)S(1)}, f32[47,8,128]{2,1,0:T(8,128)S(1)}, u32[]{:S(2)}, u32[]{:S(2)}) %collective-permute-start.2) | collective-permute-done | bytes 192544 | tf_op jit(solution)/shard_map/ppermute | solution.py:553
  16.0 0.0 collective-permute-done.3.down_ref
  16.0 1.1 %border.1 = (f32[33,9,8,128]{3,2,1,0:T(8,128)S(1)}, f32[5,33,8,128]{3,2,1,0:T(8,128)S(1)}, f32[5,33,8,128]{3,2,1,0:T(8,128)S(1)}) custom-call(f32[2,8,4224]{2,1,0:T(8,128)S(1)} %get-tuple-element.42.seen_ref, f32[47,8,128]{2,1,0:T(8,128)S(1)} %collective-permute-done.2.up_ref, f32[47,8,128]{2,1,0:T(8,128)S(1)} %collective-permute-done.3.down_ref), custom_call_target="tpu_custom_call" | custom-call | flops 6082560 | bytes 4866048 | tf_op jit(solution)/shard_map/border/pallas_call | solution.py:559
  17.2 1.7 %collective-permute-done.1.refs_0_.refs_1_ = f32[33,8,128]{2,1,0:T(8,128)S(1)} collective-permute-done((f32[33,8,128]{2,1,0:T(8,128)S(1)}, f32[33,8,128]{2,1,0:T(8,128)S(1)}, u32[]{:S(2)}, u32[]{:S(2)}) %collective-permute-start.1) | collective-permute-done | bytes 135200 | tf_op jit(solution)/shard_map/ppermute | solution.py:553
  18.9 0.5 first.3.refs_2_.refs_5_
  19.4 0.1 collective-permute-start.4
  19.5 0.0 collective-permute-done.5.refs_0_.refs_1_
  19.5 0.5 first.5.refs_4_.refs_5_
  20.1 3.8 %collective-permute-start.7 = (f32[66,8,128]{2,1,0:T(8,128)S(1)}, f32[66,8,128]{2,1,0:T(8,128)S(1)}, u32[]{:S(2)}, u32[]{:S(2)}) collective-permute-start(f32[66,8,128]{2,1,0:T(8,128)S(1)} %first.5.refs_4_.refs_5_), channel_id=1, source_target_pairs={{2,4},{4,2},{6,8},{8,6},{10,12},{12,10},{3,5},{5,3},{7,9},{9,7},{1... | collective-permute-start | bytes 811016 | tf_op jit(solution)/shard_map/ppermute | solution.py:556
  23.9 0.7 %first.4.refs_3_ = f32[33,32,128]{2,1,0:T(8,128)S(1)} custom-call(f32[33,64,128]{2,1,0:T(8,128)S(1)} %get-tuple-element.39.refs_1_.refs_0_.refs_2_.z_ref, f32[5,33,64,128]{3,2,1,0:T(8,128)S(1)} %prep.1.refs_2_.refs_1_.refs_3_), custom_call_target="tpu_custom_call" | custom-call | flops 2703360 | bytes 2162688 | tf_op jit(solution)/shard_map/first/pallas_call | solution.py:559
  24.5 1.6 %middle.2 = (f32[33,48,128]{2,1,0:T(8,128)S(1)}, f32[33,32,128]{2,1,0:T(8,128)S(1)}) custom-call(f32[33,64,128]{2,1,0:T(8,128)S(1)} %get-tuple-element.39.refs_1_.refs_0_.refs_2_.z_ref, f32[5,33,64,128]{3,2,1,0:T(8,128)S(1)} %prep.1.refs_2_.refs_1_.refs_3_, f32[66,8,128]{2,1,0:T(8,128)S(1)} %first.3.refs_2_.refs_5_, f32[33,32,128]{2,1,0:T(8,128)S(1)} %first.4.refs_3_, ...), custom_call_target="tpu_custom_call" | custom-call | flops 6758400 | bytes 5406720 | tf_op jit(solution)/shard_map/middle/pallas_call | solution.py:559
  26.1 7.7 %collective-permute-done.4.refs_0_ = f32[66,8,128]{2,1,0:T(8,128)S(1)} collective-permute-done((f32[66,8,128]{2,1,0:T(8,128)S(1)}, f32[66,8,128]{2,1,0:T(8,128)S(1)}, u32[]{:S(2)}, u32[]{:S(2)}) %collective-permute-start.4) | collective-permute-done | bytes 270368 | tf_op jit(solution)/shard_map/ppermute | solution.py:553
  33.8 1.0 %upper.2 = (f32[33,16,128]{2,1,0:T(8,128)S(1)}, f32[66,8,128]{2,1,0:T(8,128)S(1)}) custom-call(f32[66,8,128]{2,1,0:T(8,128)S(1)} %collective-permute-done.4.refs_0_, f32[33,8,128]{2,1,0:T(8,128)S(1)} %collective-permute-done.1.refs_0_.refs_1_, f32[33,64,128]{2,1,0:T(8,128)S(1)} %get-tuple-element.39.refs_1_.refs_0_.refs_2_.z_ref, ...), custom_call_target="tpu_custom_call" | custom-call | flops 2703360 | bytes 2162688 | tf_op jit(solution)/shard_map/upper/pallas_call | solution.py:559
  34.8 0.1 collective-permute-start.6
  34.9 0.0 collective-permute-done.7.refs_0_
  34.9 1.1 %lower.2 = (f32[33,16,128]{2,1,0:T(8,128)S(1)}, f32[66,8,128]{2,1,0:T(8,128)S(1)}) custom-call(f32[66,8,128]{2,1,0:T(8,128)S(1)} %collective-permute-done.7.refs_0_, f32[33,8,128]{2,1,0:T(8,128)S(1)} %collective-permute-done.5.refs_0_.refs_1_, f32[33,64,128]{2,1,0:T(8,128)S(1)} %get-tuple-element.39.refs_1_.refs_0_.refs_2_.z_ref, ...), custom_call_target="tpu_custom_call" | custom-call | flops 2703360 | bytes 2162688 | tf_op jit(solution)/shard_map/lower/pallas_call | solution.py:559
  36.0 3.8 %collective-permute-start.9 = (f32[66,8,128]{2,1,0:T(8,128)S(1)}, f32[66,8,128]{2,1,0:T(8,128)S(1)}, u32[]{:S(2)}, u32[]{:S(2)}) collective-permute-start(f32[66,8,128]{2,1,0:T(8,128)S(1)} %get-tuple-element.53.refs_4_.refs_5_), channel_id=1, source_target_pairs={{2,4},{4,2},{6,8},{8,6},{10,12},{12,10},{3,5},{5,3},{7,9},{9,7},{1... | collective-permute-start | bytes 811016 | tf_op jit(solution)/shard_map/ppermute | solution.py:556
  39.8 1.6 %middle.3 = (f32[33,48,128]{2,1,0:T(8,128)S(1)}, f32[33,32,128]{2,1,0:T(8,128)S(1)}) custom-call(f32[33,64,128]{2,1,0:T(8,128)S(1)} %get-tuple-element.39.refs_1_.refs_0_.refs_2_.z_ref, f32[5,33,64,128]{3,2,1,0:T(8,128)S(1)} %prep.1.refs_2_.refs_1_.refs_3_, f32[66,8,128]{2,1,0:T(8,128)S(1)} %get-tuple-element.50.refs_2_.refs_5_, ...), custom_call_target="tpu_custom_call" | custom-call | flops 6758400 | bytes 5406720 | tf_op jit(solution)/shard_map/middle/pallas_call | solution.py:559
  41.4 7.0 %collective-permute-done.6.refs_0_ = f32[66,8,128]{2,1,0:T(8,128)S(1)} collective-permute-done((f32[66,8,128]{2,1,0:T(8,128)S(1)}, f32[66,8,128]{2,1,0:T(8,128)S(1)}, u32[]{:S(2)}, u32[]{:S(2)}) %collective-permute-start.6) | collective-permute-done | bytes 270368 | tf_op jit(solution)/shard_map/ppermute | solution.py:553
  48.4 1.1 %upper.3 = (f32[33,16,128]{2,1,0:T(8,128)S(1)}, f32[66,8,128]{2,1,0:T(8,128)S(1)}) custom-call(f32[66,8,128]{2,1,0:T(8,128)S(1)} %collective-permute-done.6.refs_0_, f32[33,8,128]{2,1,0:T(8,128)S(1)} %collective-permute-done.1.refs_0_.refs_1_, f32[33,64,128]{2,1,0:T(8,128)S(1)} %get-tuple-element.39.refs_1_.refs_0_.refs_2_.z_ref, ...), custom_call_target="tpu_custom_call" | custom-call | flops 2703360 | bytes 2162688 | tf_op jit(solution)/shard_map/upper/pallas_call | solution.py:559
  49.4 0.1 collective-permute-start.8
  49.5 0.0 collective-permute-done.9.refs_0_
  49.5 1.1 %lower.3 = (f32[33,16,128]{2,1,0:T(8,128)S(1)}, f32[66,8,128]{2,1,0:T(8,128)S(1)}) custom-call(f32[66,8,128]{2,1,0:T(8,128)S(1)} %collective-permute-done.9.refs_0_, f32[33,8,128]{2,1,0:T(8,128)S(1)} %collective-permute-done.5.refs_0_.refs_1_, f32[33,64,128]{2,1,0:T(8,128)S(1)} %get-tuple-element.39.refs_1_.refs_0_.refs_2_.z_ref, ...), custom_call_target="tpu_custom_call" | custom-call | flops 2703360 | bytes 2162688 | tf_op jit(solution)/shard_map/lower/pallas_call | solution.py:559
  50.6 5.3 %collective-permute-start.10 = (f32[66,8,128]{2,1,0:T(8,128)S(1)}, f32[66,8,128]{2,1,0:T(8,128)S(1)}, u32[]{:S(2)}, u32[]{:S(2)}) collective-permute-start(f32[66,8,128]{2,1,0:T(8,128)S(1)} %get-tuple-element.60.refs_4_.refs_5_), channel_id=1, source_target_pairs={{2,4},{4,2},{6,8},{8,6},{10,12},{12,10},{3,5},{5,3},{7,9},{9,7},{1... | collective-permute-start | bytes 811016 | tf_op jit(solution)/shard_map/ppermute | solution.py:556
  55.9 2.4 %gradient.1 = (f32[33,48,128]{2,1,0:T(8,128)S(1)}, f32[9,8,4096]{2,1,0:T(8,128)S(1)}) custom-call(f32[33,64,128]{2,1,0:T(8,128)S(1)} %get-tuple-element.39.refs_1_.refs_0_.refs_2_.z_ref, f32[5,33,64,128]{3,2,1,0:T(8,128)S(1)} %prep.1.refs_2_.refs_1_.refs_3_, f32[66,8,128]{2,1,0:T(8,128)S(1)} %get-tuple-element.56.refs_5_.refs_2_, ...), custom_call_target="tpu_custom_call" | custom-call | flops 16220160 | bytes 12976128 | tf_op jit(solution)/shard_map/gradient/pallas_call | solution.py:559
  58.3 3.8 %collective-permute-done.8.refs_0_ = f32[66,8,128]{2,1,0:T(8,128)S(1)} collective-permute-done((f32[66,8,128]{2,1,0:T(8,128)S(1)}, f32[66,8,128]{2,1,0:T(8,128)S(1)}, u32[]{:S(2)}, u32[]{:S(2)}) %collective-permute-start.8) | collective-permute-done | bytes 270368 | tf_op jit(solution)/shard_map/ppermute | solution.py:553
  62.0 0.5 upper_end.1.over_ref
  62.6 0.0 collective-permute-done.10.refs_0_
  62.6 0.6 lower_end.1.under_ref
  63.1 2.4 %finish.1 = f32[9,8,4096]{2,1,0:T(8,128)} custom-call(f32[33,64,128]{2,1,0:T(8,128)S(1)} %get-tuple-element.39.refs_1_.refs_0_.refs_2_.z_ref, f32[33,16,128]{2,1,0:T(8,128)S(1)} %upper_end.1.over_ref, f32[33,48,128]{2,1,0:T(8,128)S(1)} %get-tuple-element.62.inner_ref, f32[33,16,128]{2,1,0:T(8,128)S(1)} %lower_end.1.under_ref, ...), custom_call_target="tpu_custom_call" | custom-call | flops 10813440 | bytes 8650752 | tf_op jit(solution)/shard_map/finish/pallas_call | solution.py:559
Async XLA Ops:
  1.7 4.8 %collective-permute-start = (f32[2,2,8,4224]{3,2,1,0:T(8,128)S(1)}, f32[2,2,8,4224]{3,2,1,0:T(8,128)S(1)}, u32[]{:S(2)}, u32[]{:S(2)}) collective-permute-start(f32[2,2,8,4224]{3,2,1,0:T(8,128)S(1)} %get-tuple-element.38), channel_id=1, source_target_pairs={{0,1},{1,0},{2,3},{3,2},{4,5},{5,4},{6,7},{7,6},{8,9},{9,8},{10,11... | collective-permute-start | bytes 1622024 | tf_op jit(solution)/shard_map/ppermute | solution.py:592
  1.8 14.3 %collective-permute-start.2 = (f32[47,8,128]{2,1,0:T(8,128)S(1)}, f32[47,8,128]{2,1,0:T(8,128)S(1)}, u32[]{:S(2)}, u32[]{:S(2)}) collective-permute-start(f32[47,8,128]{2,1,0:T(8,128)S(1)} %get-tuple-element.43), channel_id=1, source_target_pairs={{0,2},{2,0},{4,6},{6,4},{8,10},{10,8},{12,14},{14,12},{1,3},{3,1},... | collective-permute-start | bytes 577544 | tf_op jit(solution)/shard_map/ppermute | solution.py:553
  3.3 12.7 %collective-permute-start.3 = (f32[47,8,128]{2,1,0:T(8,128)S(1)}, f32[47,8,128]{2,1,0:T(8,128)S(1)}, u32[]{:S(2)}, u32[]{:S(2)}) collective-permute-start(f32[47,8,128]{2,1,0:T(8,128)S(1)} %get-tuple-element.44), channel_id=1, source_target_pairs={{2,4},{4,2},{6,8},{8,6},{10,12},{12,10},{3,5},{5,3},{7,9},{9,7},{1... | collective-permute-start | bytes 577544 | tf_op jit(solution)/shard_map/ppermute | solution.py:556
  6.8 12.1 %collective-permute-start.1 = (f32[33,8,128]{2,1,0:T(8,128)S(1)}, f32[33,8,128]{2,1,0:T(8,128)S(1)}, u32[]{:S(2)}, u32[]{:S(2)}) collective-permute-start(f32[33,8,128]{2,1,0:T(8,128)S(1)} %get-tuple-element.40), channel_id=1, source_target_pairs={{0,2},{2,0},{4,6},{6,4},{8,10},{10,8},{12,14},{14,12},{1,3},{3,1},... | collective-permute-start | bytes 405512 | tf_op jit(solution)/shard_map/ppermute | solution.py:553
  6.9 12.6 %collective-permute-start.5 = (f32[33,8,128]{2,1,0:T(8,128)S(1)}, f32[33,8,128]{2,1,0:T(8,128)S(1)}, u32[]{:S(2)}, u32[]{:S(2)}) collective-permute-start(f32[33,8,128]{2,1,0:T(8,128)S(1)} %get-tuple-element.48), channel_id=1, source_target_pairs={{2,4},{4,2},{6,8},{8,6},{10,12},{12,10},{3,5},{5,3},{7,9},{9,7},{1... | collective-permute-start | bytes 405512 | tf_op jit(solution)/shard_map/ppermute | solution.py:556
  19.4 14.4 %collective-permute-start.4 = (f32[66,8,128]{2,1,0:T(8,128)S(1)}, f32[66,8,128]{2,1,0:T(8,128)S(1)}, u32[]{:S(2)}, u32[]{:S(2)}) collective-permute-start(f32[66,8,128]{2,1,0:T(8,128)S(1)} %first.3.refs_2_.refs_5_), channel_id=1, source_target_pairs={{0,2},{2,0},{4,6},{6,4},{8,10},{10,8},{12,14},{14,12},{1,3},{3,1},... | collective-permute-start | bytes 811016 | tf_op jit(solution)/shard_map/ppermute | solution.py:553
  20.1 14.9 %collective-permute-start.7 = (f32[66,8,128]{2,1,0:T(8,128)S(1)}, f32[66,8,128]{2,1,0:T(8,128)S(1)}, u32[]{:S(2)}, u32[]{:S(2)}) collective-permute-start(f32[66,8,128]{2,1,0:T(8,128)S(1)} %first.5.refs_4_.refs_5_), channel_id=1, source_target_pairs={{2,4},{4,2},{6,8},{8,6},{10,12},{12,10},{3,5},{5,3},{7,9},{9,7},{1... | collective-permute-start | bytes 811016 | tf_op jit(solution)/shard_map/ppermute | solution.py:556
  34.8 13.5 %collective-permute-start.6 = (f32[66,8,128]{2,1,0:T(8,128)S(1)}, f32[66,8,128]{2,1,0:T(8,128)S(1)}, u32[]{:S(2)}, u32[]{:S(2)}) collective-permute-start(f32[66,8,128]{2,1,0:T(8,128)S(1)} %get-tuple-element.50.refs_2_.refs_5_), channel_id=1, source_target_pairs={{0,2},{2,0},{4,6},{6,4},{8,10},{10,8},{12,14},{14,12},{1,3},{3,1},... | collective-permute-start | bytes 811016 | tf_op jit(solution)/shard_map/ppermute | solution.py:553
  36.0 13.5 %collective-permute-start.9 = (f32[66,8,128]{2,1,0:T(8,128)S(1)}, f32[66,8,128]{2,1,0:T(8,128)S(1)}, u32[]{:S(2)}, u32[]{:S(2)}) collective-permute-start(f32[66,8,128]{2,1,0:T(8,128)S(1)} %get-tuple-element.53.refs_4_.refs_5_), channel_id=1, source_target_pairs={{2,4},{4,2},{6,8},{8,6},{10,12},{12,10},{3,5},{5,3},{7,9},{9,7},{1... | collective-permute-start | bytes 811016 | tf_op jit(solution)/shard_map/ppermute | solution.py:556
  49.4 12.6 %collective-permute-start.8 = (f32[66,8,128]{2,1,0:T(8,128)S(1)}, f32[66,8,128]{2,1,0:T(8,128)S(1)}, u32[]{:S(2)}, u32[]{:S(2)}) collective-permute-start(f32[66,8,128]{2,1,0:T(8,128)S(1)} %get-tuple-element.56.refs_5_.refs_2_), channel_id=1, source_target_pairs={{0,2},{2,0},{4,6},{6,4},{8,10},{10,8},{12,14},{14,12},{1,3},{3,1},... | collective-permute-start | bytes 811016 | tf_op jit(solution)/shard_map/ppermute | solution.py:553
  50.6 12.0 %collective-permute-start.10 = (f32[66,8,128]{2,1,0:T(8,128)S(1)}, f32[66,8,128]{2,1,0:T(8,128)S(1)}, u32[]{:S(2)}, u32[]{:S(2)}) collective-permute-start(f32[66,8,128]{2,1,0:T(8,128)S(1)} %get-tuple-element.60.refs_4_.refs_5_), channel_id=1, source_target_pairs={{2,4},{4,2},{6,8},{8,6},{10,12},{12,10},{3,5},{5,3},{7,9},{9,7},{1... | collective-permute-start | bytes 811016 | tf_op jit(solution)/shard_map/ppermute | solution.py:556

commit v9 on v8

--- a/solution.py
+++ b/solution.py
@@ -206,7 +206,7 @@
 
 def sweep(tiles, low, count, load, factor, z_row, before, constants, store):
     weight, scale = constants
-    chunk = chunk_of(tiles)
+    chunk = tiles if count <= 2 else chunk_of(tiles)
 
     def body(step, carry):
         edges = masks()
@@ -216,11 +216,15 @@
             values, sums, slopes = [], [], []
             for row in range(low - 1, low + count + 1):
                 here = load(row, tile)
-                if k == 0:
+                if k == 0 and chunk == tiles:
+                    last = jnp.zeros_like(here)
+                elif k == 0:
                     last = jnp.where(first > 0, load(row, jnp.maximum(first - 1, 0)), 0.0)
                 else:
                     last = load(row, tile - 1)
-                if k == chunk - 1:
+                if k == chunk - 1 and chunk == tiles:
+                    after = jnp.zeros_like(here)
+                elif k == chunk - 1:
                     more = first + chunk < tiles
                     after = jnp.where(more, load(row, jnp.minimum(first + chunk, tiles - 1)), 0.0)
                 else:
@@ -246,7 +250,10 @@
                 store(row, tile, total)
         return carry
 
-    lax.fori_loop(0, tiles // chunk, body, 0)
+    if chunk == tiles:
+        body(0, 0)
+    else:
+        lax.fori_loop(0, tiles // chunk, body, 0)
 
 
 def first_kernel(part, constants, tiles, *refs):
@@ -630,8 +637,9 @@
     expanded, data = lax.optimization_barrier((expanded, data))
     inner = first(1, [], rows_of(4))
     bottom = first(2, [z_down], edge_rows)
+    _, near_halo = lax.optimization_barrier((bottom, z_up))
     down = far(bottom)
-    top = first(0, [z_up], edge_rows)
+    top = first(0, [near_halo], edge_rows)
     up = near(top)
     once = None
     for order in range(CHEB - 2, 0, -2):
@@ -656,10 +664,12 @@
                 [rows_of(2), edge_rows],
             )
 
-        over, under = edge(True), edge(False)
+        under = edge(False)
+        _, up = lax.optimization_barrier((under[1], up))
+        over = edge(True)
         once = (over[0], inner_once, under[0])
         top, inner, bottom = over[1], inner_twice, under[1]
-        up, down = near(top), far(bottom)
+        down, up = far(bottom), near(top)
 
     factor = 0.5 / (probes.shape[0] * lax.axis_size("probe"))
     count = max(n for n in range(1, 5) if kept % n == 0)

time: 65.7 us -> 64.4 us (0.980)
  the two profiles are of different devices: /device:TPU:24 before, /device:TPU:0 now
where the time goes in v9:
time: 64.4 us; the launch traced here: 64.2 us
  waiting for transfers between devices  25.4 us (39%)
  starting transfers between devices  21.8 us (34%)
  Pallas kernels  16.7 us (26%)
    ppermute x5, waiting for transfers between devices, near(): return lax.ppermute(edge, 'row', near_pairs)  25.4 us
    ppermute x5, starting transfers between devices, near(): return lax.ppermute(edge, 'row', near_pairs)  17.9 us
    pallas_call x17, Pallas kernels, call(): pl.pallas_call(kernel, out_shape=outs, in_specs=in_specs or [vmem_spec()]...  16.7 us
    ppermute x5, starting transfers between devices, far(): return lax.ppermute(edge, 'row', far_pairs)  3.36 us
  transfers between devices with their start and end apart: 11, of which 5 were waited for; matrix products, arithmetic and copies ran while one was open for 0% of the time, Pallas kernels for 19%

profile of v9, /device:TPU:0, one launch (start us, length us, event | category | flops | bytes accessed | tf_op | source)
XLA Modules:
  0.0 64.2 jit_solution(13441366266791265693)
XLA Ops:
  0.0 1.7 %load.1 = (f32[2,2,8,4224]{3,2,1,0:T(8,128)S(1)}, f32[2,2,8,4224]{3,2,1,0:T(8,128)S(1)}, f32[2,8,4224]{2,1,0:T(8,128)S(1)}, f32[9,8,4224]{2,1,0:T(8,128)S(1)}, f...) custom-call(f32[2,2,8,8192]{3,2,1,0:T(8,128)} %probes_ref.1, f32[2,8,8192]{2,1,0:T(8,128)} %observed_ref.1, ...), custom_call_target="tpu_custom_call" | custom-call | flops 2048000 | bytes 1638400 | tf_op jit(solution)/shard_map/load/pallas_call | solution.py:566
  1.7 0.5 collective-permute-start
  2.2 2.6 %collective-permute-start.2 = (f32[47,8,128]{2,1,0:T(8,128)S(1)}, f32[47,8,128]{2,1,0:T(8,128)S(1)}, u32[]{:S(2)}, u32[]{:S(2)}) collective-permute-start(f32[47,8,128]{2,1,0:T(8,128)S(1)} %get-tuple-element.46), channel_id=1, source_target_pairs={{0,2},{2,0},{4,6},{6,4},{8,10},{10,8},{12,14},{14,12},{1,3},{3,1},... | collective-permute-start | bytes 577544 | tf_op jit(solution)/shard_map/ppermute | solution.py:560
  4.8 0.7 %collective-permute-start.3 = (f32[47,8,128]{2,1,0:T(8,128)S(1)}, f32[47,8,128]{2,1,0:T(8,128)S(1)}, u32[]{:S(2)}, u32[]{:S(2)}) collective-permute-start(f32[47,8,128]{2,1,0:T(8,128)S(1)} %get-tuple-element.47), channel_id=1, source_target_pairs={{2,4},{4,2},{6,8},{8,6},{10,12},{12,10},{3,5},{5,3},{7,9},{9,7},{1... | collective-permute-start | bytes 577544 | tf_op jit(solution)/shard_map/ppermute | solution.py:563
  5.5 0.8 %prep.1.refs_2_.refs_1_.refs_3_ = f32[5,33,64,128]{3,2,1,0:T(8,128)S(1)} custom-call(f32[9,8,4224]{2,1,0:T(8,128)S(1)} %get-tuple-element.39.window_ref), custom_call_target="tpu_custom_call" | custom-call | flops 27033600 | bytes 21626880 | tf_op jit(solution)/shard_map/prep/pallas_call | solution.py:566
  6.3 0.0 collective-permute-done.other_ref
  6.3 0.3 layout.1
  6.6 0.7 %collective-permute-start.1 = (f32[33,8,128]{2,1,0:T(8,128)S(1)}, f32[33,8,128]{2,1,0:T(8,128)S(1)}, u32[]{:S(2)}, u32[]{:S(2)}) collective-permute-start(f32[33,8,128]{2,1,0:T(8,128)S(1)} %get-tuple-element.43), channel_id=1, source_target_pairs={{2,4},{4,2},{6,8},{8,6},{10,12},{12,10},{3,5},{5,3},{7,9},{9,7},{1... | collective-permute-start | bytes 405512 | tf_op jit(solution)/shard_map/ppermute | solution.py:563
  7.3 5.6 %collective-permute-start.5 = (f32[33,8,128]{2,1,0:T(8,128)S(1)}, f32[33,8,128]{2,1,0:T(8,128)S(1)}, u32[]{:S(2)}, u32[]{:S(2)}) collective-permute-start(f32[33,8,128]{2,1,0:T(8,128)S(1)} %get-tuple-element.51), channel_id=1, source_target_pairs={{0,2},{2,0},{4,6},{6,4},{8,10},{10,8},{12,14},{14,12},{1,3},{3,1},... | collective-permute-start | bytes 405512 | tf_op jit(solution)/shard_map/ppermute | solution.py:560
  12.9 1.0 %collective-permute-done.2.up_ref = f32[47,8,128]{2,1,0:T(8,128)S(1)} collective-permute-done((f32[47,8,128]{2,1,0:T(8,128)S(1)}, f32[47,8,128]{2,1,0:T(8,128)S(1)}, u32[]{:S(2)}, u32[]{:S(2)}) %collective-permute-start.2) | collective-permute-done | bytes 192544 | tf_op jit(solution)/shard_map/ppermute | solution.py:560
  13.9 0.0 collective-permute-done.3.down_ref
  13.9 1.1 %border.1 = (f32[33,9,8,128]{3,2,1,0:T(8,128)S(1)}, f32[5,33,8,128]{3,2,1,0:T(8,128)S(1)}, f32[5,33,8,128]{3,2,1,0:T(8,128)S(1)}) custom-call(f32[2,8,4224]{2,1,0:T(8,128)S(1)} %get-tuple-element.45.seen_ref, f32[47,8,128]{2,1,0:T(8,128)S(1)} %collective-permute-done.2.up_ref, f32[47,8,128]{2,1,0:T(8,128)S(1)} %collective-permute-done.3.down_ref), custom_call_target="tpu_custom_call" | custom-call | flops 6082560 | bytes 4866048 | tf_op jit(solution)/shard_map/border/pallas_call | solution.py:566
  15.1 0.0 collective-permute-done.1.refs_0_.refs_1_
  15.1 0.4 first.3.refs_4_.refs_5_
  15.5 0.7 %collective-permute-start.4 = (f32[66,8,128]{2,1,0:T(8,128)S(1)}, f32[66,8,128]{2,1,0:T(8,128)S(1)}, u32[]{:S(2)}, u32[]{:S(2)}) collective-permute-start(f32[66,8,128]{2,1,0:T(8,128)S(1)} %first.3.refs_4_.refs_5_), channel_id=1, source_target_pairs={{2,4},{4,2},{6,8},{8,6},{10,12},{12,10},{3,5},{5,3},{7,9},{9,7},{1... | collective-permute-start | bytes 811016 | tf_op jit(solution)/shard_map/ppermute | solution.py:563
  16.1 3.3 %collective-permute-done.5.refs_0_.refs_1_ = f32[33,8,128]{2,1,0:T(8,128)S(1)} collective-permute-done((f32[33,8,128]{2,1,0:T(8,128)S(1)}, f32[33,8,128]{2,1,0:T(8,128)S(1)}, u32[]{:S(2)}, u32[]{:S(2)}) %collective-permute-start.5) | collective-permute-done | bytes 135200 | tf_op jit(solution)/shard_map/ppermute | solution.py:560
  19.4 0.4 first.4.refs_2_.refs_5_
  19.8 4.7 %collective-permute-start.7 = (f32[66,8,128]{2,1,0:T(8,128)S(1)}, f32[66,8,128]{2,1,0:T(8,128)S(1)}, u32[]{:S(2)}, u32[]{:S(2)}) collective-permute-start(f32[66,8,128]{2,1,0:T(8,128)S(1)} %first.4.refs_2_.refs_5_), channel_id=1, source_target_pairs={{0,2},{2,0},{4,6},{6,4},{8,10},{10,8},{12,14},{14,12},{1,3},{3,1},... | collective-permute-start | bytes 811016 | tf_op jit(solution)/shard_map/ppermute | solution.py:560
  24.4 0.7 %first.5.refs_3_ = f32[33,32,128]{2,1,0:T(8,128)S(1)} custom-call(f32[33,64,128]{2,1,0:T(8,128)S(1)} %get-tuple-element.42.refs_1_.refs_0_.refs_2_.z_ref, f32[5,33,64,128]{3,2,1,0:T(8,128)S(1)} %prep.1.refs_2_.refs_1_.refs_3_), custom_call_target="tpu_custom_call" | custom-call | flops 2703360 | bytes 2162688 | tf_op jit(solution)/shard_map/first/pallas_call | solution.py:566
  25.1 1.6 %middle.2 = (f32[33,48,128]{2,1,0:T(8,128)S(1)}, f32[33,32,128]{2,1,0:T(8,128)S(1)}) custom-call(f32[33,64,128]{2,1,0:T(8,128)S(1)} %get-tuple-element.42.refs_1_.refs_0_.refs_2_.z_ref, f32[5,33,64,128]{3,2,1,0:T(8,128)S(1)} %prep.1.refs_2_.refs_1_.refs_3_, f32[66,8,128]{2,1,0:T(8,128)S(1)} %first.4.refs_2_.refs_5_, f32[33,32,128]{2,1,0:T(8,128)S(1)} %first.5.refs_3_, ...), custom_call_target="tpu_custom_call" | custom-call | flops 6758400 | bytes 5406720 | tf_op jit(solution)/shard_map/middle/pallas_call | solution.py:566
  26.7 0.0 collective-permute-done.4.refs_0_
  26.7 0.7 %lower.2 = (f32[33,16,128]{2,1,0:T(8,128)S(1)}, f32[66,8,128]{2,1,0:T(8,128)S(1)}) custom-call(f32[66,8,128]{2,1,0:T(8,128)S(1)} %collective-permute-done.4.refs_0_, f32[33,8,128]{2,1,0:T(8,128)S(1)} %collective-permute-done.1.refs_0_.refs_1_, f32[33,64,128]{2,1,0:T(8,128)S(1)} %get-tuple-element.42.refs_1_.refs_0_.refs_2_.z_ref, ...), custom_call_target="tpu_custom_call" | custom-call | flops 2703360 | bytes 2162688 | tf_op jit(solution)/shard_map/lower/pallas_call | solution.py:566
  27.3 0.7 %collective-permute-start.6 = (f32[66,8,128]{2,1,0:T(8,128)S(1)}, f32[66,8,128]{2,1,0:T(8,128)S(1)}, u32[]{:S(2)}, u32[]{:S(2)}) collective-permute-start(f32[66,8,128]{2,1,0:T(8,128)S(1)} %get-tuple-element.54.refs_4_.refs_5_), channel_id=1, source_target_pairs={{2,4},{4,2},{6,8},{8,6},{10,12},{12,10},{3,5},{5,3},{7,9},{9,7},{1... | collective-permute-start | bytes 811016 | tf_op jit(solution)/shard_map/ppermute | solution.py:563
  28.0 10.8 %collective-permute-done.7.refs_0_ = f32[66,8,128]{2,1,0:T(8,128)S(1)} collective-permute-done((f32[66,8,128]{2,1,0:T(8,128)S(1)}, f32[66,8,128]{2,1,0:T(8,128)S(1)}, u32[]{:S(2)}, u32[]{:S(2)}) %collective-permute-start.7) | collective-permute-done | bytes 270368 | tf_op jit(solution)/shard_map/ppermute | solution.py:560
  38.8 0.7 %upper.2 = (f32[33,16,128]{2,1,0:T(8,128)S(1)}, f32[66,8,128]{2,1,0:T(8,128)S(1)}) custom-call(f32[66,8,128]{2,1,0:T(8,128)S(1)} %collective-permute-done.7.refs_0_, f32[33,8,128]{2,1,0:T(8,128)S(1)} %collective-permute-done.5.refs_0_.refs_1_, f32[33,64,128]{2,1,0:T(8,128)S(1)} %get-tuple-element.42.refs_1_.refs_0_.refs_2_.z_ref, ...), custom_call_target="tpu_custom_call" | custom-call | flops 2703360 | bytes 2162688 | tf_op jit(solution)/shard_map/upper/pallas_call | solution.py:566
  39.5 2.6 %collective-permute-start.8 = (f32[66,8,128]{2,1,0:T(8,128)S(1)}, f32[66,8,128]{2,1,0:T(8,128)S(1)}, u32[]{:S(2)}, u32[]{:S(2)}) collective-permute-start(f32[66,8,128]{2,1,0:T(8,128)S(1)} %get-tuple-element.57.refs_2_.refs_5_), channel_id=1, source_target_pairs={{0,2},{2,0},{4,6},{6,4},{8,10},{10,8},{12,14},{14,12},{1,3},{3,1},... | collective-permute-start | bytes 811016 | tf_op jit(solution)/shard_map/ppermute | solution.py:560
  42.1 1.6 %middle.3 = (f32[33,48,128]{2,1,0:T(8,128)S(1)}, f32[33,32,128]{2,1,0:T(8,128)S(1)}) custom-call(f32[33,64,128]{2,1,0:T(8,128)S(1)} %get-tuple-element.42.refs_1_.refs_0_.refs_2_.z_ref, f32[5,33,64,128]{3,2,1,0:T(8,128)S(1)} %prep.1.refs_2_.refs_1_.refs_3_, f32[66,8,128]{2,1,0:T(8,128)S(1)} %get-tuple-element.57.refs_2_.refs_5_, ...), custom_call_target="tpu_custom_call" | custom-call | flops 6758400 | bytes 5406720 | tf_op jit(solution)/shard_map/middle/pallas_call | solution.py:566
  43.6 0.0 collective-permute-done.6.refs_0_
  43.6 0.7 %lower.3 = (f32[33,16,128]{2,1,0:T(8,128)S(1)}, f32[66,8,128]{2,1,0:T(8,128)S(1)}) custom-call(f32[66,8,128]{2,1,0:T(8,128)S(1)} %collective-permute-done.6.refs_0_, f32[33,8,128]{2,1,0:T(8,128)S(1)} %collective-permute-done.1.refs_0_.refs_1_, f32[33,64,128]{2,1,0:T(8,128)S(1)} %get-tuple-element.42.refs_1_.refs_0_.refs_2_.z_ref, ...), custom_call_target="tpu_custom_call" | custom-call | flops 2703360 | bytes 2162688 | tf_op jit(solution)/shard_map/lower/pallas_call | solution.py:566
  44.3 0.7 %collective-permute-start.10 = (f32[66,8,128]{2,1,0:T(8,128)S(1)}, f32[66,8,128]{2,1,0:T(8,128)S(1)}, u32[]{:S(2)}, u32[]{:S(2)}) collective-permute-start(f32[66,8,128]{2,1,0:T(8,128)S(1)} %get-tuple-element.61.refs_4_.refs_5_), channel_id=1, source_target_pairs={{2,4},{4,2},{6,8},{8,6},{10,12},{12,10},{3,5},{5,3},{7,9},{9,7},{1... | collective-permute-start | bytes 811016 | tf_op jit(solution)/shard_map/ppermute | solution.py:563
  45.0 8.6 %collective-permute-done.8.refs_0_ = f32[66,8,128]{2,1,0:T(8,128)S(1)} collective-permute-done((f32[66,8,128]{2,1,0:T(8,128)S(1)}, f32[66,8,128]{2,1,0:T(8,128)S(1)}, u32[]{:S(2)}, u32[]{:S(2)}) %collective-permute-start.8) | collective-permute-done | bytes 270368 | tf_op jit(solution)/shard_map/ppermute | solution.py:560
  53.7 0.7 %upper.3 = (f32[33,16,128]{2,1,0:T(8,128)S(1)}, f32[66,8,128]{2,1,0:T(8,128)S(1)}) custom-call(f32[66,8,128]{2,1,0:T(8,128)S(1)} %collective-permute-done.8.refs_0_, f32[33,8,128]{2,1,0:T(8,128)S(1)} %collective-permute-done.5.refs_0_.refs_1_, f32[33,64,128]{2,1,0:T(8,128)S(1)} %get-tuple-element.42.refs_1_.refs_0_.refs_2_.z_ref, ...), custom_call_target="tpu_custom_call" | custom-call | flops 2703360 | bytes 2162688 | tf_op jit(solution)/shard_map/upper/pallas_call | solution.py:566
  54.4 2.6 %collective-permute-start.9 = (f32[66,8,128]{2,1,0:T(8,128)S(1)}, f32[66,8,128]{2,1,0:T(8,128)S(1)}, u32[]{:S(2)}, u32[]{:S(2)}) collective-permute-start(f32[66,8,128]{2,1,0:T(8,128)S(1)} %get-tuple-element.64.refs_5_.refs_2_), channel_id=1, source_target_pairs={{0,2},{2,0},{4,6},{6,4},{8,10},{10,8},{12,14},{14,12},{1,3},{3,1},... | collective-permute-start | bytes 811016 | tf_op jit(solution)/shard_map/ppermute | solution.py:560
  56.9 2.4 %gradient.1 = (f32[33,48,128]{2,1,0:T(8,128)S(1)}, f32[9,8,4096]{2,1,0:T(8,128)S(1)}) custom-call(f32[33,64,128]{2,1,0:T(8,128)S(1)} %get-tuple-element.42.refs_1_.refs_0_.refs_2_.z_ref, f32[5,33,64,128]{3,2,1,0:T(8,128)S(1)} %prep.1.refs_2_.refs_1_.refs_3_, f32[66,8,128]{2,1,0:T(8,128)S(1)} %get-tuple-element.64.refs_5_.refs_2_, ...), custom_call_target="tpu_custom_call" | custom-call | flops 16220160 | bytes 12976128 | tf_op jit(solution)/shard_map/gradient/pallas_call | solution.py:566
  59.3 0.0 collective-permute-done.10.refs_0_
  59.3 0.4 lower_end.1.under_ref
  59.7 1.7 %collective-permute-done.9.refs_0_ = f32[66,8,128]{2,1,0:T(8,128)S(1)} collective-permute-done((f32[66,8,128]{2,1,0:T(8,128)S(1)}, f32[66,8,128]{2,1,0:T(8,128)S(1)}, u32[]{:S(2)}, u32[]{:S(2)}) %collective-permute-start.9) | collective-permute-done | bytes 270368 | tf_op jit(solution)/shard_map/ppermute | solution.py:560
  61.4 0.4 upper_end.1.over_ref
  61.8 2.4 %finish.1 = f32[9,8,4096]{2,1,0:T(8,128)} custom-call(f32[33,64,128]{2,1,0:T(8,128)S(1)} %get-tuple-element.42.refs_1_.refs_0_.refs_2_.z_ref, f32[33,16,128]{2,1,0:T(8,128)S(1)} %upper_end.1.over_ref, f32[33,48,128]{2,1,0:T(8,128)S(1)} %get-tuple-element.68.inner_ref, f32[33,16,128]{2,1,0:T(8,128)S(1)} %lower_end.1.under_ref, ...), custom_call_target="tpu_custom_call" | custom-call | flops 10813440 | bytes 8650752 | tf_op jit(solution)/shard_map/finish/pallas_call | solution.py:566
Async XLA Ops:
  1.7 4.6 %collective-permute-start = (f32[2,2,8,4224]{3,2,1,0:T(8,128)S(1)}, f32[2,2,8,4224]{3,2,1,0:T(8,128)S(1)}, u32[]{:S(2)}, u32[]{:S(2)}) collective-permute-start(f32[2,2,8,4224]{3,2,1,0:T(8,128)S(1)} %get-tuple-element.41), channel_id=1, source_target_pairs={{0,1},{1,0},{2,3},{3,2},{4,5},{5,4},{6,7},{7,6},{8,9},{9,8},{10,11... | collective-permute-start | bytes 1622024 | tf_op jit(solution)/shard_map/ppermute | solution.py:599
  2.2 11.7 %collective-permute-start.2 = (f32[47,8,128]{2,1,0:T(8,128)S(1)}, f32[47,8,128]{2,1,0:T(8,128)S(1)}, u32[]{:S(2)}, u32[]{:S(2)}) collective-permute-start(f32[47,8,128]{2,1,0:T(8,128)S(1)} %get-tuple-element.46), channel_id=1, source_target_pairs={{0,2},{2,0},{4,6},{6,4},{8,10},{10,8},{12,14},{14,12},{1,3},{3,1},... | collective-permute-start | bytes 577544 | tf_op jit(solution)/shard_map/ppermute | solution.py:560
  4.8 9.1 %collective-permute-start.3 = (f32[47,8,128]{2,1,0:T(8,128)S(1)}, f32[47,8,128]{2,1,0:T(8,128)S(1)}, u32[]{:S(2)}, u32[]{:S(2)}) collective-permute-start(f32[47,8,128]{2,1,0:T(8,128)S(1)} %get-tuple-element.47), channel_id=1, source_target_pairs={{2,4},{4,2},{6,8},{8,6},{10,12},{12,10},{3,5},{5,3},{7,9},{9,7},{1... | collective-permute-start | bytes 577544 | tf_op jit(solution)/shard_map/ppermute | solution.py:563
  6.6 8.5 %collective-permute-start.1 = (f32[33,8,128]{2,1,0:T(8,128)S(1)}, f32[33,8,128]{2,1,0:T(8,128)S(1)}, u32[]{:S(2)}, u32[]{:S(2)}) collective-permute-start(f32[33,8,128]{2,1,0:T(8,128)S(1)} %get-tuple-element.43), channel_id=1, source_target_pairs={{2,4},{4,2},{6,8},{8,6},{10,12},{12,10},{3,5},{5,3},{7,9},{9,7},{1... | collective-permute-start | bytes 405512 | tf_op jit(solution)/shard_map/ppermute | solution.py:563
  7.3 12.1 %collective-permute-start.5 = (f32[33,8,128]{2,1,0:T(8,128)S(1)}, f32[33,8,128]{2,1,0:T(8,128)S(1)}, u32[]{:S(2)}, u32[]{:S(2)}) collective-permute-start(f32[33,8,128]{2,1,0:T(8,128)S(1)} %get-tuple-element.51), channel_id=1, source_target_pairs={{0,2},{2,0},{4,6},{6,4},{8,10},{10,8},{12,14},{14,12},{1,3},{3,1},... | collective-permute-start | bytes 405512 | tf_op jit(solution)/shard_map/ppermute | solution.py:560
  15.5 11.2 %collective-permute-start.4 = (f32[66,8,128]{2,1,0:T(8,128)S(1)}, f32[66,8,128]{2,1,0:T(8,128)S(1)}, u32[]{:S(2)}, u32[]{:S(2)}) collective-permute-start(f32[66,8,128]{2,1,0:T(8,128)S(1)} %first.3.refs_4_.refs_5_), channel_id=1, source_target_pairs={{2,4},{4,2},{6,8},{8,6},{10,12},{12,10},{3,5},{5,3},{7,9},{9,7},{1... | collective-permute-start | bytes 811016 | tf_op jit(solution)/shard_map/ppermute | solution.py:563
  19.8 19.1 %collective-permute-start.7 = (f32[66,8,128]{2,1,0:T(8,128)S(1)}, f32[66,8,128]{2,1,0:T(8,128)S(1)}, u32[]{:S(2)}, u32[]{:S(2)}) collective-permute-start(f32[66,8,128]{2,1,0:T(8,128)S(1)} %first.4.refs_2_.refs_5_), channel_id=1, source_target_pairs={{0,2},{2,0},{4,6},{6,4},{8,10},{10,8},{12,14},{14,12},{1,3},{3,1},... | collective-permute-start | bytes 811016 | tf_op jit(solution)/shard_map/ppermute | solution.py:560
  27.3 16.3 %collective-permute-start.6 = (f32[66,8,128]{2,1,0:T(8,128)S(1)}, f32[66,8,128]{2,1,0:T(8,128)S(1)}, u32[]{:S(2)}, u32[]{:S(2)}) collective-permute-start(f32[66,8,128]{2,1,0:T(8,128)S(1)} %get-tuple-element.54.refs_4_.refs_5_), channel_id=1, source_target_pairs={{2,4},{4,2},{6,8},{8,6},{10,12},{12,10},{3,5},{5,3},{7,9},{9,7},{1... | collective-permute-start | bytes 811016 | tf_op jit(solution)/shard_map/ppermute | solution.py:563
  39.5 14.2 %collective-permute-start.8 = (f32[66,8,128]{2,1,0:T(8,128)S(1)}, f32[66,8,128]{2,1,0:T(8,128)S(1)}, u32[]{:S(2)}, u32[]{:S(2)}) collective-permute-start(f32[66,8,128]{2,1,0:T(8,128)S(1)} %get-tuple-element.57.refs_2_.refs_5_), channel_id=1, source_target_pairs={{0,2},{2,0},{4,6},{6,4},{8,10},{10,8},{12,14},{14,12},{1,3},{3,1},... | collective-permute-start | bytes 811016 | tf_op jit(solution)/shard_map/ppermute | solution.py:560
  44.3 15.0 %collective-permute-start.10 = (f32[66,8,128]{2,1,0:T(8,128)S(1)}, f32[66,8,128]{2,1,0:T(8,128)S(1)}, u32[]{:S(2)}, u32[]{:S(2)}) collective-permute-start(f32[66,8,128]{2,1,0:T(8,128)S(1)} %get-tuple-element.61.refs_4_.refs_5_), channel_id=1, source_target_pairs={{2,4},{4,2},{6,8},{8,6},{10,12},{12,10},{3,5},{5,3},{7,9},{9,7},{1... | collective-permute-start | bytes 811016 | tf_op jit(solution)/shard_map/ppermute | solution.py:563
  54.4 7.0 %collective-permute-start.9 = (f32[66,8,128]{2,1,0:T(8,128)S(1)}, f32[66,8,128]{2,1,0:T(8,128)S(1)}, u32[]{:S(2)}, u32[]{:S(2)}) collective-permute-start(f32[66,8,128]{2,1,0:T(8,128)S(1)} %get-tuple-element.64.refs_5_.refs_2_), channel_id=1, source_target_pairs={{0,2},{2,0},{4,6},{6,4},{8,10},{10,8},{12,14},{14,12},{1,3},{3,1},... | collective-permute-start | bytes 811016 | tf_op jit(solution)/shard_map/ppermute | solution.py:560

commit v10 on v9

--- a/solution.py
+++ b/solution.py
@@ -626,6 +626,14 @@
             out,
         )
 
+    expanded, edges_up, edges_down = lax.optimization_barrier((expanded, edges_up, edges_down))
+    inner = first(1, [], rows_of(4))
+    bottom = first(2, [z_down], edge_rows)
+    _, near_halo = lax.optimization_barrier((bottom, z_up))
+    down = far(bottom)
+    top = first(0, [near_halo], edge_rows)
+    up = near(top)
+    _, seen = lax.optimization_barrier((top, seen))
     rim_shape = pltpu.VMEM((5, tiles, SUBS, LANES), f32)
     data, rim_up, rim_down = call(
         functools.partial(border_kernel, tiles),
@@ -634,13 +642,6 @@
         (seen, edges_up, edges_down),
         [pltpu.VMEM((tiles, 9, SUBS, LANES), f32), rim_shape, rim_shape],
     )
-    expanded, data = lax.optimization_barrier((expanded, data))
-    inner = first(1, [], rows_of(4))
-    bottom = first(2, [z_down], edge_rows)
-    _, near_halo = lax.optimization_barrier((bottom, z_up))
-    down = far(bottom)
-    top = first(0, [near_halo], edge_rows)
-    up = near(top)
     once = None
     for order in range(CHEB - 2, 0, -2):
         opening = weights[order] - (weights[CHEB] if order == CHEB - 2 else 0.0)
@@ -697,14 +698,15 @@
             (False, (down, z_down, z, expanded, rim_down, bottom, once[2])),
         )
     ]
-    groups = max(n for n in range(1, 5) if kept // count % n == 0)
+    wide = max(n for n in range(1, 9) if kept % n == 0)
+    groups = max(n for n in range(1, 5) if kept // wide % n == 0)
     return call(
         functools.partial(finish_kernel, tiles, factor),
         "finish",
         16 * tiles,
         (z, ends[0], series, ends[1], part),
         jax.ShapeDtypeStruct(whole, f32),
-        [products, pltpu.VMEM(whole, f32), pltpu.SemaphoreType.DMA((groups,))],
+        [pltpu.VMEM((wide, 5, SUBS * SUBS, LANES), f32), pltpu.VMEM(whole, f32), pltpu.SemaphoreType.DMA((groups,))],
         None,
         pl.BlockSpec(memory_space=pltpu.HBM),
     )

time: 64.4 us -> 64.9 us (level)
  waiting for transfers between devices: 25.4 us -> 27.1 us
  starting transfers between devices: 21.8 us -> 20.7 us
    ppermute x5, waiting for transfers between devices: 25.4 us -> 27.1 us  [near(): return lax.ppermute(edge, 'row', near_pairs)]
    ppermute x5, starting transfers between devices: 17.9 us -> 16.8 us  [near(): return lax.ppermute(edge, 'row', near_pairs)]
where the time goes in v10:
time: 64.9 us; the launch traced here: 64.7 us
  waiting for transfers between devices  27.1 us (42%)
  starting transfers between devices  20.7 us (32%)
  Pallas kernels  16.7 us (26%)
    ppermute x5, waiting for transfers between devices, near(): return lax.ppermute(edge, 'row', near_pairs)  27.1 us
    ppermute x5, starting transfers between devices, near(): return lax.ppermute(edge, 'row', near_pairs)  16.8 us
    pallas_call x17, Pallas kernels, call(): pl.pallas_call(kernel, out_shape=outs, in_specs=in_specs or [vmem_spec()]...  16.7 us
    ppermute x5, starting transfers between devices, far(): return lax.ppermute(edge, 'row', far_pairs)  3.36 us
  transfers between devices with their start and end apart: 11, of which 5 were waited for; matrix products, arithmetic and copies ran while one was open for 0% of the time, Pallas kernels for 19%

profile of v10, /device:TPU:0, one launch (start us, length us, event | category | flops | bytes accessed | tf_op | source)
XLA Modules:
  0.0 64.7 jit_solution(4549129901548565526)
XLA Ops:
  0.0 1.7 %load.1 = (f32[2,2,8,4224]{3,2,1,0:T(8,128)S(1)}, f32[2,2,8,4224]{3,2,1,0:T(8,128)S(1)}, f32[2,8,4224]{2,1,0:T(8,128)S(1)}, f32[9,8,4224]{2,1,0:T(8,128)S(1)}, f...) custom-call(f32[2,2,8,8192]{3,2,1,0:T(8,128)} %probes_ref.1, f32[2,8,8192]{2,1,0:T(8,128)} %observed_ref.1, ...), custom_call_target="tpu_custom_call" | custom-call | flops 2048000 | bytes 1638400 | tf_op jit(solution)/shard_map/load/pallas_call | solution.py:566
  1.7 0.5 collective-permute-start
  2.2 2.6 %collective-permute-start.2 = (f32[47,8,128]{2,1,0:T(8,128)S(1)}, f32[47,8,128]{2,1,0:T(8,128)S(1)}, u32[]{:S(2)}, u32[]{:S(2)}) collective-permute-start(f32[47,8,128]{2,1,0:T(8,128)S(1)} %get-tuple-element.47), channel_id=1, source_target_pairs={{0,2},{2,0},{4,6},{6,4},{8,10},{10,8},{12,14},{14,12},{1,3},{3,1},... | collective-permute-start | bytes 577544 | tf_op jit(solution)/shard_map/ppermute | solution.py:560
  4.8 0.7 %collective-permute-start.3 = (f32[47,8,128]{2,1,0:T(8,128)S(1)}, f32[47,8,128]{2,1,0:T(8,128)S(1)}, u32[]{:S(2)}, u32[]{:S(2)}) collective-permute-start(f32[47,8,128]{2,1,0:T(8,128)S(1)} %get-tuple-element.48), channel_id=1, source_target_pairs={{2,4},{4,2},{6,8},{8,6},{10,12},{12,10},{3,5},{5,3},{7,9},{9,7},{1... | collective-permute-start | bytes 577544 | tf_op jit(solution)/shard_map/ppermute | solution.py:563
  5.5 0.8 %prep.1.refs_2_.refs_1_.refs_3_ = f32[5,33,64,128]{3,2,1,0:T(8,128)S(1)} custom-call(f32[9,8,4224]{2,1,0:T(8,128)S(1)} %get-tuple-element.41.window_ref), custom_call_target="tpu_custom_call" | custom-call | flops 27033600 | bytes 21626880 | tf_op jit(solution)/shard_map/prep/pallas_call | solution.py:566
  6.3 0.0 collective-permute-done.other_ref
  6.3 0.3 layout.1
  6.6 0.7 %collective-permute-start.1 = (f32[33,8,128]{2,1,0:T(8,128)S(1)}, f32[33,8,128]{2,1,0:T(8,128)S(1)}, u32[]{:S(2)}, u32[]{:S(2)}) collective-permute-start(f32[33,8,128]{2,1,0:T(8,128)S(1)} %get-tuple-element.45), channel_id=1, source_target_pairs={{2,4},{4,2},{6,8},{8,6},{10,12},{12,10},{3,5},{5,3},{7,9},{9,7},{1... | collective-permute-start | bytes 405512 | tf_op jit(solution)/shard_map/ppermute | solution.py:563
  7.3 5.6 %collective-permute-start.5 = (f32[33,8,128]{2,1,0:T(8,128)S(1)}, f32[33,8,128]{2,1,0:T(8,128)S(1)}, u32[]{:S(2)}, u32[]{:S(2)}) collective-permute-start(f32[33,8,128]{2,1,0:T(8,128)S(1)} %get-tuple-element.50), channel_id=1, source_target_pairs={{0,2},{2,0},{4,6},{6,4},{8,10},{10,8},{12,14},{14,12},{1,3},{3,1},... | collective-permute-start | bytes 405512 | tf_op jit(solution)/shard_map/ppermute | solution.py:560
  12.9 1.0 %collective-permute-done.2.up_ref = f32[47,8,128]{2,1,0:T(8,128)S(1)} collective-permute-done((f32[47,8,128]{2,1,0:T(8,128)S(1)}, f32[47,8,128]{2,1,0:T(8,128)S(1)}, u32[]{:S(2)}, u32[]{:S(2)}) %collective-permute-start.2) | collective-permute-done | bytes 192544 | tf_op jit(solution)/shard_map/ppermute | solution.py:560
  13.9 0.0 collective-permute-done.3.down_ref
  13.9 0.0 collective-permute-done.1.refs_0_.refs_1_
  13.9 0.4 first.3.refs_4_.refs_5_
  14.3 0.7 %collective-permute-start.4 = (f32[66,8,128]{2,1,0:T(8,128)S(1)}, f32[66,8,128]{2,1,0:T(8,128)S(1)}, u32[]{:S(2)}, u32[]{:S(2)}) collective-permute-start(f32[66,8,128]{2,1,0:T(8,128)S(1)} %first.3.refs_4_.refs_5_), channel_id=1, source_target_pairs={{2,4},{4,2},{6,8},{8,6},{10,12},{12,10},{3,5},{5,3},{7,9},{9,7},{1... | collective-permute-start | bytes 811016 | tf_op jit(solution)/shard_map/ppermute | solution.py:563
  15.0 4.4 %collective-permute-done.5.refs_0_.refs_1_ = f32[33,8,128]{2,1,0:T(8,128)S(1)} collective-permute-done((f32[33,8,128]{2,1,0:T(8,128)S(1)}, f32[33,8,128]{2,1,0:T(8,128)S(1)}, u32[]{:S(2)}, u32[]{:S(2)}) %collective-permute-start.5) | collective-permute-done | bytes 135200 | tf_op jit(solution)/shard_map/ppermute | solution.py:560
  19.4 0.4 first.4.refs_2_.refs_5_
  19.8 3.5 %collective-permute-start.7 = (f32[66,8,128]{2,1,0:T(8,128)S(1)}, f32[66,8,128]{2,1,0:T(8,128)S(1)}, u32[]{:S(2)}, u32[]{:S(2)}) collective-permute-start(f32[66,8,128]{2,1,0:T(8,128)S(1)} %first.4.refs_2_.refs_5_), channel_id=1, source_target_pairs={{0,2},{2,0},{4,6},{6,4},{8,10},{10,8},{12,14},{14,12},{1,3},{3,1},... | collective-permute-start | bytes 811016 | tf_op jit(solution)/shard_map/ppermute | solution.py:560
  23.3 0.7 %first.5.refs_3_ = f32[33,32,128]{2,1,0:T(8,128)S(1)} custom-call(f32[33,64,128]{2,1,0:T(8,128)S(1)} %get-tuple-element.44.refs_1_.refs_0_.refs_2_.z_ref, f32[5,33,64,128]{3,2,1,0:T(8,128)S(1)} %prep.1.refs_2_.refs_1_.refs_3_), custom_call_target="tpu_custom_call" | custom-call | flops 2703360 | bytes 2162688 | tf_op jit(solution)/shard_map/first/pallas_call | solution.py:566
  23.9 1.2 %border.1 = (f32[33,9,8,128]{3,2,1,0:T(8,128)S(1)}, f32[5,33,8,128]{3,2,1,0:T(8,128)S(1)}, f32[5,33,8,128]{3,2,1,0:T(8,128)S(1)}) custom-call(f32[2,8,4224]{2,1,0:T(8,128)S(1)} %get-tuple-element.53.seen_ref, f32[47,8,128]{2,1,0:T(8,128)S(1)} %collective-permute-done.2.up_ref, f32[47,8,128]{2,1,0:T(8,128)S(1)} %collective-permute-done.3.down_ref), custom_call_target="tpu_custom_call" | custom-call | flops 6082560 | bytes 4866048 | tf_op jit(solution)/shard_map/border/pallas_call | solution.py:566
  25.1 1.6 %middle.2 = (f32[33,48,128]{2,1,0:T(8,128)S(1)}, f32[33,32,128]{2,1,0:T(8,128)S(1)}) custom-call(f32[33,64,128]{2,1,0:T(8,128)S(1)} %get-tuple-element.44.refs_1_.refs_0_.refs_2_.z_ref, f32[5,33,64,128]{3,2,1,0:T(8,128)S(1)} %prep.1.refs_2_.refs_1_.refs_3_, f32[66,8,128]{2,1,0:T(8,128)S(1)} %first.4.refs_2_.refs_5_, f32[33,32,128]{2,1,0:T(8,128)S(1)} %first.5.refs_3_, ...), custom_call_target="tpu_custom_call" | custom-call | flops 6758400 | bytes 5406720 | tf_op jit(solution)/shard_map/middle/pallas_call | solution.py:566
  26.7 0.0 collective-permute-done.4.refs_0_
  26.7 0.7 %lower.2 = (f32[33,16,128]{2,1,0:T(8,128)S(1)}, f32[66,8,128]{2,1,0:T(8,128)S(1)}) custom-call(f32[66,8,128]{2,1,0:T(8,128)S(1)} %collective-permute-done.4.refs_0_, f32[33,8,128]{2,1,0:T(8,128)S(1)} %collective-permute-done.1.refs_0_.refs_1_, f32[33,64,128]{2,1,0:T(8,128)S(1)} %get-tuple-element.44.refs_1_.refs_0_.refs_2_.z_ref, ...), custom_call_target="tpu_custom_call" | custom-call | flops 2703360 | bytes 2162688 | tf_op jit(solution)/shard_map/lower/pallas_call | solution.py:566
  27.3 0.7 %collective-permute-start.6 = (f32[66,8,128]{2,1,0:T(8,128)S(1)}, f32[66,8,128]{2,1,0:T(8,128)S(1)}, u32[]{:S(2)}, u32[]{:S(2)}) collective-permute-start(f32[66,8,128]{2,1,0:T(8,128)S(1)} %get-tuple-element.58.refs_4_.refs_5_), channel_id=1, source_target_pairs={{2,4},{4,2},{6,8},{8,6},{10,12},{12,10},{3,5},{5,3},{7,9},{9,7},{1... | collective-permute-start | bytes 811016 | tf_op jit(solution)/shard_map/ppermute | solution.py:563
  28.0 10.8 %collective-permute-done.7.refs_0_ = f32[66,8,128]{2,1,0:T(8,128)S(1)} collective-permute-done((f32[66,8,128]{2,1,0:T(8,128)S(1)}, f32[66,8,128]{2,1,0:T(8,128)S(1)}, u32[]{:S(2)}, u32[]{:S(2)}) %collective-permute-start.7) | collective-permute-done | bytes 270368 | tf_op jit(solution)/shard_map/ppermute | solution.py:560
  38.8 0.7 %upper.2 = (f32[33,16,128]{2,1,0:T(8,128)S(1)}, f32[66,8,128]{2,1,0:T(8,128)S(1)}) custom-call(f32[66,8,128]{2,1,0:T(8,128)S(1)} %collective-permute-done.7.refs_0_, f32[33,8,128]{2,1,0:T(8,128)S(1)} %collective-permute-done.5.refs_0_.refs_1_, f32[33,64,128]{2,1,0:T(8,128)S(1)} %get-tuple-element.44.refs_1_.refs_0_.refs_2_.z_ref, ...), custom_call_target="tpu_custom_call" | custom-call | flops 2703360 | bytes 2162688 | tf_op jit(solution)/shard_map/upper/pallas_call | solution.py:566
  39.5 2.6 %collective-permute-start.8 = (f32[66,8,128]{2,1,0:T(8,128)S(1)}, f32[66,8,128]{2,1,0:T(8,128)S(1)}, u32[]{:S(2)}, u32[]{:S(2)}) collective-permute-start(f32[66,8,128]{2,1,0:T(8,128)S(1)} %get-tuple-element.61.refs_2_.refs_5_), channel_id=1, source_target_pairs={{0,2},{2,0},{4,6},{6,4},{8,10},{10,8},{12,14},{14,12},{1,3},{3,1},... | collective-permute-start | bytes 811016 | tf_op jit(solution)/shard_map/ppermute | solution.py:560
  42.1 1.6 %middle.3 = (f32[33,48,128]{2,1,0:T(8,128)S(1)}, f32[33,32,128]{2,1,0:T(8,128)S(1)}) custom-call(f32[33,64,128]{2,1,0:T(8,128)S(1)} %get-tuple-element.44.refs_1_.refs_0_.refs_2_.z_ref, f32[5,33,64,128]{3,2,1,0:T(8,128)S(1)} %prep.1.refs_2_.refs_1_.refs_3_, f32[66,8,128]{2,1,0:T(8,128)S(1)} %get-tuple-element.61.refs_2_.refs_5_, ...), custom_call_target="tpu_custom_call" | custom-call | flops 6758400 | bytes 5406720 | tf_op jit(solution)/shard_map/middle/pallas_call | solution.py:566
  43.6 0.0 collective-permute-done.6.refs_0_
  43.6 0.7 %lower.3 = (f32[33,16,128]{2,1,0:T(8,128)S(1)}, f32[66,8,128]{2,1,0:T(8,128)S(1)}) custom-call(f32[66,8,128]{2,1,0:T(8,128)S(1)} %collective-permute-done.6.refs_0_, f32[33,8,128]{2,1,0:T(8,128)S(1)} %collective-permute-done.1.refs_0_.refs_1_, f32[33,64,128]{2,1,0:T(8,128)S(1)} %get-tuple-element.44.refs_1_.refs_0_.refs_2_.z_ref, ...), custom_call_target="tpu_custom_call" | custom-call | flops 2703360 | bytes 2162688 | tf_op jit(solution)/shard_map/lower/pallas_call | solution.py:566
  44.3 0.7 %collective-permute-start.10 = (f32[66,8,128]{2,1,0:T(8,128)S(1)}, f32[66,8,128]{2,1,0:T(8,128)S(1)}, u32[]{:S(2)}, u32[]{:S(2)}) collective-permute-start(f32[66,8,128]{2,1,0:T(8,128)S(1)} %get-tuple-element.65.refs_4_.refs_5_), channel_id=1, source_target_pairs={{2,4},{4,2},{6,8},{8,6},{10,12},{12,10},{3,5},{5,3},{7,9},{9,7},{1... | collective-permute-start | bytes 811016 | tf_op jit(solution)/shard_map/ppermute | solution.py:563
  45.0 9.2 %collective-permute-done.8.refs_0_ = f32[66,8,128]{2,1,0:T(8,128)S(1)} collective-permute-done((f32[66,8,128]{2,1,0:T(8,128)S(1)}, f32[66,8,128]{2,1,0:T(8,128)S(1)}, u32[]{:S(2)}, u32[]{:S(2)}) %collective-permute-start.8) | collective-permute-done | bytes 270368 | tf_op jit(solution)/shard_map/ppermute | solution.py:560
  54.2 0.7 %upper.3 = (f32[33,16,128]{2,1,0:T(8,128)S(1)}, f32[66,8,128]{2,1,0:T(8,128)S(1)}) custom-call(f32[66,8,128]{2,1,0:T(8,128)S(1)} %collective-permute-done.8.refs_0_, f32[33,8,128]{2,1,0:T(8,128)S(1)} %collective-permute-done.5.refs_0_.refs_1_, f32[33,64,128]{2,1,0:T(8,128)S(1)} %get-tuple-element.44.refs_1_.refs_0_.refs_2_.z_ref, ...), custom_call_target="tpu_custom_call" | custom-call | flops 2703360 | bytes 2162688 | tf_op jit(solution)/shard_map/upper/pallas_call | solution.py:566
  54.9 2.6 %collective-permute-start.9 = (f32[66,8,128]{2,1,0:T(8,128)S(1)}, f32[66,8,128]{2,1,0:T(8,128)S(1)}, u32[]{:S(2)}, u32[]{:S(2)}) collective-permute-start(f32[66,8,128]{2,1,0:T(8,128)S(1)} %get-tuple-element.68.refs_5_.refs_2_), channel_id=1, source_target_pairs={{0,2},{2,0},{4,6},{6,4},{8,10},{10,8},{12,14},{14,12},{1,3},{3,1},... | collective-permute-start | bytes 811016 | tf_op jit(solution)/shard_map/ppermute | solution.py:560
  57.5 2.4 %gradient.1 = (f32[33,48,128]{2,1,0:T(8,128)S(1)}, f32[9,8,4096]{2,1,0:T(8,128)S(1)}) custom-call(f32[33,64,128]{2,1,0:T(8,128)S(1)} %get-tuple-element.44.refs_1_.refs_0_.refs_2_.z_ref, f32[5,33,64,128]{3,2,1,0:T(8,128)S(1)} %prep.1.refs_2_.refs_1_.refs_3_, f32[66,8,128]{2,1,0:T(8,128)S(1)} %get-tuple-element.68.refs_5_.refs_2_, ...), custom_call_target="tpu_custom_call" | custom-call | flops 16220160 | bytes 12976128 | tf_op jit(solution)/shard_map/gradient/pallas_call | solution.py:566
  59.8 0.0 collective-permute-done.10.refs_0_
  59.9 0.4 lower_end.1.under_ref
  60.2 1.7 %collective-permute-done.9.refs_0_ = f32[66,8,128]{2,1,0:T(8,128)S(1)} collective-permute-done((f32[66,8,128]{2,1,0:T(8,128)S(1)}, f32[66,8,128]{2,1,0:T(8,128)S(1)}, u32[]{:S(2)}, u32[]{:S(2)}) %collective-permute-start.9) | collective-permute-done | bytes 270368 | tf_op jit(solution)/shard_map/ppermute | solution.py:560
  61.9 0.4 upper_end.1.over_ref
  62.3 2.4 %finish.1 = f32[9,8,4096]{2,1,0:T(8,128)} custom-call(f32[33,64,128]{2,1,0:T(8,128)S(1)} %get-tuple-element.44.refs_1_.refs_0_.refs_2_.z_ref, f32[33,16,128]{2,1,0:T(8,128)S(1)} %upper_end.1.over_ref, f32[33,48,128]{2,1,0:T(8,128)S(1)} %get-tuple-element.72.inner_ref, f32[33,16,128]{2,1,0:T(8,128)S(1)} %lower_end.1.under_ref, ...), custom_call_target="tpu_custom_call" | custom-call | flops 10813440 | bytes 8650752 | tf_op jit(solution)/shard_map/finish/pallas_call | solution.py:566
Async XLA Ops:
  1.7 4.6 %collective-permute-start = (f32[2,2,8,4224]{3,2,1,0:T(8,128)S(1)}, f32[2,2,8,4224]{3,2,1,0:T(8,128)S(1)}, u32[]{:S(2)}, u32[]{:S(2)}) collective-permute-start(f32[2,2,8,4224]{3,2,1,0:T(8,128)S(1)} %get-tuple-element.43), channel_id=1, source_target_pairs={{0,1},{1,0},{2,3},{3,2},{4,5},{5,4},{6,7},{7,6},{8,9},{9,8},{10,11... | collective-permute-start | bytes 1622024 | tf_op jit(solution)/shard_map/ppermute | solution.py:599
  2.2 11.7 %collective-permute-start.2 = (f32[47,8,128]{2,1,0:T(8,128)S(1)}, f32[47,8,128]{2,1,0:T(8,128)S(1)}, u32[]{:S(2)}, u32[]{:S(2)}) collective-permute-start(f32[47,8,128]{2,1,0:T(8,128)S(1)} %get-tuple-element.47), channel_id=1, source_target_pairs={{0,2},{2,0},{4,6},{6,4},{8,10},{10,8},{12,14},{14,12},{1,3},{3,1},... | collective-permute-start | bytes 577544 | tf_op jit(solution)/shard_map/ppermute | solution.py:560
  4.8 9.1 %collective-permute-start.3 = (f32[47,8,128]{2,1,0:T(8,128)S(1)}, f32[47,8,128]{2,1,0:T(8,128)S(1)}, u32[]{:S(2)}, u32[]{:S(2)}) collective-permute-start(f32[47,8,128]{2,1,0:T(8,128)S(1)} %get-tuple-element.48), channel_id=1, source_target_pairs={{2,4},{4,2},{6,8},{8,6},{10,12},{12,10},{3,5},{5,3},{7,9},{9,7},{1... | collective-permute-start | bytes 577544 | tf_op jit(solution)/shard_map/ppermute | solution.py:563
  6.6 7.3 %collective-permute-start.1 = (f32[33,8,128]{2,1,0:T(8,128)S(1)}, f32[33,8,128]{2,1,0:T(8,128)S(1)}, u32[]{:S(2)}, u32[]{:S(2)}) collective-permute-start(f32[33,8,128]{2,1,0:T(8,128)S(1)} %get-tuple-element.45), channel_id=1, source_target_pairs={{2,4},{4,2},{6,8},{8,6},{10,12},{12,10},{3,5},{5,3},{7,9},{9,7},{1... | collective-permute-start | bytes 405512 | tf_op jit(solution)/shard_map/ppermute | solution.py:563
  7.3 12.1 %collective-permute-start.5 = (f32[33,8,128]{2,1,0:T(8,128)S(1)}, f32[33,8,128]{2,1,0:T(8,128)S(1)}, u32[]{:S(2)}, u32[]{:S(2)}) collective-permute-start(f32[33,8,128]{2,1,0:T(8,128)S(1)} %get-tuple-element.50), channel_id=1, source_target_pairs={{0,2},{2,0},{4,6},{6,4},{8,10},{10,8},{12,14},{14,12},{1,3},{3,1},... | collective-permute-start | bytes 405512 | tf_op jit(solution)/shard_map/ppermute | solution.py:560
  14.3 12.4 %collective-permute-start.4 = (f32[66,8,128]{2,1,0:T(8,128)S(1)}, f32[66,8,128]{2,1,0:T(8,128)S(1)}, u32[]{:S(2)}, u32[]{:S(2)}) collective-permute-start(f32[66,8,128]{2,1,0:T(8,128)S(1)} %first.3.refs_4_.refs_5_), channel_id=1, source_target_pairs={{2,4},{4,2},{6,8},{8,6},{10,12},{12,10},{3,5},{5,3},{7,9},{9,7},{1... | collective-permute-start | bytes 811016 | tf_op jit(solution)/shard_map/ppermute | solution.py:563
  19.8 19.1 %collective-permute-start.7 = (f32[66,8,128]{2,1,0:T(8,128)S(1)}, f32[66,8,128]{2,1,0:T(8,128)S(1)}, u32[]{:S(2)}, u32[]{:S(2)}) collective-permute-start(f32[66,8,128]{2,1,0:T(8,128)S(1)} %first.4.refs_2_.refs_5_), channel_id=1, source_target_pairs={{0,2},{2,0},{4,6},{6,4},{8,10},{10,8},{12,14},{14,12},{1,3},{3,1},... | collective-permute-start | bytes 811016 | tf_op jit(solution)/shard_map/ppermute | solution.py:560
  27.3 16.3 %collective-permute-start.6 = (f32[66,8,128]{2,1,0:T(8,128)S(1)}, f32[66,8,128]{2,1,0:T(8,128)S(1)}, u32[]{:S(2)}, u32[]{:S(2)}) collective-permute-start(f32[66,8,128]{2,1,0:T(8,128)S(1)} %get-tuple-element.58.refs_4_.refs_5_), channel_id=1, source_target_pairs={{2,4},{4,2},{6,8},{8,6},{10,12},{12,10},{3,5},{5,3},{7,9},{9,7},{1... | collective-permute-start | bytes 811016 | tf_op jit(solution)/shard_map/ppermute | solution.py:563
  39.5 14.7 %collective-permute-start.8 = (f32[66,8,128]{2,1,0:T(8,128)S(1)}, f32[66,8,128]{2,1,0:T(8,128)S(1)}, u32[]{:S(2)}, u32[]{:S(2)}) collective-permute-start(f32[66,8,128]{2,1,0:T(8,128)S(1)} %get-tuple-element.61.refs_2_.refs_5_), channel_id=1, source_target_pairs={{0,2},{2,0},{4,6},{6,4},{8,10},{10,8},{12,14},{14,12},{1,3},{3,1},... | collective-permute-start | bytes 811016 | tf_op jit(solution)/shard_map/ppermute | solution.py:560
  44.3 15.5 %collective-permute-start.10 = (f32[66,8,128]{2,1,0:T(8,128)S(1)}, f32[66,8,128]{2,1,0:T(8,128)S(1)}, u32[]{:S(2)}, u32[]{:S(2)}) collective-permute-start(f32[66,8,128]{2,1,0:T(8,128)S(1)} %get-tuple-element.65.refs_4_.refs_5_), channel_id=1, source_target_pairs={{2,4},{4,2},{6,8},{8,6},{10,12},{12,10},{3,5},{5,3},{7,9},{9,7},{1... | collective-permute-start | bytes 811016 | tf_op jit(solution)/shard_map/ppermute | solution.py:563
  54.9 7.0 %collective-permute-start.9 = (f32[66,8,128]{2,1,0:T(8,128)S(1)}, f32[66,8,128]{2,1,0:T(8,128)S(1)}, u32[]{:S(2)}, u32[]{:S(2)}) collective-permute-start(f32[66,8,128]{2,1,0:T(8,128)S(1)} %get-tuple-element.68.refs_5_.refs_2_), channel_id=1, source_target_pairs={{0,2},{2,0},{4,6},{6,4},{8,10},{10,8},{12,14},{14,12},{1,3},{3,1},... | collective-permute-start | bytes 811016 | tf_op jit(solution)/shard_map/ppermute | solution.py:560

commit v11 on v9

--- a/solution.py
+++ b/solution.py
@@ -452,28 +452,29 @@
             lax.fori_loop(0, kept // count, functools.partial(body, turned), 0)
 
 
-def end_kernel(upper, constants, tiles, *refs):
-    edge_product(upper, constants, tiles, *refs)
-
-
-def finish_kernel(tiles, factor, z_ref, over_ref, inner_ref, under_ref, part_ref, out_ref, products, target, sem):
+def end_kernel(upper, constants, tiles, factor, *refs):
+    halo_ref, z_halo_ref, z_ref, expanded_ref, rim_ref, edge_ref, older_ref, inner_ref, part_ref, out_ref, once_ref, products = refs[:12]
+    target = refs[12] if upper else out_ref
+    products[...] = jnp.zeros_like(products)
+    edge_product(
+        upper, constants, tiles, halo_ref, z_halo_ref, z_ref, expanded_ref, rim_ref, edge_ref, older_ref, once_ref
+    )
+    low = -1 if upper else 7
+
     def series(row, tile):
-        if row < 1:
-            return over_ref[tile, sub(row + 1), :]
-        if row > 6:
-            return under_ref[tile, sub(row - 7), :]
-        return inner_ref[tile, sub(row - 1), :]
+        if 1 <= row <= 6:
+            return inner_ref[tile, sub(row - 1), :]
+        return once_ref[tile, sub(row - low), :]
 
     kept = target.shape[2] // LANES
     offset = lax.axis_index("probe") * (tiles - kept)
     count = products.shape[0]
-    products[...] = jnp.zeros_like(products)
+    steps = kept // count
 
     def body(turned, step, carry):
         for k in range(count):
             tile = step * count + k + offset
-            for low in (0, 6):
-                gradient_rows(low, 2, tile, k, series, z_ref, factor, tiles, products, turned)
+            gradient_rows(0 if upper else 6, 2, tile, k, series, z_ref, factor, tiles, products, turned)
         for k in range(count):
             cols = tile_columns(step * count + k)
 
@@ -483,10 +484,12 @@
             gradient_sums(k, products, lambda channel: part_ref[channel, :, cols], put)
         return carry
 
-    steps = kept // count
-    groups = sem.shape[0]
-
     def run(turned):
+        if not upper:
+            lax.fori_loop(0, steps, functools.partial(body, turned), 0)
+            return
+        sem = refs[13]
+        groups = sem.shape[0]
         copies = []
         for group in range(groups):
             span = (group * steps // groups, (group + 1) * steps // groups)
@@ -684,27 +687,22 @@
         [rows_of(6), pltpu.VMEM(whole, f32)],
         [products],
     )
-    ends = [
-        call(
-            functools.partial(end_kernel, upper, constants, tiles),
-            "upper_end" if upper else "lower_end",
-            2 * tiles,
-            operands,
-            rows_of(2),
-        )
-        for upper, operands in (
-            (True, (up, z_up, z, expanded, rim_up, top, once[0])),
-            (False, (down, z_down, z, expanded, rim_down, bottom, once[2])),
-        )
-    ]
+    part = call(
+        functools.partial(end_kernel, False, constants, tiles, factor),
+        "far_end",
+        8 * tiles,
+        (down, z_down, z, expanded, rim_down, bottom, once[2], series, part),
+        pltpu.VMEM(whole, f32),
+        [rows_of(2), products],
+    )
     groups = max(n for n in range(1, 5) if kept // count % n == 0)
     return call(
-        functools.partial(finish_kernel, tiles, factor),
+        functools.partial(end_kernel, True, constants, tiles, factor),
         "finish",
-        16 * tiles,
-        (z, ends[0], series, ends[1], part),
+        8 * tiles,
+        (up, z_up, z, expanded, rim_up, top, once[0], series, part),
         jax.ShapeDtypeStruct(whole, f32),
-        [products, pltpu.VMEM(whole, f32), pltpu.SemaphoreType.DMA((groups,))],
+        [rows_of(2), products, pltpu.VMEM(whole, f32), pltpu.SemaphoreType.DMA((groups,))],
         None,
         pl.BlockSpec(memory_space=pltpu.HBM),
     )

time: 64.4 us -> 64.1 us (level)
  waiting for transfers between devices: 25.4 us -> 23.9 us
  Pallas kernels: 16.7 us -> 18.1 us
    ppermute x5, waiting for transfers between devices: 25.4 us -> 23.9 us  [near(): return lax.ppermute(edge, 'row', near_pairs)]
    pallas_call x17 -> x16, Pallas kernels: 16.7 us -> 18.1 us  [call(): pl.pallas_call(kernel, out_shape=outs, in_specs=in_specs or [vmem_spec()]...]
  transfers between devices with their start and end apart: 11 -> 11, of which waited for: 5 -> 5; matrix products, arithmetic and copies ran while one was open for 0% -> 0% of each run, Pallas kernels for 19% -> 22%
where the time goes in v11:
time: 64.1 us; the launch traced here: 63.9 us
  waiting for transfers between devices  23.9 us (37%)
  starting transfers between devices  21.7 us (34%)
  Pallas kernels  18.1 us (28%)
    ppermute x5, waiting for transfers between devices, near(): return lax.ppermute(edge, 'row', near_pairs)  23.9 us
    pallas_call x16, Pallas kernels, call(): pl.pallas_call(kernel, out_shape=outs, in_specs=in_specs or [vmem_spec()]...  18.1 us
    ppermute x5, starting transfers between devices, near(): return lax.ppermute(edge, 'row', near_pairs)  17.9 us
    ppermute x5, starting transfers between devices, far(): return lax.ppermute(edge, 'row', far_pairs)  3.36 us
  transfers between devices with their start and end apart: 11, of which 5 were waited for; matrix products, arithmetic and copies ran while one was open for 0% of the time, Pallas kernels for 22%

profile of v11, /device:TPU:0, one launch (start us, length us, event | category | flops | bytes accessed | tf_op | source)
XLA Modules:
  0.0 63.9 jit_solution(9284091678615625056)
XLA Ops:
  0.0 1.7 %load.1 = (f32[2,2,8,4224]{3,2,1,0:T(8,128)S(1)}, f32[2,2,8,4224]{3,2,1,0:T(8,128)S(1)}, f32[2,8,4224]{2,1,0:T(8,128)S(1)}, f32[9,8,4224]{2,1,0:T(8,128)S(1)}, f...) custom-call(f32[2,2,8,8192]{3,2,1,0:T(8,128)} %probes_ref.1, f32[2,8,8192]{2,1,0:T(8,128)} %observed_ref.1, ...), custom_call_target="tpu_custom_call" | custom-call | flops 2048000 | bytes 1638400 | tf_op jit(solution)/shard_map/load/pallas_call | solution.py:569
  1.7 0.5 collective-permute-start
  2.2 2.6 %collective-permute-start.2 = (f32[47,8,128]{2,1,0:T(8,128)S(1)}, f32[47,8,128]{2,1,0:T(8,128)S(1)}, u32[]{:S(2)}, u32[]{:S(2)}) collective-permute-start(f32[47,8,128]{2,1,0:T(8,128)S(1)} %get-tuple-element.46), channel_id=1, source_target_pairs={{0,2},{2,0},{4,6},{6,4},{8,10},{10,8},{12,14},{14,12},{1,3},{3,1},... | collective-permute-start | bytes 577544 | tf_op jit(solution)/shard_map/ppermute | solution.py:563
  4.8 0.7 %collective-permute-start.3 = (f32[47,8,128]{2,1,0:T(8,128)S(1)}, f32[47,8,128]{2,1,0:T(8,128)S(1)}, u32[]{:S(2)}, u32[]{:S(2)}) collective-permute-start(f32[47,8,128]{2,1,0:T(8,128)S(1)} %get-tuple-element.47), channel_id=1, source_target_pairs={{2,4},{4,2},{6,8},{8,6},{10,12},{12,10},{3,5},{5,3},{7,9},{9,7},{1... | collective-permute-start | bytes 577544 | tf_op jit(solution)/shard_map/ppermute | solution.py:566
  5.5 0.8 %prep.1.refs_2_.refs_1_.refs_3_ = f32[5,33,64,128]{3,2,1,0:T(8,128)S(1)} custom-call(f32[9,8,4224]{2,1,0:T(8,128)S(1)} %get-tuple-element.39.window_ref), custom_call_target="tpu_custom_call" | custom-call | flops 27033600 | bytes 21626880 | tf_op jit(solution)/shard_map/prep/pallas_call | solution.py:569
  6.3 0.0 collective-permute-done.other_ref
  6.3 0.3 layout.1
  6.6 0.7 %collective-permute-start.1 = (f32[33,8,128]{2,1,0:T(8,128)S(1)}, f32[33,8,128]{2,1,0:T(8,128)S(1)}, u32[]{:S(2)}, u32[]{:S(2)}) collective-permute-start(f32[33,8,128]{2,1,0:T(8,128)S(1)} %get-tuple-element.42), channel_id=1, source_target_pairs={{2,4},{4,2},{6,8},{8,6},{10,12},{12,10},{3,5},{5,3},{7,9},{9,7},{1... | collective-permute-start | bytes 405512 | tf_op jit(solution)/shard_map/ppermute | solution.py:566
  7.3 5.6 %collective-permute-start.5 = (f32[33,8,128]{2,1,0:T(8,128)S(1)}, f32[33,8,128]{2,1,0:T(8,128)S(1)}, u32[]{:S(2)}, u32[]{:S(2)}) collective-permute-start(f32[33,8,128]{2,1,0:T(8,128)S(1)} %get-tuple-element.51), channel_id=1, source_target_pairs={{0,2},{2,0},{4,6},{6,4},{8,10},{10,8},{12,14},{14,12},{1,3},{3,1},... | collective-permute-start | bytes 405512 | tf_op jit(solution)/shard_map/ppermute | solution.py:563
  12.9 1.0 %collective-permute-done.2.up_ref = f32[47,8,128]{2,1,0:T(8,128)S(1)} collective-permute-done((f32[47,8,128]{2,1,0:T(8,128)S(1)}, f32[47,8,128]{2,1,0:T(8,128)S(1)}, u32[]{:S(2)}, u32[]{:S(2)}) %collective-permute-start.2) | collective-permute-done | bytes 192544 | tf_op jit(solution)/shard_map/ppermute | solution.py:563
  13.9 0.0 collective-permute-done.3.down_ref
  13.9 1.1 %border.1 = (f32[33,9,8,128]{3,2,1,0:T(8,128)S(1)}, f32[5,33,8,128]{3,2,1,0:T(8,128)S(1)}, f32[5,33,8,128]{3,2,1,0:T(8,128)S(1)}) custom-call(f32[2,8,4224]{2,1,0:T(8,128)S(1)} %get-tuple-element.45.seen_ref, f32[47,8,128]{2,1,0:T(8,128)S(1)} %collective-permute-done.2.up_ref, f32[47,8,128]{2,1,0:T(8,128)S(1)} %collective-permute-done.3.down_ref), custom_call_target="tpu_custom_call" | custom-call | flops 6082560 | bytes 4866048 | tf_op jit(solution)/shard_map/border/pallas_call | solution.py:569
  15.1 0.0 collective-permute-done.1.refs_0_.refs_1_
  15.1 0.4 first.3.refs_4_.refs_5_
  15.5 0.7 %collective-permute-start.4 = (f32[66,8,128]{2,1,0:T(8,128)S(1)}, f32[66,8,128]{2,1,0:T(8,128)S(1)}, u32[]{:S(2)}, u32[]{:S(2)}) collective-permute-start(f32[66,8,128]{2,1,0:T(8,128)S(1)} %first.3.refs_4_.refs_5_), channel_id=1, source_target_pairs={{2,4},{4,2},{6,8},{8,6},{10,12},{12,10},{3,5},{5,3},{7,9},{9,7},{1... | collective-permute-start | bytes 811016 | tf_op jit(solution)/shard_map/ppermute | solution.py:566
  16.2 3.2 %collective-permute-done.5.refs_0_.refs_1_ = f32[33,8,128]{2,1,0:T(8,128)S(1)} collective-permute-done((f32[33,8,128]{2,1,0:T(8,128)S(1)}, f32[33,8,128]{2,1,0:T(8,128)S(1)}, u32[]{:S(2)}, u32[]{:S(2)}) %collective-permute-start.5) | collective-permute-done | bytes 135200 | tf_op jit(solution)/shard_map/ppermute | solution.py:563
  19.4 0.4 first.4.refs_2_.refs_5_
  19.8 4.7 %collective-permute-start.7 = (f32[66,8,128]{2,1,0:T(8,128)S(1)}, f32[66,8,128]{2,1,0:T(8,128)S(1)}, u32[]{:S(2)}, u32[]{:S(2)}) collective-permute-start(f32[66,8,128]{2,1,0:T(8,128)S(1)} %first.4.refs_2_.refs_5_), channel_id=1, source_target_pairs={{0,2},{2,0},{4,6},{6,4},{8,10},{10,8},{12,14},{14,12},{1,3},{3,1},... | collective-permute-start | bytes 811016 | tf_op jit(solution)/shard_map/ppermute | solution.py:563
  24.4 0.7 %first.5.refs_3_ = f32[33,32,128]{2,1,0:T(8,128)S(1)} custom-call(f32[33,64,128]{2,1,0:T(8,128)S(1)} %get-tuple-element.43.refs_1_.refs_0_.refs_2_, f32[5,33,64,128]{3,2,1,0:T(8,128)S(1)} %prep.1.refs_2_.refs_1_.refs_3_), custom_call_target="tpu_custom_call" | custom-call | flops 2703360 | bytes 2162688 | tf_op jit(solution)/shard_map/first/pallas_call | solution.py:569
  25.1 1.6 %middle.2 = (f32[33,48,128]{2,1,0:T(8,128)S(1)}, f32[33,32,128]{2,1,0:T(8,128)S(1)}) custom-call(f32[33,64,128]{2,1,0:T(8,128)S(1)} %get-tuple-element.43.refs_1_.refs_0_.refs_2_, f32[5,33,64,128]{3,2,1,0:T(8,128)S(1)} %prep.1.refs_2_.refs_1_.refs_3_, f32[66,8,128]{2,1,0:T(8,128)S(1)} %first.4.refs_2_.refs_5_, f32[33,32,128]{2,1,0:T(8,128)S(1)} %first.5.refs_3_, ...), custom_call_target="tpu_custom_call" | custom-call | flops 6758400 | bytes 5406720 | tf_op jit(solution)/shard_map/middle/pallas_call | solution.py:569
  26.7 0.0 collective-permute-done.4.refs_0_
  26.7 0.7 %lower.2 = (f32[33,16,128]{2,1,0:T(8,128)S(1)}, f32[66,8,128]{2,1,0:T(8,128)S(1)}) custom-call(f32[66,8,128]{2,1,0:T(8,128)S(1)} %collective-permute-done.4.refs_0_, f32[33,8,128]{2,1,0:T(8,128)S(1)} %collective-permute-done.1.refs_0_.refs_1_, f32[33,64,128]{2,1,0:T(8,128)S(1)} %get-tuple-element.43.refs_1_.refs_0_.refs_2_, ...), custom_call_target="tpu_custom_call" | custom-call | flops 2703360 | bytes 2162688 | tf_op jit(solution)/shard_map/lower/pallas_call | solution.py:569
  27.4 0.7 %collective-permute-start.6 = (f32[66,8,128]{2,1,0:T(8,128)S(1)}, f32[66,8,128]{2,1,0:T(8,128)S(1)}, u32[]{:S(2)}, u32[]{:S(2)}) collective-permute-start(f32[66,8,128]{2,1,0:T(8,128)S(1)} %get-tuple-element.54.refs_4_.refs_5_), channel_id=1, source_target_pairs={{2,4},{4,2},{6,8},{8,6},{10,12},{12,10},{3,5},{5,3},{7,9},{9,7},{1... | collective-permute-start | bytes 811016 | tf_op jit(solution)/shard_map/ppermute | solution.py:566
  28.1 10.7 %collective-permute-done.7.refs_0_ = f32[66,8,128]{2,1,0:T(8,128)S(1)} collective-permute-done((f32[66,8,128]{2,1,0:T(8,128)S(1)}, f32[66,8,128]{2,1,0:T(8,128)S(1)}, u32[]{:S(2)}, u32[]{:S(2)}) %collective-permute-start.7) | collective-permute-done | bytes 270368 | tf_op jit(solution)/shard_map/ppermute | solution.py:563
  38.8 0.7 %upper.2 = (f32[33,16,128]{2,1,0:T(8,128)S(1)}, f32[66,8,128]{2,1,0:T(8,128)S(1)}) custom-call(f32[66,8,128]{2,1,0:T(8,128)S(1)} %collective-permute-done.7.refs_0_, f32[33,8,128]{2,1,0:T(8,128)S(1)} %collective-permute-done.5.refs_0_.refs_1_, f32[33,64,128]{2,1,0:T(8,128)S(1)} %get-tuple-element.43.refs_1_.refs_0_.refs_2_, ...), custom_call_target="tpu_custom_call" | custom-call | flops 2703360 | bytes 2162688 | tf_op jit(solution)/shard_map/upper/pallas_call | solution.py:569
  39.5 2.5 %collective-permute-start.8 = (f32[66,8,128]{2,1,0:T(8,128)S(1)}, f32[66,8,128]{2,1,0:T(8,128)S(1)}, u32[]{:S(2)}, u32[]{:S(2)}) collective-permute-start(f32[66,8,128]{2,1,0:T(8,128)S(1)} %get-tuple-element.57.refs_2_.refs_5_), channel_id=1, source_target_pairs={{0,2},{2,0},{4,6},{6,4},{8,10},{10,8},{12,14},{14,12},{1,3},{3,1},... | collective-permute-start | bytes 811016 | tf_op jit(solution)/shard_map/ppermute | solution.py:563
  42.0 1.6 %middle.3 = (f32[33,48,128]{2,1,0:T(8,128)S(1)}, f32[33,32,128]{2,1,0:T(8,128)S(1)}) custom-call(f32[33,64,128]{2,1,0:T(8,128)S(1)} %get-tuple-element.43.refs_1_.refs_0_.refs_2_, f32[5,33,64,128]{3,2,1,0:T(8,128)S(1)} %prep.1.refs_2_.refs_1_.refs_3_, f32[66,8,128]{2,1,0:T(8,128)S(1)} %get-tuple-element.57.refs_2_.refs_5_, ...), custom_call_target="tpu_custom_call" | custom-call | flops 6758400 | bytes 5406720 | tf_op jit(solution)/shard_map/middle/pallas_call | solution.py:569
  43.6 0.0 collective-permute-done.6.refs_0_
  43.6 0.7 %lower.3 = (f32[33,16,128]{2,1,0:T(8,128)S(1)}, f32[66,8,128]{2,1,0:T(8,128)S(1)}) custom-call(f32[66,8,128]{2,1,0:T(8,128)S(1)} %collective-permute-done.6.refs_0_, f32[33,8,128]{2,1,0:T(8,128)S(1)} %collective-permute-done.1.refs_0_.refs_1_, f32[33,64,128]{2,1,0:T(8,128)S(1)} %get-tuple-element.43.refs_1_.refs_0_.refs_2_, ...), custom_call_target="tpu_custom_call" | custom-call | flops 2703360 | bytes 2162688 | tf_op jit(solution)/shard_map/lower/pallas_call | solution.py:569
  44.3 0.7 %collective-permute-start.10 = (f32[66,8,128]{2,1,0:T(8,128)S(1)}, f32[66,8,128]{2,1,0:T(8,128)S(1)}, u32[]{:S(2)}, u32[]{:S(2)}) collective-permute-start(f32[66,8,128]{2,1,0:T(8,128)S(1)} %get-tuple-element.61.refs_4_.refs_5_), channel_id=1, source_target_pairs={{2,4},{4,2},{6,8},{8,6},{10,12},{12,10},{3,5},{5,3},{7,9},{9,7},{1... | collective-permute-start | bytes 811016 | tf_op jit(solution)/shard_map/ppermute | solution.py:566
  45.0 8.6 %collective-permute-done.8.refs_0_ = f32[66,8,128]{2,1,0:T(8,128)S(1)} collective-permute-done((f32[66,8,128]{2,1,0:T(8,128)S(1)}, f32[66,8,128]{2,1,0:T(8,128)S(1)}, u32[]{:S(2)}, u32[]{:S(2)}) %collective-permute-start.8) | collective-permute-done | bytes 270368 | tf_op jit(solution)/shard_map/ppermute | solution.py:563
  53.6 0.7 %upper.3 = (f32[33,16,128]{2,1,0:T(8,128)S(1)}, f32[66,8,128]{2,1,0:T(8,128)S(1)}) custom-call(f32[66,8,128]{2,1,0:T(8,128)S(1)} %collective-permute-done.8.refs_0_, f32[33,8,128]{2,1,0:T(8,128)S(1)} %collective-permute-done.5.refs_0_.refs_1_, f32[33,64,128]{2,1,0:T(8,128)S(1)} %get-tuple-element.43.refs_1_.refs_0_.refs_2_, ...), custom_call_target="tpu_custom_call" | custom-call | flops 2703360 | bytes 2162688 | tf_op jit(solution)/shard_map/upper/pallas_call | solution.py:569
  54.4 2.5 %collective-permute-start.9 = (f32[66,8,128]{2,1,0:T(8,128)S(1)}, f32[66,8,128]{2,1,0:T(8,128)S(1)}, u32[]{:S(2)}, u32[]{:S(2)}) collective-permute-start(f32[66,8,128]{2,1,0:T(8,128)S(1)} %get-tuple-element.64.refs_2_.refs_5_), channel_id=1, source_target_pairs={{0,2},{2,0},{4,6},{6,4},{8,10},{10,8},{12,14},{14,12},{1,3},{3,1},... | collective-permute-start | bytes 811016 | tf_op jit(solution)/shard_map/ppermute | solution.py:563
  56.9 2.4 %gradient.1 = (f32[33,48,128]{2,1,0:T(8,128)S(1)}, f32[9,8,4096]{2,1,0:T(8,128)S(1)}) custom-call(f32[33,64,128]{2,1,0:T(8,128)S(1)} %get-tuple-element.43.refs_1_.refs_0_.refs_2_, f32[5,33,64,128]{3,2,1,0:T(8,128)S(1)} %prep.1.refs_2_.refs_1_.refs_3_, f32[66,8,128]{2,1,0:T(8,128)S(1)} %get-tuple-element.64.refs_2_.refs_5_, ...), custom_call_target="tpu_custom_call" | custom-call | flops 16220160 | bytes 12976128 | tf_op jit(solution)/shard_map/gradient/pallas_call | solution.py:569
  59.3 0.0 collective-permute-done.10.refs_0_
  59.3 1.8 %far_end.1.refs_8_ = f32[9,8,4096]{2,1,0:T(8,128)S(1)} custom-call(f32[66,8,128]{2,1,0:T(8,128)S(1)} %collective-permute-done.10.refs_0_, f32[33,8,128]{2,1,0:T(8,128)S(1)} %collective-permute-done.1.refs_0_.refs_1_, f32[33,64,128]{2,1,0:T(8,128)S(1)} %get-tuple-element.43.refs_1_.refs_0_.refs_2_, f32[5,33,64,128]{3,2,1,0:T(8,128)S(1)} %prep.1.refs_2_.refs_1_.refs_3_, ...), custom_call_target="tpu_custom_call" | custom-call | flops 5406720 | bytes 4325376 | tf_op jit(solution)/shard_map/far_end/pallas_call | solution.py:569
  61.1 0.3 collective-permute-done.9.refs_0_
  61.3 2.5 %finish.1 = f32[9,8,4096]{2,1,0:T(8,128)} custom-call(f32[66,8,128]{2,1,0:T(8,128)S(1)} %collective-permute-done.9.refs_0_, f32[33,8,128]{2,1,0:T(8,128)S(1)} %collective-permute-done.5.refs_0_.refs_1_, f32[33,64,128]{2,1,0:T(8,128)S(1)} %get-tuple-element.43.refs_1_.refs_0_.refs_2_, f32[5,33,64,128]{3,2,1,0:T(8,128)S(1)} %prep.1.refs_2_.refs_1_.refs_3_, ...), custom_call_target="tpu_custom_call" | custom-call | flops 5406720 | bytes 4325376 | tf_op jit(solution)/shard_map/finish/pallas_call | solution.py:569
Async XLA Ops:
  1.7 4.6 %collective-permute-start = (f32[2,2,8,4224]{3,2,1,0:T(8,128)S(1)}, f32[2,2,8,4224]{3,2,1,0:T(8,128)S(1)}, u32[]{:S(2)}, u32[]{:S(2)}) collective-permute-start(f32[2,2,8,4224]{3,2,1,0:T(8,128)S(1)} %get-tuple-element.41), channel_id=1, source_target_pairs={{0,1},{1,0},{2,3},{3,2},{4,5},{5,4},{6,7},{7,6},{8,9},{9,8},{10,11... | collective-permute-start | bytes 1622024 | tf_op jit(solution)/shard_map/ppermute | solution.py:602
  2.2 11.7 %collective-permute-start.2 = (f32[47,8,128]{2,1,0:T(8,128)S(1)}, f32[47,8,128]{2,1,0:T(8,128)S(1)}, u32[]{:S(2)}, u32[]{:S(2)}) collective-permute-start(f32[47,8,128]{2,1,0:T(8,128)S(1)} %get-tuple-element.46), channel_id=1, source_target_pairs={{0,2},{2,0},{4,6},{6,4},{8,10},{10,8},{12,14},{14,12},{1,3},{3,1},... | collective-permute-start | bytes 577544 | tf_op jit(solution)/shard_map/ppermute | solution.py:563
  4.8 9.1 %collective-permute-start.3 = (f32[47,8,128]{2,1,0:T(8,128)S(1)}, f32[47,8,128]{2,1,0:T(8,128)S(1)}, u32[]{:S(2)}, u32[]{:S(2)}) collective-permute-start(f32[47,8,128]{2,1,0:T(8,128)S(1)} %get-tuple-element.47), channel_id=1, source_target_pairs={{2,4},{4,2},{6,8},{8,6},{10,12},{12,10},{3,5},{5,3},{7,9},{9,7},{1... | collective-permute-start | bytes 577544 | tf_op jit(solution)/shard_map/ppermute | solution.py:566
  6.6 8.5 %collective-permute-start.1 = (f32[33,8,128]{2,1,0:T(8,128)S(1)}, f32[33,8,128]{2,1,0:T(8,128)S(1)}, u32[]{:S(2)}, u32[]{:S(2)}) collective-permute-start(f32[33,8,128]{2,1,0:T(8,128)S(1)} %get-tuple-element.42), channel_id=1, source_target_pairs={{2,4},{4,2},{6,8},{8,6},{10,12},{12,10},{3,5},{5,3},{7,9},{9,7},{1... | collective-permute-start | bytes 405512 | tf_op jit(solution)/shard_map/ppermute | solution.py:566
  7.3 12.1 %collective-permute-start.5 = (f32[33,8,128]{2,1,0:T(8,128)S(1)}, f32[33,8,128]{2,1,0:T(8,128)S(1)}, u32[]{:S(2)}, u32[]{:S(2)}) collective-permute-start(f32[33,8,128]{2,1,0:T(8,128)S(1)} %get-tuple-element.51), channel_id=1, source_target_pairs={{0,2},{2,0},{4,6},{6,4},{8,10},{10,8},{12,14},{14,12},{1,3},{3,1},... | collective-permute-start | bytes 405512 | tf_op jit(solution)/shard_map/ppermute | solution.py:563
  15.5 11.2 %collective-permute-start.4 = (f32[66,8,128]{2,1,0:T(8,128)S(1)}, f32[66,8,128]{2,1,0:T(8,128)S(1)}, u32[]{:S(2)}, u32[]{:S(2)}) collective-permute-start(f32[66,8,128]{2,1,0:T(8,128)S(1)} %first.3.refs_4_.refs_5_), channel_id=1, source_target_pairs={{2,4},{4,2},{6,8},{8,6},{10,12},{12,10},{3,5},{5,3},{7,9},{9,7},{1... | collective-permute-start | bytes 811016 | tf_op jit(solution)/shard_map/ppermute | solution.py:566
  19.8 19.0 %collective-permute-start.7 = (f32[66,8,128]{2,1,0:T(8,128)S(1)}, f32[66,8,128]{2,1,0:T(8,128)S(1)}, u32[]{:S(2)}, u32[]{:S(2)}) collective-permute-start(f32[66,8,128]{2,1,0:T(8,128)S(1)} %first.4.refs_2_.refs_5_), channel_id=1, source_target_pairs={{0,2},{2,0},{4,6},{6,4},{8,10},{10,8},{12,14},{14,12},{1,3},{3,1},... | collective-permute-start | bytes 811016 | tf_op jit(solution)/shard_map/ppermute | solution.py:563
  27.4 16.2 %collective-permute-start.6 = (f32[66,8,128]{2,1,0:T(8,128)S(1)}, f32[66,8,128]{2,1,0:T(8,128)S(1)}, u32[]{:S(2)}, u32[]{:S(2)}) collective-permute-start(f32[66,8,128]{2,1,0:T(8,128)S(1)} %get-tuple-element.54.refs_4_.refs_5_), channel_id=1, source_target_pairs={{2,4},{4,2},{6,8},{8,6},{10,12},{12,10},{3,5},{5,3},{7,9},{9,7},{1... | collective-permute-start | bytes 811016 | tf_op jit(solution)/shard_map/ppermute | solution.py:566
  39.5 14.1 %collective-permute-start.8 = (f32[66,8,128]{2,1,0:T(8,128)S(1)}, f32[66,8,128]{2,1,0:T(8,128)S(1)}, u32[]{:S(2)}, u32[]{:S(2)}) collective-permute-start(f32[66,8,128]{2,1,0:T(8,128)S(1)} %get-tuple-element.57.refs_2_.refs_5_), channel_id=1, source_target_pairs={{0,2},{2,0},{4,6},{6,4},{8,10},{10,8},{12,14},{14,12},{1,3},{3,1},... | collective-permute-start | bytes 811016 | tf_op jit(solution)/shard_map/ppermute | solution.py:563
  44.3 15.0 %collective-permute-start.10 = (f32[66,8,128]{2,1,0:T(8,128)S(1)}, f32[66,8,128]{2,1,0:T(8,128)S(1)}, u32[]{:S(2)}, u32[]{:S(2)}) collective-permute-start(f32[66,8,128]{2,1,0:T(8,128)S(1)} %get-tuple-element.61.refs_4_.refs_5_), channel_id=1, source_target_pairs={{2,4},{4,2},{6,8},{8,6},{10,12},{12,10},{3,5},{5,3},{7,9},{9,7},{1... | collective-permute-start | bytes 811016 | tf_op jit(solution)/shard_map/ppermute | solution.py:566
  54.4 7.0 %collective-permute-start.9 = (f32[66,8,128]{2,1,0:T(8,128)S(1)}, f32[66,8,128]{2,1,0:T(8,128)S(1)}, u32[]{:S(2)}, u32[]{:S(2)}) collective-permute-start(f32[66,8,128]{2,1,0:T(8,128)S(1)} %get-tuple-element.64.refs_2_.refs_5_), channel_id=1, source_target_pairs={{0,2},{2,0},{4,6},{6,4},{8,10},{10,8},{12,14},{14,12},{1,3},{3,1},... | collective-permute-start | bytes 811016 | tf_op jit(solution)/shard_map/ppermute | solution.py:563
